TPU v7x, 128 devices: a whole 4x4x4 slice. The times are simulated.
128 devices in a mesh: row: 4 (over x_hi, core), col: 32 (over x_lo, z, y).
Axes of the slice: x: 4 (x_hi: 2, x_lo: 2; x = x_hi * 2 + x_lo), y: 4, z: 4, core: 2. Of those that a mesh axis runs over, the one named last changes fastest.
Arguments:
- block_in: bfloat16 [32, 512, 2048], P('col', 'row'), may hold values from -6 to 6
- gain_attn: float32 [2048], replicated, may hold values from 0.25 to 1.75
- w_query: bfloat16 [2048, 2048], P('col', 'row'), may hold values from -0.125 to 0.125
- w_keyval: bfloat16 [2048, 4, 256], P('col', 'row'), may hold values from -0.125 to 0.125
- w_out: bfloat16 [2048, 2048], P('col', 'row'), may hold values from -0.5 to 0.5
- gain_ffn: float32 [2048], replicated, may hold values from 0.25 to 1.75
- w_shared_in: bfloat16 [2048, 2, 512], P('col', None, 'row'), may hold values from -0.125 to 0.125
- w_shared_out: bfloat16 [2048, 512], P('col', 'row'), may hold values from -0.5 to 0.5
- w_router: bfloat16 [2048, 256], replicated, may hold values from -0.0625 to 0.0625
- w_expert_in: bfloat16 [256, 2048, 1024], P(('row', 'col')), may hold values from -0.125 to 0.125
- w_expert_out: bfloat16 [256, 2048, 512], P(('row', 'col')), may hold values from -1 to 1
- doc_lengths: int32 [32, 4], P('col'), may hold values from 1 to 385, 512 in all within a row
- routes: int32 [32, 512, 8], P('col', 'row'), may hold values from 0 to 255, all different within a row; in each aligned block of 128 rows (0 to 127, 128 to 255, ..., all dimensions but the last counted through in order) at most 6 rows name the same one
- cotangent: bfloat16 [32, 512, 2048], P('col', 'row'), may hold values from -6 to 6
Outputs:
- block_out: bfloat16 [32, 512, 2048], P('col', 'row')
- grad_input: float32 [32, 512, 2048], P('col', 'row')
- grad_gain_attn: float32 [2048], replicated
- grad_query: float32 [2048, 2048], P('col', 'row')
- grad_keyval: float32 [2048, 4, 256], P('col', 'row')
- grad_out: float32 [2048, 2048], P('col', 'row')
- grad_gain_ffn: float32 [2048], replicated
- grad_shared_in: float32 [2048, 2, 512], P('col', None, 'row')
- grad_shared_out: float32 [2048, 512], P('col', 'row')
- grad_router: float32 [2048, 256], replicated
- grad_expert_in: float32 [256, 2048, 1024], P(('row', 'col'))
- grad_expert_out: float32 [256, 2048, 512], P(('row', 'col'))
Inputs may be any that keep to these rules, and one draw needn't show every extreme that they name: Among the routes of the 128 tokens of one device (groups and rows in order) no expert is named more than 6 times. `doc_lengths`: each group's documents fill its 512 tokens in order; the longest has 385 tokens.
All inputs are finite; a program needn't handle non-finite values.
Results may differ from a plain program's by a relative error of at most 0.028.
Values may be sent and summed in bfloat16 or wider, within the bound.
A program may use at most 256 MiB of HBM per device.

v0:
```python
import jax
import jax.numpy as jnp
from jax import lax
from jax.sharding import PartitionSpec as P

epsilon = 1e-06
rope_base = 10000.0
masked_score = -1e30


def layout(lengths, token_count):
    bounds = jnp.cumsum(lengths)
    places = jnp.arange(token_count, dtype=jnp.int32)
    segment = jnp.sum((places[:, None] >= bounds[None, :]).astype(jnp.int32), axis=1)
    starts = bounds - lengths
    owners = segment[:, None] == jnp.arange(lengths.shape[0], dtype=jnp.int32)[None, :]
    begins = jnp.sum(jnp.where(owners, starts[None, :], 0), axis=1)
    return (segment, places - begins)


def rotary(positions, head_size):
    half_size = head_size // 2
    spread = jnp.arange(half_size, dtype=jnp.float32) * (2.0 / head_size)
    frequency = rope_base ** (-spread)
    angles = positions.astype(jnp.float32)[:, None] * frequency[None, :]
    return (jnp.cos(angles), jnp.sin(angles))


def rotate(values, cosine, sine_table):
    half_size = values.shape[-1] // 2
    leading = values[..., :half_size]
    trailing = values[..., half_size:]
    cosine = cosine[:, None, :]
    sine_table = sine_table[:, None, :]
    return jnp.concatenate(
        [leading * cosine - trailing * sine_table, trailing * cosine + leading * sine_table],
        axis=-1,
    )


def normalize(values, gain):
    factor = lax.rsqrt(jnp.mean(values * values, axis=1, keepdims=True) + epsilon)
    return (factor, (values * factor * gain).astype(jnp.bfloat16))


def norm_back(values, factor, gain, incoming):
    weighted = gain * incoming
    gain_grad = jnp.sum(incoming * values * factor, axis=0)
    input_grad = factor * weighted - values * factor**3 * jnp.mean(
        weighted * values, axis=1, keepdims=True
    )
    return (gain_grad, input_grad)


def swish_parts(pre_act):
    logistic = jax.nn.sigmoid(pre_act)
    return (pre_act * logistic, logistic * (1.0 + pre_act * (1.0 - logistic)))


def matmul(matrix, partner):
    return jnp.dot(matrix, partner, preferred_element_type=jnp.float32)


def matmul_t(matrix, partner):
    return lax.dot_general(
        matrix, partner, (((1,), (1,)), ((), ())), preferred_element_type=jnp.float32
    )


def outer_sum(matrix, partner):
    return lax.dot_general(
        matrix, partner, (((0,), (0,)), ((), ())), preferred_element_type=jnp.float32
    )


def group_rows(values):
    return lax.all_gather(values, "row", axis=0, tiled=True)


def group_sums(producer, rows_dev):
    return lax.psum_scatter(
        producer(jnp.int32(0), lax.axis_size("row") * rows_dev),
        "row",
        scatter_dimension=0,
        tiled=True,
    )


def to_experts(values):
    return lax.all_to_all(values, ("row", "col"), split_axis=0, concat_axis=1, tiled=True)


def from_experts(values):
    return lax.all_to_all(values, ("row", "col"), split_axis=1, concat_axis=0, tiled=True)


def per_device(
    block_in,
    gain_attn,
    w_query,
    w_keyval,
    w_out,
    gain_ffn,
    w_shared_in,
    w_shared_out,
    w_router,
    w_expert_in,
    w_expert_out,
    doc_lengths,
    routes,
    cotangent,
):
    row_count = lax.axis_size("row")
    rows_dev = block_in.shape[1]
    model_width = block_in.shape[2]
    group_tok = rows_dev * row_count
    head_size = w_keyval.shape[2] // 2
    local_heads = w_query.shape[1] // head_size
    local_kv = w_keyval.shape[1]
    group_size = local_heads // local_kv
    expert_count = w_router.shape[1]
    expert_ff = w_expert_out.shape[2]
    top_k = routes.shape[2]
    capacity = max(2, 3 * rows_dev * top_k // (2 * expert_count))
    block_rows = min(512, group_tok)
    block_total = group_tok // block_rows
    inv_root = head_size ** (-0.5)
    inputs = block_in.reshape(rows_dev, model_width).astype(jnp.float32)
    full_query, full_keyval, full_out, full_shared_in, full_shared_out = (
        lax.all_gather(w_query, "col", axis=0, tiled=True),
        lax.all_gather(w_keyval, "col", axis=0, tiled=True),
        lax.all_gather(w_out, "col", axis=0, tiled=True),
        lax.all_gather(w_shared_in, "col", axis=0, tiled=True),
        lax.all_gather(w_shared_out, "col", axis=0, tiled=True),
    )
    scale_one, normed_one = normalize(inputs, gain_attn)
    group_one = group_rows(normed_one)
    segment, position = layout(doc_lengths.reshape(-1), group_tok)
    cosine, sine_table = rotary(position, head_size)
    query_pre = matmul(group_one, full_query).reshape(group_tok, local_heads, head_size)
    query_rot = rotate(query_pre, cosine, sine_table).astype(jnp.bfloat16)
    keyval_pre = jnp.einsum(
        "td,dah->tah", group_one, full_keyval, preferred_element_type=jnp.float32
    )
    key_rows = rotate(keyval_pre[..., :head_size], cosine, sine_table).astype(jnp.bfloat16)
    value_rows = keyval_pre[..., head_size:].astype(jnp.bfloat16)
    places = jnp.arange(group_tok, dtype=jnp.int32)

    def block_scores(block_index):
        first_row = block_index * block_rows
        query_block = query_rot.reshape(block_rows, local_kv, group_size, head_size)
        rows_here = first_row + jnp.arange(block_rows, dtype=jnp.int32)
        allowed = (segment[:, None] == segment[None, :]) & (rows_here[:, None] >= places[None, :])
        scores = (
            jnp.einsum("qagd,kad->agqk", query_block, key_rows, preferred_element_type=jnp.float32)
            * inv_root
        )
        return (query_block, jnp.where(allowed[None, None], scores, masked_score))

    def attend_block(block_index):
        query_block, scores = block_scores(block_index)
        highest = jnp.max(scores, axis=3, keepdims=True)
        weights = jnp.exp(scores - highest)
        totals = jnp.sum(weights, axis=3, keepdims=True)
        weights_low = (weights / totals).astype(jnp.bfloat16)
        blended = jnp.einsum(
            "agqk,kad->qagd", weights_low, value_rows, preferred_element_type=jnp.float32
        )
        return (
            blended.reshape(block_rows, local_heads * head_size).astype(jnp.bfloat16),
            highest + jnp.log(totals),
        )

    attended, log_totals = lax.map(attend_block, jnp.arange(block_total, dtype=jnp.int32))
    attended = attended.reshape(group_tok, local_heads * head_size)

    def attn_term(offset, amount):
        return matmul_t(attended, full_out)

    hidden_state = inputs + group_sums(attn_term, rows_dev)
    scale_two, normed_two = normalize(hidden_state, gain_ffn)
    group_two = group_rows(normed_two)
    shared_pre = jnp.einsum(
        "td,dcf->tcf", group_two, full_shared_in, preferred_element_type=jnp.float32
    )
    shared_act, shared_slope = swish_parts(shared_pre[:, 0])
    shared_hidden = (shared_act * shared_pre[:, 1]).astype(jnp.bfloat16)

    def shared_term(offset, amount):
        return matmul_t(shared_hidden, full_shared_out)

    shared_branch = group_sums(shared_term, rows_dev)
    route_ids = routes.reshape(rows_dev, top_k)
    logits = matmul(normed_two, w_router)
    chosen = route_ids[:, :, None] == jnp.arange(expert_count, dtype=jnp.int32)[None, None, :]
    picked = jnp.sum(jnp.where(chosen, logits[:, None, :], 0.0), axis=2)
    scores_sig = jax.nn.sigmoid(picked)
    score_sum = jnp.sum(scores_sig, axis=1, keepdims=True)
    gate_weights = scores_sig / score_sum
    flat_routes = route_ids.reshape(-1)
    onehot = (flat_routes[:, None] == jnp.arange(expert_count, dtype=jnp.int32)[None, :]).astype(
        jnp.int32
    )
    earlier = jnp.cumsum(onehot, axis=0) - onehot
    route_rank = jnp.sum(earlier * onehot, axis=1)
    slot_index = flat_routes * capacity + route_rank
    slot_table = (
        jnp.zeros((expert_count * capacity,), jnp.int32)
        .at[slot_index]
        .set(jnp.arange(rows_dev * top_k, dtype=jnp.int32) + 1)
    )
    filled = slot_table > 0
    route_of = jnp.maximum(slot_table - 1, 0)
    zero_low = jnp.zeros((), jnp.bfloat16)
    send_rows = jnp.where(filled[:, None], normed_two[route_of // top_k], zero_low).reshape(
        expert_count, capacity, model_width
    )
    received = to_experts(send_rows)
    expert_pre = jnp.einsum(
        "esd,edf->esf", received, w_expert_in, preferred_element_type=jnp.float32
    )
    expert_act, expert_slope = swish_parts(expert_pre[..., :expert_ff])
    expert_hidden = (expert_act * expert_pre[..., expert_ff:]).astype(jnp.bfloat16)
    expert_out = jnp.einsum(
        "esf,edf->esd", expert_hidden, w_expert_out, preferred_element_type=jnp.float32
    ).astype(jnp.bfloat16)
    returned = from_experts(expert_out).reshape(expert_count * capacity, model_width)
    per_route = returned[slot_index].reshape(rows_dev, top_k, model_width)
    routed_branch = jnp.sum(gate_weights[:, :, None] * per_route, axis=1)
    block_out = (hidden_state + shared_branch + routed_branch).astype(jnp.bfloat16)
    full_query, full_keyval, full_out, full_shared_in, full_shared_out = (
        lax.all_gather(w_query, "col", axis=0, tiled=True),
        lax.all_gather(w_keyval, "col", axis=0, tiled=True),
        lax.all_gather(w_out, "col", axis=0, tiled=True),
        lax.all_gather(w_shared_in, "col", axis=0, tiled=True),
        lax.all_gather(w_shared_out, "col", axis=0, tiled=True),
    )
    grad_low = cotangent.reshape(rows_dev, model_width)
    grad_rows = grad_low.astype(jnp.float32)
    gate_grad = jnp.sum(grad_rows[:, None, :] * per_route, axis=2)
    score_grad = (gate_grad - jnp.sum(gate_grad * gate_weights, axis=1, keepdims=True)) / score_sum
    picked_grad = score_grad * scores_sig * (1.0 - scores_sig)
    logit_grad = jnp.sum(jnp.where(chosen, picked_grad[:, :, None], 0.0), axis=1).astype(
        jnp.bfloat16
    )
    router_grad = outer_sum(normed_two, logit_grad)
    router_input = matmul_t(logit_grad, w_router)
    route_grad = (
        (gate_weights[:, :, None] * grad_rows[:, None, :])
        .reshape(rows_dev * top_k, model_width)
        .astype(jnp.bfloat16)
    )
    send_grad = jnp.where(filled[:, None], route_grad[route_of], zero_low).reshape(
        expert_count, capacity, model_width
    )
    received_grad = to_experts(send_grad)
    hidden_grad = jnp.einsum(
        "esd,edf->esf", received_grad, w_expert_out, preferred_element_type=jnp.float32
    )
    grad_expert_out = jnp.einsum(
        "esd,esf->edf", received_grad, expert_hidden, preferred_element_type=jnp.float32
    )
    expert_pre_grad = jnp.concatenate(
        [hidden_grad * expert_pre[..., expert_ff:] * expert_slope, hidden_grad * expert_act], axis=2
    ).astype(jnp.bfloat16)
    grad_expert_in = jnp.einsum(
        "esd,esf->edf", received, expert_pre_grad, preferred_element_type=jnp.float32
    )
    slot_grad = jnp.einsum(
        "esf,edf->esd", expert_pre_grad, w_expert_in, preferred_element_type=jnp.float32
    ).astype(jnp.bfloat16)
    returned_grad = from_experts(slot_grad).reshape(expert_count * capacity, model_width)
    routed_input = jnp.sum(
        returned_grad[slot_index].reshape(rows_dev, top_k, model_width), axis=1, dtype=jnp.float32
    )
    group_grad = group_rows(grad_low)
    shared_hidden_grad = matmul(group_grad, full_shared_out)
    grad_shared_out = outer_sum(group_grad, shared_hidden)
    shared_pre_grad = jnp.stack(
        [shared_hidden_grad * shared_pre[:, 1] * shared_slope, shared_hidden_grad * shared_act],
        axis=1,
    ).astype(jnp.bfloat16)
    grad_shared_in = jnp.einsum(
        "td,tcf->dcf", group_two, shared_pre_grad, preferred_element_type=jnp.float32
    )

    def shared_back(offset, amount):
        return jnp.einsum(
            "tcf,dcf->td", shared_pre_grad, full_shared_in, preferred_element_type=jnp.float32
        )

    normed_two_grad = group_sums(shared_back, rows_dev) + router_input + routed_input
    gain_ffn_grad, hidden_back = norm_back(hidden_state, scale_two, gain_ffn, normed_two_grad)
    hidden_total = grad_rows + hidden_back
    branch_low = hidden_total.astype(jnp.bfloat16)
    group_branch = group_rows(branch_low)
    attended_grad = matmul(group_branch, full_out).astype(jnp.bfloat16)
    grad_out_w = outer_sum(group_branch, attended)

    def back_block(accums, block_index):
        key_acc, value_acc = accums
        query_block, scores = block_scores(block_index)
        out_block = attended_grad.reshape(block_rows, local_kv, group_size, head_size)
        probs_full = jnp.exp(scores - log_totals[block_index])
        prob_grad = jnp.einsum(
            "qagd,kad->agqk", out_block, value_rows, preferred_element_type=jnp.float32
        )
        row_delta = jnp.sum(probs_full * prob_grad, axis=3, keepdims=True)
        score_low = (probs_full * (prob_grad - row_delta)).astype(jnp.bfloat16)
        query_grad = (
            jnp.einsum("agqk,kad->qagd", score_low, key_rows, preferred_element_type=jnp.float32)
            * inv_root
        )
        key_acc = (
            key_acc
            + jnp.einsum(
                "agqk,qagd->kad", score_low, query_block, preferred_element_type=jnp.float32
            )
            * inv_root
        )
        value_acc = value_acc + jnp.einsum(
            "agqk,qagd->kad",
            probs_full.astype(jnp.bfloat16),
            out_block,
            preferred_element_type=jnp.float32,
        )
        return ((key_acc, value_acc), query_grad.reshape(block_rows, local_heads, head_size))

    zeros_kv = jnp.zeros((group_tok, local_kv, head_size), jnp.float32)
    (key_grad, value_grad), query_grad = lax.scan(
        back_block, (zeros_kv, zeros_kv), jnp.arange(block_total, dtype=jnp.int32)
    )
    query_grad = query_grad.reshape(group_tok, local_heads, head_size)
    query_pre_grad = (
        rotate(query_grad, cosine, -sine_table)
        .astype(jnp.bfloat16)
        .reshape(group_tok, local_heads * head_size)
    )
    keyval_pre_grad = jnp.concatenate(
        [rotate(key_grad, cosine, -sine_table), value_grad], axis=2
    ).astype(jnp.bfloat16)
    grad_query_w = outer_sum(group_one, query_pre_grad)
    grad_keyval_w = jnp.einsum(
        "td,tah->dah", group_one, keyval_pre_grad, preferred_element_type=jnp.float32
    )

    def attn_back(offset, amount):
        part_query = matmul_t(query_pre_grad, full_query)
        part_keyval = jnp.einsum(
            "tah,dah->td", keyval_pre_grad, full_keyval, preferred_element_type=jnp.float32
        )
        return part_query + part_keyval

    normed_one_grad = group_sums(attn_back, rows_dev)
    gain_attn_grad, input_back = norm_back(inputs, scale_one, gain_attn, normed_one_grad)
    input_total = hidden_total + input_back
    sum_query, sum_keyval, sum_out, sum_shared_in, sum_shared_out = (
        lax.psum_scatter(
            grad_query_w.astype(jnp.bfloat16), "col", scatter_dimension=0, tiled=True
        ).astype(jnp.float32),
        lax.psum_scatter(
            grad_keyval_w.astype(jnp.bfloat16), "col", scatter_dimension=0, tiled=True
        ).astype(jnp.float32),
        lax.psum_scatter(
            grad_out_w.astype(jnp.bfloat16), "col", scatter_dimension=0, tiled=True
        ).astype(jnp.float32),
        lax.psum_scatter(
            grad_shared_in.astype(jnp.bfloat16), "col", scatter_dimension=0, tiled=True
        ).astype(jnp.float32),
        lax.psum_scatter(
            grad_shared_out.astype(jnp.bfloat16), "col", scatter_dimension=0, tiled=True
        ).astype(jnp.float32),
    )
    gain_attn_sum, gain_ffn_sum, router_sum = lax.psum(
        (gain_attn_grad, gain_ffn_grad, router_grad), ("row", "col")
    )
    return (
        block_out.reshape(1, rows_dev, model_width),
        input_total.reshape(1, rows_dev, model_width),
        gain_attn_sum,
        sum_query,
        sum_keyval,
        sum_out,
        gain_ffn_sum,
        sum_shared_in,
        sum_shared_out,
        router_sum,
        grad_expert_in,
        grad_expert_out,
    )


def solution(mesh):
    in_specs = (
        P("col", "row", None),
        P(),
        P("col", "row"),
        P("col", "row", None),
        P("col", "row"),
        P(),
        P("col", None, "row"),
        P("col", "row"),
        P(),
        P(("row", "col"), None, None),
        P(("row", "col"), None, None),
        P("col", None),
        P("col", "row", None),
        P("col", "row", None),
    )
    out_specs = (
        P("col", "row", None),
        P("col", "row", None),
        P(),
        P("col", "row"),
        P("col", "row", None),
        P("col", "row"),
        P(),
        P("col", None, "row"),
        P("col", "row"),
        P(),
        P(("row", "col"), None, None),
        P(("row", "col"), None, None),
    )
    return jax.shard_map(
        per_device, mesh=mesh, in_specs=in_specs, out_specs=out_specs, check_vma=False
    )
```

profile of v0, /device:TPU:1, one launch (start us, length us, event | category | flops | bytes accessed | tf_op | source)
XLA Modules:
  0.0 2343.2 jit_solution(2436920851714893849)
XLA Ops:
  18.1 124.3 %all-gather.12.cloned.1.call-done = bf16[2048,1,256]{2,0,1:T(8,128)(2,1)} async-done(((bf16[64,1,256]{2,0,1:T(8,128)(2,1)}), bf16[2048,1,256]{2,0,1:T(8,128)(2,1)}) %all-gather.12.cloned.1.call-update) | async-done | bytes 1048592 | tf_op jit(solution)/shard_map/all_gather | solution.py:131
  142.5 51.0 %all-gather.10.cloned.1.call-done = bf16[512,2048]{1,0:T(8,128)(2,1)} async-done(((bf16[128,2048]{1,0:T(8,128)(2,1)}), bf16[512,2048]{1,0:T(8,128)(2,1)}) %all-gather.10.cloned.1.call-update) | async-done | bytes 2097168 | tf_op jit(solution)/shard_map/all_gather | solution.py:77
  197.5 128.9 %all-gather.14.cloned.1.call-done = bf16[2048,512]{1,0:T(8,128)(2,1)} async-done(((bf16[64,512]{1,0:T(8,128)(2,1)}), bf16[2048,512]{1,0:T(8,128)(2,1)}) %all-gather.14.cloned.1.call-update) | async-done | bytes 2097168 | tf_op jit(solution)/shard_map/all_gather | solution.py:130
  340.5 141.3 %all-gather.16.cloned.1.call-done = bf16[2048,512]{1,0:T(8,128)(2,1)} async-done(((bf16[64,512]{1,0:T(8,128)(2,1)}), bf16[2048,512]{1,0:T(8,128)(2,1)}) %all-gather.16.cloned.1.call-update) | async-done | bytes 2097168 | tf_op jit(solution)/shard_map/all_gather | solution.py:132
  494.1 64.9 %reduce-scatter.12.cloned.1.call-done = f32[128,2048]{1,0:T(8,128)} async-done(((f32[512,2048]{1,0:T(8,128)}), f32[128,2048]{1,0:T(8,128)}) %reduce-scatter.12.cloned.1.call-update) | async-done | bytes 1048592 | tf_op jit(solution)/shard_map/reduce_scatter | solution.py:81
  565.6 15.4 gather_fusion.2
  609.9 11.7 broadcast_select_fusion
  631.3 102.1 %all-to-all-done.2 = bf16[256,6,2048]{2,1,0:T(8,128)(2,1)} async-done(((bf16[256,6,2048]{2,1,0:T(8,128)(2,1)}), bf16[256,6,2048]{2,1,0:T(8,128)(2,1)}, u32[]{:S(2)}, u32[]{:S(2)}) %all-to-all-start.2) | async-done | bytes 6291488 | tf_op jit(solution)/shard_map/all_to_all | solution.py:90
  733.4 12.0 all-to-all-start
  746.2 165.0 %all_gather.38 = bf16[2048,128]{1,0:T(8,128)(2,1)S(1)} all-gather(bf16[64,128]{1,0:T(8,128)(2,1)S(1)} %copy-done.61), channel_id=1, replica_groups=mesh['row'=4,'col'=32] {'col'}, dimensions={0}, use_global_device_ids=true | all-gather | bytes 540672 | tf_op jit(solution)/shard_map/all_gather | solution.py:134
  924.3 24.9 %all-gather.24.cloned.1.call-done = bf16[1,512,2048]{2,1,0:T(8,128)(2,1)} async-done(((bf16[1,128,2048]{2,1,0:T(8,128)(2,1)}), bf16[1,512,2048]{2,1,0:T(8,128)(2,1)}) %all-gather.24.cloned.1.call-update) | async-done | bytes 2097168 | tf_op jit(solution)/shard_map/all_gather | solution.py:77
  965.1 16.3 copy.246
  991.8 16.3 copy.245
  1008.2 13.1 fusion.117
  1037.0 18.8 copy.222
  1076.4 18.8 copy.234
  1095.1 65.7 %all-to-all-done.1 = bf16[2,768,2048]{2,0,1:T(2,128)(2,1)} async-done(((bf16[2,768,2048]{2,0,1:T(2,128)(2,1)}), bf16[2,768,2048]{2,0,1:T(2,128)(2,1)}, u32[]{:S(2)}, u32[]{:S(2)}) %all-to-all-start.1) | async-done | bytes 6291488 | tf_op jit(solution)/shard_map/all_to_all | solution.py:94
  1178.8 11.3 reshape.606
  1190.1 12.5 gather_fusion.1
  1208.7 35.1 %all-to-all-done.3 = bf16[2,768,2048]{2,0,1:T(2,128)(2,1)} async-done(((bf16[2,768,2048]{2,0,1:T(2,128)(2,1)}), bf16[2,768,2048]{2,0,1:T(2,128)(2,1)}, u32[]{:S(2)}, u32[]{:S(2)}) %all-to-all-start.3) | async-done | bytes 6291488 | tf_op jit(solution)/shard_map/all_to_all | solution.py:94
  1254.4 11.0 reshape.610
  1265.4 12.8 gather_fusion.3
  1298.9 22.5 all-gather.22.cloned.1.call-done
  1350.3 107.0 %reduce-scatter.28.cloned.1.call-done = bf16[64,128]{1,0:T(8,128)(2,1)} async-done(((bf16[2048,128]{1,0:T(8,128)(2,1)}), bf16[64,128]{1,0:T(8,128)(2,1)}) %reduce-scatter.28.cloned.1.call-update) | async-done | bytes 16400
  1458.8 159.6 %reduce-scatter.26.cloned.1.call-done = bf16[64,2,128]{2,0,1:T(8,128)(2,1)} async-done(((bf16[2048,2,128]{2,0,1:T(8,128)(2,1)}), bf16[64,2,128]{2,0,1:T(8,128)(2,1)}) %reduce-scatter.26.cloned.1.call-update) | async-done | bytes 32784 | tf_op jit(solution)/shard_map/reduce_scatter | solution.py:367
  1619.8 12.7 fusion.25
  1644.5 133.8 %reduce-scatter.22.cloned.1.call-done = bf16[64,1,256]{2,0,1:T(8,128)(2,1)} async-done(((bf16[2048,1,256]{2,0,1:T(8,128)(2,1)}), bf16[64,1,256]{2,0,1:T(8,128)(2,1)}) %reduce-scatter.22.cloned.1.call-update) | async-done | bytes 32784 | tf_op jit(solution)/shard_map/reduce_scatter | solution.py:361
  1779.8 161.0 %reduce-scatter.24.cloned.1.call-done = bf16[64,512]{1,0:T(8,128)(2,1)} async-done(((bf16[2048,512]{1,0:T(8,128)(2,1)}), bf16[64,512]{1,0:T(8,128)(2,1)}) %reduce-scatter.24.cloned.1.call-update) | async-done | bytes 65552 | tf_op jit(solution)/shard_map/reduce_scatter | solution.py:364
  1942.3 161.2 %reduce-scatter.20.cloned.1.call-done = bf16[64,512]{1,0:T(8,128)(2,1)} async-done(((bf16[2048,512]{1,0:T(8,128)(2,1)}), bf16[64,512]{1,0:T(8,128)(2,1)}) %reduce-scatter.20.cloned.1.call-update) | async-done | bytes 65552 | tf_op jit(solution)/shard_map/reduce_scatter | solution.py:358
  2105.0 72.6 %reduce-scatter.18.cloned.1.call-done = f32[128,2048]{1,0:T(8,128)} async-done(((f32[512,2048]{1,0:T(8,128)}), f32[128,2048]{1,0:T(8,128)}) %reduce-scatter.18.cloned.1.call-update) | async-done | bytes 1048592 | tf_op jit(solution)/shard_map/reduce_scatter | solution.py:81
  2179.2 65.4 %all-reduce = (f32[2048]{0:T(1024)}, f32[2048]{0:T(1024)}) all-reduce(f32[2048]{0:T(1024)S(1)} %get-tuple-element.145, f32[2048]{0:T(1024)S(1)} %copy-done.59), channel_id=1, replica_groups=mesh['row'=4,'col'=32] {'row','col'}, use_global_device_ids=true, to_apply=%region_26.27 | all-reduce | flops 4096 | bytes 32768 | tf_op jit(solution)/shard_map/psum | solution.py:374
  2247.3 85.8 %all-reduce.3.cloned.1.call-done = f32[2048,256]{1,0:T(8,128)} async-done(((f32[2048,256]{1,0:T(8,128)}), f32[2048,256]{1,0:T(8,128)}) %all-reduce.3.cloned.1.call-update) | async-done | bytes 2097168 | tf_op jit(solution)/shard_map/psum | solution.py:374
  (314 shorter events, 272.7 us)
Async XLA Ops:
  7.2 554.3 %copy-start = (bf16[2048,256]{1,0:T(8,128)(2,1)S(1)}, bf16[2048,256]{1,0:T(8,128)(2,1)}, u32[]{:S(2)}) copy-start(bf16[2048,256]{1,0:T(8,128)(2,1)} %param.22) | copy-start | bytes 3145732
  7.2 135.3 %all-gather.12.cloned.1.call-start = ((), (), s32[]{:S(2)}) async-start(), calls=%async_computation.14 | async-start | bytes 1081344 | tf_op jit(solution)/shard_map/all_gather | solution.py:131
  7.9 185.6 %all-gather.10.cloned.1.call-start = ((), (), s32[]{:S(2)}) async-start(), calls=%async_computation.13 | async-start | bytes 2621440 | tf_op jit(solution)/shard_map/all_gather | solution.py:77
  12.4 314.0 %all-gather.14.cloned.1.call-start = ((), (), s32[]{:S(2)}) async-start(), calls=%async_computation.15 | async-start | bytes 2162688 | tf_op jit(solution)/shard_map/all_gather | solution.py:130
  13.1 468.6 %all-gather.16.cloned.1.call-start = ((), (), s32[]{:S(2)}) async-start(), calls=%async_computation.16 | async-start | bytes 2162688 | tf_op jit(solution)/shard_map/all_gather | solution.py:132
  13.7 545.2 %reduce-scatter.12.cloned.1.call-start = ((), (), s32[]{:S(2)}) async-start(), calls=%async_computation.17 | async-start | bytes 5242880 | tf_op jit(solution)/shard_map/reduce_scatter | solution.py:81
  14.6 315.4 %copy-start.68 = (f32[64]{0:T(128)}, f32[64]{0:T(128)S(1)}, u32[]{:S(2)}) copy-start(f32[64]{0:T(128)S(1)} %negate_power_fusion) | copy-start | bytes 772
  15.4 314.5 %copy-start.55 = (f32[512]{0:T(512)}, f32[512]{0:T(512)S(1)}, u32[]{:S(2)}) copy-start(f32[512]{0:T(512)S(1)} %subtract_convert_fusion.2) | copy-start | bytes 6148
  18.1 314.4 %copy-start.18 = (f32[512,64]{1,0:T(8,128)}, f32[512,64]{1,0:T(8,128)S(1)}, u32[]{:S(2)}) copy-start(f32[512,64]{1,0:T(8,128)S(1)} %get-tuple-element.176) | copy-start | bytes 393220
  621.6 111.7 %all-to-all-start.2 = ((bf16[256,6,2048]{2,1,0:T(8,128)(2,1)}), bf16[256,6,2048]{2,1,0:T(8,128)(2,1)}, u32[]{:S(2)}, u32[]{:S(2)}) async-start(bf16[256,6,2048]{2,1,0:T(8,128)(2,1)} %get-tuple-element.170), calls=%async_computation.5 | async-start | bytes 16777216 | tf_op jit(solution)/shard_map/all_to_all | solution.py:90
  629.8 281.3 %all-gather.20.cloned.1.call-start = ((), (), s32[]{:S(2)}) async-start(), calls=%async_computation.19 | async-start | bytes 1081344 | tf_op jit(solution)/shard_map/all_gather | solution.py:133
  630.5 291.2 %all-gather.18.cloned.1.call-start = ((), (), s32[]{:S(2)}) async-start(), calls=%async_computation.18 | async-start | bytes 2621440 | tf_op jit(solution)/shard_map/all_gather | solution.py:77
  733.4 248.1 %all-to-all-start = ((bf16[256,6,2048]{2,1,0:T(8,128)(2,1)}), bf16[256,6,2048]{2,1,0:T(8,128)(2,1)}, u32[]{:S(2)}, u32[]{:S(2)}) async-start(bf16[256,6,2048]{2,1,0:T(8,128)(2,1)} %get-tuple-element.171), calls=%async_computation.2 | async-start | bytes 16777216 | tf_op jit(solution)/shard_map/all_to_all | solution.py:90
  745.4 203.8 %all-gather.24.cloned.1.call-start = ((), (), s32[]{:S(2)}) async-start(), calls=%async_computation.29 | async-start | bytes 2621440 | tf_op jit(solution)/shard_map/all_gather | solution.py:77
  746.1 538.6 %reduce-scatter.16.cloned.1.call-start = ((), (), s32[]{:S(2)}) async-start(), calls=%async_computation.21 | async-start | bytes 5242880 | tf_op jit(solution)/shard_map/reduce_scatter | solution.py:81
  1055.8 105.0 %all-to-all-start.1 = ((bf16[2,768,2048]{2,0,1:T(2,128)(2,1)}), bf16[2,768,2048]{2,0,1:T(2,128)(2,1)}, u32[]{:S(2)}, u32[]{:S(2)}) async-start(bf16[2,768,2048]{2,0,1:T(2,128)(2,1)} %copy.222), calls=%async_computation.3 | async-start | bytes 12582912 | tf_op jit(solution)/shard_map/all_to_all | solution.py:94
  1063.7 224.8 %reduce-scatter.14.cloned.1.call-start = ((), (), s32[]{:S(2)}) async-start(), calls=%async_computation.20 | async-start | bytes 5242880 | tf_op jit(solution)/shard_map/reduce_scatter | solution.py:81
  1160.8 83.0 %all-to-all-start.3 = ((bf16[2,768,2048]{2,0,1:T(2,128)(2,1)}), bf16[2,768,2048]{2,0,1:T(2,128)(2,1)}, u32[]{:S(2)}, u32[]{:S(2)}) async-start(bf16[2,768,2048]{2,0,1:T(2,128)(2,1)} %copy.234), calls=%async_computation.6 | async-start | bytes 12582912 | tf_op jit(solution)/shard_map/all_to_all | solution.py:94
  1168.1 153.2 %all-gather.22.cloned.1.call-start = ((), (), s32[]{:S(2)}) async-start(), calls=%async_computation.22 | async-start | bytes 2621440 | tf_op jit(solution)/shard_map/all_gather | solution.py:77
  1292.1 165.2 %reduce-scatter.28.cloned.1.call-start = ((), (), s32[]{:S(2)}) async-start(), calls=%async_computation.30 | async-start | bytes 540672
  1295.3 323.1 %reduce-scatter.26.cloned.1.call-start = ((), (), s32[]{:S(2)}) async-start(), calls=%async_computation.27 | async-start | bytes 1081344 | tf_op jit(solution)/shard_map/reduce_scatter | solution.py:367
  1298.9 479.5 %reduce-scatter.22.cloned.1.call-start = ((), (), s32[]{:S(2)}) async-start(), calls=%async_computation.25 | async-start | bytes 1081344 | tf_op jit(solution)/shard_map/reduce_scatter | solution.py:361
  1331.8 609.0 %reduce-scatter.24.cloned.1.call-start = ((), (), s32[]{:S(2)}) async-start(), calls=%async_computation.26 | async-start | bytes 2162688 | tf_op jit(solution)/shard_map/reduce_scatter | solution.py:364
  1336.4 767.2 %reduce-scatter.20.cloned.1.call-start = ((), (), s32[]{:S(2)}) async-start(), calls=%async_computation.24 | async-start | bytes 2162688 | tf_op jit(solution)/shard_map/reduce_scatter | solution.py:358
  1344.4 833.2 %reduce-scatter.18.cloned.1.call-start = ((), (), s32[]{:S(2)}) async-start(), calls=%async_computation.23 | async-start | bytes 5242880 | tf_op jit(solution)/shard_map/reduce_scatter | solution.py:81
  1350.0 983.1 %all-reduce.3.cloned.1.call-start = ((), (), s32[]{:S(2)}) async-start(), calls=%async_computation.28 | async-start | bytes 4194304 | tf_op jit(solution)/shard_map/psum | solution.py:374
  1634.3 543.4 %copy-start.8 = (bf16[1,128,2048]{2,1,0:T(8,128)(2,1)S(1)}, bf16[1,128,2048]{2,1,0:T(8,128)(2,1)}, u32[]{:S(2)}) copy-start(bf16[1,128,2048]{2,1,0:T(8,128)(2,1)} %param.14) | copy-start | bytes 1572868
  1634.3 543.4 %copy-start.51 = (f32[2048]{0:T(1024)S(1)}, f32[2048]{0:T(1024)}, u32[]{:S(2)}) copy-start(f32[2048]{0:T(1024)} %param.15) | copy-start | bytes 24580
  1634.3 543.3 %copy-start.65 = (f32[128]{0:T(128)S(1)}, f32[128]{0:T(128)}, u32[]{:S(2)}) copy-start(f32[128]{0:T(128)} %copy-done.64) | copy-start | bytes 1540
  1634.3 544.9 %copy-start.59 = (f32[2048]{0:T(1024)S(1)}, f32[2048]{0:T(1024)}, u32[]{:S(2)}) copy-start(f32[2048]{0:T(1024)} %get-tuple-element.143) | copy-start | bytes 24580
  1634.4 610.3 %copy-start.17 = (f32[128,2048]{1,0:T(8,128)S(1)}, f32[128,2048]{1,0:T(8,128)}, u32[]{:S(2)}) copy-start(f32[128,2048]{1,0:T(8,128)} %get-tuple-element.150) | copy-start | bytes 3145732
  1634.4 610.3 %copy-start.70 = (f32[128]{0:T(128)S(1)}, f32[128]{0:T(128)}, u32[]{:S(2)}) copy-start(f32[128]{0:T(128)} %get-tuple-element.177) | copy-start | bytes 1540
  (68 other events, 1448.3 us)
Sparse Core Ops, SparseCore 0:
  9.7 132.7 all-gather.11
  144.7 48.7 all-gather.9
  195.2 131.2 all-gather.13
  327.9 153.7 all-gather.15
  486.8 72.0 reduce-scatter.11
  632.7 243.7 all-gather.19
  878.2 43.4 all-gather.17
  923.5 25.6 all-gather.23
  954.4 50.4 reduce-scatter.15
  1066.8 75.6 reduce-scatter.13
  1292.3 29.0 all-gather.21
  1323.7 133.5 reduce-scatter.27
  1460.2 158.1 reduce-scatter.25
  1620.7 157.5 reduce-scatter.21
  1780.5 160.2 reduce-scatter.23
  1943.7 159.7 reduce-scatter.19
  2106.0 71.6 reduce-scatter.17
  2183.1 149.8 all-reduce.2
where the time goes:
time: 2350 us; the launch traced here: 2340 us
  waiting for transfers between devices  1660 us (71%)
  local copies, waits for them, and re-layouts  230 us (10%)
  blocking collectives  230 us (10%)
  matrix products  120 us (5%)
  other arithmetic  54.8 us (2%)
  starting transfers between devices  36.5 us (2%)
    all_gather x1, blocking collectives, per_device(): lax.all_gather(w_shared_out, 'col', axis=0, tiled=True)  165 us
    reduce_scatter x1, waiting for transfers between devices, per_device(): lax.psum_scatter(grad_query_w.astype(jnp.bfloat16), 'col', scatter_dimens...  161 us
    reduce_scatter x1, waiting for transfers between devices, per_device(): lax.psum_scatter(grad_out_w.astype(jnp.bfloat16), 'col', scatter_dimensio...  161 us
    reduce_scatter x1, waiting for transfers between devices, per_device(): lax.psum_scatter(grad_shared_in.astype(jnp.bfloat16), 'col', scatter_dime...  160 us
    all_gather x1, waiting for transfers between devices, per_device(): lax.all_gather(w_out, 'col', axis=0, tiled=True)  141 us
    reduce_scatter x4, waiting for transfers between devices, group_sums(): lax.psum_scatter(producer(jnp.int32(0), lax.axis_size('row') * rows_dev),...  138 us
    reduce_scatter x1, waiting for transfers between devices, per_device(): lax.psum_scatter(grad_keyval_w.astype(jnp.bfloat16), 'col', scatter_dimen...  134 us
    all_gather x1, waiting for transfers between devices, per_device(): lax.all_gather(w_query, 'col', axis=0, tiled=True)  129 us
  transfers between devices with their start and end apart: 22, of which 18 were waited for; matrix products, arithmetic and copies ran while one was open for 14% of the time, Pallas kernels for 0%

commit v1 on v0

--- a/solution.py
+++ b/solution.py
@@ -1,6 +1,10 @@
+import functools
+
 import jax
 import jax.numpy as jnp
 from jax import lax
+from jax.experimental import pallas as pl
+from jax.experimental.pallas import tpu as pltpu
 from jax.sharding import PartitionSpec as P
 
 epsilon = 1e-06
@@ -71,6 +75,74 @@
     return lax.dot_general(
         matrix, partner, (((0,), (0,)), ((), ())), preferred_element_type=jnp.float32
     )
+
+
+def push_kernel(count, *refs):
+    sources, targets = refs[:count], refs[count : 2 * count]
+    send_sem, recv_sem, own_sem = refs[2 * count :]
+    members = targets[0].shape[0]
+    row, me = lax.axis_index("row"), lax.axis_index("col")
+    barrier = pltpu.get_barrier_semaphore()
+
+    def greet(step, carry):
+        peer = lax.rem(me + step, members)
+        pl.semaphore_signal(
+            barrier, inc=1, device_id=(row, peer), device_id_type=pl.DeviceIdType.MESH
+        )
+        return carry
+
+    lax.fori_loop(1, members, greet, 0)
+    own = [
+        pltpu.make_async_copy(sources[i], targets[i].at[me], own_sem.at[i]) for i in range(count)
+    ]
+    for copy in own:
+        copy.start()
+    pl.semaphore_wait(barrier, members - 1)
+    for i in range(count):
+
+        def push(step, carry, i=i):
+            peer = lax.rem(me + step, members)
+            pltpu.make_async_remote_copy(
+                src_ref=sources[i],
+                dst_ref=targets[i].at[me],
+                send_sem=send_sem.at[i],
+                recv_sem=recv_sem.at[i],
+                device_id=(row, peer),
+                device_id_type=pl.DeviceIdType.MESH,
+            ).start()
+            return carry
+
+        lax.fori_loop(1, members, push, 0)
+    for copy in own:
+        copy.wait()
+    for i in range(count):
+        others = targets[i].at[pl.ds(0, members - 1)]
+        pltpu.make_async_copy(others, others, recv_sem.at[i]).wait()
+        pltpu.make_async_copy(others, others, send_sem.at[i]).wait()
+
+
+def gather_weights(shards):
+    members = lax.axis_size("col")
+    count = len(shards)
+    space = pl.BlockSpec(memory_space=pl.ANY)
+    return pl.pallas_call(
+        functools.partial(push_kernel, count),
+        out_shape=[
+            jax.ShapeDtypeStruct((members, *shard.shape), shard.dtype) for shard in shards
+        ],
+        in_specs=[space] * count,
+        out_specs=[space] * count,
+        scratch_shapes=[pltpu.SemaphoreType.DMA((count,))] * 3,
+        compiler_params=pltpu.CompilerParams(collective_id=0, has_side_effects=True),
+        name="gather_weights",
+    )(*shards)
+
+
+def scatter_sum(values):
+    members = lax.axis_size("col")
+    parts = values.reshape(members, values.shape[0] // members, values.shape[1])
+    parts = lax.all_to_all(parts, "col", split_axis=0, concat_axis=0, tiled=True)
+    return jnp.sum(parts, axis=0, dtype=jnp.float32)
 
 
 def group_rows(values):
@@ -126,13 +198,20 @@
     block_total = group_tok // block_rows
     inv_root = head_size ** (-0.5)
     inputs = block_in.reshape(rows_dev, model_width).astype(jnp.float32)
-    full_query, full_keyval, full_out, full_shared_in, full_shared_out = (
-        lax.all_gather(w_query, "col", axis=0, tiled=True),
-        lax.all_gather(w_keyval, "col", axis=0, tiled=True),
-        lax.all_gather(w_out, "col", axis=0, tiled=True),
-        lax.all_gather(w_shared_in, "col", axis=0, tiled=True),
-        lax.all_gather(w_shared_out, "col", axis=0, tiled=True),
-    )
+    gathered = gather_weights(
+        [
+            w_query,
+            w_keyval.reshape(w_keyval.shape[0], -1),
+            w_out,
+            w_shared_in.reshape(w_shared_in.shape[0], -1),
+            w_shared_out,
+        ]
+    )
+    full_query, full_out, full_shared_out = (
+        gathered[i].reshape(-1, gathered[i].shape[2]) for i in (0, 2, 4)
+    )
+    full_keyval = gathered[1].reshape(-1, *w_keyval.shape[1:])
+    full_shared_in = gathered[3].reshape(-1, *w_shared_in.shape[1:])
     scale_one, normed_one = normalize(inputs, gain_attn)
     group_one = group_rows(normed_one)
     segment, position = layout(doc_lengths.reshape(-1), group_tok)
@@ -228,13 +307,6 @@
     per_route = returned[slot_index].reshape(rows_dev, top_k, model_width)
     routed_branch = jnp.sum(gate_weights[:, :, None] * per_route, axis=1)
     block_out = (hidden_state + shared_branch + routed_branch).astype(jnp.bfloat16)
-    full_query, full_keyval, full_out, full_shared_in, full_shared_out = (
-        lax.all_gather(w_query, "col", axis=0, tiled=True),
-        lax.all_gather(w_keyval, "col", axis=0, tiled=True),
-        lax.all_gather(w_out, "col", axis=0, tiled=True),
-        lax.all_gather(w_shared_in, "col", axis=0, tiled=True),
-        lax.all_gather(w_shared_out, "col", axis=0, tiled=True),
-    )
     grad_low = cotangent.reshape(rows_dev, model_width)
     grad_rows = grad_low.astype(jnp.float32)
     gate_grad = jnp.sum(grad_rows[:, None, :] * per_route, axis=2)
@@ -354,26 +426,34 @@
     normed_one_grad = group_sums(attn_back, rows_dev)
     gain_attn_grad, input_back = norm_back(inputs, scale_one, gain_attn, normed_one_grad)
     input_total = hidden_total + input_back
-    sum_query, sum_keyval, sum_out, sum_shared_in, sum_shared_out = (
-        lax.psum_scatter(
-            grad_query_w.astype(jnp.bfloat16), "col", scatter_dimension=0, tiled=True
-        ).astype(jnp.float32),
-        lax.psum_scatter(
-            grad_keyval_w.astype(jnp.bfloat16), "col", scatter_dimension=0, tiled=True
-        ).astype(jnp.float32),
-        lax.psum_scatter(
-            grad_out_w.astype(jnp.bfloat16), "col", scatter_dimension=0, tiled=True
-        ).astype(jnp.float32),
-        lax.psum_scatter(
-            grad_shared_in.astype(jnp.bfloat16), "col", scatter_dimension=0, tiled=True
-        ).astype(jnp.float32),
-        lax.psum_scatter(
-            grad_shared_out.astype(jnp.bfloat16), "col", scatter_dimension=0, tiled=True
-        ).astype(jnp.float32),
-    )
-    gain_attn_sum, gain_ffn_sum, router_sum = lax.psum(
-        (gain_attn_grad, gain_ffn_grad, router_grad), ("row", "col")
-    )
+    sum_first = scatter_sum(
+        jnp.concatenate(
+            [
+                grad_out_w.astype(jnp.bfloat16),
+                grad_shared_in.reshape(model_width, -1).astype(jnp.bfloat16),
+                grad_shared_out.astype(jnp.bfloat16),
+            ],
+            axis=1,
+        )
+    )
+    sum_last = scatter_sum(
+        jnp.concatenate(
+            [
+                grad_query_w.astype(jnp.bfloat16),
+                grad_keyval_w.reshape(model_width, -1).astype(jnp.bfloat16),
+            ],
+            axis=1,
+        )
+    )
+    out_end = w_out.shape[1]
+    in_end = out_end + w_shared_in.shape[1] * w_shared_in.shape[2]
+    sum_out = sum_first[:, :out_end]
+    sum_shared_in = sum_first[:, out_end:in_end].reshape(w_shared_in.shape)
+    sum_shared_out = sum_first[:, in_end:]
+    sum_query = sum_last[:, : w_query.shape[1]]
+    sum_keyval = sum_last[:, w_query.shape[1] :].reshape(w_keyval.shape)
+    router_sum = lax.psum(router_grad, ("row", "col"))
+    gain_attn_sum, gain_ffn_sum = lax.psum((gain_attn_grad, gain_ffn_grad), ("row", "col"))
     return (
         block_out.reshape(1, rows_dev, model_width),
         input_total.reshape(1, rows_dev, model_width),

time: 2350 us -> 1160 us (0.49)
  waiting for transfers between devices: 1660 us -> 510 us
  blocking collectives: 230 us -> 66.3 us
  Pallas kernels: 0 us -> 101 us
    reduce_scatter x4 -> x0, waiting for transfers between devices: 616 us -> none  [the longest x1 161 us: per_device(): lax.psum_scatter(grad_query_w.astype(jnp.bfloat16), 'col', scatter_dimens...]
    all_gather x4 -> x0, waiting for transfers between devices: 395 us -> none  [the longest x1 141 us: per_device(): lax.all_gather(w_out, 'col', axis=0, tiled=True)]
    all_gather x1 -> x0, blocking collectives: 165 us -> none  [per_device(): lax.all_gather(w_shared_out, 'col', axis=0, tiled=True)]
    unnamed x19 -> x9, waiting for transfers between devices: 110 us -> 1.32 us
    pallas_call x0 -> x1, Pallas kernels: none -> 101 us  [gather_weights(): pl.pallas_call(functools.partial(push_kernel, count), out_shape=[jax.Shap...]
    reduce_scatter x4, waiting for transfers between devices: 138 us -> 50.4 us  [group_sums(): lax.psum_scatter(producer(jnp.int32(0), lax.axis_size('row') * rows_dev),...]
    all_to_all x2, waiting for transfers between devices: 102 us -> 166 us  [to_experts(): lax.all_to_all(values, ('row', 'col'), split_axis=0, concat_axis=1, tiled...]
    all_to_all x0 -> x2, waiting for transfers between devices: none -> 62.9 us  [scatter_sum(): lax.all_to_all(parts, 'col', split_axis=0, concat_axis=0, tiled=True)]
  transfers between devices with their start and end apart: 22 -> 15, of which waited for: 18 -> 10; matrix products, arithmetic and copies ran while one was open for 14% -> 26% of each run, Pallas kernels for 0% -> 9%
where the time goes in v1:
time: 1160 us; the launch traced here: 1150 us
  waiting for transfers between devices  510 us (44%)
  local copies, waits for them, and re-layouts  243 us (21%)
  matrix products  104 us (9%)
  Pallas kernels  101 us (9%)
  blocking collectives  66.3 us (6%)
  other arithmetic  57.3 us (5%)
  starting transfers between devices  50.7 us (4%)
  between operations  15.5 us (1%)
    all_to_all x2, waiting for transfers between devices, to_experts(): lax.all_to_all(values, ('row', 'col'), split_axis=0, concat_axis=1, tiled...  166 us
    pallas_call x1, Pallas kernels, gather_weights(): pl.pallas_call(functools.partial(push_kernel, count), out_shape=[jax.Shap...  101 us
    all_to_all x2, waiting for transfers between devices, from_experts(): lax.all_to_all(values, ('row', 'col'), split_axis=1, concat_axis=0, tiled...  99.6 us
    all_gather x4, waiting for transfers between devices, group_rows(): return lax.all_gather(values, 'row', axis=0, tiled=True)  67.5 us
    psum x1, blocking collectives, per_device(): lax.psum((gain_attn_grad, gain_ffn_grad), ('row', 'col'))  66.3 us
    all_to_all x2, waiting for transfers between devices, scatter_sum(): lax.all_to_all(parts, 'col', split_axis=0, concat_axis=0, tiled=True)  62.9 us
    psum x1, waiting for transfers between devices, per_device(): router_sum = lax.psum(router_grad, ('row', 'col'))  62.2 us
    all_to_all x4, local copies, waits for them, and re-layouts, to_experts(): lax.all_to_all(values, ('row', 'col'), split_axis=0, concat_axis=1, tiled...  53.4 us
  transfers between devices with their start and end apart: 15, of which 10 were waited for; matrix products, arithmetic and copies ran while one was open for 26% of the time, Pallas kernels for 9%

profile of v1, /device:TPU:1, one launch (start us, length us, event | category | flops | bytes accessed | tf_op | source)
XLA Modules:
  0.0 1147.6 jit_solution(10270685486490773947)
XLA Ops:
  13.2 100.6 %gather_weights.1 = (bf16[32,64,512]{2,1,0:T(8,128)(2,1)}, bf16[32,64,256]{2,1,0:T(8,128)(2,1)}, bf16[32,64,512]{2,1,0:T(8,128)(2,1)}, bf16[32,64,256]{2,1,0:T(8,128)(2,1)}, bf16[32,64,128]{2,1,0:T(8,128)(2,1)}) custom-call(bf16[64,512]{1,0:T(8,128)(2,1)} %refs_0_.1, bf16[64,256]{1,0:T(8,128)(2,1)} %bitcast.314, bf16[64,512]{1,0:T(8,128)(2,1)} %refs_2_.1, ...), custom_call_target="tpu_custom_call" | custom-call | tf_op jit(solution)/shard_map/gather_weights/pallas_call | solution.py:128
  141.3 50.4 %reduce-scatter.5.cloned.1.call-done = f32[128,2048]{1,0:T(8,128)} async-done(((f32[512,2048]{1,0:T(8,128)}), f32[128,2048]{1,0:T(8,128)}) %reduce-scatter.5.cloned.1.call-update) | async-done | bytes 1048592 | tf_op jit(solution)/shard_map/reduce_scatter | solution.py:153
  198.4 15.4 %gather_fusion.2 = bf16[1536,2048]{1,0:T(8,128)(2,1)} fusion(bf16[1024,2048]{1,0:T(8,128)(2,1)} %fusion.2, s32[2048]{0:T(1024)S(1)} %get-tuple-element.121), kind=kCustom, calls=%fused_computation.2 | custom fusion | bytes 12589056 | tf_op jit(solution)/shard_map/gather | solution.py:325
  213.8 10.9 gather.20
  231.8 10.9 gather.17
  242.7 11.7 %broadcast_select_fusion = (bf16[256,6,2048]{2,1,0:T(8,128)(2,1)}, bf16[256,6,2048]{2,1,0:T(8,128)(2,1)}) fusion(bf16[256,6,2048]{2,1,0:T(8,128)(2,1)} %gather.20, pred[256,6]{1,0:T(8,128)(4,1)S(1)} %broadcast_in_dim.168, bf16[256,6,2048]{2,1,0:T(8,128)(2,1)} %gather.17), kind=kLoop, calls=%fused_computation.12 | loop fusion | flops 6291456 | bytes 25167360 | tf_op jit(solution)/shard_map/jit(_where)/select_n | solution.py:325
  263.4 108.8 %all-to-all-done.2 = bf16[256,6,2048]{2,1,0:T(8,128)(2,1)} async-done(((bf16[256,6,2048]{2,1,0:T(8,128)(2,1)}), bf16[256,6,2048]{2,1,0:T(8,128)(2,1)}, u32[]{:S(2)}, u32[]{:S(2)}) %all-to-all-start.2) | async-done | bytes 6291488 | tf_op jit(solution)/shard_map/all_to_all | solution.py:162
  372.1 11.3 all-to-all-start
  387.2 38.4 %all-gather.12.cloned.1.call-done = bf16[1,512,2048]{2,1,0:T(8,128)(2,1)} async-done(((bf16[1,128,2048]{2,1,0:T(8,128)(2,1)}), bf16[1,512,2048]{2,1,0:T(8,128)(2,1)}) %all-gather.12.cloned.1.call-update) | async-done | bytes 2097168 | tf_op jit(solution)/shard_map/all_gather | solution.py:149
  431.4 10.4 copy.252
  441.8 16.4 %copy.236 = bf16[2,768,2048]{1,2,0:T(8,128)(2,1)} copy(bf16[2,768,2048]{2,0,1:T(2,128)(2,1)} %bitcast.287) | data formatting | bytes 12582912 | tf_op jit(solution)/shard_map/all_to_all | solution.py:162
  458.1 57.4 %all-to-all-done = bf16[256,6,2048]{2,1,0:T(8,128)(2,1)} async-done(((bf16[256,6,2048]{2,1,0:T(8,128)(2,1)}), bf16[256,6,2048]{2,1,0:T(8,128)(2,1)}, u32[]{:S(2)}, u32[]{:S(2)}) %all-to-all-start) | async-done | bytes 6291488 | tf_op jit(solution)/shard_map/all_to_all | solution.py:162
  515.6 10.4 copy.250
  526.0 16.3 %copy.235 = bf16[2,768,2048]{1,2,0:T(8,128)(2,1)} copy(bf16[2,768,2048]{2,0,1:T(2,128)(2,1)} %bitcast.288) | data formatting | bytes 12582912 | tf_op jit(solution)/shard_map/all_to_all | solution.py:162
  542.3 13.1 %fusion.127 = f32[2,768,1024]{2,1,0:T(8,128)} fusion(bf16[2,768,2048]{1,2,0:T(8,128)(2,1)} %copy.235, bf16[2,2048,1024]{2,1,0:T(8,128)(2,1)} %param.23), kind=kOutput, calls=%fused_computation.224 | convolution fusion | flops 6442450944 | bytes 20971520 | tf_op jit(solution)/shard_map/esd,edf->esf/dot_general | solution.py:298
  571.1 18.9 %copy.211 = bf16[2,768,2048]{2,0,1:T(2,128)(2,1)} copy(bf16[2,768,2048]{2,1,0:T(8,128)(2,1)S(1)} %convolution_convert_fusion.1) | data formatting | bytes 12582912 | tf_op jit(solution)/shard_map/convert_element_type | solution.py:305
  603.2 9.6 convolution_convert_fusion
  612.8 18.8 %copy.225 = bf16[2,768,2048]{2,0,1:T(2,128)(2,1)} copy(bf16[2,768,2048]{2,1,0:T(8,128)(2,1)S(1)} %convolution_convert_fusion) | data formatting | bytes 12582912 | tf_op jit(solution)/shard_map/convert_element_type | solution.py:343
  631.6 64.6 %all-to-all-done.1 = bf16[2,768,2048]{2,0,1:T(2,128)(2,1)} async-done(((bf16[2,768,2048]{2,0,1:T(2,128)(2,1)}), bf16[2,768,2048]{2,0,1:T(2,128)(2,1)}, u32[]{:S(2)}, u32[]{:S(2)}) %all-to-all-start.1) | async-done | bytes 6291488 | tf_op jit(solution)/shard_map/all_to_all | solution.py:166
  703.6 10.6 copy.212
  714.2 11.4 reshape.656
  725.6 12.5 %gather_fusion.1 = bf16[1024,2048]{1,0:T(8,128)(2,1)} fusion(bf16[1536,2048]{1,0:T(8,128)(2,1)} %reshape.656, s32[1024]{0:T(1024)S(1)} %broadcast_clamp_fusion), kind=kCustom, calls=%fused_computation.1 | custom fusion | bytes 8392704 | tf_op jit(solution)/shard_map/gather | solution.py:307
  744.2 35.0 %all-to-all-done.3 = bf16[2,768,2048]{2,0,1:T(2,128)(2,1)} async-done(((bf16[2,768,2048]{2,0,1:T(2,128)(2,1)}), bf16[2,768,2048]{2,0,1:T(2,128)(2,1)}, u32[]{:S(2)}, u32[]{:S(2)}) %all-to-all-start.3) | async-done | bytes 6291488 | tf_op jit(solution)/shard_map/all_to_all | solution.py:166
  779.2 10.6 copy.226
  789.8 11.0 reshape.660
  800.8 12.6 %gather_fusion.3 = bf16[1024,2048]{1,0:T(8,128)(2,1)} fusion(bf16[1536,2048]{1,0:T(8,128)(2,1)} %reshape.660, s32[1024]{0:T(1024)S(1)} %broadcast_clamp_fusion), kind=kCustom, calls=%fused_computation.3 | custom fusion | bytes 8392704 | tf_op jit(solution)/shard_map/gather | solution.py:346
  826.8 29.0 %all-gather.10.cloned.1.call-done = bf16[512,2048]{1,0:T(8,128)(2,1)} async-done(((bf16[128,2048]{1,0:T(8,128)(2,1)}), bf16[512,2048]{1,0:T(8,128)(2,1)}) %all-gather.10.cloned.1.call-update) | async-done | bytes 2097168 | tf_op jit(solution)/shard_map/all_gather | solution.py:149
  903.6 44.7 %all-to-all-done.4 = bf16[32,64,768]{2,1,0:T(8,128)(2,1)} async-done(((bf16[32,64,768]{2,1,0:T(8,128)(2,1)}), bf16[32,64,768]{2,1,0:T(8,128)(2,1)}, u32[]{:S(2)}, u32[]{:S(2)}) %all-to-all-start.4) | async-done | bytes 3145760 | tf_op jit(solution)/shard_map/all_to_all | solution.py:144
  963.3 13.3 %fusion.25 = f32[2,2048,1024]{2,1,0:T(8,128)} fusion(bf16[2,768,2048]{1,2,0:T(8,128)(2,1)} %copy.235, bf16[2,768,512]{2,1,0:T(8,128)(2,1)S(1)} %copy-done.77, bf16[2,768,512]{2,1,0:T(8,128)(2,1)S(1)} %copy-done.76), kind=kOutput, calls=%fused_computation.65 | convolution fusion | flops 6448742400 | bytes 26214400 | tf_op jit(solution)/shard_map/esd,esf->edf/dot_general | solution.py:338
  982.2 18.2 %all-to-all-done.5 = bf16[32,64,896]{2,1,0:T(8,128)(2,1)} async-done(((bf16[32,64,896]{2,1,0:T(8,128)(2,1)}), bf16[32,64,896]{2,1,0:T(8,128)(2,1)}, u32[]{:S(2)}, u32[]{:S(2)}) %all-to-all-start.5) | async-done | bytes 3670048 | tf_op jit(solution)/shard_map/all_to_all | solution.py:144
  1006.5 66.3 %all-reduce = (f32[2048]{0:T(1024)}, f32[2048]{0:T(1024)}) all-reduce(f32[2048]{0:T(1024)S(1)} %get-tuple-element.83, f32[2048]{0:T(1024)S(1)} %get-tuple-element.81), channel_id=1, replica_groups=mesh['row'=4,'col'=32] {'row','col'}, use_global_device_ids=true, to_apply=%region_26.27 | all-reduce | flops 4096 | bytes 32768 | tf_op jit(solution)/shard_map/psum | solution.py:456
  1075.4 62.2 %all-reduce.3.cloned.1.call-done = f32[2048,256]{1,0:T(8,128)} async-done(((f32[2048,256]{1,0:T(8,128)}), f32[2048,256]{1,0:T(8,128)}) %all-reduce.3.cloned.1.call-update) | async-done | bytes 2097168 | tf_op jit(solution)/shard_map/psum | solution.py:455
  (302 shorter events, 200.5 us)
Async XLA Ops:
  7.2 187.1 %copy-start = (bf16[2048,256]{1,0:T(8,128)(2,1)S(1)}, bf16[2048,256]{1,0:T(8,128)(2,1)}, u32[]{:S(2)}) copy-start(bf16[2048,256]{1,0:T(8,128)(2,1)} %param.22) | copy-start | bytes 3145732
  7.2 109.5 %copy-start.72 = (s32[1,4]{1,0:T(1,128)S(1)}, s32[1,4]{1,0:T(1,128)}, u32[]{:S(2)}) copy-start(s32[1,4]{1,0:T(1,128)} %param.25) | copy-start | bytes 52
  7.2 112.0 %all-gather.6.cloned.1.call-start = ((), (), s32[]{:S(2)}) async-start(), calls=%async_computation.10 | async-start | bytes 2621440 | tf_op jit(solution)/shard_map/all_gather | solution.py:149
  11.7 180.0 %reduce-scatter.5.cloned.1.call-start = ((), (), s32[]{:S(2)}) async-start(), calls=%async_computation.11 | async-start | bytes 5242880 | tf_op jit(solution)/shard_map/reduce_scatter | solution.py:153
  134.9 56.8 %copy-start.7 = (bf16[1,128,2048]{2,1,0:T(8,128)(2,1)S(1)}, bf16[1,128,2048]{2,1,0:T(8,128)(2,1)}, u32[]{:S(2)}) copy-start(bf16[1,128,2048]{2,1,0:T(8,128)(2,1)} %param.14) | copy-start | bytes 1572868
  135.2 59.4 %copy-start.30 = (s32[128,8]{1,0:T(8,128)}, s32[128,8]{1,0:T(8,128)S(1)}, u32[]{:S(2)}) copy-start(s32[128,8]{1,0:T(8,128)S(1)} %copy.200) | copy-start | bytes 12292
  135.7 58.5 %copy-start.51 = (f32[2048]{0:T(1024)S(1)}, f32[2048]{0:T(1024)}, u32[]{:S(2)}) copy-start(f32[2048]{0:T(1024)} %param.19) | copy-start | bytes 24580
  141.3 57.1 %copy-start.9 = (f32[128,2048]{1,0:T(8,128)}, f32[128,2048]{1,0:T(8,128)S(1)}, u32[]{:S(2)}) copy-start(f32[128,2048]{1,0:T(8,128)S(1)} %bitcast_convert_fusion) | copy-start | bytes 3145732
  194.3 30.4 %copy-start.1 = (bf16[128,2048]{1,0:T(8,128)(2,1)}, bf16[128,2048]{1,0:T(8,128)(2,1)S(1)}, u32[]{:S(2)}) copy-start(bf16[128,2048]{1,0:T(8,128)(2,1)S(1)} %multiply_convert_fusion.3) | copy-start | bytes 1572868
  195.7 18.1 %copy-start.61 = (f32[128]{0:T(128)}, f32[128]{0:T(128)S(1)}, u32[]{:S(2)}) copy-start(f32[128]{0:T(128)S(1)} %fusion.110) | copy-start | bytes 1540
  254.4 117.7 %all-to-all-start.2 = ((bf16[256,6,2048]{2,1,0:T(8,128)(2,1)}), bf16[256,6,2048]{2,1,0:T(8,128)(2,1)}, u32[]{:S(2)}, u32[]{:S(2)}) async-start(bf16[256,6,2048]{2,1,0:T(8,128)(2,1)} %get-tuple-element.105), calls=%async_computation.5 | async-start | bytes 16777216 | tf_op jit(solution)/shard_map/all_to_all | solution.py:162
  262.6 122.2 %all-gather.8.cloned.1.call-start = ((), (), s32[]{:S(2)}) async-start(), calls=%async_computation.12 | async-start | bytes 2621440 | tf_op jit(solution)/shard_map/all_gather | solution.py:149
  372.1 143.4 %all-to-all-start = ((bf16[256,6,2048]{2,1,0:T(8,128)(2,1)}), bf16[256,6,2048]{2,1,0:T(8,128)(2,1)}, u32[]{:S(2)}, u32[]{:S(2)}) async-start(bf16[256,6,2048]{2,1,0:T(8,128)(2,1)} %get-tuple-element.106), calls=%async_computation.2 | async-start | bytes 16777216 | tf_op jit(solution)/shard_map/all_to_all | solution.py:162
  383.4 42.2 %all-gather.12.cloned.1.call-start = ((), (), s32[]{:S(2)}) async-start(), calls=%async_computation.18 | async-start | bytes 2621440 | tf_op jit(solution)/shard_map/all_gather | solution.py:149
  384.0 436.0 %reduce-scatter.9.cloned.1.call-start = ((), (), s32[]{:S(2)}) async-start(), calls=%async_computation.14 | async-start | bytes 5242880 | tf_op jit(solution)/shard_map/reduce_scatter | solution.py:153
  384.8 40.8 %copy-start.33 = (bf16[32,64,128]{2,1,0:T(8,128)(2,1)S(1)}, bf16[32,64,128]{2,1,0:T(8,128)(2,1)}, u32[]{:S(2)}) copy-start(bf16[32,64,128]{2,1,0:T(8,128)(2,1)} %get-tuple-element.78) | copy-start | bytes 1572868
  387.2 44.2 %copy-start.41 = (f32[512,2,128]{2,0,1:T(8,128)}, f32[512,2,128]{2,0,1:T(8,128)S(1)}, u32[]{:S(2)}) copy-start(f32[512,2,128]{2,0,1:T(8,128)S(1)} %fusion.18) | copy-start | bytes 1572868
  526.0 29.4 %slice-start = ((s8[6291456]{0:T(1024)(128)(4,1)}), s8[2097152]{0:T(1024)(128)(4,1)S(1)}, s32[]{:S(2)}) async-start(s8[6291456]{0:T(1024)(128)(4,1)} %bitcast.294), calls=%async_computation.19 | async-start | bytes 4194304
  590.0 106.2 %all-to-all-start.1 = ((bf16[2,768,2048]{2,0,1:T(2,128)(2,1)}), bf16[2,768,2048]{2,0,1:T(2,128)(2,1)}, u32[]{:S(2)}, u32[]{:S(2)}) async-start(bf16[2,768,2048]{2,0,1:T(2,128)(2,1)} %copy.211), calls=%async_computation.3 | async-start | bytes 12582912 | tf_op jit(solution)/shard_map/all_to_all | solution.py:166
  599.1 224.0 %reduce-scatter.7.cloned.1.call-start = ((), (), s32[]{:S(2)}) async-start(), calls=%async_computation.13 | async-start | bytes 5242880 | tf_op jit(solution)/shard_map/reduce_scatter | solution.py:153
  696.2 83.0 %all-to-all-start.3 = ((bf16[2,768,2048]{2,0,1:T(2,128)(2,1)}), bf16[2,768,2048]{2,0,1:T(2,128)(2,1)}, u32[]{:S(2)}, u32[]{:S(2)}) async-start(bf16[2,768,2048]{2,0,1:T(2,128)(2,1)} %copy.225), calls=%async_computation.6 | async-start | bytes 12582912 | tf_op jit(solution)/shard_map/all_to_all | solution.py:166
  703.5 152.3 %all-gather.10.cloned.1.call-start = ((), (), s32[]{:S(2)}) async-start(), calls=%async_computation.15 | async-start | bytes 2621440 | tf_op jit(solution)/shard_map/all_gather | solution.py:149
  826.7 178.2 %reduce-scatter.11.cloned.1.call-start = ((), (), s32[]{:S(2)}) async-start(), calls=%async_computation.16 | async-start | bytes 5242880 | tf_op jit(solution)/shard_map/reduce_scatter | solution.py:153
  881.7 66.5 %all-to-all-start.4 = ((bf16[32,64,768]{2,1,0:T(8,128)(2,1)}), bf16[32,64,768]{2,1,0:T(8,128)(2,1)}, u32[]{:S(2)}, u32[]{:S(2)}) async-start(bf16[32,64,768]{2,1,0:T(8,128)(2,1)} %bitcast.290), calls=%async_computation.8 | async-start | bytes 6291456 | tf_op jit(solution)/shard_map/all_to_all | solution.py:144
  903.6 51.1 %copy-start.74 = (bf16[2,768,512]{2,1,0:T(8,128)(2,1)S(1)}, bf16[2,768,512]{2,1,0:T(8,128)(2,1)}, u32[]{:S(2)}) copy-start(bf16[2,768,512]{2,1,0:T(8,128)(2,1)} %copy-done.73) | copy-start | bytes 4718596
  948.2 52.2 %all-to-all-start.5 = ((bf16[32,64,896]{2,1,0:T(8,128)(2,1)}), bf16[32,64,896]{2,1,0:T(8,128)(2,1)}, u32[]{:S(2)}, u32[]{:S(2)}) async-start(bf16[32,64,896]{2,1,0:T(8,128)(2,1)} %bitcast.289), calls=%async_computation.9 | async-start | bytes 7340032 | tf_op jit(solution)/shard_map/all_to_all | solution.py:144
  954.6 183.0 %all-reduce.3.cloned.1.call-start = ((), (), s32[]{:S(2)}) async-start(), calls=%async_computation.17 | async-start | bytes 4194304 | tf_op jit(solution)/shard_map/psum | solution.py:455
  978.4 26.6 %copy-start.8 = (bf16[1,128,2048]{2,1,0:T(8,128)(2,1)S(1)}, bf16[1,128,2048]{2,1,0:T(8,128)(2,1)}, u32[]{:S(2)}) copy-start(bf16[1,128,2048]{2,1,0:T(8,128)(2,1)} %param.14) | copy-start | bytes 1572868
  978.4 26.6 %copy-start.53 = (f32[2048]{0:T(1024)S(1)}, f32[2048]{0:T(1024)}, u32[]{:S(2)}) copy-start(f32[2048]{0:T(1024)} %param.15) | copy-start | bytes 24580
  978.4 26.6 %copy-start.64 = (f32[128]{0:T(128)S(1)}, f32[128]{0:T(128)}, u32[]{:S(2)}) copy-start(f32[128]{0:T(128)} %copy-done.63) | copy-start | bytes 1540
  978.4 94.4 %copy-start.14 = (f32[128,2048]{1,0:T(8,128)S(1)}, f32[128,2048]{1,0:T(8,128)}, u32[]{:S(2)}) copy-start(f32[128,2048]{1,0:T(8,128)} %get-tuple-element.88) | copy-start | bytes 3145732
  978.4 94.4 %copy-start.69 = (f32[128]{0:T(128)S(1)}, f32[128]{0:T(128)}, u32[]{:S(2)}) copy-start(f32[128]{0:T(128)} %get-tuple-element.112) | copy-start | bytes 1540
  (63 other events, 311.4 us)
Sparse Core Ops, SparseCore 0:
  11.8 41.5 all-gather.5
  134.1 57.5 reduce-scatter.4
  265.3 39.8 all-gather.7
  385.7 39.8 all-gather.11
  431.5 73.2 reduce-scatter.8
  602.3 75.6 reduce-scatter.6
  826.8 28.9 all-gather.9
  869.7 73.2 reduce-scatter.10
  978.5 159.0 all-reduce.2

commit v2 on v0

v2 whole, which is shorter than its diff:
```python
import functools

import jax
import jax.numpy as jnp
from jax import lax
from jax.experimental import pallas as pl
from jax.experimental.pallas import tpu as pltpu
from jax.sharding import PartitionSpec as P

epsilon = 1e-06
rope_base = 10000.0
masked_score = -1e30

EXPERT_ROWS = 6
PAIR_ROWS = 12
PACKED_ROWS = 16
BLOCK_PAIRS = 16
BLOCK = BLOCK_PAIRS * PACKED_ROWS
BLOCK_EXPERTS = 2 * BLOCK_PAIRS
BLOCK_SLOTS = BLOCK_PAIRS * EXPERT_ROWS
QUARTER = 512
SIDE = 128
MESH = pl.DeviceIdType.MESH


def layout(lengths, token_count):
    bounds = jnp.cumsum(lengths)
    places = jnp.arange(token_count, dtype=jnp.int32)
    segment = jnp.sum((places[:, None] >= bounds[None, :]).astype(jnp.int32), axis=1)
    starts = bounds - lengths
    owners = segment[:, None] == jnp.arange(lengths.shape[0], dtype=jnp.int32)[None, :]
    begins = jnp.sum(jnp.where(owners, starts[None, :], 0), axis=1)
    return (segment, places - begins)


def rotary(positions, head_size):
    half_size = head_size // 2
    spread = jnp.arange(half_size, dtype=jnp.float32) * (2.0 / head_size)
    frequency = rope_base ** (-spread)
    angles = positions.astype(jnp.float32)[:, None] * frequency[None, :]
    return (jnp.cos(angles), jnp.sin(angles))


def rotate(values, cosine, sine_table):
    half_size = values.shape[-1] // 2
    leading = values[..., :half_size]
    trailing = values[..., half_size:]
    cosine = cosine[:, None, :]
    sine_table = sine_table[:, None, :]
    return jnp.concatenate(
        [leading * cosine - trailing * sine_table, trailing * cosine + leading * sine_table],
        axis=-1,
    )


def normalize(values, gain):
    factor = lax.rsqrt(jnp.mean(values * values, axis=1, keepdims=True) + epsilon)
    return (factor, (values * factor * gain).astype(jnp.bfloat16))


def norm_back(values, factor, gain, incoming):
    weighted = gain * incoming
    gain_grad = jnp.sum(incoming * values * factor, axis=0)
    input_grad = factor * weighted - values * factor**3 * jnp.mean(
        weighted * values, axis=1, keepdims=True
    )
    return (gain_grad, input_grad)


def swish_parts(pre_act):
    logistic = jax.nn.sigmoid(pre_act)
    return (pre_act * logistic, logistic * (1.0 + pre_act * (1.0 - logistic)))


def matmul(matrix, partner):
    return jnp.dot(matrix, partner, preferred_element_type=jnp.float32)


def matmul_t(matrix, partner):
    return lax.dot_general(
        matrix, partner, (((1,), (1,)), ((), ())), preferred_element_type=jnp.float32
    )


def outer_sum(matrix, partner):
    return lax.dot_general(
        matrix, partner, (((0,), (0,)), ((), ())), preferred_element_type=jnp.float32
    )


def split_low(values):
    high = values.astype(jnp.bfloat16)
    return high, (values - high.astype(jnp.float32)).astype(jnp.bfloat16)


def row_places():
    row, col = lax.axis_index("row"), lax.axis_index("col")
    chip, core = row // 2, lax.rem(row, 2)
    sibling = chip * 2 + (1 - core)
    partner = (1 - chip) * 2 + core
    across = (1 - chip) * 2 + (1 - core)
    return row, col, sibling, partner, across


def row_copies(sources, targets, send_sem, recv_sem):
    row, col, sibling, partner, _ = row_places()

    def send(origin, target, peer, i):
        return pltpu.make_async_remote_copy(
            src_ref=origin,
            dst_ref=target,
            send_sem=send_sem.at[i],
            recv_sem=recv_sem.at[i],
            device_id=(peer, col),
            device_id_type=MESH,
        )

    far, near, onward = [], [], []
    for i, (source, target) in enumerate(zip(sources, targets)):
        far.append(send(source, target.at[row], partner, 3 * i))
        near.append(send(source, target.at[row], sibling, 3 * i + 1))
        onward.append(send(target.at[partner], target.at[partner], sibling, 3 * i + 2))
    return far, near, onward


def greet(peers):
    barrier = pltpu.get_barrier_semaphore()
    for peer in peers:
        pl.semaphore_signal(barrier, inc=1, device_id=peer, device_id_type=MESH)


def await_greetings(count):
    pl.semaphore_wait(pltpu.get_barrier_semaphore(), count)


def row_gather_kernel(count, *refs):
    sources, targets = refs[:count], refs[count : 2 * count]
    send_sem, recv_sem, own_sem = refs[2 * count :]
    row, col, sibling, partner, _ = row_places()
    greet([(sibling, col), (partner, col)])
    own = [
        pltpu.make_async_copy(sources[i], targets[i].at[row], own_sem.at[i]) for i in range(count)
    ]
    for copy in own:
        copy.start()
    await_greetings(2)
    far, near, onward = row_copies(sources, targets, send_sem, recv_sem)
    for copy in far + near:
        copy.start()
    for first, second in zip(far, onward):
        first.wait_recv()
        second.start()
    for copy in own:
        copy.wait()
    for copy in far:
        copy.wait_send()
    for copy in near + onward:
        copy.wait()


def group_rows(values, call):
    count = len(values)
    space = pl.BlockSpec(memory_space=pl.ANY)
    gathered = pl.pallas_call(
        functools.partial(row_gather_kernel, count),
        out_shape=[jax.ShapeDtypeStruct((4, *part.shape), part.dtype) for part in values],
        in_specs=[space] * count,
        out_specs=[space] * count,
        scratch_shapes=[
            pltpu.SemaphoreType.DMA((3 * count,)),
            pltpu.SemaphoreType.DMA((3 * count,)),
            pltpu.SemaphoreType.DMA((count,)),
        ],
        compiler_params=pltpu.CompilerParams(collective_id=1 + call, has_side_effects=True),
        cost_estimate=pl.CostEstimate(flops=0, bytes_accessed=64 << 20, transcendentals=0),
        name="group_rows",
    )(*values)
    return [part.reshape(-1, part.shape[2]) for part in gathered]


def gather_kernel(shard, normed, grads, full, group_one, group_grad, *sems):
    send_sem, recv_sem, own_sem, row_send, row_recv = sems
    row, col, sibling, partner, _ = row_places()
    along_x, along_z, along_y = col // 16, lax.rem(col // 4, 4), lax.rem(col, 4)
    other_x = 1 - along_x
    half_rows = shard.shape[0] // 2

    def place(x, z, y):
        return x * 16 + z * 4 + y

    z_near = [lax.rem(along_z + i, 4) for i in (1, 3, 2)]
    y_near = [lax.rem(along_y + i, 4) for i in (1, 3, 2)]
    z_peers = [place(along_x, z, along_y) for z in z_near]
    y_peers = [place(along_x, along_z, y) for y in y_near]
    x_peer = place(other_x, along_z, along_y)
    greet([(row, peer) for peer in z_peers + y_peers + [x_peer]])
    greet([(sibling, col), (partner, col)])
    own = [
        pltpu.make_async_copy(shard, full.at[col], own_sem.at[0]),
        pltpu.make_async_copy(normed, group_one.at[row], own_sem.at[1]),
        pltpu.make_async_copy(grads, group_grad.at[row], own_sem.at[2]),
    ]
    for copy in own:
        copy.start()
    await_greetings(9)

    def pass_on(owner, half, peers, origin=None):
        rows = pl.ds(half * half_rows, half_rows)
        target = full.at[owner, rows]
        for peer in peers:
            pltpu.make_async_remote_copy(
                src_ref=target if origin is None else origin.at[rows],
                dst_ref=target,
                send_sem=send_sem,
                recv_sem=recv_sem.at[half * 32 + owner],
                device_id=(row, peer),
                device_id_type=MESH,
            ).start()

    def await_half(owner, half):
        target = full.at[owner, pl.ds(half * half_rows, half_rows)]
        pltpu.make_async_copy(target, target, recv_sem.at[half * 32 + owner]).wait()

    pass_on(col, 0, [x_peer], shard)
    pass_on(col, 1, [x_peer], shard)
    pass_on(col, 0, z_peers, shard)
    pass_on(col, 1, y_peers, shard)
    far, near, onward = row_copies([normed, grads], [group_one, group_grad], row_send, row_recv)
    far[0].start()
    near[0].start()
    await_half(x_peer, 0)
    pass_on(x_peer, 0, z_peers)
    await_half(x_peer, 1)
    pass_on(x_peer, 1, y_peers)
    pass_on(col, 0, y_peers, shard)
    pass_on(col, 1, z_peers, shard)
    pass_on(x_peer, 0, y_peers)
    pass_on(x_peer, 1, z_peers)
    far[1].start()
    near[1].start()
    for i in range(3):
        for x in (along_x, other_x):
            owner = place(x, z_near[i], along_y)
            await_half(owner, 0)
            pass_on(owner, 0, y_peers)
            owner = place(x, along_z, y_near[i])
            await_half(owner, 1)
            pass_on(owner, 1, z_peers)
    for first, second in zip(far, onward):
        first.wait_recv()
        second.start()
    for x in (along_x, other_x):
        for i in range(4):
            for j in range(3):
                await_half(place(x, lax.rem(along_z + i, 4), y_near[j]), 0)
                await_half(place(x, z_near[j], lax.rem(along_y + i, 4)), 1)
    for copy in own:
        copy.wait()
    for copy in far:
        copy.wait_send()
    for copy in near + onward:
        copy.wait()
    sent = full.at[pl.ds(0, 31)]
    pltpu.make_async_copy(sent, sent, send_sem).wait()


def gather_start(shard, normed, grads):
    space = pl.BlockSpec(memory_space=pl.ANY)
    full, group_one, group_grad = pl.pallas_call(
        gather_kernel,
        out_shape=[
            jax.ShapeDtypeStruct((32, *shard.shape), shard.dtype),
            jax.ShapeDtypeStruct((4, *normed.shape), normed.dtype),
            jax.ShapeDtypeStruct((4, *grads.shape), grads.dtype),
        ],
        in_specs=[space] * 3,
        out_specs=[space] * 3,
        scratch_shapes=[
            pltpu.SemaphoreType.DMA,
            pltpu.SemaphoreType.DMA((64,)),
            pltpu.SemaphoreType.DMA((3,)),
            pltpu.SemaphoreType.DMA((6,)),
            pltpu.SemaphoreType.DMA((6,)),
        ],
        compiler_params=pltpu.CompilerParams(collective_id=0, has_side_effects=True),
        cost_estimate=pl.CostEstimate(flops=0, bytes_accessed=200 << 20, transcendentals=0),
        name="gather_start",
    )(shard, normed, grads)
    return [part.reshape(-1, part.shape[2]) for part in (full, group_one, group_grad)]


def row_sum_kernel(parts, total, near, far, outgoing, send_sem, recv_sem):
    row, col, sibling, partner, across = row_places()
    barrier = pltpu.get_barrier_semaphore()
    for peer in (sibling, partner):
        pl.semaphore_signal(barrier, inc=1, device_id=(peer, col), device_id_type=MESH)
    pl.semaphore_wait(barrier, 2)

    def send(origin, target, peer, i):
        return pltpu.make_async_remote_copy(
            src_ref=origin,
            dst_ref=target,
            send_sem=send_sem.at[i],
            recv_sem=recv_sem.at[i],
            device_id=(peer, col),
            device_id_type=MESH,
        )

    first = send(parts.at[across], near.at[0], sibling, 0)
    second = send(parts.at[sibling], near.at[1], sibling, 1)
    first.start()
    second.start()
    first.wait_recv()
    outgoing[...] = (
        parts[partner].astype(jnp.float32) + near[0].astype(jnp.float32)
    ).astype(jnp.bfloat16)
    third = send(outgoing, far, partner, 2)
    third.start()
    second.wait_recv()
    total[...] = parts[row].astype(jnp.float32) + near[1].astype(jnp.float32)
    third.wait_recv()
    total[...] += far[...].astype(jnp.float32)
    first.wait_send()
    second.wait_send()
    third.wait_send()


def group_sums(partial_sums, call):
    width = partial_sums.shape[1]
    parts = partial_sums.astype(jnp.bfloat16).reshape(4, -1, width)
    rows = parts.shape[1]
    space = pl.BlockSpec(memory_space=pltpu.VMEM)
    return pl.pallas_call(
        row_sum_kernel,
        out_shape=jax.ShapeDtypeStruct((rows, width), jnp.float32),
        in_specs=[space],
        out_specs=space,
        scratch_shapes=[
            pltpu.VMEM((2, rows, width), jnp.bfloat16),
            pltpu.VMEM((rows, width), jnp.bfloat16),
            pltpu.VMEM((rows, width), jnp.bfloat16),
            pltpu.SemaphoreType.DMA((3,)),
            pltpu.SemaphoreType.DMA((3,)),
        ],
        compiler_params=pltpu.CompilerParams(
            collective_id=8 + call, has_side_effects=True, vmem_limit_bytes=32 << 20
        ),
        cost_estimate=pl.CostEstimate(flops=0, bytes_accessed=64 << 20, transcendentals=0),
        name="group_sums",
    )(parts)


def scatter_sum(values):
    parts = [part.astype(jnp.bfloat16).reshape(32, 64, -1) for part in values]
    widths = [part.shape[2] for part in parts]
    swapped = lax.all_to_all(
        jnp.concatenate(parts, axis=2), "col", split_axis=0, concat_axis=0, tiled=True
    )
    total = jnp.sum(swapped, axis=0, dtype=jnp.float32)
    ends = [sum(widths[: i + 1]) for i in range(len(widths))]
    return [total[:, end - width : end] for end, width in zip(ends, widths)]


def finish_kernel(gains, share, total, router, values, buffers, *sems):
    send_sem, recv_sem, own_sem, col_send, col_recv, row_send, row_recv = sems
    row, col, sibling, partner, _ = row_places()
    along_x, along_z, along_y = col // 16, lax.rem(col // 4, 4), lax.rem(col, 4)
    stages = (
        [(lax.rem(row + i, 4), col) for i in (1, 2, 3)],
        [(row, along_x * 16 + along_z * 4 + lax.rem(along_y + i, 4)) for i in (1, 2, 3)],
        [(row, along_x * 16 + lax.rem(along_z + i, 4) * 4 + along_y) for i in (1, 2, 3)],
        [(row, lax.rem(col + 16, 32))],
    )
    greet(stages[0])
    barrier = pltpu.get_barrier_semaphore()

    def greet_col(step, carry):
        peer = (row, lax.rem(col + step, 32))
        pl.semaphore_signal(barrier, inc=1, device_id=peer, device_id_type=MESH)
        return carry

    lax.fori_loop(1, 32, greet_col, 0)
    own = pltpu.make_async_copy(share, router.at[row, col], own_sem)
    own.start()
    values[0] = gains[...]
    await_greetings(34)

    def push(step, carry):
        pltpu.make_async_remote_copy(
            src_ref=share,
            dst_ref=router.at[row, col],
            send_sem=col_send,
            recv_sem=col_recv,
            device_id=(row, lax.rem(col + step, 32)),
            device_id_type=MESH,
        ).start()
        return carry

    lax.fori_loop(1, 32, push, 0)
    at = 0
    for stage, peers in enumerate(stages):
        copies = []
        for i, peer in enumerate(peers):
            copies.append(
                pltpu.make_async_remote_copy(
                    src_ref=values.at[stage],
                    dst_ref=buffers.at[at + i],
                    send_sem=send_sem.at[at + i],
                    recv_sem=recv_sem.at[at + i],
                    device_id=peer,
                    device_id_type=MESH,
                )
            )
        for copy in copies:
            copy.start()
        if stage == 0:
            own.wait()
            arrived = router.at[row, pl.ds(0, 31)]
            pltpu.make_async_copy(arrived, arrived, col_recv).wait()
            far, near, onward = row_copies([router.at[row]], [router], row_send, row_recv)
            far[0].start()
            near[0].start()
        for copy in copies:
            copy.wait()
        result = values[stage]
        for i in range(len(peers)):
            result = result + buffers[at + i]
        values[stage + 1] = result
        at += len(peers)
    total[...] = values[len(stages)]
    far[0].wait_recv()
    onward[0].start()
    sent = router.at[row, pl.ds(0, 31)]
    pltpu.make_async_copy(sent, sent, col_send).wait()
    far[0].wait_send()
    near[0].wait()
    onward[0].wait()


def finish(gains, share):
    space = pl.BlockSpec(memory_space=pltpu.VMEM)
    away = pl.BlockSpec(memory_space=pl.ANY)
    return pl.pallas_call(
        finish_kernel,
        out_shape=[
            jax.ShapeDtypeStruct(gains.shape, gains.dtype),
            jax.ShapeDtypeStruct((4, 32, *share.shape), share.dtype),
        ],
        in_specs=[space, away],
        out_specs=[space, away],
        scratch_shapes=[
            pltpu.VMEM((5, *gains.shape), gains.dtype),
            pltpu.VMEM((10, *gains.shape), gains.dtype),
            pltpu.SemaphoreType.DMA((10,)),
            pltpu.SemaphoreType.DMA((10,)),
            pltpu.SemaphoreType.DMA,
            pltpu.SemaphoreType.DMA,
            pltpu.SemaphoreType.DMA,
            pltpu.SemaphoreType.DMA((3,)),
            pltpu.SemaphoreType.DMA((3,)),
        ],
        compiler_params=pltpu.CompilerParams(collective_id=16, has_side_effects=True),
        cost_estimate=pl.CostEstimate(flops=0, bytes_accessed=64 << 20, transcendentals=0),
        name="finish",
    )(gains, share)


def packed_places(shape, axis):
    index = lax.broadcasted_iota(jnp.int32, shape, axis)
    pair, place = index // PACKED_ROWS, lax.rem(index, PACKED_ROWS)
    found = []
    for part in range(-1, 3):
        if part < 0:
            valid, slot = place < PAIR_ROWS, place
        else:
            valid, slot = place >= PAIR_ROWS, 3 * (place - PAIR_ROWS) + part
        second = (slot >= EXPERT_ROWS).astype(jnp.int32)
        found.append((valid, pair, second, slot - EXPERT_ROWS * second))
    return found


def token_marks(code_block):
    marks = []
    wide = (BLOCK, BLOCK_EXPERTS)
    lanes = lax.broadcasted_iota(jnp.int32, wide, 1)
    for (valid, pair, second, _), (tall, _, _, order) in zip(
        packed_places(wide, 0), packed_places((BLOCK, SIDE), 0)
    ):
        owner = ((lanes == 2 * pair + second) & valid).astype(jnp.float32).astype(jnp.bfloat16)
        found = matmul(owner, code_block)
        hit = (found == order.astype(jnp.float32)) & tall
        marks.append((owner, hit.astype(jnp.float32)))
    return marks


def pack_tokens_kernel(with_gates, code, values, *refs):
    packed = refs[-1]
    marks = token_marks(code[0])
    main = marks[0][1].astype(jnp.bfloat16)
    last = values[:, 3 * QUARTER :]
    for part in range(3):
        columns = slice(part * QUARTER, (part + 1) * QUARTER)
        both = jnp.concatenate([main, marks[part + 1][1].astype(jnp.bfloat16)], axis=1)
        rows = jnp.concatenate([values[:, columns], last], axis=0)
        packed[:, columns] = matmul(both, rows).astype(jnp.bfloat16)
    if with_gates:
        high, low = refs[0], refs[1]
        owner, hit = marks[0]
        lanes = lax.broadcasted_iota(jnp.int32, (BLOCK, SIDE), 1)
        of_high = jnp.sum(hit * matmul(owner, high[0]), axis=1, keepdims=True)
        of_low = jnp.sum(hit * matmul(owner, low[0]), axis=1, keepdims=True)
        side = jnp.where(lanes == 0, of_high, jnp.where(lanes == 1, of_low, 0.0))
        packed[:, 3 * QUARTER :] = side.astype(jnp.bfloat16)


def pack_tokens(code, values, gates=None):
    blocks = code.shape[0]
    width = 3 * QUARTER + (SIDE if gates is not None else 0)
    small = pl.BlockSpec((1, BLOCK_EXPERTS, SIDE), lambda i: (i, 0, 0))
    extra = [] if gates is None else list(gates)
    return pl.pallas_call(
        functools.partial(pack_tokens_kernel, gates is not None),
        grid=(blocks,),
        out_shape=jax.ShapeDtypeStruct((blocks * BLOCK, width), jnp.bfloat16),
        in_specs=[small, pl.BlockSpec(values.shape, lambda i: (0, 0))] + [small] * len(extra),
        out_specs=pl.BlockSpec((BLOCK, width), lambda i: (i, 0)),
        compiler_params=pltpu.CompilerParams(vmem_limit_bytes=32 << 20),
        cost_estimate=pl.CostEstimate(
            flops=blocks * BLOCK * 256 * width * 2, bytes_accessed=8 << 20, transcendentals=0
        ),
        name="pack_tokens",
    )(code, values, *extra)


def slot_marks():
    shape = (2 * BLOCK_SLOTS, BLOCK)
    rows = lax.broadcasted_iota(jnp.int32, shape, 0)
    marks = []
    for valid, pair, second, order in packed_places(shape, 1):
        hit = (rows == second * BLOCK_SLOTS + pair * EXPERT_ROWS + order) & valid
        marks.append(hit.astype(jnp.float32).astype(jnp.bfloat16))
    return marks


def unpack_slots_kernel(with_gates, packed, values, *refs):
    marks = slot_marks()
    last = jnp.zeros((2 * BLOCK_SLOTS, QUARTER), jnp.float32)
    for part in range(3):
        columns = slice(part * QUARTER, (part + 1) * QUARTER)
        found = matmul(marks[0], packed[:, columns]).astype(jnp.bfloat16)
        values[0, :, columns] = found[:BLOCK_SLOTS]
        values[1, :, columns] = found[BLOCK_SLOTS:]
        last = last + matmul(marks[part + 1], packed[:, columns])
    last = last.astype(jnp.bfloat16)
    values[0, :, 3 * QUARTER :] = last[:BLOCK_SLOTS]
    values[1, :, 3 * QUARTER :] = last[BLOCK_SLOTS:]
    if with_gates:
        side = matmul(marks[0], packed[:, 3 * QUARTER :])
        gate = side[:, 0:1] + side[:, 1:2]
        wide = jnp.broadcast_to(gate, (2 * BLOCK_SLOTS, SIDE))
        refs[0][0] = wide[:BLOCK_SLOTS]
        refs[0][1] = wide[BLOCK_SLOTS:]


def unpack_slots(packed, with_gates):
    blocks = packed.shape[0] // BLOCK
    width = packed.shape[1]
    slots = blocks * BLOCK_SLOTS
    shapes = [jax.ShapeDtypeStruct((2, slots, 4 * QUARTER), jnp.bfloat16)]
    specs = [pl.BlockSpec((2, BLOCK_SLOTS, 4 * QUARTER), lambda i: (0, i, 0))]
    if with_gates:
        shapes.append(jax.ShapeDtypeStruct((2, slots, SIDE), jnp.float32))
        specs.append(pl.BlockSpec((2, BLOCK_SLOTS, SIDE), lambda i: (0, i, 0)))
    return pl.pallas_call(
        functools.partial(unpack_slots_kernel, with_gates),
        grid=(blocks,),
        out_shape=shapes,
        in_specs=[pl.BlockSpec((BLOCK, width), lambda i: (i, 0))],
        out_specs=specs,
        compiler_params=pltpu.CompilerParams(vmem_limit_bytes=32 << 20),
        cost_estimate=pl.CostEstimate(
            flops=blocks * 2 * BLOCK_SLOTS * BLOCK * 6 * QUARTER * 2,
            bytes_accessed=14 << 20,
            transcendentals=0,
        ),
        name="unpack_slots",
    )(packed)


def pack_slots_kernel(with_side, values, *refs):
    packed = refs[-1]
    marks = slot_marks()
    last = jnp.concatenate([values[0, :, 3 * QUARTER :], values[1, :, 3 * QUARTER :]], axis=0)
    for part in range(3):
        columns = slice(part * QUARTER, (part + 1) * QUARTER)
        rows = jnp.concatenate([values[0, :, columns], values[1, :, columns]], axis=0)
        found = outer_sum(marks[0], rows) + outer_sum(marks[part + 1], last)
        packed[:, columns] = found.astype(jnp.bfloat16)
    if with_side:
        side = jnp.concatenate([refs[0][0], refs[0][1]], axis=0)
        packed[:, 3 * QUARTER :] = outer_sum(marks[0], side).astype(jnp.bfloat16)


def pack_slots(values, side=None):
    slots = values.shape[1]
    blocks = slots // BLOCK_SLOTS
    width = 3 * QUARTER + (SIDE if side is not None else 0)
    extra = [] if side is None else [side]
    return pl.pallas_call(
        functools.partial(pack_slots_kernel, side is not None),
        grid=(blocks,),
        out_shape=jax.ShapeDtypeStruct((blocks * BLOCK, width), jnp.bfloat16),
        in_specs=[pl.BlockSpec((2, BLOCK_SLOTS, 4 * QUARTER), lambda i: (0, i, 0))]
        + [pl.BlockSpec((2, BLOCK_SLOTS, SIDE), lambda i: (0, i, 0))] * len(extra),
        out_specs=pl.BlockSpec((BLOCK, width), lambda i: (i, 0)),
        compiler_params=pltpu.CompilerParams(vmem_limit_bytes=32 << 20),
        cost_estimate=pl.CostEstimate(
            flops=blocks * 2 * BLOCK_SLOTS * BLOCK * 6 * QUARTER * 2,
            bytes_accessed=14 << 20,
            transcendentals=0,
        ),
        name="pack_slots",
    )(values, *extra)


def sum_tokens_kernel(with_side, code, packed, total, *refs):
    @pl.when(pl.program_id(0) == 0)
    def _():
        total[...] = jnp.zeros_like(total)

    marks = token_marks(code[0])
    main = marks[0][1].astype(jnp.bfloat16)
    last = jnp.zeros((total.shape[0], QUARTER), jnp.float32)
    for part in range(3):
        columns = slice(part * QUARTER, (part + 1) * QUARTER)
        total[:, columns] += outer_sum(main, packed[:, columns])
        last = last + outer_sum(marks[part + 1][1].astype(jnp.bfloat16), packed[:, columns])
    total[:, 3 * QUARTER :] += last
    if with_side:
        owner = marks[0][0].astype(jnp.float32)
        side = packed[:, 3 * QUARTER :].astype(jnp.float32)
        spread = [(side[:, i : i + 1] * owner).astype(jnp.bfloat16) for i in range(2)]
        refs[0][0] = outer_sum(main, spread[0]) + outer_sum(main, spread[1])


def sum_tokens(code, packed, with_side):
    blocks = code.shape[0]
    tokens, width = code.shape[2], packed.shape[1]
    shapes = [jax.ShapeDtypeStruct((tokens, 4 * QUARTER), jnp.float32)]
    specs = [pl.BlockSpec((tokens, 4 * QUARTER), lambda i: (0, 0))]
    if with_side:
        shapes.append(jax.ShapeDtypeStruct((blocks, tokens, BLOCK_EXPERTS), jnp.float32))
        specs.append(pl.BlockSpec((1, tokens, BLOCK_EXPERTS), lambda i: (i, 0, 0)))
    return pl.pallas_call(
        functools.partial(sum_tokens_kernel, with_side),
        grid=(blocks,),
        out_shape=shapes,
        in_specs=[
            pl.BlockSpec((1, BLOCK_EXPERTS, tokens), lambda i: (i, 0, 0)),
            pl.BlockSpec((BLOCK, width), lambda i: (i, 0)),
        ],
        out_specs=specs,
        compiler_params=pltpu.CompilerParams(vmem_limit_bytes=32 << 20),
        cost_estimate=pl.CostEstimate(
            flops=blocks * BLOCK * 128 * 6 * QUARTER * 2,
            bytes_accessed=8 << 20,
            transcendentals=0,
        ),
        name="sum_tokens",
    )(code, packed)


def exchange(packed):
    pairs = packed.reshape(-1, PACKED_ROWS, packed.shape[1])
    swapped = lax.all_to_all(pairs, ("row", "col"), split_axis=0, concat_axis=0, tiled=True)
    return swapped.reshape(packed.shape)


def per_device(
    block_in,
    gain_attn,
    w_query,
    w_keyval,
    w_out,
    gain_ffn,
    w_shared_in,
    w_shared_out,
    w_router,
    w_expert_in,
    w_expert_out,
    doc_lengths,
    routes,
    cotangent,
):
    row_count = lax.axis_size("row")
    rows_dev = block_in.shape[1]
    model_width = block_in.shape[2]
    group_tok = rows_dev * row_count
    head_size = w_keyval.shape[2] // 2
    local_heads = w_query.shape[1] // head_size
    local_kv = w_keyval.shape[1]
    group_size = local_heads // local_kv
    expert_count = w_router.shape[1]
    expert_ff = w_expert_out.shape[2]
    top_k = routes.shape[2]
    inv_root = head_size ** (-0.5)

    route_ids = routes.reshape(rows_dev, top_k)
    experts = jnp.arange(expert_count, dtype=jnp.int32)
    chosen = jnp.any(route_ids[:, :, None] == experts[None, None, :], axis=1)
    chosen_low = chosen.astype(jnp.bfloat16)
    tokens = jnp.arange(rows_dev, dtype=jnp.int32)
    before = (tokens[None, :] < tokens[:, None]).astype(jnp.bfloat16)
    order = matmul(before, chosen_low)
    code = jnp.where(chosen, order, -1.0).astype(jnp.bfloat16).T
    code = code.reshape(-1, BLOCK_EXPERTS, rows_dev)

    inputs = block_in.reshape(rows_dev, model_width).astype(jnp.float32)
    grad_low = cotangent.reshape(rows_dev, model_width)
    grad_rows = grad_low.astype(jnp.float32)
    scale_one, normed_one = normalize(inputs, gain_attn)
    shards = [w_query, w_keyval, w_out, w_shared_in, w_shared_out]
    shards = [part.reshape(part.shape[0], -1) for part in shards]
    full, group_one, group_grad = gather_start(
        jnp.concatenate(shards, axis=1), normed_one, grad_low
    )
    full_parts, end = [], 0
    for part in shards:
        full_parts.append(full[:, end : end + part.shape[1]])
        end += part.shape[1]
    full_query, full_keyval, full_out, full_shared_in, full_shared_out = full_parts

    segment, position = layout(doc_lengths.reshape(-1), group_tok)
    cosine, sine_table = rotary(position, head_size)
    query_pre = matmul(group_one, full_query).reshape(group_tok, local_heads, head_size)
    query_rot = rotate(query_pre, cosine, sine_table).astype(jnp.bfloat16)
    keyval_pre = matmul(group_one, full_keyval).reshape(group_tok, local_kv, 2 * head_size)
    key_rows = rotate(keyval_pre[..., :head_size], cosine, sine_table).astype(jnp.bfloat16)
    value_rows = keyval_pre[..., head_size:].astype(jnp.bfloat16)
    places = jnp.arange(group_tok, dtype=jnp.int32)
    allowed = (segment[:, None] == segment[None, :]) & (places[:, None] >= places[None, :])
    query_block = query_rot.reshape(group_tok, local_kv, group_size, head_size)

    def block_scores():
        scores = (
            jnp.einsum("qagd,kad->agqk", query_block, key_rows, preferred_element_type=jnp.float32)
            * inv_root
        )
        return jnp.where(allowed[None, None], scores, masked_score)

    scores = block_scores()
    highest = jnp.max(scores, axis=3, keepdims=True)
    weights = jnp.exp(scores - highest)
    totals = jnp.sum(weights, axis=3, keepdims=True)
    weights_low = (weights / totals).astype(jnp.bfloat16)
    attended = (
        jnp.einsum("agqk,kad->qagd", weights_low, value_rows, preferred_element_type=jnp.float32)
        .reshape(group_tok, local_heads * head_size)
        .astype(jnp.bfloat16)
    )
    log_totals = highest + jnp.log(totals)
    hidden_state = inputs + group_sums(matmul_t(attended, full_out), 0)
    scale_two, normed_two = normalize(hidden_state, gain_ffn)

    logits = matmul(normed_two, w_router)
    scores_sig = jnp.where(chosen, jax.nn.sigmoid(logits), 0.0)
    score_sum = jnp.sum(scores_sig, axis=1, keepdims=True)
    gate_weights = scores_sig / score_sum
    gates = [
        part.T.reshape(-1, BLOCK_EXPERTS, rows_dev) for part in split_low(gate_weights)
    ]
    received = exchange(pack_tokens(code, normed_two, gates))
    send_grads, received = lax.optimization_barrier((pack_tokens(code, grad_low), received))
    received_grads = exchange(send_grads)

    group_two = lax.all_gather(normed_two, "row", axis=0, tiled=True)
    shared_width = full_shared_in.shape[1] // 2
    shared_pre = matmul(group_two, full_shared_in)
    shared_gate, shared_up = shared_pre[:, :shared_width], shared_pre[:, shared_width:]
    shared_act, shared_slope = swish_parts(shared_gate)
    shared_hidden = (shared_act * shared_up).astype(jnp.bfloat16)
    shared_hidden_grad = matmul(group_grad, full_shared_out)
    grad_shared_out = outer_sum(group_grad, shared_hidden)
    shared_pre_grad = jnp.concatenate(
        [shared_hidden_grad * shared_up * shared_slope, shared_hidden_grad * shared_act], axis=1
    ).astype(jnp.bfloat16)
    grad_shared_in = outer_sum(group_two, shared_pre_grad)
    shared_sums = lax.psum_scatter(
        jnp.concatenate(
            [
                matmul_t(shared_hidden, full_shared_out).astype(jnp.bfloat16),
                matmul_t(shared_pre_grad, full_shared_in).astype(jnp.bfloat16),
            ],
            axis=1,
        ),
        "row",
        scatter_dimension=0,
        tiled=True,
    ).astype(jnp.float32)
    shared_branch, shared_input = shared_sums[:, :model_width], shared_sums[:, model_width:]

    expert_in, gate_wide = unpack_slots(received, True)
    gate = gate_wide[:, :, :1]
    expert_pre = jnp.einsum(
        "esd,edf->esf", expert_in, w_expert_in, preferred_element_type=jnp.float32
    )
    expert_act, expert_slope = swish_parts(expert_pre[..., :expert_ff])
    expert_hidden = (expert_act * expert_pre[..., expert_ff:]).astype(jnp.bfloat16)
    expert_out = (
        gate
        * jnp.einsum(
            "esf,edf->esd", expert_hidden, w_expert_out, preferred_element_type=jnp.float32
        )
    ).astype(jnp.bfloat16)
    send_out, received_grads = lax.optimization_barrier((pack_slots(expert_out), received_grads))
    returned = exchange(send_out)

    (expert_grads,) = unpack_slots(received_grads, False)
    plain_grad = jnp.einsum(
        "esd,edf->esf", expert_grads, w_expert_out, preferred_element_type=jnp.float32
    )
    gate_grad = jnp.sum(plain_grad * expert_hidden.astype(jnp.float32), axis=2, keepdims=True)
    gate_high, gate_low = split_low(gate_grad)
    lanes = jnp.arange(SIDE, dtype=jnp.int32)[None, None, :]
    side = jnp.where(lanes == 0, gate_high, jnp.where(lanes == 1, gate_low, 0)).astype(jnp.bfloat16)
    hidden_grad = gate * plain_grad
    expert_pre_grad = jnp.concatenate(
        [hidden_grad * expert_pre[..., expert_ff:] * expert_slope, hidden_grad * expert_act], axis=2
    ).astype(jnp.bfloat16)
    slot_grad = jnp.einsum(
        "esf,edf->esd", expert_pre_grad, w_expert_in, preferred_element_type=jnp.float32
    ).astype(jnp.bfloat16)
    send_back, returned = lax.optimization_barrier((pack_slots(slot_grad, side), returned))
    returned_grad = exchange(send_back)
    out_grad = (gate * expert_grads.astype(jnp.float32)).astype(jnp.bfloat16)
    grad_expert_out = jnp.einsum(
        "esd,esf->edf", out_grad, expert_hidden, preferred_element_type=jnp.float32
    )
    grad_expert_in = jnp.einsum(
        "esd,esf->edf", expert_in, expert_pre_grad, preferred_element_type=jnp.float32
    )
    (routed_branch,) = sum_tokens(code, returned, False)
    block_out = (hidden_state + shared_branch + routed_branch).astype(jnp.bfloat16)

    routed_input, gate_grads = sum_tokens(code, returned_grad, True)
    gate_grads = gate_grads.transpose(1, 0, 2).reshape(rows_dev, expert_count)
    score_grad = (
        gate_grads - jnp.sum(gate_grads * gate_weights, axis=1, keepdims=True)
    ) / score_sum
    logit_grad = (score_grad * scores_sig * (1.0 - scores_sig)).astype(jnp.bfloat16)
    router_input = matmul_t(logit_grad, w_router)
    normed_two_grad = shared_input + router_input + routed_input
    gain_ffn_grad, hidden_back = norm_back(hidden_state, scale_two, gain_ffn, normed_two_grad)
    hidden_total = grad_rows + hidden_back
    group_branch, group_logit = group_rows([hidden_total.astype(jnp.bfloat16), logit_grad], 0)
    attended_grad = matmul(group_branch, full_out).astype(jnp.bfloat16)
    grad_out_w = outer_sum(group_branch, attended)
    share_width = model_width // row_count
    router_part = outer_sum(
        lax.dynamic_slice_in_dim(group_two, lax.axis_index("row") * share_width, share_width, 1),
        group_logit,
    )
    sum_shared_in, sum_shared_out, sum_out, router_share = scatter_sum(
        [grad_shared_in, grad_shared_out, grad_out_w, router_part]
    )

    out_block = attended_grad.reshape(group_tok, local_kv, group_size, head_size)
    probs_full = jnp.exp(block_scores() - log_totals)
    prob_grad = jnp.einsum(
        "qagd,kad->agqk", out_block, value_rows, preferred_element_type=jnp.float32
    )
    row_delta = jnp.sum(probs_full * prob_grad, axis=3, keepdims=True)
    score_low = (probs_full * (prob_grad - row_delta)).astype(jnp.bfloat16)
    query_grad = (
        jnp.einsum("agqk,kad->qagd", score_low, key_rows, preferred_element_type=jnp.float32)
        * inv_root
    ).reshape(group_tok, local_heads, head_size)
    key_grad = (
        jnp.einsum("agqk,qagd->kad", score_low, query_block, preferred_element_type=jnp.float32)
        * inv_root
    )
    value_grad = jnp.einsum(
        "agqk,qagd->kad",
        probs_full.astype(jnp.bfloat16),
        out_block,
        preferred_element_type=jnp.float32,
    )
    query_pre_grad = (
        rotate(query_grad, cosine, -sine_table)
        .astype(jnp.bfloat16)
        .reshape(group_tok, local_heads * head_size)
    )
    keyval_pre_grad = (
        jnp.concatenate([rotate(key_grad, cosine, -sine_table), value_grad], axis=2)
        .astype(jnp.bfloat16)
        .reshape(group_tok, local_kv * 2 * head_size)
    )
    grad_query_w = outer_sum(group_one, query_pre_grad)
    grad_keyval_w = outer_sum(group_one, keyval_pre_grad)
    normed_one_grad = group_sums(
        matmul_t(query_pre_grad, full_query) + matmul_t(keyval_pre_grad, full_keyval), 3
    )
    gain_attn_grad, input_back = norm_back(inputs, scale_one, gain_attn, normed_one_grad)
    input_total = hidden_total + input_back

    sum_query, sum_keyval = scatter_sum([grad_query_w, grad_keyval_w])
    gain_sums, router_sum = finish(
        jnp.stack([gain_attn_grad, gain_ffn_grad]).reshape(-1, 128),
        router_share.reshape(-1, expert_count).astype(jnp.bfloat16),
    )
    gain_sums = gain_sums.reshape(2, model_width)
    return (
        block_out.reshape(1, rows_dev, model_width),
        input_total.reshape(1, rows_dev, model_width),
        gain_sums[0],
        sum_query,
        sum_keyval.reshape(w_keyval.shape),
        sum_out,
        gain_sums[1],
        sum_shared_in.reshape(w_shared_in.shape),
        sum_shared_out,
        router_sum.reshape(model_width, expert_count).astype(jnp.float32),
        grad_expert_in,
        grad_expert_out,
    )


def solution(mesh):
    in_specs = (
        P("col", "row", None),
        P(),
        P("col", "row"),
        P("col", "row", None),
        P("col", "row"),
        P(),
        P("col", None, "row"),
        P("col", "row"),
        P(),
        P(("row", "col"), None, None),
        P(("row", "col"), None, None),
        P("col", None),
        P("col", "row", None),
        P("col", "row", None),
    )
    out_specs = (
        P("col", "row", None),
        P("col", "row", None),
        P(),
        P("col", "row"),
        P("col", "row", None),
        P("col", "row"),
        P(),
        P("col", None, "row"),
        P("col", "row"),
        P(),
        P(("row", "col"), None, None),
        P(("row", "col"), None, None),
    )
    return jax.shard_map(
        per_device, mesh=mesh, in_specs=in_specs, out_specs=out_specs, check_vma=False
    )
```

time: 2350 us -> 721 us (0.31)
  waiting for transfers between devices: 1660 us -> 275 us
  blocking collectives: 230 us -> 0 us
  Pallas kernels: 0 us -> 208 us
  local copies, waits for them, and re-layouts: 230 us -> 34.1 us
    reduce_scatter x8 -> x1, waiting for transfers between devices: 753 us -> 0.02 us  [per_device(): lax.psum_scatter(jnp.concatenate([matmul_t(shared_hidden, full_shared_out...]
    all_gather x8 -> x1, waiting for transfers between devices: 503 us -> 0.02 us  [per_device(): group_two = lax.all_gather(normed_two, 'row', axis=0, tiled=True)]
    pallas_call x0 -> x13, Pallas kernels: none -> 208 us  [the longest x1 54.6 us: gather_start(): pl.pallas_call(gather_kernel, out_shape=[jax.ShapeDtypeStruct((32, *shard...]
    all_gather x1 -> x0, blocking collectives: 165 us -> none  [per_device(): lax.all_gather(w_shared_out, 'col', axis=0, tiled=True)]
    unnamed x19 -> x2, waiting for transfers between devices: 110 us -> 0.7 us
    psum x1 -> x0, waiting for transfers between devices: 85.8 us -> none  [per_device(): lax.psum((gain_attn_grad, gain_ffn_grad, router_grad), ('row', 'col'))]
    all_to_all x6 -> x0, local copies, waits for them, and re-layouts: 75 us -> none  [the longest x4 53.9 us: to_experts(): lax.all_to_all(values, ('row', 'col'), split_axis=0, concat_axis=1, tiled...]
    all_to_all x4 -> x6, waiting for transfers between devices: 203 us -> 274 us  [the longest x4 242 us: exchange(): lax.all_to_all(pairs, ('row', 'col'), split_axis=0, concat_axis=0, tiled=...]
  transfers between devices with their start and end apart: 22 -> 8, of which waited for: 18 -> 5; matrix products, arithmetic and copies ran while one was open for 14% -> 13% of each run, Pallas kernels for 0% -> 10%
where the time goes in v2:
time: 721 us; the launch traced here: 710 us
  waiting for transfers between devices  275 us (38%)
  Pallas kernels  208 us (29%)
  matrix products  97.3 us (13%)
  starting transfers between devices  45.2 us (6%)
  other arithmetic  34.6 us (5%)
  local copies, waits for them, and re-layouts  34.1 us (5%)
  between operations  15.9 us (2%)
    all_to_all x4, waiting for transfers between devices, exchange(): lax.all_to_all(pairs, ('row', 'col'), split_axis=0, concat_axis=0, tiled=...  242 us
    pallas_call x1, Pallas kernels, gather_start(): pl.pallas_call(gather_kernel, out_shape=[jax.ShapeDtypeStruct((32, *shard...  54.6 us
    pallas_call x2, Pallas kernels, group_sums(): pl.pallas_call(row_sum_kernel, out_shape=jax.ShapeDtypeStruct((rows, widt...  54.5 us
    all_to_all x2, waiting for transfers between devices, scatter_sum(): lax.all_to_all(jnp.concatenate(parts, axis=2), 'col', split_axis=0, conca...  32.1 us
    all_to_all x4, starting transfers between devices, exchange(): lax.all_to_all(pairs, ('row', 'col'), split_axis=0, concat_axis=0, tiled=...  31.8 us
    pallas_call x1, Pallas kernels, finish(): pl.pallas_call(finish_kernel, out_shape=[jax.ShapeDtypeStruct(gains.shape...  29 us
    unnamed x146, local copies, waits for them, and re-layouts  20.5 us
    pallas_call x1, Pallas kernels, group_rows(): pl.pallas_call(functools.partial(row_gather_kernel, count), out_shape=[ja...  19.1 us
  transfers between devices with their start and end apart: 8, of which 5 were waited for; matrix products, arithmetic and copies ran while one was open for 13% of the time, Pallas kernels for 10%

profile of v2, /device:TPU:1, one launch (start us, length us, event | category | flops | bytes accessed | tf_op | source)
XLA Modules:
  0.0 710.3 jit_solution(5471423254357875912)
XLA Ops:
  15.1 54.6 %gather_start.1 = (bf16[32,64,1664]{2,1,0:T(8,128)(2,1)}, bf16[4,128,2048]{2,1,0:T(8,128)(2,1)}, bf16[4,128,2048]{2,1,0:T(8,128)(2,1)}) custom-call(bf16[64,1664]{1,0:T(8,128)(2,1)} %copy-done.35, bf16[128,2048]{1,0:T(8,128)(2,1)} %fusion.45.normed, bf16[128,2048]{1,0:T(8,128)(2,1)} %bitcast.223), custom_call_target="tpu_custom_call" | custom-call | bytes 209715200 | tf_op jit(solution)/shard_map/gather_start/pallas_call | solution.py:269
  84.3 3.1 convolution_convert_fusion.5
  87.4 20.5 %group_sums.2 = f32[128,2048]{1,0:T(8,128)S(1)} custom-call(bf16[4,128,2048]{2,1,0:T(8,128)(2,1)S(1)} %bitcast.225), custom_call_target="tpu_custom_call" | custom-call | bytes 67108864 | tf_op jit(solution)/shard_map/group_sums/pallas_call | solution.py:333
  110.6 4.8 pack_tokens.3
  118.3 5.6 all-to-all-start
  123.9 3.7 pack_tokens.2
  130.3 75.5 %all-to-all-done = bf16[128,16,1664]{2,1,0:T(8,128)(2,1)} async-done(((bf16[128,16,1664]{2,1,0:T(8,128)(2,1)}), bf16[128,16,1664]{2,1,0:T(8,128)(2,1)}, u32[]{:S(2)}, u32[]{:S(2)}) %all-to-all-start) | async-done | bytes 6815776 | tf_op jit(solution)/shard_map/all_to_all | solution.py:675
  205.8 9.3 %all-to-all-start.1 = ((bf16[128,16,1536]{2,1,0:T(8,128)(2,1)}), bf16[128,16,1536]{2,1,0:T(8,128)(2,1)}, u32[]{:S(2)}, u32[]{:S(2)}) async-start(bf16[128,16,1536]{2,1,0:T(8,128)(2,1)} %bitcast.221), calls=%async_computation.2 | async-start | bytes 12582912 | tf_op jit(solution)/shard_map/all_to_all | solution.py:675
  215.8 8.2 %unpack_slots.2 = (bf16[2,768,2048]{2,1,0:T(8,128)(2,1)S(1)}, f32[2,768,128]{2,1,0:T(8,128)S(1)}) custom-call(bf16[2048,1664]{1,0:T(8,128)(2,1)} %bitcast.34.packed), custom_call_target="tpu_custom_call" | custom-call | flops 2415919104 | bytes 14680064 | tf_op jit(solution)/shard_map/unpack_slots/pallas_call | solution.py:574
  224.0 11.3 %fusion.112 = f32[2,768,1024]{2,1,0:T(8,128)S(1)} fusion(bf16[2,768,2048]{2,1,0:T(8,128)(2,1)S(1)} %get-tuple-element.34, bf16[2,2048,1024]{2,1,0:T(8,128)(2,1)} %param.23), kind=kOutput, calls=%fused_computation.203 | convolution fusion | flops 6442450944 | bytes 20971520 | tf_op jit(solution)/shard_map/esd,edf->esf/dot_general | solution.py:804
  239.9 3.7 multiply_convert_fusion.1.values
  243.6 5.4 pack_slots.2
  251.7 46.5 %all-to-all-done.1 = bf16[128,16,1536]{2,1,0:T(8,128)(2,1)} async-done(((bf16[128,16,1536]{2,1,0:T(8,128)(2,1)}), bf16[128,16,1536]{2,1,0:T(8,128)(2,1)}, u32[]{:S(2)}, u32[]{:S(2)}) %all-to-all-start.1) | async-done | bytes 6291488 | tf_op jit(solution)/shard_map/all_to_all | solution.py:675
  298.3 9.4 %all-to-all-start.2 = ((bf16[128,16,1536]{2,1,0:T(8,128)(2,1)}), bf16[128,16,1536]{2,1,0:T(8,128)(2,1)}, u32[]{:S(2)}, u32[]{:S(2)}) async-start(bf16[128,16,1536]{2,1,0:T(8,128)(2,1)} %bitcast.220), calls=%async_computation.3 | async-start | bytes 12582912 | tf_op jit(solution)/shard_map/all_to_all | solution.py:675
  319.7 7.8 %unpack_slots.3 = bf16[2,768,2048]{2,1,0:T(8,128)(2,1)S(1)} custom-call(bf16[2048,1536]{1,0:T(8,128)(2,1)} %bitcast.36.packed), custom_call_target="tpu_custom_call" | custom-call | flops 2415919104 | bytes 14680064 | tf_op jit(solution)/shard_map/unpack_slots/pallas_call | solution.py:574
  327.6 9.2 %multiply_convert_fusion.4 = (bf16[2,768,512]{2,1,0:T(8,128)(2,1)S(1)}, bf16[2,768,512]{2,1,0:T(8,128)(2,1)S(1)}, f32[2,768]{1,0:T(2,128)S(1)}) fusion(f32[2,768,1024]{2,1,0:T(8,128)} %copy-done.18, f32[2,768]{1,0:T(2,128)S(1)} %slice_reduce_fusion, bf16[2,768,512]{2,1,0:T(8,128)(2,1)S(1)} %copy-done.24, bf16[2,768,2048]{2,1,0:T(8,128)(2,1)S(1)} %unpack_slots.3, ...), kind=kOutput, calls=%fused_computation.25 | convolution fusion | flops 3234593280 | bytes 21508096 | tf_op jit(solution)/shard_map/esd,edf->esf/dot_general | solution.py:819
  337.3 11.1 %convolution_convert_fusion.values = bf16[2,768,2048]{2,1,0:T(8,128)(2,1)S(1)} fusion(bf16[2,2048,1024]{2,1,0:T(8,128)(2,1)} %param.23, bf16[2,768,512]{2,1,0:T(8,128)(2,1)S(1)} %get-tuple-element.57, bf16[2,768,512]{2,1,0:T(8,128)(2,1)S(1)} %get-tuple-element.56), kind=kOutput, calls=%fused_computation.6 | convolution fusion | flops 6451888128 | bytes 17825792 | tf_op jit(solution)/shard_map/esf,edf->esd/dot_general | solution.py:830
  348.5 5.8 pack_slots.3
  357.1 48.4 %all-to-all-done.2 = bf16[128,16,1536]{2,1,0:T(8,128)(2,1)} async-done(((bf16[128,16,1536]{2,1,0:T(8,128)(2,1)}), bf16[128,16,1536]{2,1,0:T(8,128)(2,1)}, u32[]{:S(2)}, u32[]{:S(2)}) %all-to-all-start.2) | async-done | bytes 6291488 | tf_op jit(solution)/shard_map/all_to_all | solution.py:675
  405.5 7.6 %all-to-all-start.3 = ((bf16[128,16,1664]{2,1,0:T(8,128)(2,1)}), bf16[128,16,1664]{2,1,0:T(8,128)(2,1)}, u32[]{:S(2)}, u32[]{:S(2)}) async-start(bf16[128,16,1664]{2,1,0:T(8,128)(2,1)} %bitcast.218), calls=%async_computation.4 | async-start | bytes 13631488 | tf_op jit(solution)/shard_map/all_to_all | solution.py:675
  415.9 7.6 %sum_tokens.2 = f32[128,2048]{1,0:T(8,128)S(1)} custom-call(bf16[8,32,128]{2,1,0:T(8,128)(2,1)S(1)} %bitcast.228, bf16[2048,1536]{1,0:T(8,128)(2,1)} %bitcast.38.packed), custom_call_target="tpu_custom_call" | custom-call | flops 1610612736 | bytes 8388608 | tf_op jit(solution)/shard_map/sum_tokens/pallas_call | solution.py:654
  423.5 71.6 %all-to-all-done.3 = bf16[128,16,1664]{2,1,0:T(8,128)(2,1)} async-done(((bf16[128,16,1664]{2,1,0:T(8,128)(2,1)}), bf16[128,16,1664]{2,1,0:T(8,128)(2,1)}, u32[]{:S(2)}, u32[]{:S(2)}) %all-to-all-start.3) | async-done | bytes 6815776 | tf_op jit(solution)/shard_map/all_to_all | solution.py:675
  495.1 7.9 %sum_tokens.3 = (f32[128,2048]{1,0:T(8,128)S(1)}, f32[8,128,32]{2,1,0:T(8,128)S(1)}) custom-call(bf16[8,32,128]{2,1,0:T(8,128)(2,1)S(1)} %bitcast.229, bf16[2048,1664]{1,0:T(8,128)(2,1)} %bitcast.41.packed), custom_call_target="tpu_custom_call" | custom-call | flops 1610612736 | bytes 8388608 | tf_op jit(solution)/shard_map/sum_tokens/pallas_call | solution.py:654
  510.7 19.1 %group_rows.1 = (bf16[4,128,2048]{2,1,0:T(8,128)(2,1)}, bf16[4,128,256]{2,1,0:T(8,128)(2,1)}) custom-call(bf16[128,2048]{1,0:T(8,128)(2,1)} %get-tuple-element.50.refs_0_, bf16[128,256]{1,0:T(8,128)(2,1)} %copy-done.29), custom_call_target="tpu_custom_call" | custom-call | bytes 67108864 | tf_op jit(solution)/shard_map/group_rows/pallas_call | solution.py:164
  529.8 3.7 fusion.22
  542.9 7.2 %all-to-all-start.5 = ((bf16[32,64,768]{2,1,0:T(8,128)(2,1)}), bf16[32,64,768]{2,1,0:T(8,128)(2,1)}, u32[]{:S(2)}, u32[]{:S(2)}) async-start(bf16[32,64,768]{2,1,0:T(8,128)(2,1)} %pad_maximum_fusion.3), calls=%async_computation.6 | async-start | bytes 6291456 | tf_op jit(solution)/shard_map/all_to_all | solution.py:356
  558.8 32.1 %all-to-all-done.5 = bf16[32,64,768]{2,1,0:T(8,128)(2,1)} async-done(((bf16[32,64,768]{2,1,0:T(8,128)(2,1)}), bf16[32,64,768]{2,1,0:T(8,128)(2,1)}, u32[]{:S(2)}, u32[]{:S(2)}) %all-to-all-start.5) | async-done | bytes 3145760 | tf_op jit(solution)/shard_map/all_to_all | solution.py:356
  591.0 5.7 all-to-all-start.4
  596.7 10.5 %fusion = f32[2,2048,512]{2,1,0:T(8,128)} fusion(bf16[2,768,512]{2,1,0:T(8,128)(2,1)} %copy-done.23, bf16[2,768,2048]{2,1,0:T(8,128)(2,1)} %copy-done.5, f32[2,768]{1,0:T(2,128)S(1)} %copy-done.49), kind=kOutput, calls=%fused_computation.3 | convolution fusion | flops 3230662656 | bytes 16259072 | tf_op jit(solution)/shard_map/esd,esf->edf/dot_general | solution.py:836
  607.2 10.6 %fusion.16 = f32[2,2048,1024]{2,1,0:T(8,128)} fusion(bf16[2,768,2048]{2,1,0:T(8,128)(2,1)S(1)} %bitcast.234, bf16[2,768,512]{2,1,0:T(8,128)(2,1)S(1)} %copy-done.68, bf16[2,768,512]{2,1,0:T(8,128)(2,1)S(1)} %copy-done.66), kind=kOutput, calls=%fused_computation.51 | convolution fusion | flops 6448742400 | bytes 26214400 | tf_op jit(solution)/shard_map/esd,esf->edf/dot_general | solution.py:839
  622.9 34.0 %group_sums.3 = f32[128,2048]{1,0:T(8,128)S(1)} custom-call(bf16[4,128,2048]{2,1,0:T(8,128)(2,1)S(1)} %bitcast.222), custom_call_target="tpu_custom_call" | custom-call | bytes 67108864 | tf_op jit(solution)/shard_map/group_sums/pallas_call | solution.py:333
  669.3 29.0 %finish.1 = (f32[32,128]{1,0:T(8,128)}, bf16[4,32,16,256]{3,2,1,0:T(8,128)(2,1)}) custom-call(f32[32,128]{1,0:T(8,128)} %reshape.571.gains, bf16[16,256]{1,0:T(8,128)(2,1)} %convert_element_type.250.share), custom_call_target="tpu_custom_call" | custom-call | bytes 67108864 | tf_op jit(solution)/shard_map/finish/pallas_call | solution.py:443
  (242 shorter events, 104.0 us)
Async XLA Ops:
  7.2 102.6 %copy-start = (bf16[2048,256]{1,0:T(8,128)(2,1)S(1)}, bf16[2048,256]{1,0:T(8,128)(2,1)}, u32[]{:S(2)}) copy-start(bf16[2048,256]{1,0:T(8,128)(2,1)} %param.22) | copy-start | bytes 3145732
  84.3 23.7 %copy-start.14 = (bf16[1,128,2048]{2,1,0:T(8,128)(2,1)S(1)}, bf16[1,128,2048]{2,1,0:T(8,128)(2,1)}, u32[]{:S(2)}) copy-start(bf16[1,128,2048]{2,1,0:T(8,128)(2,1)} %param.14) | copy-start | bytes 1572868
  87.4 21.4 %copy-start.54 = (s32[1,128,8]{1,2,0:T(8,128)S(1)}, s32[1,128,8]{1,2,0:T(8,128)}, u32[]{:S(2)}) copy-start(s32[1,128,8]{1,2,0:T(8,128)} %param.26) | copy-start | bytes 12292
  87.4 22.2 %copy-start.46 = (f32[2048]{0:T(1024)S(1)}, f32[2048]{0:T(1024)}, u32[]{:S(2)}) copy-start(f32[2048]{0:T(1024)} %param.19) | copy-start | bytes 24580
  118.3 87.5 %all-to-all-start = ((bf16[128,16,1664]{2,1,0:T(8,128)(2,1)}), bf16[128,16,1664]{2,1,0:T(8,128)(2,1)}, u32[]{:S(2)}, u32[]{:S(2)}) async-start(bf16[128,16,1664]{2,1,0:T(8,128)(2,1)} %bitcast.219), calls=%async_computation.1 | async-start | bytes 13631488 | tf_op jit(solution)/shard_map/all_to_all | solution.py:675
  205.8 92.4 %all-to-all-start.1 = ((bf16[128,16,1536]{2,1,0:T(8,128)(2,1)}), bf16[128,16,1536]{2,1,0:T(8,128)(2,1)}, u32[]{:S(2)}, u32[]{:S(2)}) async-start(bf16[128,16,1536]{2,1,0:T(8,128)(2,1)} %bitcast.221), calls=%async_computation.2 | async-start | bytes 12582912 | tf_op jit(solution)/shard_map/all_to_all | solution.py:675
  215.1 93.0 %all-gather.2.cloned.1.call-start = ((), (), s32[]{:S(2)}) async-start(), calls=%async_computation.7 | async-start | bytes 2621440 | tf_op jit(solution)/shard_map/all_gather | solution.py:776
  224.0 11.4 %copy-start.9 = (bf16[2,768,2048]{2,1,0:T(8,128)(2,1)}, bf16[2,768,2048]{2,1,0:T(8,128)(2,1)S(1)}, u32[]{:S(2)}) copy-start(bf16[2,768,2048]{2,1,0:T(8,128)(2,1)S(1)} %get-tuple-element.34) | copy-start | bytes 18874372
  238.6 88.9 %copy-start.48 = (f32[2,768]{1,0:T(2,128)}, f32[2,768]{1,0:T(2,128)S(1)}, u32[]{:S(2)}) copy-start(f32[2,768]{1,0:T(2,128)S(1)} %slice_reduce_fusion) | copy-start | bytes 18436
  298.3 107.2 %all-to-all-start.2 = ((bf16[128,16,1536]{2,1,0:T(8,128)(2,1)}), bf16[128,16,1536]{2,1,0:T(8,128)(2,1)}, u32[]{:S(2)}, u32[]{:S(2)}) async-start(bf16[128,16,1536]{2,1,0:T(8,128)(2,1)} %bitcast.220), calls=%async_computation.3 | async-start | bytes 12582912 | tf_op jit(solution)/shard_map/all_to_all | solution.py:675
  307.6 105.5 %reduce-scatter.2.cloned.1.call-start = ((), (), s32[]{:S(2)}) async-start(), calls=%async_computation.8 | async-start | bytes 5242880 | tf_op jit(solution)/shard_map/reduce_scatter | solution.py:788
  319.7 7.9 %copy-start.24 = (bf16[2,768,512]{2,1,0:T(8,128)(2,1)S(1)}, bf16[2,768,512]{2,1,0:T(8,128)(2,1)}, u32[]{:S(2)}) copy-start(bf16[2,768,512]{2,1,0:T(8,128)(2,1)} %copy-done.23) | copy-start | bytes 4718596
  319.7 7.9 %copy-start.58 = (bf16[2,2048,512]{2,1,0:T(8,128)(2,1)S(1)}, bf16[2,2048,512]{2,1,0:T(8,128)(2,1)}, u32[]{:S(2)}) copy-start(bf16[2,2048,512]{2,1,0:T(8,128)(2,1)} %param.24) | copy-start | bytes 12582916
  327.6 9.2 %copy-start.5 = (bf16[2,768,2048]{2,1,0:T(8,128)(2,1)}, bf16[2,768,2048]{2,1,0:T(8,128)(2,1)S(1)}, u32[]{:S(2)}) copy-start(bf16[2,768,2048]{2,1,0:T(8,128)(2,1)S(1)} %unpack_slots.3) | copy-start | bytes 18874372
  336.8 11.7 %copy-start.65 = (bf16[2,768,512]{2,1,0:T(8,128)(2,1)}, bf16[2,768,512]{2,1,0:T(8,128)(2,1)S(1)}, u32[]{:S(2)}) copy-start(bf16[2,768,512]{2,1,0:T(8,128)(2,1)S(1)} %get-tuple-element.56) | copy-start | bytes 4718596
  336.8 11.7 %copy-start.67 = (bf16[2,768,512]{2,1,0:T(8,128)(2,1)}, bf16[2,768,512]{2,1,0:T(8,128)(2,1)S(1)}, u32[]{:S(2)}) copy-start(bf16[2,768,512]{2,1,0:T(8,128)(2,1)S(1)} %get-tuple-element.57) | copy-start | bytes 4718596
  405.5 89.6 %all-to-all-start.3 = ((bf16[128,16,1664]{2,1,0:T(8,128)(2,1)}), bf16[128,16,1664]{2,1,0:T(8,128)(2,1)}, u32[]{:S(2)}, u32[]{:S(2)}) async-start(bf16[128,16,1664]{2,1,0:T(8,128)(2,1)} %bitcast.218), calls=%async_computation.4 | async-start | bytes 13631488 | tf_op jit(solution)/shard_map/all_to_all | solution.py:675
  495.1 11.0 %copy-start.53 = (f32[128]{0:T(128)S(1)}, f32[128]{0:T(128)}, u32[]{:S(2)}) copy-start(f32[128]{0:T(128)} %copy-done.52) | copy-start | bytes 1540
  542.9 7.2 %copy-start.17 = (bf16[4,128,2048]{2,1,0:T(8,128)(2,1)S(1)}, bf16[4,128,2048]{2,1,0:T(8,128)(2,1)}, u32[]{:S(2)}) copy-start(bf16[4,128,2048]{2,1,0:T(8,128)(2,1)} %get-tuple-element.31) | copy-start | bytes 6291460
  542.9 7.2 %copy-start.34 = (bf16[512,128]{0,1:T(8,128)(2,1)S(1)}, bf16[512,128]{0,1:T(8,128)(2,1)}, u32[]{:S(2)}) copy-start(bf16[512,128]{0,1:T(8,128)(2,1)} %copy-done.33) | copy-start | bytes 393220
  542.9 48.1 %all-to-all-start.5 = ((bf16[32,64,768]{2,1,0:T(8,128)(2,1)}), bf16[32,64,768]{2,1,0:T(8,128)(2,1)}, u32[]{:S(2)}, u32[]{:S(2)}) async-start(bf16[32,64,768]{2,1,0:T(8,128)(2,1)} %pad_maximum_fusion.3), calls=%async_computation.6 | async-start | bytes 6291456 | tf_op jit(solution)/shard_map/all_to_all | solution.py:356
  558.8 37.8 %copy-start.49 = (f32[2,768]{1,0:T(2,128)S(1)}, f32[2,768]{1,0:T(2,128)}, u32[]{:S(2)}) copy-start(f32[2,768]{1,0:T(2,128)} %copy-done.48) | copy-start | bytes 18436
  591.0 16.2 %slice-start = ((s8[6291456]{0:T(1024)(128)(4,1)}), s8[2097152]{0:T(1024)(128)(4,1)S(1)}, s32[]{:S(2)}) async-start(s8[6291456]{0:T(1024)(128)(4,1)} %bitcast.233), calls=%async_computation.9 | async-start | bytes 4194304
  591.0 73.2 %all-to-all-start.4 = ((bf16[32,64,960]{2,1,0:T(8,128)(2,1)}), bf16[32,64,960]{2,1,0:T(8,128)(2,1)}, u32[]{:S(2)}, u32[]{:S(2)}) async-start(bf16[32,64,960]{2,1,0:T(8,128)(2,1)} %pad_maximum_fusion.1), calls=%async_computation.5 | async-start | bytes 8388608 | tf_op jit(solution)/shard_map/all_to_all | solution.py:356
  596.7 10.5 %slice-start.1 = ((s8[6291456]{0:T(1024)(128)(4,1)}), s8[4194304]{0:T(1024)(128)(4,1)S(1)}, s32[]{:S(2)}) async-start(s8[6291456]{0:T(1024)(128)(4,1)} %bitcast.233), calls=%async_computation.10 | async-start | bytes 8388608
  596.7 10.5 %copy-start.66 = (bf16[2,768,512]{2,1,0:T(8,128)(2,1)S(1)}, bf16[2,768,512]{2,1,0:T(8,128)(2,1)}, u32[]{:S(2)}) copy-start(bf16[2,768,512]{2,1,0:T(8,128)(2,1)} %copy-done.65) | copy-start | bytes 4718596
  596.7 10.5 %copy-start.68 = (bf16[2,768,512]{2,1,0:T(8,128)(2,1)S(1)}, bf16[2,768,512]{2,1,0:T(8,128)(2,1)}, u32[]{:S(2)}) copy-start(bf16[2,768,512]{2,1,0:T(8,128)(2,1)} %copy-done.67) | copy-start | bytes 4718596
  607.2 10.6 %copy-start.37 = (bf16[512,64]{0,1:T(8,128)(2,1)S(1)}, bf16[512,64]{0,1:T(8,128)(2,1)}, u32[]{:S(2)}) copy-start(bf16[512,64]{0,1:T(8,128)(2,1)} %copy-done.36) | copy-start | bytes 196612
  619.9 37.0 %copy-start.15 = (bf16[1,128,2048]{2,1,0:T(8,128)(2,1)S(1)}, bf16[1,128,2048]{2,1,0:T(8,128)(2,1)}, u32[]{:S(2)}) copy-start(bf16[1,128,2048]{2,1,0:T(8,128)(2,1)} %param.14) | copy-start | bytes 1572868
  619.9 37.0 %copy-start.47 = (f32[2048]{0:T(1024)S(1)}, f32[2048]{0:T(1024)}, u32[]{:S(2)}) copy-start(f32[2048]{0:T(1024)} %param.15) | copy-start | bytes 24580
  619.9 37.0 %copy-start.51 = (f32[128]{0:T(128)S(1)}, f32[128]{0:T(128)}, u32[]{:S(2)}) copy-start(f32[128]{0:T(128)} %copy-done.50) | copy-start | bytes 1540
  622.9 35.0 %copy-start.55 = (f32[128]{0:T(128)S(1)}, f32[128]{0:T(128)}, u32[]{:S(2)}) copy-start(f32[128]{0:T(128)} %get-tuple-element.78) | copy-start | bytes 1540
  (47 other events, 143.5 us)
Sparse Core Ops, SparseCore 0:
  218.2 39.8 all-gather.1
  319.8 75.6 reduce-scatter.1

commit v3 on v2

--- a/solution.py
+++ b/solution.py
@@ -350,119 +350,201 @@
     )(parts)
 
 
-def scatter_sum(values):
-    parts = [part.astype(jnp.bfloat16).reshape(32, 64, -1) for part in values]
-    widths = [part.shape[2] for part in parts]
-    swapped = lax.all_to_all(
-        jnp.concatenate(parts, axis=2), "col", split_axis=0, concat_axis=0, tiled=True
-    )
-    total = jnp.sum(swapped, axis=0, dtype=jnp.float32)
-    ends = [sum(widths[: i + 1]) for i in range(len(widths))]
-    return [total[:, end - width : end] for end, width in zip(ends, widths)]
-
-
-def finish_kernel(gains, share, total, router, values, buffers, *sems):
-    send_sem, recv_sem, own_sem, col_send, col_recv, row_send, row_recv = sems
-    row, col, sibling, partner, _ = row_places()
-    along_x, along_z, along_y = col // 16, lax.rem(col // 4, 4), lax.rem(col, 4)
-    stages = (
-        [(lax.rem(row + i, 4), col) for i in (1, 2, 3)],
-        [(row, along_x * 16 + along_z * 4 + lax.rem(along_y + i, 4)) for i in (1, 2, 3)],
-        [(row, along_x * 16 + lax.rem(along_z + i, 4) * 4 + along_y) for i in (1, 2, 3)],
-        [(row, lax.rem(col + 16, 32))],
-    )
-    greet(stages[0])
-    barrier = pltpu.get_barrier_semaphore()
-
-    def greet_col(step, carry):
-        peer = (row, lax.rem(col + step, 32))
-        pl.semaphore_signal(barrier, inc=1, device_id=peer, device_id_type=MESH)
-        return carry
-
-    lax.fori_loop(1, 32, greet_col, 0)
-    own = pltpu.make_async_copy(share, router.at[row, col], own_sem)
-    own.start()
-    values[0] = gains[...]
-    await_greetings(34)
-
-    def push(step, carry):
-        pltpu.make_async_remote_copy(
-            src_ref=share,
-            dst_ref=router.at[row, col],
-            send_sem=col_send,
-            recv_sem=col_recv,
-            device_id=(row, lax.rem(col + step, 32)),
+def finish_kernel(
+    parts, grads, hidden, inputs, scale, gain, gain_ffn, result, summed, gains, *scratch
+):
+    near, far, outgoing, first, first_sum, second, second_sum, third = scratch[:8]
+    values, buffers = scratch[8:10]
+    row_send, row_recv, one_send, one_recv, two_send, two_recv = scratch[10:16]
+    three_send, three_recv, gain_send, gain_recv = scratch[16:]
+    row, col, sibling, partner, across = row_places()
+    x, z, y = col // 16, lax.rem(col // 4, 4), lax.rem(col, 4)
+    other_x = 1 - x
+    half_rows = grads.shape[3] // 2
+    y_peers = [(row, x * 16 + z * 4 + lax.rem(y + i, 4)) for i in (1, 2, 3)]
+    z_peers = [(row, x * 16 + lax.rem(z + i, 4) * 4 + y) for i in (1, 2, 3)]
+    x_peer = (row, other_x * 16 + z * 4 + y)
+    row_peers = [(peer, col) for peer in (sibling, partner, across)]
+
+    def copy(source, target, sems, at, peer):
+        return pltpu.make_async_remote_copy(
+            src_ref=source,
+            dst_ref=target,
+            send_sem=sems[0].at[at],
+            recv_sem=sems[1].at[at],
+            device_id=peer,
             device_id_type=MESH,
-        ).start()
-        return carry
-
-    lax.fori_loop(1, 32, push, 0)
-    at = 0
-    for stage, peers in enumerate(stages):
-        copies = []
-        for i, peer in enumerate(peers):
-            copies.append(
-                pltpu.make_async_remote_copy(
-                    src_ref=values.at[stage],
-                    dst_ref=buffers.at[at + i],
-                    send_sem=send_sem.at[at + i],
-                    recv_sem=recv_sem.at[at + i],
-                    device_id=peer,
-                    device_id_type=MESH,
+        )
+
+    greet(row_peers + y_peers + z_peers + [x_peer])
+    await_greetings(10)
+
+    row_sems = (row_send, row_recv)
+    row_copies_ = [
+        copy(parts.at[across], near.at[0], row_sems, 0, row_peers[0]),
+        copy(parts.at[sibling], near.at[1], row_sems, 1, row_peers[0]),
+        copy(outgoing, far, row_sems, 2, row_peers[1]),
+    ]
+    row_copies_[0].start()
+    row_copies_[1].start()
+    row_copies_[0].wait_recv()
+    outgoing[...] = (parts[partner].astype(jnp.float32) + near[0].astype(jnp.float32)).astype(
+        jnp.bfloat16
+    )
+    row_copies_[2].start()
+
+    def halves(half):
+        return pl.ds(half * half_rows, half_rows)
+
+    one, two, three = (one_send, one_recv), (two_send, two_recv), (three_send, three_recv)
+    one_copies, two_copies, three_copies = {}, {}, []
+    for turn, owner_x in enumerate((other_x, x)):
+        for half in range(2):
+            for i in range(3):
+                if half == 0:
+                    source = grads.at[owner_x, :, lax.rem(y + i + 1, 4), halves(0)]
+                else:
+                    source = grads.at[owner_x, lax.rem(z + i + 1, 4), :, halves(1)]
+                at = (turn * 2 + half) * 3 + i
+                peer = (y_peers, z_peers)[half][i]
+                one_copies[turn, half, i] = copy(source, first.at[turn, half, i], one, at, peer)
+                one_copies[turn, half, i].start()
+
+    def add_first(turn):
+        owner_x = (other_x, x)[turn]
+        for half in range(2):
+            for i in range(3):
+                one_copies[turn, half, i].wait_recv()
+
+            def add(k, carry, half=half):
+                if half == 0:
+                    total = grads[owner_x, k, y, halves(0)].astype(jnp.float32)
+                else:
+                    total = grads[owner_x, z, k, halves(1)].astype(jnp.float32)
+                for i in range(3):
+                    total = total + first[turn, half, i, k].astype(jnp.float32)
+                first_sum[turn, half, k] = total.astype(jnp.bfloat16)
+                return carry
+
+            lax.fori_loop(0, 4, add, 0)
+            for i in range(3):
+                away = lax.rem((z, y)[half] + i + 1, 4)
+                two_copies[turn, half, i] = copy(
+                    first_sum.at[turn, half, away],
+                    second.at[turn, half, i],
+                    two,
+                    (turn * 2 + half) * 3 + i,
+                    (z_peers, y_peers)[half][i],
                 )
+                two_copies[turn, half, i].start()
+
+    def add_second(turn, half):
+        for i in range(3):
+            two_copies[turn, half, i].wait_recv()
+        total = first_sum[turn, half, (z, y)[half]].astype(jnp.float32)
+        for i in range(3):
+            total = total + second[turn, half, i].astype(jnp.float32)
+        return total
+
+    row_copies_[1].wait_recv()
+    incoming = parts[row].astype(jnp.float32) + near[1].astype(jnp.float32)
+    row_copies_[2].wait_recv()
+    incoming = incoming + far[...].astype(jnp.float32)
+    rows = inputs[...].astype(jnp.float32)
+    factor = scale[...]
+    weighted = gain[...] * incoming
+    mean = jnp.mean(weighted * rows, axis=1, keepdims=True)
+    result[...] = hidden[...] + factor * weighted - rows * (factor * factor * factor * mean)
+    values[0, 0:1] = jnp.sum(incoming * rows * factor, axis=0, keepdims=True)
+    values[0, 1:2] = gain_ffn[...]
+
+    gain_sems = (gain_send, gain_recv)
+    gain_copies = []
+    stages = (row_peers, y_peers, z_peers, [x_peer])
+
+    def start_gains(stage):
+        at = 3 * stage
+        for i, peer in enumerate(stages[stage]):
+            gain_copies.append(
+                copy(values.at[stage], buffers.at[at + i], gain_sems, at + i, peer)
             )
-        for copy in copies:
-            copy.start()
-        if stage == 0:
-            own.wait()
-            arrived = router.at[row, pl.ds(0, 31)]
-            pltpu.make_async_copy(arrived, arrived, col_recv).wait()
-            far, near, onward = row_copies([router.at[row]], [router], row_send, row_recv)
-            far[0].start()
-            near[0].start()
-        for copy in copies:
-            copy.wait()
-        result = values[stage]
-        for i in range(len(peers)):
-            result = result + buffers[at + i]
-        values[stage + 1] = result
-        at += len(peers)
-    total[...] = values[len(stages)]
-    far[0].wait_recv()
-    onward[0].start()
-    sent = router.at[row, pl.ds(0, 31)]
-    pltpu.make_async_copy(sent, sent, col_send).wait()
-    far[0].wait_send()
-    near[0].wait()
-    onward[0].wait()
-
-
-def finish(gains, share):
+            gain_copies[-1].start()
+
+    def add_gains(stage):
+        at = 3 * stage
+        total = values[stage]
+        for i in range(len(stages[stage])):
+            gain_copies[at + i].wait_recv()
+            total = total + buffers[at + i]
+        values[stage + 1] = total
+
+    start_gains(0)
+    add_first(0)
+    add_gains(0)
+    start_gains(1)
+    add_first(1)
+    add_gains(1)
+    start_gains(2)
+    for half in range(2):
+        second_sum[half] = add_second(0, half).astype(jnp.bfloat16)
+        three_copies.append(copy(second_sum.at[half], third.at[half], three, half, x_peer))
+        three_copies[half].start()
+    add_gains(2)
+    start_gains(3)
+    for half in range(2):
+        total = add_second(1, half)
+        three_copies[half].wait_recv()
+        summed[halves(half)] = total + third[half].astype(jnp.float32)
+    add_gains(3)
+    gains[...] = values[4]
+    for done in [*row_copies_, *one_copies.values(), *two_copies.values()]:
+        done.wait_send()
+    for done in [*three_copies, *gain_copies]:
+        done.wait_send()
+
+
+def finish(parts, grads, hidden, inputs, scale, gain, gain_ffn):
     space = pl.BlockSpec(memory_space=pltpu.VMEM)
-    away = pl.BlockSpec(memory_space=pl.ANY)
+    rows, width = hidden.shape
+    half_rows, depth = grads.shape[3] // 2, grads.shape[4]
+    low = jnp.bfloat16
     return pl.pallas_call(
         finish_kernel,
         out_shape=[
-            jax.ShapeDtypeStruct(gains.shape, gains.dtype),
-            jax.ShapeDtypeStruct((4, 32, *share.shape), share.dtype),
+            jax.ShapeDtypeStruct((rows, width), jnp.float32),
+            jax.ShapeDtypeStruct((2 * half_rows, depth), jnp.float32),
+            jax.ShapeDtypeStruct((2, width), jnp.float32),
         ],
-        in_specs=[space, away],
-        out_specs=[space, away],
+        in_specs=[space] * 7,
+        out_specs=[space] * 3,
         scratch_shapes=[
-            pltpu.VMEM((5, *gains.shape), gains.dtype),
-            pltpu.VMEM((10, *gains.shape), gains.dtype),
+            pltpu.VMEM((2, rows, width), low),
+            pltpu.VMEM((rows, width), low),
+            pltpu.VMEM((rows, width), low),
+            pltpu.VMEM((2, 2, 3, 4, half_rows, depth), low),
+            pltpu.VMEM((2, 2, 4, half_rows, depth), low),
+            pltpu.VMEM((2, 2, 3, half_rows, depth), low),
+            pltpu.VMEM((2, half_rows, depth), low),
+            pltpu.VMEM((2, half_rows, depth), low),
+            pltpu.VMEM((5, 2, width), jnp.float32),
+            pltpu.VMEM((10, 2, width), jnp.float32),
+            pltpu.SemaphoreType.DMA((3,)),
+            pltpu.SemaphoreType.DMA((3,)),
+            pltpu.SemaphoreType.DMA((12,)),
+            pltpu.SemaphoreType.DMA((12,)),
+            pltpu.SemaphoreType.DMA((12,)),
+            pltpu.SemaphoreType.DMA((12,)),
+            pltpu.SemaphoreType.DMA((2,)),
+            pltpu.SemaphoreType.DMA((2,)),
             pltpu.SemaphoreType.DMA((10,)),
             pltpu.SemaphoreType.DMA((10,)),
-            pltpu.SemaphoreType.DMA,
-            pltpu.SemaphoreType.DMA,
-            pltpu.SemaphoreType.DMA,
-            pltpu.SemaphoreType.DMA((3,)),
-            pltpu.SemaphoreType.DMA((3,)),
         ],
-        compiler_params=pltpu.CompilerParams(collective_id=16, has_side_effects=True),
-        cost_estimate=pl.CostEstimate(flops=0, bytes_accessed=64 << 20, transcendentals=0),
+        compiler_params=pltpu.CompilerParams(
+            collective_id=16, has_side_effects=True, vmem_limit_bytes=56 << 20
+        ),
+        cost_estimate=pl.CostEstimate(flops=0, bytes_accessed=200 << 20, transcendentals=0),
         name="finish",
-    )(gains, share)
+    )(parts, grads, hidden, inputs, scale, gain, gain_ffn)
 
 
 def packed_places(shape, axis):
@@ -493,43 +575,43 @@
     return marks
 
 
+def gate_weights_of(owner, hit, high, low):
+    weights = hit * (matmul(owner, high) + matmul(owner, low))
+    return split_low(weights)
+
+
 def pack_tokens_kernel(with_gates, code, values, *refs):
     packed = refs[-1]
     marks = token_marks(code[0])
-    main = marks[0][1].astype(jnp.bfloat16)
+    if with_gates:
+        weights = [gate_weights_of(owner, hit, refs[0][0], refs[1][0]) for owner, hit in marks]
+    else:
+        weights = [(hit.astype(jnp.bfloat16),) for _, hit in marks]
+    copies = len(weights[0])
     last = values[:, 3 * QUARTER :]
     for part in range(3):
         columns = slice(part * QUARTER, (part + 1) * QUARTER)
-        both = jnp.concatenate([main, marks[part + 1][1].astype(jnp.bfloat16)], axis=1)
-        rows = jnp.concatenate([values[:, columns], last], axis=0)
+        both = jnp.concatenate([*weights[0], *weights[part + 1]], axis=1)
+        rows = jnp.concatenate([values[:, columns]] * copies + [last] * copies, axis=0)
         packed[:, columns] = matmul(both, rows).astype(jnp.bfloat16)
-    if with_gates:
-        high, low = refs[0], refs[1]
-        owner, hit = marks[0]
-        lanes = lax.broadcasted_iota(jnp.int32, (BLOCK, SIDE), 1)
-        of_high = jnp.sum(hit * matmul(owner, high[0]), axis=1, keepdims=True)
-        of_low = jnp.sum(hit * matmul(owner, low[0]), axis=1, keepdims=True)
-        side = jnp.where(lanes == 0, of_high, jnp.where(lanes == 1, of_low, 0.0))
-        packed[:, 3 * QUARTER :] = side.astype(jnp.bfloat16)
-
-
-def pack_tokens(code, values, gates=None):
+
+
+def pack_tokens(code, values, gates=()):
     blocks = code.shape[0]
-    width = 3 * QUARTER + (SIDE if gates is not None else 0)
+    width = 3 * QUARTER
     small = pl.BlockSpec((1, BLOCK_EXPERTS, SIDE), lambda i: (i, 0, 0))
-    extra = [] if gates is None else list(gates)
     return pl.pallas_call(
-        functools.partial(pack_tokens_kernel, gates is not None),
+        functools.partial(pack_tokens_kernel, len(gates) > 0),
         grid=(blocks,),
         out_shape=jax.ShapeDtypeStruct((blocks * BLOCK, width), jnp.bfloat16),
-        in_specs=[small, pl.BlockSpec(values.shape, lambda i: (0, 0))] + [small] * len(extra),
+        in_specs=[small, pl.BlockSpec(values.shape, lambda i: (0, 0))] + [small] * len(gates),
         out_specs=pl.BlockSpec((BLOCK, width), lambda i: (i, 0)),
         compiler_params=pltpu.CompilerParams(vmem_limit_bytes=32 << 20),
         cost_estimate=pl.CostEstimate(
             flops=blocks * BLOCK * 256 * width * 2, bytes_accessed=8 << 20, transcendentals=0
         ),
         name="pack_tokens",
-    )(code, values, *extra)
+    )(code, values, *gates)
 
 
 def slot_marks():
@@ -542,7 +624,7 @@
     return marks
 
 
-def unpack_slots_kernel(with_gates, packed, values, *refs):
+def unpack_slots_kernel(packed, values):
     marks = slot_marks()
     last = jnp.zeros((2 * BLOCK_SLOTS, QUARTER), jnp.float32)
     for part in range(3):
@@ -554,29 +636,17 @@
     last = last.astype(jnp.bfloat16)
     values[0, :, 3 * QUARTER :] = last[:BLOCK_SLOTS]
     values[1, :, 3 * QUARTER :] = last[BLOCK_SLOTS:]
-    if with_gates:
-        side = matmul(marks[0], packed[:, 3 * QUARTER :])
-        gate = side[:, 0:1] + side[:, 1:2]
-        wide = jnp.broadcast_to(gate, (2 * BLOCK_SLOTS, SIDE))
-        refs[0][0] = wide[:BLOCK_SLOTS]
-        refs[0][1] = wide[BLOCK_SLOTS:]
-
-
-def unpack_slots(packed, with_gates):
+
+
+def unpack_slots(packed):
     blocks = packed.shape[0] // BLOCK
-    width = packed.shape[1]
     slots = blocks * BLOCK_SLOTS
-    shapes = [jax.ShapeDtypeStruct((2, slots, 4 * QUARTER), jnp.bfloat16)]
-    specs = [pl.BlockSpec((2, BLOCK_SLOTS, 4 * QUARTER), lambda i: (0, i, 0))]
-    if with_gates:
-        shapes.append(jax.ShapeDtypeStruct((2, slots, SIDE), jnp.float32))
-        specs.append(pl.BlockSpec((2, BLOCK_SLOTS, SIDE), lambda i: (0, i, 0)))
     return pl.pallas_call(
-        functools.partial(unpack_slots_kernel, with_gates),
+        unpack_slots_kernel,
         grid=(blocks,),
-        out_shape=shapes,
-        in_specs=[pl.BlockSpec((BLOCK, width), lambda i: (i, 0))],
-        out_specs=specs,
+        out_shape=jax.ShapeDtypeStruct((2, slots, 4 * QUARTER), jnp.bfloat16),
+        in_specs=[pl.BlockSpec((BLOCK, 3 * QUARTER), lambda i: (i, 0))],
+        out_specs=pl.BlockSpec((2, BLOCK_SLOTS, 4 * QUARTER), lambda i: (0, i, 0)),
         compiler_params=pltpu.CompilerParams(vmem_limit_bytes=32 << 20),
         cost_estimate=pl.CostEstimate(
             flops=blocks * 2 * BLOCK_SLOTS * BLOCK * 6 * QUARTER * 2,
@@ -587,8 +657,7 @@
     )(packed)
 
 
-def pack_slots_kernel(with_side, values, *refs):
-    packed = refs[-1]
+def pack_slots_kernel(values, packed):
     marks = slot_marks()
     last = jnp.concatenate([values[0, :, 3 * QUARTER :], values[1, :, 3 * QUARTER :]], axis=0)
     for part in range(3):
@@ -596,23 +665,17 @@
         rows = jnp.concatenate([values[0, :, columns], values[1, :, columns]], axis=0)
         found = outer_sum(marks[0], rows) + outer_sum(marks[part + 1], last)
         packed[:, columns] = found.astype(jnp.bfloat16)
-    if with_side:
-        side = jnp.concatenate([refs[0][0], refs[0][1]], axis=0)
-        packed[:, 3 * QUARTER :] = outer_sum(marks[0], side).astype(jnp.bfloat16)
-
-
-def pack_slots(values, side=None):
+
+
+def pack_slots(values):
     slots = values.shape[1]
     blocks = slots // BLOCK_SLOTS
-    width = 3 * QUARTER + (SIDE if side is not None else 0)
-    extra = [] if side is None else [side]
     return pl.pallas_call(
-        functools.partial(pack_slots_kernel, side is not None),
+        pack_slots_kernel,
         grid=(blocks,),
-        out_shape=jax.ShapeDtypeStruct((blocks * BLOCK, width), jnp.bfloat16),
-        in_specs=[pl.BlockSpec((2, BLOCK_SLOTS, 4 * QUARTER), lambda i: (0, i, 0))]
-        + [pl.BlockSpec((2, BLOCK_SLOTS, SIDE), lambda i: (0, i, 0))] * len(extra),
-        out_specs=pl.BlockSpec((BLOCK, width), lambda i: (i, 0)),
+        out_shape=jax.ShapeDtypeStruct((blocks * BLOCK, 3 * QUARTER), jnp.bfloat16),
+        in_specs=[pl.BlockSpec((2, BLOCK_SLOTS, 4 * QUARTER), lambda i: (0, i, 0))],
+        out_specs=pl.BlockSpec((BLOCK, 3 * QUARTER), lambda i: (i, 0)),
         compiler_params=pltpu.CompilerParams(vmem_limit_bytes=32 << 20),
         cost_estimate=pl.CostEstimate(
             flops=blocks * 2 * BLOCK_SLOTS * BLOCK * 6 * QUARTER * 2,
@@ -620,46 +683,65 @@
             transcendentals=0,
         ),
         name="pack_slots",
-    )(values, *extra)
-
-
-def sum_tokens_kernel(with_side, code, packed, total, *refs):
+    )(values)
+
+
+def sum_tokens_kernel(code, packed, total):
     @pl.when(pl.program_id(0) == 0)
     def _():
         total[...] = jnp.zeros_like(total)
 
-    marks = token_marks(code[0])
-    main = marks[0][1].astype(jnp.bfloat16)
+    marks = [hit.astype(jnp.bfloat16) for _, hit in token_marks(code[0])]
     last = jnp.zeros((total.shape[0], QUARTER), jnp.float32)
     for part in range(3):
         columns = slice(part * QUARTER, (part + 1) * QUARTER)
-        total[:, columns] += outer_sum(main, packed[:, columns])
-        last = last + outer_sum(marks[part + 1][1].astype(jnp.bfloat16), packed[:, columns])
+        total[:, columns] += outer_sum(marks[0], packed[:, columns])
+        last = last + outer_sum(marks[part + 1], packed[:, columns])
     total[:, 3 * QUARTER :] += last
-    if with_side:
-        owner = marks[0][0].astype(jnp.float32)
-        side = packed[:, 3 * QUARTER :].astype(jnp.float32)
-        spread = [(side[:, i : i + 1] * owner).astype(jnp.bfloat16) for i in range(2)]
-        refs[0][0] = outer_sum(main, spread[0]) + outer_sum(main, spread[1])
-
-
-def sum_tokens(code, packed, with_side):
-    blocks = code.shape[0]
-    tokens, width = code.shape[2], packed.shape[1]
-    shapes = [jax.ShapeDtypeStruct((tokens, 4 * QUARTER), jnp.float32)]
-    specs = [pl.BlockSpec((tokens, 4 * QUARTER), lambda i: (0, 0))]
-    if with_side:
-        shapes.append(jax.ShapeDtypeStruct((blocks, tokens, BLOCK_EXPERTS), jnp.float32))
-        specs.append(pl.BlockSpec((1, tokens, BLOCK_EXPERTS), lambda i: (i, 0, 0)))
+
+
+def sum_gated_kernel(code, packed, grads, high, low, total, gate_grads):
+    @pl.when(pl.program_id(0) == 0)
+    def _():
+        total[...] = jnp.zeros_like(total)
+
+    marks = token_marks(code[0])
+    weights = [gate_weights_of(owner, hit, high[0], low[0]) for owner, hit in marks]
+    last = jnp.zeros((total.shape[0], QUARTER), jnp.float32)
+    whole = jnp.zeros((BLOCK, 1), jnp.float32)
+    products = []
+    for part in range(3):
+        columns = slice(part * QUARTER, (part + 1) * QUARTER)
+        rows = packed[:, columns]
+        total[:, columns] += outer_sum(weights[0][0], rows) + outer_sum(weights[0][1], rows)
+        last = last + outer_sum(weights[part + 1][0], rows) + outer_sum(weights[part + 1][1], rows)
+        dots = jnp.sum(
+            rows.astype(jnp.float32) * grads[:, columns].astype(jnp.float32),
+            axis=1,
+            keepdims=True,
+        )
+        whole = whole + dots
+        products.append(dots)
+    total[:, 3 * QUARTER :] += last
+    found = jnp.zeros(gate_grads.shape[1:], jnp.float32)
+    for (owner, hit), dots in zip(marks, [whole, *products]):
+        hit = hit.astype(jnp.bfloat16)
+        for spread in split_low(dots * owner.astype(jnp.float32)):
+            found = found + outer_sum(hit, spread)
+    gate_grads[0] = found
+
+
+def sum_tokens(code, packed):
+    blocks, _, tokens = code.shape
     return pl.pallas_call(
-        functools.partial(sum_tokens_kernel, with_side),
+        sum_tokens_kernel,
         grid=(blocks,),
-        out_shape=shapes,
+        out_shape=jax.ShapeDtypeStruct((tokens, 4 * QUARTER), jnp.float32),
         in_specs=[
             pl.BlockSpec((1, BLOCK_EXPERTS, tokens), lambda i: (i, 0, 0)),
-            pl.BlockSpec((BLOCK, width), lambda i: (i, 0)),
+            pl.BlockSpec((BLOCK, 3 * QUARTER), lambda i: (i, 0)),
         ],
-        out_specs=specs,
+        out_specs=pl.BlockSpec((tokens, 4 * QUARTER), lambda i: (0, 0)),
         compiler_params=pltpu.CompilerParams(vmem_limit_bytes=32 << 20),
         cost_estimate=pl.CostEstimate(
             flops=blocks * BLOCK * 128 * 6 * QUARTER * 2,
@@ -668,6 +750,32 @@
         ),
         name="sum_tokens",
     )(code, packed)
+
+
+def sum_gated(code, packed, grads, gates):
+    blocks, _, tokens = code.shape
+    small = pl.BlockSpec((1, BLOCK_EXPERTS, tokens), lambda i: (i, 0, 0))
+    wide = pl.BlockSpec((BLOCK, 3 * QUARTER), lambda i: (i, 0))
+    return pl.pallas_call(
+        sum_gated_kernel,
+        grid=(blocks,),
+        out_shape=[
+            jax.ShapeDtypeStruct((tokens, 4 * QUARTER), jnp.float32),
+            jax.ShapeDtypeStruct((blocks, tokens, BLOCK_EXPERTS), jnp.float32),
+        ],
+        in_specs=[small, wide, wide, small, small],
+        out_specs=[
+            pl.BlockSpec((tokens, 4 * QUARTER), lambda i: (0, 0)),
+            pl.BlockSpec((1, tokens, BLOCK_EXPERTS), lambda i: (i, 0, 0)),
+        ],
+        compiler_params=pltpu.CompilerParams(vmem_limit_bytes=32 << 20),
+        cost_estimate=pl.CostEstimate(
+            flops=blocks * BLOCK * 128 * 12 * QUARTER * 2,
+            bytes_accessed=14 << 20,
+            transcendentals=0,
+        ),
+        name="sum_gated",
+    )(code, packed, grads, *gates)
 
 
 def exchange(packed):
@@ -769,8 +877,8 @@
     gates = [
         part.T.reshape(-1, BLOCK_EXPERTS, rows_dev) for part in split_low(gate_weights)
     ]
-    received = exchange(pack_tokens(code, normed_two, gates))
-    send_grads, received = lax.optimization_barrier((pack_tokens(code, grad_low), received))
+    received = exchange(pack_tokens(code, normed_two))
+    send_grads, received = lax.optimization_barrier((pack_tokens(code, grad_low, gates), received))
     received_grads = exchange(send_grads)
 
     group_two = lax.all_gather(normed_two, "row", axis=0, tiled=True)
@@ -799,70 +907,57 @@
     ).astype(jnp.float32)
     shared_branch, shared_input = shared_sums[:, :model_width], shared_sums[:, model_width:]
 
-    expert_in, gate_wide = unpack_slots(received, True)
-    gate = gate_wide[:, :, :1]
+    expert_in = unpack_slots(received)
     expert_pre = jnp.einsum(
         "esd,edf->esf", expert_in, w_expert_in, preferred_element_type=jnp.float32
     )
     expert_act, expert_slope = swish_parts(expert_pre[..., :expert_ff])
     expert_hidden = (expert_act * expert_pre[..., expert_ff:]).astype(jnp.bfloat16)
-    expert_out = (
-        gate
-        * jnp.einsum(
-            "esf,edf->esd", expert_hidden, w_expert_out, preferred_element_type=jnp.float32
-        )
+    expert_out = jnp.einsum(
+        "esf,edf->esd", expert_hidden, w_expert_out, preferred_element_type=jnp.float32
     ).astype(jnp.bfloat16)
     send_out, received_grads = lax.optimization_barrier((pack_slots(expert_out), received_grads))
     returned = exchange(send_out)
 
-    (expert_grads,) = unpack_slots(received_grads, False)
-    plain_grad = jnp.einsum(
-        "esd,edf->esf", expert_grads, w_expert_out, preferred_element_type=jnp.float32
-    )
-    gate_grad = jnp.sum(plain_grad * expert_hidden.astype(jnp.float32), axis=2, keepdims=True)
-    gate_high, gate_low = split_low(gate_grad)
-    lanes = jnp.arange(SIDE, dtype=jnp.int32)[None, None, :]
-    side = jnp.where(lanes == 0, gate_high, jnp.where(lanes == 1, gate_low, 0)).astype(jnp.bfloat16)
-    hidden_grad = gate * plain_grad
+    out_grad = unpack_slots(received_grads)
+    hidden_grad = jnp.einsum(
+        "esd,edf->esf", out_grad, w_expert_out, preferred_element_type=jnp.float32
+    )
     expert_pre_grad = jnp.concatenate(
         [hidden_grad * expert_pre[..., expert_ff:] * expert_slope, hidden_grad * expert_act], axis=2
     ).astype(jnp.bfloat16)
     slot_grad = jnp.einsum(
         "esf,edf->esd", expert_pre_grad, w_expert_in, preferred_element_type=jnp.float32
     ).astype(jnp.bfloat16)
-    send_back, returned = lax.optimization_barrier((pack_slots(slot_grad, side), returned))
+    send_back, returned = lax.optimization_barrier((pack_slots(slot_grad), returned))
     returned_grad = exchange(send_back)
-    out_grad = (gate * expert_grads.astype(jnp.float32)).astype(jnp.bfloat16)
     grad_expert_out = jnp.einsum(
         "esd,esf->edf", out_grad, expert_hidden, preferred_element_type=jnp.float32
     )
     grad_expert_in = jnp.einsum(
         "esd,esf->edf", expert_in, expert_pre_grad, preferred_element_type=jnp.float32
     )
-    (routed_branch,) = sum_tokens(code, returned, False)
+    routed_branch, gate_grads = sum_gated(code, returned, send_grads, gates)
     block_out = (hidden_state + shared_branch + routed_branch).astype(jnp.bfloat16)
-
-    routed_input, gate_grads = sum_tokens(code, returned_grad, True)
     gate_grads = gate_grads.transpose(1, 0, 2).reshape(rows_dev, expert_count)
-    score_grad = (
-        gate_grads - jnp.sum(gate_grads * gate_weights, axis=1, keepdims=True)
-    ) / score_sum
-    logit_grad = (score_grad * scores_sig * (1.0 - scores_sig)).astype(jnp.bfloat16)
-    router_input = matmul_t(logit_grad, w_router)
-    normed_two_grad = shared_input + router_input + routed_input
+    logit_grad = (
+        (1.0 - scores_sig)
+        * (gate_grads - gate_weights * jnp.sum(gate_grads, axis=1, keepdims=True))
+    ).astype(jnp.bfloat16)
+    router_sum = lax.psum(outer_sum(normed_two, logit_grad), ("row", "col"))
+    router_input = shared_input + matmul_t(logit_grad, w_router)
+    returned_grad, router_input, block_out, grad_expert_in, grad_expert_out = (
+        lax.optimization_barrier(
+            (returned_grad, router_input, block_out, grad_expert_in, grad_expert_out)
+        )
+    )
+
+    normed_two_grad = router_input + sum_tokens(code, returned_grad)
     gain_ffn_grad, hidden_back = norm_back(hidden_state, scale_two, gain_ffn, normed_two_grad)
     hidden_total = grad_rows + hidden_back
-    group_branch, group_logit = group_rows([hidden_total.astype(jnp.bfloat16), logit_grad], 0)
+    (group_branch,) = group_rows([hidden_total.astype(jnp.bfloat16)], 0)
     attended_grad = matmul(group_branch, full_out).astype(jnp.bfloat16)
     grad_out_w = outer_sum(group_branch, attended)
-    share_width = model_width // row_count
-    router_part = outer_sum(
-        lax.dynamic_slice_in_dim(group_two, lax.axis_index("row") * share_width, share_width, 1),
-        group_logit,
-    )
-    sum_shared_in, sum_shared_out, sum_out, router_share = scatter_sum(
-        [grad_shared_in, grad_shared_out, grad_out_w, router_part]
-    )
 
     out_block = attended_grad.reshape(group_tok, local_kv, group_size, head_size)
     probs_full = jnp.exp(block_scores() - log_totals)
@@ -897,29 +992,35 @@
     )
     grad_query_w = outer_sum(group_one, query_pre_grad)
     grad_keyval_w = outer_sum(group_one, keyval_pre_grad)
-    normed_one_grad = group_sums(
-        matmul_t(query_pre_grad, full_query) + matmul_t(keyval_pre_grad, full_keyval), 3
-    )
-    gain_attn_grad, input_back = norm_back(inputs, scale_one, gain_attn, normed_one_grad)
-    input_total = hidden_total + input_back
-
-    sum_query, sum_keyval = scatter_sum([grad_query_w, grad_keyval_w])
-    gain_sums, router_sum = finish(
-        jnp.stack([gain_attn_grad, gain_ffn_grad]).reshape(-1, 128),
-        router_share.reshape(-1, expert_count).astype(jnp.bfloat16),
-    )
-    gain_sums = gain_sums.reshape(2, model_width)
+    normed_one_parts = matmul_t(query_pre_grad, full_query) + matmul_t(
+        keyval_pre_grad, full_keyval
+    )
+    shard_grads = [grad_query_w, grad_keyval_w, grad_out_w, grad_shared_in, grad_shared_out]
+    shard_grads = jnp.concatenate([part.astype(jnp.bfloat16) for part in shard_grads], axis=1)
+    input_total, shard_sums, gain_sums = finish(
+        normed_one_parts.astype(jnp.bfloat16).reshape(row_count, rows_dev, model_width),
+        shard_grads.reshape(2, 4, 4, -1, shard_grads.shape[1]),
+        hidden_total,
+        block_in.reshape(rows_dev, model_width),
+        scale_one,
+        gain_attn[None],
+        gain_ffn_grad[None],
+    )
+    sums, end = [], 0
+    for part, like in zip(shards, (w_query, w_keyval, w_out, w_shared_in, w_shared_out)):
+        sums.append(shard_sums[:, end : end + part.shape[1]].reshape(like.shape))
+        end += part.shape[1]
     return (
         block_out.reshape(1, rows_dev, model_width),
         input_total.reshape(1, rows_dev, model_width),
         gain_sums[0],
-        sum_query,
-        sum_keyval.reshape(w_keyval.shape),
-        sum_out,
+        sums[0],
+        sums[1],
+        sums[2],
         gain_sums[1],
-        sum_shared_in.reshape(w_shared_in.shape),
-        sum_shared_out,
-        router_sum.reshape(model_width, expert_count).astype(jnp.float32),
+        sums[3],
+        sums[4],
+        router_sum,
         grad_expert_in,
         grad_expert_out,
     )

time: 721 us -> 673 us (0.933)
  waiting for transfers between devices: 275 us -> 208 us
  local copies, waits for them, and re-layouts: 34.1 us -> 51.9 us
  other arithmetic: 34.6 us -> 24.8 us
    all_to_all x4, waiting for transfers between devices: 242 us -> 181 us  [exchange(): lax.all_to_all(pairs, ('row', 'col'), split_axis=0, concat_axis=0, tiled=...]
    pallas_call x9, Pallas kernels: 80.2 us -> 120 us  [the longest x1 65.4 us: finish(): pl.pallas_call(finish_kernel, out_shape=[jax.ShapeDtypeStruct((rows, widt...]
    pallas_call x2 -> x1, Pallas kernels: 54.5 us -> 20.6 us  [group_sums(): pl.pallas_call(row_sum_kernel, out_shape=jax.ShapeDtypeStruct((rows, widt...]
    all_to_all x2 -> x0, waiting for transfers between devices: 32.1 us -> none  [scatter_sum(): lax.all_to_all(jnp.concatenate(parts, axis=2), 'col', split_axis=0, conca...]
    psum x0 -> x1, waiting for transfers between devices: none -> 25.4 us  [per_device(): router_sum = lax.psum(outer_sum(normed_two, logit_grad), ('row', 'col'))]
    all_to_all x2 -> x0, starting transfers between devices: 12.9 us -> none  [scatter_sum(): lax.all_to_all(jnp.concatenate(parts, axis=2), 'col', split_axis=0, conca...]
    reduce_scatter x1, starting transfers between devices: 0.45 us -> 11.3 us  [per_device(): lax.psum_scatter(jnp.concatenate([matmul_t(shared_hidden, full_shared_out...]
    concatenate x0 -> x1, local copies, waits for them, and re-layouts: none -> 9.96 us  [per_device(): jnp.concatenate([part.astype(jnp.bfloat16) for part in shard_grads], axis=1)]
  transfers between devices with their start and end apart: 8 -> 7, of which waited for: 5 -> 5; matrix products, arithmetic and copies ran while one was open for 13% -> 19% of each run, Pallas kernels for 10% -> 20%
where the time goes in v3:
time: 673 us; the launch traced here: 661 us
  Pallas kernels  213 us (32%)
  waiting for transfers between devices  208 us (31%)
  matrix products  103 us (15%)
  local copies, waits for them, and re-layouts  51.9 us (8%)
  starting transfers between devices  43.6 us (6%)
  other arithmetic  24.8 us (4%)
  between operations  16.9 us (3%)
    all_to_all x4, waiting for transfers between devices, exchange(): lax.all_to_all(pairs, ('row', 'col'), split_axis=0, concat_axis=0, tiled=...  181 us
    pallas_call x1, Pallas kernels, finish(): pl.pallas_call(finish_kernel, out_shape=[jax.ShapeDtypeStruct((rows, widt...  65.4 us
    pallas_call x1, Pallas kernels, gather_start(): pl.pallas_call(gather_kernel, out_shape=[jax.ShapeDtypeStruct((32, *shard...  54.6 us
    all_to_all x4, starting transfers between devices, exchange(): lax.all_to_all(pairs, ('row', 'col'), split_axis=0, concat_axis=0, tiled=...  32.2 us
    unnamed x119, local copies, waits for them, and re-layouts  25.7 us
    psum x1, waiting for transfers between devices, per_device(): router_sum = lax.psum(outer_sum(normed_two, logit_grad), ('row', 'col'))  25.4 us
    pallas_call x1, Pallas kernels, group_sums(): pl.pallas_call(row_sum_kernel, out_shape=jax.ShapeDtypeStruct((rows, widt...  20.6 us
    dot_general x6, matrix products, matmul_t(): lax.dot_general(matrix, partner, (((1,), (1,)), ((), ())), preferred_elem...  18.9 us
  transfers between devices with their start and end apart: 7, of which 5 were waited for; matrix products, arithmetic and copies ran while one was open for 19% of the time, Pallas kernels for 20%

profile of v3, /device:TPU:1, one launch (start us, length us, event | category | flops | bytes accessed | tf_op | source)
XLA Modules:
  0.0 661.3 jit_solution(1278139149052036764)
XLA Ops:
  16.9 54.6 %gather_start.1 = (bf16[32,64,1664]{2,1,0:T(8,128)(2,1)}, bf16[4,128,2048]{2,1,0:T(8,128)(2,1)}, bf16[4,128,2048]{2,1,0:T(8,128)(2,1)}) custom-call(bf16[64,1664]{1,0:T(8,128)(2,1)} %copy-done.28, bf16[128,2048]{1,0:T(8,128)(2,1)} %fusion.47.normed, bf16[128,2048]{1,0:T(8,128)(2,1)} %bitcast.220), custom_call_target="tpu_custom_call" | custom-call | bytes 209715200 | tf_op jit(solution)/shard_map/gather_start/pallas_call | solution.py:269
  74.6 3.9 copy.67
  92.9 20.6 %group_sums.1 = f32[128,2048]{1,0:T(8,128)S(1)} custom-call(bf16[4,128,2048]{2,1,0:T(8,128)(2,1)S(1)} %bitcast.222), custom_call_target="tpu_custom_call" | custom-call | bytes 67108864 | tf_op jit(solution)/shard_map/group_sums/pallas_call | solution.py:333
  114.4 3.7 pack_tokens.3
  120.8 5.2 all-to-all-start
  128.4 6.8 %pack_tokens.2.grads = bf16[2048,1536]{1,0:T(8,128)(2,1)S(1)} custom-call(bf16[8,32,128]{2,1,0:T(8,128)(2,1)S(1)} %bitcast.225, bf16[128,2048]{1,0:T(8,128)(2,1)S(1)} %bitcast.221, bf16[8,32,128]{2,1,0:T(8,128)(2,1)S(1)} %bitcast.230, bf16[8,32,128]{2,1,0:T(8,128)(2,1)S(1)} %bitcast.228), custom_call_target="tpu_custom_call" | custom-call | flops 1610612736 | bytes 8388608 | tf_op jit(solution)/shard_map/pack_tokens/pallas_call | solution.py:603
  137.9 71.3 %all-to-all-done = bf16[128,16,1536]{2,1,0:T(8,128)(2,1)} async-done(((bf16[128,16,1536]{2,1,0:T(8,128)(2,1)}), bf16[128,16,1536]{2,1,0:T(8,128)(2,1)}, u32[]{:S(2)}, u32[]{:S(2)}) %all-to-all-start) | async-done | bytes 6291488 | tf_op jit(solution)/shard_map/all_to_all | solution.py:783
  209.2 9.8 %all-to-all-start.1 = ((bf16[128,16,1536]{2,1,0:T(8,128)(2,1)}), bf16[128,16,1536]{2,1,0:T(8,128)(2,1)}, u32[]{:S(2)}, u32[]{:S(2)}) async-start(bf16[128,16,1536]{2,1,0:T(8,128)(2,1)} %bitcast.212), calls=%async_computation.1 | async-start | bytes 12582912 | tf_op jit(solution)/shard_map/all_to_all | solution.py:783
  230.9 7.6 %unpack_slots.2 = bf16[2,768,2048]{2,1,0:T(8,128)(2,1)S(1)} custom-call(bf16[2048,1536]{1,0:T(8,128)(2,1)} %bitcast.32.packed), custom_call_target="tpu_custom_call" | custom-call | flops 2415919104 | bytes 14680064 | tf_op jit(solution)/shard_map/unpack_slots/pallas_call | solution.py:644
  238.6 6.6 %fusion.111 = f32[2,768,1024]{2,1,0:T(8,128)S(1)} fusion(bf16[2,768,2048]{2,1,0:T(8,128)(2,1)S(1)} %unpack_slots.2, bf16[2,2048,1024]{2,1,0:T(8,128)(2,1)S(1)} %bitcast.264), kind=kOutput, calls=%fused_computation.180 | convolution fusion | flops 6442450944 | bytes 20971520 | tf_op jit(solution)/shard_map/esd,edf->esf/dot_general | solution.py:911
  250.1 3.7 convolution_convert_fusion.1.values
  253.8 5.4 pack_slots.2
  261.9 32.7 %all-to-all-done.1 = bf16[128,16,1536]{2,1,0:T(8,128)(2,1)} async-done(((bf16[128,16,1536]{2,1,0:T(8,128)(2,1)}), bf16[128,16,1536]{2,1,0:T(8,128)(2,1)}, u32[]{:S(2)}, u32[]{:S(2)}) %all-to-all-start.1) | async-done | bytes 6291488 | tf_op jit(solution)/shard_map/all_to_all | solution.py:783
  294.7 10.0 %all-to-all-start.2 = ((bf16[128,16,1536]{2,1,0:T(8,128)(2,1)}), bf16[128,16,1536]{2,1,0:T(8,128)(2,1)}, u32[]{:S(2)}, u32[]{:S(2)}) async-start(bf16[128,16,1536]{2,1,0:T(8,128)(2,1)} %bitcast.216), calls=%async_computation.2 | async-start | bytes 12582912 | tf_op jit(solution)/shard_map/all_to_all | solution.py:783
  304.7 11.3 %reduce-scatter.2.cloned.1.call-start = ((), (), s32[]{:S(2)}) async-start(), calls=%async_computation.6 | async-start | bytes 5242880 | tf_op jit(solution)/shard_map/reduce_scatter | solution.py:896
  316.0 4.7 pad_maximum_fusion
  320.7 7.5 %unpack_slots.3 = bf16[2,768,2048]{2,1,0:T(8,128)(2,1)S(1)} custom-call(bf16[2048,1536]{1,0:T(8,128)(2,1)} %bitcast.34.packed), custom_call_target="tpu_custom_call" | custom-call | flops 2415919104 | bytes 14680064 | tf_op jit(solution)/shard_map/unpack_slots/pallas_call | solution.py:644
  328.3 8.9 %multiply_convert_fusion.1 = (bf16[2,768,512]{2,1,0:T(8,128)(2,1)S(1)}, bf16[2,768,512]{2,1,0:T(8,128)(2,1)S(1)}) fusion(f32[2,768,1024]{2,1,0:T(8,128)} %copy-done.17, bf16[2,768,2048]{2,1,0:T(8,128)(2,1)S(1)} %unpack_slots.3, bf16[2,2048,512]{2,1,0:T(8,128)(2,1)S(1)} %copy-done.40), kind=kOutput, calls=%fused_computation.17 | convolution fusion | flops 3231449088 | bytes 19922944 | tf_op jit(solution)/shard_map/esd,edf->esf/dot_general | solution.py:923
  337.2 11.7 %convolution_convert_fusion.values = bf16[2,768,2048]{2,1,0:T(8,128)(2,1)S(1)} fusion(bf16[2,2048,1024]{2,1,0:T(8,128)(2,1)} %param.23, bf16[2,768,512]{2,1,0:T(8,128)(2,1)S(1)} %get-tuple-element.93, bf16[2,768,512]{2,1,0:T(8,128)(2,1)S(1)} %get-tuple-element.92), kind=kOutput, calls=%fused_computation | convolution fusion | flops 6451888128 | bytes 17825792 | tf_op jit(solution)/shard_map/esf,edf->esd/dot_general | solution.py:929
  348.9 5.4 pack_slots.3
  357.0 45.6 %all-to-all-done.2 = bf16[128,16,1536]{2,1,0:T(8,128)(2,1)} async-done(((bf16[128,16,1536]{2,1,0:T(8,128)(2,1)}), bf16[128,16,1536]{2,1,0:T(8,128)(2,1)}, u32[]{:S(2)}, u32[]{:S(2)}) %all-to-all-start.2) | async-done | bytes 6291488 | tf_op jit(solution)/shard_map/all_to_all | solution.py:783
  402.6 7.3 %all-to-all-start.3 = ((bf16[128,16,1536]{2,1,0:T(8,128)(2,1)}), bf16[128,16,1536]{2,1,0:T(8,128)(2,1)}, u32[]{:S(2)}, u32[]{:S(2)}) async-start(bf16[128,16,1536]{2,1,0:T(8,128)(2,1)} %bitcast.215), calls=%async_computation.3 | async-start | bytes 12582912 | tf_op jit(solution)/shard_map/all_to_all | solution.py:783
  413.6 10.2 %fusion.112 = f32[2,2048,512]{2,1,0:T(8,128)} fusion(bf16[2,768,2048]{2,1,0:T(8,128)(2,1)} %copy-done.8, bf16[2,768,512]{2,1,0:T(8,128)(2,1)} %copy-done.21), kind=kOutput, calls=%fused_computation.181 | convolution fusion | flops 3221225472 | bytes 16252928 | tf_op jit(solution)/shard_map/esd,esf->edf/dot_general | solution.py:934
  423.9 10.4 %fusion.18 = f32[2,2048,1024]{2,1,0:T(8,128)} fusion(bf16[2,768,2048]{2,1,0:T(8,128)(2,1)S(1)} %bitcast.219, bf16[2,768,512]{2,1,0:T(8,128)(2,1)S(1)} %copy-done.49, bf16[2,768,512]{2,1,0:T(8,128)(2,1)S(1)} %copy-done.47), kind=kOutput, calls=%fused_computation.41 | convolution fusion | flops 6448742400 | bytes 26214400 | tf_op jit(solution)/shard_map/esd,esf->edf/dot_general | solution.py:937
  434.3 10.3 %sum_gated.1 = (f32[128,2048]{1,0:T(8,128)S(1)}, f32[8,128,32]{2,1,0:T(8,128)S(1)}) custom-call(bf16[8,32,128]{2,1,0:T(8,128)(2,1)S(1)} %bitcast.226, bf16[2048,1536]{1,0:T(8,128)(2,1)} %bitcast.36.packed, bf16[2048,1536]{1,0:T(8,128)(2,1)S(1)} %bitcast.214, bf16[8,32,128]{2,1,0:T(8,128)(2,1)S(1)} %bitcast.231, bf16[8,32,128]{2,1,0:T(8,128)(2,1)S(1)} %bitcast.229), custom_call_target="tpu_custom_call" | custom-call | flops 3221225472 | bytes 14680064 | tf_op jit(solution)/shard_map/sum_gated/pallas_call | solution.py:759
  454.9 31.9 %all-to-all-done.3 = bf16[128,16,1536]{2,1,0:T(8,128)(2,1)} async-done(((bf16[128,16,1536]{2,1,0:T(8,128)(2,1)}), bf16[128,16,1536]{2,1,0:T(8,128)(2,1)}, u32[]{:S(2)}, u32[]{:S(2)}) %all-to-all-start.3) | async-done | bytes 6291488 | tf_op jit(solution)/shard_map/all_to_all | solution.py:783
  486.8 8.0 %sum_tokens.1 = f32[128,2048]{1,0:T(8,128)S(1)} custom-call(bf16[8,32,128]{2,1,0:T(8,128)(2,1)S(1)} %bitcast.227, bf16[2048,1536]{1,0:T(8,128)(2,1)} %bitcast.38.packed), custom_call_target="tpu_custom_call" | custom-call | flops 1610612736 | bytes 8388608 | tf_op jit(solution)/shard_map/sum_tokens/pallas_call | solution.py:736
  497.2 18.0 %group_rows.1 = bf16[4,128,2048]{2,1,0:T(8,128)(2,1)} custom-call(bf16[128,2048]{1,0:T(8,128)(2,1)} %get-tuple-element.88.refs_0_), custom_call_target="tpu_custom_call" | custom-call | bytes 67108864 | tf_op jit(solution)/shard_map/group_rows/pallas_call | solution.py:164
  528.9 4.4 add_convert_fusion
  540.6 10.0 %copy.84 = bf16[2048,1664]{1,0:T(8,128)(2,1)} copy(bf16[2048,1664]{0,1:T(8,128)(2,1)} %fusion.10) | data formatting | bytes 13631488 | tf_op jit(solution)/shard_map/concatenate | solution.py:999
  550.6 65.4 %finish.1 = (f32[128,2048]{1,0:T(8,128)}, f32[64,1664]{1,0:T(8,128)}, f32[2,2048]{1,0:T(2,128)}) custom-call(bf16[4,128,2048]{2,1,0:T(8,128)(2,1)} %bitcast.233, bf16[2,4,4,64,1664]{4,3,2,1,0:T(8,128)(2,1)} %bitcast.232, f32[128,2048]{1,0:T(8,128)} %get-tuple-element.89.hidden, bf16[128,2048]{1,0:T(8,128)(2,1)} %bitcast.234, f32[128,1]{1,0:T(8,128)} %copy.85.scale, ...), custom_call_target="tpu_custom_call" | custom-call | bytes 209715200 | tf_op jit(solution)/shard_map/finish/pallas_call | solution.py:511
  622.7 25.4 %all-reduce.2.cloned.1.call-done = f32[2048,256]{1,0:T(8,128)} async-done(((f32[2048,256]{1,0:T(8,128)}), f32[2048,256]{1,0:T(8,128)}) %all-reduce.2.cloned.1.call-update) | async-done | bytes 2097168 | tf_op jit(solution)/shard_map/psum | solution.py:947
  (196 shorter events, 106.5 us)
Async XLA Ops:
  8.0 118.8 %copy-start = (bf16[2048,256]{1,0:T(8,128)(2,1)S(1)}, bf16[2048,256]{1,0:T(8,128)(2,1)}, u32[]{:S(2)}) copy-start(bf16[2048,256]{1,0:T(8,128)(2,1)} %param.22) | copy-start | bytes 3145732
  71.5 7.0 %copy-start.43 = (s32[1,4]{1,0:T(1,128)S(1)}, s32[1,4]{1,0:T(1,128)}, u32[]{:S(2)}) copy-start(s32[1,4]{1,0:T(1,128)} %param.25) | copy-start | bytes 52
  89.7 23.7 %copy-start.16 = (bf16[1,128,2048]{2,1,0:T(8,128)(2,1)S(1)}, bf16[1,128,2048]{2,1,0:T(8,128)(2,1)}, u32[]{:S(2)}) copy-start(bf16[1,128,2048]{2,1,0:T(8,128)(2,1)} %param.14) | copy-start | bytes 1572868
  92.9 21.4 %copy-start.37 = (f32[2048]{0:T(1024)S(1)}, f32[2048]{0:T(1024)}, u32[]{:S(2)}) copy-start(f32[2048]{0:T(1024)} %param.19) | copy-start | bytes 24580
  120.8 7.6 %copy-start.9 = (bf16[1,128,2048]{2,1,0:T(8,128)(2,1)S(1)}, bf16[1,128,2048]{2,1,0:T(8,128)(2,1)}, u32[]{:S(2)}) copy-start(bf16[1,128,2048]{2,1,0:T(8,128)(2,1)} %param.27) | copy-start | bytes 1572868
  120.8 88.4 %all-to-all-start = ((bf16[128,16,1536]{2,1,0:T(8,128)(2,1)}), bf16[128,16,1536]{2,1,0:T(8,128)(2,1)}, u32[]{:S(2)}, u32[]{:S(2)}) async-start(bf16[128,16,1536]{2,1,0:T(8,128)(2,1)} %bitcast.217), calls=%async_computation | async-start | bytes 12582912 | tf_op jit(solution)/shard_map/all_to_all | solution.py:783
  126.0 93.0 %all-gather.2.cloned.1.call-start = ((), (), s32[]{:S(2)}) async-start(), calls=%async_computation.5 | async-start | bytes 2621440 | tf_op jit(solution)/shard_map/all_gather | solution.py:884
  128.4 80.9 %copy-start.25 = (f32[128,256]{0,1:T(8,128)}, f32[128,256]{0,1:T(8,128)S(1)}, u32[]{:S(2)}) copy-start(f32[128,256]{0,1:T(8,128)S(1)} %get-tuple-element.123) | copy-start | bytes 393220
  209.2 85.5 %all-to-all-start.1 = ((bf16[128,16,1536]{2,1,0:T(8,128)(2,1)}), bf16[128,16,1536]{2,1,0:T(8,128)(2,1)}, u32[]{:S(2)}, u32[]{:S(2)}) async-start(bf16[128,16,1536]{2,1,0:T(8,128)(2,1)} %bitcast.212), calls=%async_computation.1 | async-start | bytes 12582912 | tf_op jit(solution)/shard_map/all_to_all | solution.py:783
  224.2 14.3 %copy-start.26 = (bf16[512,128]{0,1:T(8,128)(2,1)}, bf16[512,128]{0,1:T(8,128)(2,1)S(1)}, u32[]{:S(2)}) copy-start(bf16[512,128]{0,1:T(8,128)(2,1)S(1)} %get-tuple-element.102) | copy-start | bytes 393220
  224.2 14.3 %copy-start.33 = (bf16[512,128]{0,1:T(8,128)(2,1)}, bf16[512,128]{0,1:T(8,128)(2,1)S(1)}, u32[]{:S(2)}) copy-start(bf16[512,128]{0,1:T(8,128)(2,1)S(1)} %get-tuple-element.98) | copy-start | bytes 393220
  224.2 14.3 %copy-start.35 = (bf16[512,128]{0,1:T(8,128)(2,1)}, bf16[512,128]{0,1:T(8,128)(2,1)S(1)}, u32[]{:S(2)}) copy-start(bf16[512,128]{0,1:T(8,128)(2,1)S(1)} %get-tuple-element.99) | copy-start | bytes 393220
  227.5 11.1 %slice-start.4 = ((s8[8388608]{0:T(1024)(128)(4,1)}), s8[4194304]{0:T(1024)(128)(4,1)S(1)}, s32[]{:S(2)}) async-start(s8[8388608]{0:T(1024)(128)(4,1)} %bitcast.263), calls=%async_computation.12 | async-start | bytes 8388608
  230.9 7.6 %slice-start.5 = ((s8[8388608]{0:T(1024)(128)(4,1)}), s8[4194304]{0:T(1024)(128)(4,1)S(1)}, s32[]{:S(2)}) async-start(s8[8388608]{0:T(1024)(128)(4,1)} %bitcast.263), calls=%async_computation.13 | async-start | bytes 8388608
  294.7 107.9 %all-to-all-start.2 = ((bf16[128,16,1536]{2,1,0:T(8,128)(2,1)}), bf16[128,16,1536]{2,1,0:T(8,128)(2,1)}, u32[]{:S(2)}, u32[]{:S(2)}) async-start(bf16[128,16,1536]{2,1,0:T(8,128)(2,1)} %bitcast.216), calls=%async_computation.2 | async-start | bytes 12582912 | tf_op jit(solution)/shard_map/all_to_all | solution.py:783
  304.7 106.0 %reduce-scatter.2.cloned.1.call-start = ((), (), s32[]{:S(2)}) async-start(), calls=%async_computation.6 | async-start | bytes 5242880 | tf_op jit(solution)/shard_map/reduce_scatter | solution.py:896
  320.7 7.5 %copy-start.40 = (bf16[2,2048,512]{2,1,0:T(8,128)(2,1)S(1)}, bf16[2,2048,512]{2,1,0:T(8,128)(2,1)}, u32[]{:S(2)}) copy-start(bf16[2,2048,512]{2,1,0:T(8,128)(2,1)} %param.24) | copy-start | bytes 12582916
  328.3 8.9 %copy-start.8 = (bf16[2,768,2048]{2,1,0:T(8,128)(2,1)}, bf16[2,768,2048]{2,1,0:T(8,128)(2,1)S(1)}, u32[]{:S(2)}) copy-start(bf16[2,768,2048]{2,1,0:T(8,128)(2,1)S(1)} %unpack_slots.3) | copy-start | bytes 18874372
  337.2 11.7 %copy-start.46 = (bf16[2,768,512]{2,1,0:T(8,128)(2,1)}, bf16[2,768,512]{2,1,0:T(8,128)(2,1)S(1)}, u32[]{:S(2)}) copy-start(bf16[2,768,512]{2,1,0:T(8,128)(2,1)S(1)} %get-tuple-element.92) | copy-start | bytes 4718596
  337.2 11.7 %copy-start.48 = (bf16[2,768,512]{2,1,0:T(8,128)(2,1)}, bf16[2,768,512]{2,1,0:T(8,128)(2,1)S(1)}, u32[]{:S(2)}) copy-start(bf16[2,768,512]{2,1,0:T(8,128)(2,1)S(1)} %get-tuple-element.93) | copy-start | bytes 4718596
  402.6 84.2 %all-to-all-start.3 = ((bf16[128,16,1536]{2,1,0:T(8,128)(2,1)}), bf16[128,16,1536]{2,1,0:T(8,128)(2,1)}, u32[]{:S(2)}, u32[]{:S(2)}) async-start(bf16[128,16,1536]{2,1,0:T(8,128)(2,1)} %bitcast.215), calls=%async_computation.3 | async-start | bytes 12582912 | tf_op jit(solution)/shard_map/all_to_all | solution.py:783
  409.8 238.3 %all-reduce.2.cloned.1.call-start = ((), (), s32[]{:S(2)}) async-start(), calls=%async_computation.7 | async-start | bytes 4194304 | tf_op jit(solution)/shard_map/psum | solution.py:947
  410.7 13.2 %slice-start.2 = ((s8[6291456]{0:T(1024)(128)(4,1)}), s8[4194304]{0:T(1024)(128)(4,1)S(1)}, s32[]{:S(2)}) async-start(s8[6291456]{0:T(1024)(128)(4,1)} %bitcast.218), calls=%async_computation.10 | async-start | bytes 8388608
  413.6 10.3 %slice-start.3 = ((s8[6291456]{0:T(1024)(128)(4,1)}), s8[2097152]{0:T(1024)(128)(4,1)S(1)}, s32[]{:S(2)}) async-start(s8[6291456]{0:T(1024)(128)(4,1)} %bitcast.218), calls=%async_computation.11 | async-start | bytes 4194304
  413.6 10.3 %copy-start.47 = (bf16[2,768,512]{2,1,0:T(8,128)(2,1)S(1)}, bf16[2,768,512]{2,1,0:T(8,128)(2,1)}, u32[]{:S(2)}) copy-start(bf16[2,768,512]{2,1,0:T(8,128)(2,1)} %copy-done.46) | copy-start | bytes 4718596
  413.6 10.3 %copy-start.49 = (bf16[2,768,512]{2,1,0:T(8,128)(2,1)S(1)}, bf16[2,768,512]{2,1,0:T(8,128)(2,1)}, u32[]{:S(2)}) copy-start(bf16[2,768,512]{2,1,0:T(8,128)(2,1)} %copy-done.48) | copy-start | bytes 4718596
  413.6 20.7 %slice-start = ((s8[6291456]{0:T(1024)(128)(4,1)}), s8[4194304]{0:T(1024)(128)(4,1)S(1)}, s32[]{:S(2)}) async-start(s8[6291456]{0:T(1024)(128)(4,1)} %bitcast.213), calls=%async_computation.8 | async-start | bytes 8388608
  423.9 10.5 %slice-start.1 = ((s8[6291456]{0:T(1024)(128)(4,1)}), s8[2097152]{0:T(1024)(128)(4,1)S(1)}, s32[]{:S(2)}) async-start(s8[6291456]{0:T(1024)(128)(4,1)} %bitcast.213), calls=%async_computation.9 | async-start | bytes 4194304
  434.3 13.2 %copy-start.6 = (bf16[128,2048]{1,0:T(8,128)(2,1)S(1)}, bf16[128,2048]{1,0:T(8,128)(2,1)}, u32[]{:S(2)}) copy-start(bf16[128,2048]{1,0:T(8,128)(2,1)} %copy-done.5) | copy-start | bytes 1572868
  486.8 8.0 %copy-start.14 = (f32[128,2048]{1,0:T(8,128)S(1)}, f32[128,2048]{1,0:T(8,128)}, u32[]{:S(2)}) copy-start(f32[128,2048]{1,0:T(8,128)} %copy-done.13) | copy-start | bytes 3145732
  486.8 8.0 %copy-start.15 = (f32[128,2048]{1,0:T(8,128)S(1)}, f32[128,2048]{1,0:T(8,128)}, u32[]{:S(2)}) copy-start(f32[128,2048]{1,0:T(8,128)} %convolution_add_fusion) | copy-start | bytes 3145732
  486.8 8.9 %copy-start.38 = (f32[128]{0:T(128)S(1)}, f32[128]{0:T(128)}, u32[]{:S(2)}) copy-start(f32[128]{0:T(128)} %get-tuple-element.118) | copy-start | bytes 1540
  (31 other events, 109.8 us)
Sparse Core Ops, SparseCore 0:
  129.1 39.8 all-gather.1
  320.8 75.6 reduce-scatter.1
Sparse Core Ops, SparseCore 1:
  449.4 198.6 all-reduce.1

commit v4 on v3

--- a/solution.py
+++ b/solution.py
@@ -41,18 +41,6 @@
     return (jnp.cos(angles), jnp.sin(angles))
 
 
-def rotate(values, cosine, sine_table):
-    half_size = values.shape[-1] // 2
-    leading = values[..., :half_size]
-    trailing = values[..., half_size:]
-    cosine = cosine[:, None, :]
-    sine_table = sine_table[:, None, :]
-    return jnp.concatenate(
-        [leading * cosine - trailing * sine_table, trailing * cosine + leading * sine_table],
-        axis=-1,
-    )
-
-
 def normalize(values, gain):
     factor = lax.rsqrt(jnp.mean(values * values, axis=1, keepdims=True) + epsilon)
     return (factor, (values * factor * gain).astype(jnp.bfloat16))
@@ -133,57 +121,13 @@
     pl.semaphore_wait(pltpu.get_barrier_semaphore(), count)
 
 
-def row_gather_kernel(count, *refs):
-    sources, targets = refs[:count], refs[count : 2 * count]
-    send_sem, recv_sem, own_sem = refs[2 * count :]
-    row, col, sibling, partner, _ = row_places()
-    greet([(sibling, col), (partner, col)])
-    own = [
-        pltpu.make_async_copy(sources[i], targets[i].at[row], own_sem.at[i]) for i in range(count)
-    ]
-    for copy in own:
-        copy.start()
-    await_greetings(2)
-    far, near, onward = row_copies(sources, targets, send_sem, recv_sem)
-    for copy in far + near:
-        copy.start()
-    for first, second in zip(far, onward):
-        first.wait_recv()
-        second.start()
-    for copy in own:
-        copy.wait()
-    for copy in far:
-        copy.wait_send()
-    for copy in near + onward:
-        copy.wait()
-
-
-def group_rows(values, call):
-    count = len(values)
-    space = pl.BlockSpec(memory_space=pl.ANY)
-    gathered = pl.pallas_call(
-        functools.partial(row_gather_kernel, count),
-        out_shape=[jax.ShapeDtypeStruct((4, *part.shape), part.dtype) for part in values],
-        in_specs=[space] * count,
-        out_specs=[space] * count,
-        scratch_shapes=[
-            pltpu.SemaphoreType.DMA((3 * count,)),
-            pltpu.SemaphoreType.DMA((3 * count,)),
-            pltpu.SemaphoreType.DMA((count,)),
-        ],
-        compiler_params=pltpu.CompilerParams(collective_id=1 + call, has_side_effects=True),
-        cost_estimate=pl.CostEstimate(flops=0, bytes_accessed=64 << 20, transcendentals=0),
-        name="group_rows",
-    )(*values)
-    return [part.reshape(-1, part.shape[2]) for part in gathered]
-
-
-def gather_kernel(shard, normed, grads, full, group_one, group_grad, *sems):
-    send_sem, recv_sem, own_sem, row_send, row_recv = sems
+def gather_kernel(count, normed, grads, *refs):
+    shards, (full, group_one, group_grad) = refs[:count], refs[count : count + 3]
+    mine, send_sem, recv_sem, own_sem, row_send, row_recv = refs[count + 3 :]
     row, col, sibling, partner, _ = row_places()
     along_x, along_z, along_y = col // 16, lax.rem(col // 4, 4), lax.rem(col, 4)
     other_x = 1 - along_x
-    half_rows = shard.shape[0] // 2
+    half_rows = full.shape[1] // 2
 
     def place(x, z, y):
         return x * 16 + z * 4 + y
@@ -196,10 +140,14 @@
     greet([(row, peer) for peer in z_peers + y_peers + [x_peer]])
     greet([(sibling, col), (partner, col)])
     own = [
-        pltpu.make_async_copy(shard, full.at[col], own_sem.at[0]),
-        pltpu.make_async_copy(normed, group_one.at[row], own_sem.at[1]),
-        pltpu.make_async_copy(grads, group_grad.at[row], own_sem.at[2]),
+        pltpu.make_async_copy(normed, group_one.at[row], own_sem.at[0]),
+        pltpu.make_async_copy(grads, group_grad.at[row], own_sem.at[1]),
     ]
+    start = 0
+    for shard in shards:
+        start += shard.shape[1]
+        mine[:, start - shard.shape[1] : start] = shard[...]
+    own.append(pltpu.make_async_copy(mine, full.at[col], own_sem.at[2]))
     for copy in own:
         copy.start()
     await_greetings(9)
@@ -221,10 +169,10 @@
         target = full.at[owner, pl.ds(half * half_rows, half_rows)]
         pltpu.make_async_copy(target, target, recv_sem.at[half * 32 + owner]).wait()
 
-    pass_on(col, 0, [x_peer], shard)
-    pass_on(col, 1, [x_peer], shard)
-    pass_on(col, 0, z_peers, shard)
-    pass_on(col, 1, y_peers, shard)
+    pass_on(col, 0, [x_peer], mine)
+    pass_on(col, 1, [x_peer], mine)
+    pass_on(col, 0, z_peers, mine)
+    pass_on(col, 1, y_peers, mine)
     far, near, onward = row_copies([normed, grads], [group_one, group_grad], row_send, row_recv)
     far[0].start()
     near[0].start()
@@ -232,8 +180,8 @@
     pass_on(x_peer, 0, z_peers)
     await_half(x_peer, 1)
     pass_on(x_peer, 1, y_peers)
-    pass_on(col, 0, y_peers, shard)
-    pass_on(col, 1, z_peers, shard)
+    pass_on(col, 0, y_peers, mine)
+    pass_on(col, 1, z_peers, mine)
     pass_on(x_peer, 0, y_peers)
     pass_on(x_peer, 1, z_peers)
     far[1].start()
@@ -264,18 +212,21 @@
     pltpu.make_async_copy(sent, sent, send_sem).wait()
 
 
-def gather_start(shard, normed, grads):
+def gather_start(shards, normed, grads):
     space = pl.BlockSpec(memory_space=pl.ANY)
+    count = len(shards)
+    width = sum(shard.shape[1] for shard in shards)
     full, group_one, group_grad = pl.pallas_call(
-        gather_kernel,
+        functools.partial(gather_kernel, count),
         out_shape=[
-            jax.ShapeDtypeStruct((32, *shard.shape), shard.dtype),
+            jax.ShapeDtypeStruct((32, shards[0].shape[0], width), jnp.bfloat16),
             jax.ShapeDtypeStruct((4, *normed.shape), normed.dtype),
             jax.ShapeDtypeStruct((4, *grads.shape), grads.dtype),
         ],
-        in_specs=[space] * 3,
+        in_specs=[space] * 2 + [pl.BlockSpec(memory_space=pltpu.VMEM)] * count,
         out_specs=[space] * 3,
         scratch_shapes=[
+            pltpu.VMEM((shards[0].shape[0], width), jnp.bfloat16),
             pltpu.SemaphoreType.DMA,
             pltpu.SemaphoreType.DMA((64,)),
             pltpu.SemaphoreType.DMA((3,)),
@@ -285,56 +236,293 @@
         compiler_params=pltpu.CompilerParams(collective_id=0, has_side_effects=True),
         cost_estimate=pl.CostEstimate(flops=0, bytes_accessed=200 << 20, transcendentals=0),
         name="gather_start",
-    )(shard, normed, grads)
+    )(normed, grads, *shards)
     return [part.reshape(-1, part.shape[2]) for part in (full, group_one, group_grad)]
 
 
-def row_sum_kernel(parts, total, near, far, outgoing, send_sem, recv_sem):
-    row, col, sibling, partner, across = row_places()
-    barrier = pltpu.get_barrier_semaphore()
-    for peer in (sibling, partner):
-        pl.semaphore_signal(barrier, inc=1, device_id=(peer, col), device_id_type=MESH)
-    pl.semaphore_wait(barrier, 2)
-
-    def send(origin, target, peer, i):
-        return pltpu.make_async_remote_copy(
-            src_ref=origin,
-            dst_ref=target,
-            send_sem=send_sem.at[i],
-            recv_sem=recv_sem.at[i],
-            device_id=(peer, col),
-            device_id_type=MESH,
-        )
-
-    first = send(parts.at[across], near.at[0], sibling, 0)
-    second = send(parts.at[sibling], near.at[1], sibling, 1)
-    first.start()
-    second.start()
-    first.wait_recv()
-    outgoing[...] = (
-        parts[partner].astype(jnp.float32) + near[0].astype(jnp.float32)
-    ).astype(jnp.bfloat16)
-    third = send(outgoing, far, partner, 2)
-    third.start()
-    second.wait_recv()
-    total[...] = parts[row].astype(jnp.float32) + near[1].astype(jnp.float32)
-    third.wait_recv()
-    total[...] += far[...].astype(jnp.float32)
-    first.wait_send()
-    second.wait_send()
-    third.wait_send()
-
-
-def group_sums(partial_sums, call):
-    width = partial_sums.shape[1]
-    parts = partial_sums.astype(jnp.bfloat16).reshape(4, -1, width)
-    rows = parts.shape[1]
+def turn(values, cosine, sine):
+    return values * cosine + pltpu.roll(values, 64, 1) * sine
+
+
+def score_bias(begin):
+    shape = (begin.shape[0], begin.shape[0])
+    keys = lax.broadcasted_iota(jnp.int32, shape, 1)
+    allowed = (keys >= begin) & (keys <= lax.broadcasted_iota(jnp.int32, shape, 0))
+    return jnp.where(allowed, 0.0, masked_score)
+
+
+def attention_kernel(
+    group_one, full, cosine, sine, begin, query, keys, values, attended, norms, parts, *scratch
+):
+    rows, w_pre, w_back, pre, bias, sems = scratch
+    size = keys.shape[1]
+    heads = query.shape[1] // size
+    pre_width = w_pre.shape[1]
+    loads = [
+        pltpu.make_async_copy(group_one, rows, sems.at[0]),
+        pltpu.make_async_copy(full.at[:, pl.ds(0, pre_width)], w_pre, sems.at[1]),
+        pltpu.make_async_copy(full.at[:, pl.ds(pre_width, w_back.shape[1])], w_back, sems.at[2]),
+    ]
+    for load in loads:
+        load.start()
+    bias[...] = score_bias(begin[...])
+    loads[0].wait()
+    loads[1].wait()
+    pre[...] = matmul(rows[...], w_pre[...])
+    key_start = heads * size
+    keys[...] = turn(pre[:, key_start : key_start + size], cosine[...], sine[...]).astype(
+        jnp.bfloat16
+    )
+    values[...] = pre[:, key_start + size :].astype(jnp.bfloat16)
+    lanes = lax.broadcasted_iota(jnp.int32, norms.shape, 1)
+    log_totals = jnp.zeros(norms.shape, jnp.float32)
+    for head in range(heads):
+        columns = slice(head * size, (head + 1) * size)
+        turned = turn(pre[:, columns], cosine[...], sine[...]).astype(jnp.bfloat16)
+        query[:, columns] = turned
+        scores = matmul_t(turned, keys[...]) * (size ** (-0.5)) + bias[...]
+        highest = jnp.max(scores, axis=1, keepdims=True)
+        weights = jnp.exp(scores - highest)
+        total = jnp.sum(weights, axis=1, keepdims=True)
+        weights = (weights * (1.0 / total)).astype(jnp.bfloat16)
+        attended[:, columns] = matmul(weights, values[...]).astype(jnp.bfloat16)
+        log_totals = jnp.where(lanes == head, highest + jnp.log(total), log_totals)
+    norms[...] = log_totals
+    loads[2].wait()
+    parts[...] = matmul_t(attended[...], w_back[...]).astype(jnp.bfloat16)
+
+
+def attention_forward(group_one, full, cosine, sine, begin, heads):
+    tokens, width = group_one.shape
+    size = cosine.shape[1]
+    inner = heads * size
+    pre_width = inner + 2 * size
+    space = pl.BlockSpec(memory_space=pltpu.VMEM)
+    away = pl.BlockSpec(memory_space=pl.ANY)
+    low = jnp.bfloat16
+    return pl.pallas_call(
+        attention_kernel,
+        out_shape=[
+            jax.ShapeDtypeStruct((tokens, inner), low),
+            jax.ShapeDtypeStruct((tokens, size), low),
+            jax.ShapeDtypeStruct((tokens, size), low),
+            jax.ShapeDtypeStruct((tokens, inner), low),
+            jax.ShapeDtypeStruct((tokens, 128), jnp.float32),
+            jax.ShapeDtypeStruct((tokens, width), low),
+        ],
+        in_specs=[away, away, space, space, space],
+        out_specs=[space] * 6,
+        scratch_shapes=[
+            pltpu.VMEM((tokens, width), low),
+            pltpu.VMEM((width, pre_width), low),
+            pltpu.VMEM((width, inner), low),
+            pltpu.VMEM((tokens, pre_width), jnp.float32),
+            pltpu.VMEM((tokens, tokens), jnp.float32),
+            pltpu.SemaphoreType.DMA((3,)),
+        ],
+        compiler_params=pltpu.CompilerParams(vmem_limit_bytes=56 << 20),
+        cost_estimate=pl.CostEstimate(
+            flops=2 * tokens * width * (pre_width + inner) + 8 * tokens * tokens * inner,
+            bytes_accessed=12 << 20,
+            transcendentals=heads * tokens * tokens,
+        ),
+        name="attention_forward",
+    )(group_one, full, cosine, sine, begin)
+
+
+def attention_back_kernel(
+    group_branch,
+    group_one_t,
+    full,
+    query,
+    keys,
+    values,
+    attended,
+    norms,
+    cosine,
+    sine,
+    begin,
+    begin_row,
+    parts,
+    grads,
+    *scratch,
+):
+    branch, rows_t, w_pre, w_back, pre_grad, back, bias, deltas, staged, sems = scratch
+    size = keys.shape[1]
+    heads = query.shape[1] // size
+    inner = heads * size
+    pre_width = w_pre.shape[1]
+    low = jnp.bfloat16
+    loads = [
+        pltpu.make_async_copy(group_branch, branch, sems.at[0]),
+        pltpu.make_async_copy(full.at[:, pl.ds(pre_width, inner)], w_back, sems.at[1]),
+        pltpu.make_async_copy(group_one_t, rows_t, sems.at[2]),
+        pltpu.make_async_copy(full.at[:, pl.ds(0, pre_width)], w_pre, sems.at[3]),
+    ]
+    for load in loads:
+        load.start()
+    bias[...] = score_bias(begin[...])
+    loads[0].wait()
+    loads[1].wait()
+    back[...] = matmul(branch[...], w_back[...]).astype(low)
+    scale = size ** (-0.5)
+    lanes = lax.broadcasted_iota(jnp.int32, deltas.shape, 1)
+    all_deltas = jnp.zeros(deltas.shape, jnp.float32)
+    for head in range(heads):
+        columns = slice(head * size, (head + 1) * size)
+        turned, outer = query[:, columns], back[:, columns]
+        scores = matmul_t(turned, keys[...]) * scale + bias[...]
+        probs = jnp.exp(scores - norms[:, head : head + 1])
+        prob_grad = matmul_t(outer, values[...])
+        delta = jnp.sum(probs * prob_grad, axis=1, keepdims=True)
+        all_deltas = jnp.where(lanes == head, delta, all_deltas)
+        score_grad = (probs * (prob_grad - delta)).astype(low)
+        query_grad = matmul(score_grad, keys[...]) * scale
+        pre_grad[:, columns] = turn(query_grad, cosine[...], -sine[...]).astype(low)
+    deltas[...] = all_deltas
+    deltas_t = jnp.transpose(deltas[...])
+    norms_t = jnp.transpose(norms[...])
+    shape = bias.shape
+    key_places = lax.broadcasted_iota(jnp.int32, shape, 0)
+    allowed = (key_places >= begin_row[...]) & (
+        key_places <= lax.broadcasted_iota(jnp.int32, shape, 1)
+    )
+    bias[...] = jnp.where(allowed, 0.0, masked_score)
+    key_grad = jnp.zeros(keys.shape, jnp.float32)
+    value_grad = jnp.zeros(values.shape, jnp.float32)
+    for head in range(heads):
+        columns = slice(head * size, (head + 1) * size)
+        turned, outer = query[:, columns], back[:, columns]
+        scores = matmul_t(keys[...], turned) * scale + bias[...]
+        probs = jnp.exp(scores - norms_t[head : head + 1])
+        prob_grad = matmul_t(values[...], outer)
+        score_grad = (probs * (prob_grad - deltas_t[head : head + 1])).astype(low)
+        key_grad = key_grad + matmul(score_grad, turned)
+        value_grad = value_grad + matmul(probs.astype(low), outer)
+    pre_grad[:, inner : inner + size] = turn(key_grad * scale, cosine[...], -sine[...]).astype(low)
+    pre_grad[:, inner + size :] = value_grad.astype(low)
+    loads[2].wait()
+    loads[3].wait()
+    parts[...] = matmul_t(pre_grad[...], w_pre[...]).astype(low)
+    blocks, depth = 4, branch.shape[1] // 4
+    copies = []
+    for i in range(blocks):
+        block = slice(i * depth, (i + 1) * depth)
+        staged[i, :, :pre_width] = matmul(rows_t[block], pre_grad[...]).astype(low)
+        staged[i, :, pre_width:] = outer_sum(branch[:, block], attended[...]).astype(low)
+        target = grads.at[pl.ds(i * depth, depth)]
+        copies.append(pltpu.make_async_copy(staged.at[i], target, sems.at[4 + i]))
+        copies[i].start()
+    for copy in copies:
+        copy.wait()
+
+
+def attention_back(group_branch, group_one_t, full, kept, cosine, sine, begin):
+    tokens, width = group_branch.shape
+    size = cosine.shape[1]
+    inner = kept[0].shape[1]
+    pre_width = inner + 2 * size
+    space = pl.BlockSpec(memory_space=pltpu.VMEM)
+    away = pl.BlockSpec(memory_space=pl.ANY)
+    low = jnp.bfloat16
+    return pl.pallas_call(
+        attention_back_kernel,
+        out_shape=[
+            jax.ShapeDtypeStruct((tokens, width), low),
+            jax.ShapeDtypeStruct((width, pre_width + inner), low),
+        ],
+        in_specs=[away] * 3 + [space] * 9,
+        out_specs=[space, away],
+        scratch_shapes=[
+            pltpu.VMEM((tokens, width), low),
+            pltpu.VMEM((width, tokens), low),
+            pltpu.VMEM((width, pre_width), low),
+            pltpu.VMEM((width, inner), low),
+            pltpu.VMEM((tokens, pre_width), low),
+            pltpu.VMEM((tokens, inner), low),
+            pltpu.VMEM((tokens, tokens), jnp.float32),
+            pltpu.VMEM((tokens, 128), jnp.float32),
+            pltpu.VMEM((4, width // 4, pre_width + inner), low),
+            pltpu.SemaphoreType.DMA((8,)),
+        ],
+        compiler_params=pltpu.CompilerParams(vmem_limit_bytes=56 << 20),
+        cost_estimate=pl.CostEstimate(
+            flops=4 * tokens * width * (pre_width + inner) + 20 * tokens * tokens * inner,
+            bytes_accessed=20 << 20,
+            transcendentals=4 * tokens * tokens,
+        ),
+        name="attention_back",
+    )(group_branch, group_one_t, full, *kept, cosine, sine, begin, begin.reshape(1, -1))
+
+
+def remote(source, target, sems, at, peer):
+    return pltpu.make_async_remote_copy(
+        src_ref=source,
+        dst_ref=target,
+        send_sem=sems[0].at[at],
+        recv_sem=sems[1].at[at],
+        device_id=peer,
+        device_id_type=MESH,
+    )
+
+
+def row_sum_copies(parts, near, far, outgoing, sems, at):
+    _, col, sibling, partner, across = row_places()
+    return [
+        remote(parts.at[across], near.at[0], sems, at, (sibling, col)),
+        remote(parts.at[sibling], near.at[1], sems, at + 1, (sibling, col)),
+        remote(outgoing, far, sems, at + 2, (partner, col)),
+    ]
+
+
+def row_sum_forward(parts, near, outgoing, copies):
+    _, _, _, partner, _ = row_places()
+    copies[0].wait_recv()
+    outgoing[...] = (parts[partner].astype(jnp.float32) + near[0].astype(jnp.float32)).astype(
+        jnp.bfloat16
+    )
+    copies[2].start()
+
+
+def row_sum_total(parts, near, far, copies):
+    row = row_places()[0]
+    copies[1].wait_recv()
+    total = parts[row].astype(jnp.float32) + near[1].astype(jnp.float32)
+    copies[2].wait_recv()
+    return total + far[...].astype(jnp.float32)
+
+
+def norm_rows_kernel(
+    parts, inputs, gain, hidden, normed, scale, near, far, outgoing, send_sem, recv_sem
+):
+    row, col, sibling, partner, _ = row_places()
+    greet([(sibling, col), (partner, col)])
+    await_greetings(2)
+    copies = row_sum_copies(parts, near, far, outgoing, (send_sem, recv_sem), 0)
+    copies[0].start()
+    copies[1].start()
+    row_sum_forward(parts, near, outgoing, copies)
+    total = inputs[...].astype(jnp.float32) + row_sum_total(parts, near, far, copies)
+    hidden[...] = total
+    factor = lax.rsqrt(jnp.mean(total * total, axis=1, keepdims=True) + epsilon)
+    normed[...] = (total * factor * gain[...]).astype(jnp.bfloat16)
+    scale[...] = factor
+    for copy in copies:
+        copy.wait_send()
+
+
+def norm_rows(partial_sums, inputs, gain):
+    rows, width = inputs.shape
     space = pl.BlockSpec(memory_space=pltpu.VMEM)
     return pl.pallas_call(
-        row_sum_kernel,
-        out_shape=jax.ShapeDtypeStruct((rows, width), jnp.float32),
-        in_specs=[space],
-        out_specs=space,
+        norm_rows_kernel,
+        out_shape=[
+            jax.ShapeDtypeStruct((rows, width), jnp.float32),
+            jax.ShapeDtypeStruct((rows, width), jnp.bfloat16),
+            jax.ShapeDtypeStruct((rows, 1), jnp.float32),
+        ],
+        in_specs=[space] * 3,
+        out_specs=[space] * 3,
         scratch_shapes=[
             pltpu.VMEM((2, rows, width), jnp.bfloat16),
             pltpu.VMEM((rows, width), jnp.bfloat16),
@@ -343,130 +531,275 @@
             pltpu.SemaphoreType.DMA((3,)),
         ],
         compiler_params=pltpu.CompilerParams(
-            collective_id=8 + call, has_side_effects=True, vmem_limit_bytes=32 << 20
+            collective_id=8, has_side_effects=True, vmem_limit_bytes=32 << 20
         ),
         cost_estimate=pl.CostEstimate(flops=0, bytes_accessed=64 << 20, transcendentals=0),
-        name="group_sums",
-    )(parts)
-
-
-def finish_kernel(
-    parts, grads, hidden, inputs, scale, gain, gain_ffn, result, summed, gains, *scratch
-):
-    near, far, outgoing, first, first_sum, second, second_sum, third = scratch[:8]
-    values, buffers = scratch[8:10]
-    row_send, row_recv, one_send, one_recv, two_send, two_recv = scratch[10:16]
-    three_send, three_recv, gain_send, gain_recv = scratch[16:]
-    row, col, sibling, partner, across = row_places()
-    x, z, y = col // 16, lax.rem(col // 4, 4), lax.rem(col, 4)
-    other_x = 1 - x
-    half_rows = grads.shape[3] // 2
-    y_peers = [(row, x * 16 + z * 4 + lax.rem(y + i, 4)) for i in (1, 2, 3)]
-    z_peers = [(row, x * 16 + lax.rem(z + i, 4) * 4 + y) for i in (1, 2, 3)]
-    x_peer = (row, other_x * 16 + z * 4 + y)
-    row_peers = [(peer, col) for peer in (sibling, partner, across)]
-
-    def copy(source, target, sems, at, peer):
-        return pltpu.make_async_remote_copy(
-            src_ref=source,
-            dst_ref=target,
-            send_sem=sems[0].at[at],
-            recv_sem=sems[1].at[at],
-            device_id=peer,
-            device_id_type=MESH,
-        )
-
-    greet(row_peers + y_peers + z_peers + [x_peer])
-    await_greetings(10)
-
-    row_sems = (row_send, row_recv)
-    row_copies_ = [
-        copy(parts.at[across], near.at[0], row_sems, 0, row_peers[0]),
-        copy(parts.at[sibling], near.at[1], row_sems, 1, row_peers[0]),
-        copy(outgoing, far, row_sems, 2, row_peers[1]),
-    ]
-    row_copies_[0].start()
-    row_copies_[1].start()
-    row_copies_[0].wait_recv()
-    outgoing[...] = (parts[partner].astype(jnp.float32) + near[0].astype(jnp.float32)).astype(
-        jnp.bfloat16
-    )
-    row_copies_[2].start()
-
-    def halves(half):
-        return pl.ds(half * half_rows, half_rows)
-
-    one, two, three = (one_send, one_recv), (two_send, two_recv), (three_send, three_recv)
-    one_copies, two_copies, three_copies = {}, {}, []
-    for turn, owner_x in enumerate((other_x, x)):
+        name="norm_rows",
+    )(partial_sums.reshape(4, rows, width), inputs, gain)
+
+
+class ScatterSum:
+    def __init__(self, grads, scratch):
+        self.grads = grads
+        self.first, self.first_sum, self.second, self.second_sum, self.third = scratch[:5]
+        self.one, self.two, self.three = scratch[5:7], scratch[7:9], scratch[9:11]
+        row, col = lax.axis_index("row"), lax.axis_index("col")
+        x, z, y = col // 16, lax.rem(col // 4, 4), lax.rem(col, 4)
+        self.place = (x, z, y)
+        self.half_rows = grads.shape[3] // 2
+        self.y_peers = [(row, x * 16 + z * 4 + lax.rem(y + i, 4)) for i in (1, 2, 3)]
+        self.z_peers = [(row, x * 16 + lax.rem(z + i, 4) * 4 + y) for i in (1, 2, 3)]
+        self.x_peer = (row, (1 - x) * 16 + z * 4 + y)
+        self.one_copies, self.two_copies, self.three_copies = {}, {}, []
+
+    @staticmethod
+    def scratch(grads):
+        half_rows, depth = grads.shape[3] // 2, grads.shape[4]
+        low = jnp.bfloat16
+        return [
+            pltpu.VMEM((2, 2, 3, 4, half_rows, depth), low),
+            pltpu.VMEM((2, 2, 4, half_rows, depth), low),
+            pltpu.VMEM((2, 2, 3, half_rows, depth), low),
+            pltpu.VMEM((2, half_rows, depth), low),
+            pltpu.VMEM((2, half_rows, depth), low),
+        ] + [pltpu.SemaphoreType.DMA((count,)) for count in (12, 12, 12, 12, 2, 2)]
+
+    def half(self, half):
+        return pl.ds(half * self.half_rows, self.half_rows)
+
+    def start(self):
+        x, z, y = self.place
+        for turn, owner_x in enumerate((1 - x, x)):
+            for i in range(3):
+                for half in range(2):
+                    if half == 0:
+                        source = self.grads.at[owner_x, :, lax.rem(y + i + 1, 4), self.half(0)]
+                    else:
+                        source = self.grads.at[owner_x, lax.rem(z + i + 1, 4), :, self.half(1)]
+                    at = (turn * 2 + half) * 3 + i
+                    peer = (self.y_peers, self.z_peers)[half][i]
+                    copy = remote(source, self.first.at[turn, half, i], self.one, at, peer)
+                    self.one_copies[turn, half, i] = copy
+                    copy.start()
+
+    def add_first(self, turn):
+        x, z, y = self.place
+        owner_x = (1 - x, x)[turn]
         for half in range(2):
             for i in range(3):
-                if half == 0:
-                    source = grads.at[owner_x, :, lax.rem(y + i + 1, 4), halves(0)]
-                else:
-                    source = grads.at[owner_x, lax.rem(z + i + 1, 4), :, halves(1)]
-                at = (turn * 2 + half) * 3 + i
-                peer = (y_peers, z_peers)[half][i]
-                one_copies[turn, half, i] = copy(source, first.at[turn, half, i], one, at, peer)
-                one_copies[turn, half, i].start()
-
-    def add_first(turn):
-        owner_x = (other_x, x)[turn]
-        for half in range(2):
-            for i in range(3):
-                one_copies[turn, half, i].wait_recv()
+                self.one_copies[turn, half, i].wait_recv()
 
             def add(k, carry, half=half):
                 if half == 0:
-                    total = grads[owner_x, k, y, halves(0)].astype(jnp.float32)
+                    total = self.grads[owner_x, k, y, self.half(0)].astype(jnp.float32)
                 else:
-                    total = grads[owner_x, z, k, halves(1)].astype(jnp.float32)
+                    total = self.grads[owner_x, z, k, self.half(1)].astype(jnp.float32)
                 for i in range(3):
-                    total = total + first[turn, half, i, k].astype(jnp.float32)
-                first_sum[turn, half, k] = total.astype(jnp.bfloat16)
+                    total = total + self.first[turn, half, i, k].astype(jnp.float32)
+                self.first_sum[turn, half, k] = total.astype(jnp.bfloat16)
                 return carry
 
             lax.fori_loop(0, 4, add, 0)
             for i in range(3):
                 away = lax.rem((z, y)[half] + i + 1, 4)
-                two_copies[turn, half, i] = copy(
-                    first_sum.at[turn, half, away],
-                    second.at[turn, half, i],
-                    two,
+                copy = remote(
+                    self.first_sum.at[turn, half, away],
+                    self.second.at[turn, half, i],
+                    self.two,
                     (turn * 2 + half) * 3 + i,
-                    (z_peers, y_peers)[half][i],
+                    (self.z_peers, self.y_peers)[half][i],
                 )
-                two_copies[turn, half, i].start()
-
-    def add_second(turn, half):
+                self.two_copies[turn, half, i] = copy
+                copy.start()
+
+    def second_total(self, turn, half):
+        _, z, y = self.place
         for i in range(3):
-            two_copies[turn, half, i].wait_recv()
-        total = first_sum[turn, half, (z, y)[half]].astype(jnp.float32)
+            self.two_copies[turn, half, i].wait_recv()
+        total = self.first_sum[turn, half, (z, y)[half]].astype(jnp.float32)
         for i in range(3):
-            total = total + second[turn, half, i].astype(jnp.float32)
+            total = total + self.second[turn, half, i].astype(jnp.float32)
         return total
 
-    row_copies_[1].wait_recv()
-    incoming = parts[row].astype(jnp.float32) + near[1].astype(jnp.float32)
-    row_copies_[2].wait_recv()
-    incoming = incoming + far[...].astype(jnp.float32)
+    def add_second(self):
+        for half in range(2):
+            self.second_sum[half] = self.second_total(0, half).astype(jnp.bfloat16)
+            copy = remote(
+                self.second_sum.at[half], self.third.at[half], self.three, half, self.x_peer
+            )
+            self.three_copies.append(copy)
+            copy.start()
+
+    def add_third(self, pieces):
+        for half in range(2):
+            total = self.second_total(1, half)
+            self.three_copies[half].wait_recv()
+            total = total + self.third[half].astype(jnp.float32)
+            start = 0
+            for piece in pieces:
+                piece[self.half(half)] = total[:, start : start + piece.shape[1]]
+                start += piece.shape[1]
+
+    def end(self):
+        for copy in [*self.one_copies.values(), *self.two_copies.values(), *self.three_copies]:
+            copy.wait_send()
+
+
+def branch_rows_kernel(branch, router, grads, group, router_sum, *refs):
+    pieces, scratch = refs[:2], refs[2:]
+    near, far, outgoing, send, recv, own_sem, row_send, row_recv = scratch[:8]
+    row, col, sibling, partner, _ = row_places()
+    scatter = ScatterSum(grads, scratch[8:])
+    greet([(sibling, col), (partner, col)])
+    greet(scatter.y_peers + scatter.z_peers + [scatter.x_peer])
+    own = pltpu.make_async_copy(branch, group.at[row], own_sem)
+    own.start()
+    await_greetings(9)
+    far_rows, near_rows, onward = row_copies([branch], [group], send, recv)
+    far_rows[0].start()
+    near_rows[0].start()
+    copies = row_sum_copies(router, near, far, outgoing, (row_send, row_recv), 0)
+    copies[0].start()
+    copies[1].start()
+    scatter.start()
+    row_sum_forward(router, near, outgoing, copies)
+    scatter.add_first(0)
+    scatter.add_first(1)
+    far_rows[0].wait_recv()
+    onward[0].start()
+    scatter.add_second()
+    router_sum[...] = row_sum_total(router, near, far, copies).astype(jnp.bfloat16)
+    scatter.add_third(pieces)
+    own.wait()
+    far_rows[0].wait_send()
+    near_rows[0].wait()
+    onward[0].wait()
+    for copy in copies:
+        copy.wait_send()
+    scatter.end()
+
+
+def branch_rows(branch, router, grads, widths):
+    away = pl.BlockSpec(memory_space=pl.ANY)
+    space = pl.BlockSpec(memory_space=pltpu.VMEM)
+    _, rows, width = router.shape
+    group, router_sum, *sums = pl.pallas_call(
+        branch_rows_kernel,
+        out_shape=[
+            jax.ShapeDtypeStruct((4, *branch.shape), branch.dtype),
+            jax.ShapeDtypeStruct((rows, width), jnp.bfloat16),
+        ]
+        + [jax.ShapeDtypeStruct((grads.shape[3], part), jnp.float32) for part in widths],
+        in_specs=[away, space, space],
+        out_specs=[away, space] + [space] * len(widths),
+        scratch_shapes=[
+            pltpu.VMEM((2, rows, width), jnp.bfloat16),
+            pltpu.VMEM((rows, width), jnp.bfloat16),
+            pltpu.VMEM((rows, width), jnp.bfloat16),
+            pltpu.SemaphoreType.DMA((3,)),
+            pltpu.SemaphoreType.DMA((3,)),
+            pltpu.SemaphoreType.DMA,
+            pltpu.SemaphoreType.DMA((3,)),
+            pltpu.SemaphoreType.DMA((3,)),
+            *ScatterSum.scratch(grads),
+        ],
+        compiler_params=pltpu.CompilerParams(
+            collective_id=1, has_side_effects=True, vmem_limit_bytes=32 << 20
+        ),
+        cost_estimate=pl.CostEstimate(flops=0, bytes_accessed=64 << 20, transcendentals=0),
+        name="branch_rows",
+    )(branch, router, grads)
+    return group.reshape(-1, branch.shape[1]), router_sum, sums
+
+
+def finish_kernel(
+    parts,
+    grads,
+    shared_parts,
+    router_part,
+    stream,
+    inputs,
+    scale,
+    gain,
+    gain_ffn,
+    result,
+    block_out,
+    router,
+    gains,
+    *refs,
+):
+    pieces, scratch = refs[:3], refs[3:]
+    near, far, outgoing, values, buffers, router_in, router_own = scratch[:7]
+    row_send, row_recv, gain_send, gain_recv, own_sem = scratch[7:12]
+    col_send, col_recv, pass_send, pass_recv = scratch[12:16]
+    scatter = ScatterSum(grads, scratch[16:])
+    row, col, sibling, partner, across = row_places()
+    row_peers = [(peer, col) for peer in (sibling, partner, across)]
+
+    greet(row_peers)
+    barrier = pltpu.get_barrier_semaphore()
+
+    def greet_col(step, carry):
+        peer = (row, lax.rem(col + step, 32))
+        pl.semaphore_signal(barrier, inc=1, device_id=peer, device_id_type=MESH)
+        return carry
+
+    lax.fori_loop(1, 32, greet_col, 0)
+    await_greetings(34)
+
+    row_sems = (row_send, row_recv)
+    attn_copies = row_sum_copies(parts, near.at[0], far.at[0], outgoing.at[0], row_sems, 0)
+    shared_copies = row_sum_copies(
+        shared_parts, near.at[1], far.at[1], outgoing.at[1], row_sems, 3
+    )
+    for copies in (attn_copies, shared_copies):
+        copies[0].start()
+        copies[1].start()
+    row_sum_forward(parts, near.at[0], outgoing.at[0], attn_copies)
+
+    def push(source, target, at):
+        def step(i, carry):
+            peer = lax.rem(col + i, 32)
+            pltpu.make_async_remote_copy(
+                src_ref=source(peer),
+                dst_ref=target,
+                send_sem=col_send.at[at],
+                recv_sem=col_recv.at[at],
+                device_id=(row, peer),
+                device_id_type=MESH,
+            ).start()
+            return carry
+
+        lax.fori_loop(1, 32, step, 0)
+
+    def await_pushes(target, sem):
+        others = target.at[pl.ds(0, 31)]
+        pltpu.make_async_copy(others, others, sem).wait()
+
+    push(lambda peer: router_part.at[peer], router_in.at[col], 0)
+    router_in[col] = router_part[col]
+
+    scatter.start()
+
+    row_sum_forward(shared_parts, near.at[1], outgoing.at[1], shared_copies)
+    incoming = row_sum_total(parts, near.at[0], far.at[0], attn_copies)
     rows = inputs[...].astype(jnp.float32)
     factor = scale[...]
     weighted = gain[...] * incoming
     mean = jnp.mean(weighted * rows, axis=1, keepdims=True)
-    result[...] = hidden[...] + factor * weighted - rows * (factor * factor * factor * mean)
+    result[...] = factor * weighted - rows * (factor * factor * factor * mean)
     values[0, 0:1] = jnp.sum(incoming * rows * factor, axis=0, keepdims=True)
     values[0, 1:2] = gain_ffn[...]
 
     gain_sems = (gain_send, gain_recv)
     gain_copies = []
-    stages = (row_peers, y_peers, z_peers, [x_peer])
+    stages = (row_peers, scatter.y_peers, scatter.z_peers, [scatter.x_peer])
 
     def start_gains(stage):
         at = 3 * stage
         for i, peer in enumerate(stages[stage]):
             gain_copies.append(
-                copy(values.at[stage], buffers.at[at + i], gain_sems, at + i, peer)
+                remote(values.at[stage], buffers.at[at + i], gain_sems, at + i, peer)
             )
             gain_copies[-1].start()
 
@@ -479,72 +812,84 @@
         values[stage + 1] = total
 
     start_gains(0)
-    add_first(0)
+    await_pushes(router_in, col_recv.at[0])
+    router_own[...] = jnp.sum(router_in[...].astype(jnp.float32), axis=0).astype(jnp.bfloat16)
+    push(lambda peer: router_own, router.at[row, col], 1)
+    own = pltpu.make_async_copy(router_own, router.at[row, col], own_sem)
+    own.start()
+    scatter.add_first(0)
     add_gains(0)
     start_gains(1)
-    add_first(1)
+    own.wait()
+    await_pushes(router.at[row], col_recv.at[1])
+    far_rows, near_rows, onward = row_copies([router.at[row]], [router], pass_send, pass_recv)
+    far_rows[0].start()
+    near_rows[0].start()
+    scatter.add_first(1)
     add_gains(1)
     start_gains(2)
-    for half in range(2):
-        second_sum[half] = add_second(0, half).astype(jnp.bfloat16)
-        three_copies.append(copy(second_sum.at[half], third.at[half], three, half, x_peer))
-        three_copies[half].start()
+    shared = row_sum_total(shared_parts, near.at[1], far.at[1], shared_copies)
+    block_out[...] = (stream[...] + shared).astype(jnp.bfloat16)
+    far_rows[0].wait_recv()
+    onward[0].start()
+    scatter.add_second()
     add_gains(2)
     start_gains(3)
-    for half in range(2):
-        total = add_second(1, half)
-        three_copies[half].wait_recv()
-        summed[halves(half)] = total + third[half].astype(jnp.float32)
+    scatter.add_third(pieces)
     add_gains(3)
     gains[...] = values[4]
-    for done in [*row_copies_, *one_copies.values(), *two_copies.values()]:
+    await_pushes(router_in, col_send.at[0])
+    await_pushes(router.at[row], col_send.at[1])
+    far_rows[0].wait_send()
+    near_rows[0].wait()
+    onward[0].wait()
+    for done in [*attn_copies, *shared_copies, *gain_copies]:
         done.wait_send()
-    for done in [*three_copies, *gain_copies]:
-        done.wait_send()
-
-
-def finish(parts, grads, hidden, inputs, scale, gain, gain_ffn):
+    scatter.end()
+
+
+def finish(parts, grads, shared_parts, router_part, stream, inputs, scale, gain, gain_ffn, widths):
     space = pl.BlockSpec(memory_space=pltpu.VMEM)
-    rows, width = hidden.shape
-    half_rows, depth = grads.shape[3] // 2, grads.shape[4]
+    away = pl.BlockSpec(memory_space=pl.ANY)
+    rows, width = inputs.shape
     low = jnp.bfloat16
+    share = router_part.shape[1:]
     return pl.pallas_call(
         finish_kernel,
         out_shape=[
             jax.ShapeDtypeStruct((rows, width), jnp.float32),
-            jax.ShapeDtypeStruct((2 * half_rows, depth), jnp.float32),
+            jax.ShapeDtypeStruct((rows, width), low),
+            jax.ShapeDtypeStruct((4, 32, *share), low),
             jax.ShapeDtypeStruct((2, width), jnp.float32),
-        ],
-        in_specs=[space] * 7,
-        out_specs=[space] * 3,
+        ]
+        + [jax.ShapeDtypeStruct((grads.shape[3], part), jnp.float32) for part in widths],
+        in_specs=[space] * 9,
+        out_specs=[space, space, away, space] + [space] * len(widths),
         scratch_shapes=[
+            pltpu.VMEM((2, 2, rows, width), low),
             pltpu.VMEM((2, rows, width), low),
-            pltpu.VMEM((rows, width), low),
-            pltpu.VMEM((rows, width), low),
-            pltpu.VMEM((2, 2, 3, 4, half_rows, depth), low),
-            pltpu.VMEM((2, 2, 4, half_rows, depth), low),
-            pltpu.VMEM((2, 2, 3, half_rows, depth), low),
-            pltpu.VMEM((2, half_rows, depth), low),
-            pltpu.VMEM((2, half_rows, depth), low),
+            pltpu.VMEM((2, rows, width), low),
             pltpu.VMEM((5, 2, width), jnp.float32),
             pltpu.VMEM((10, 2, width), jnp.float32),
+            pltpu.VMEM((32, *share), low),
+            pltpu.VMEM(share, low),
+            pltpu.SemaphoreType.DMA((6,)),
+            pltpu.SemaphoreType.DMA((6,)),
+            pltpu.SemaphoreType.DMA((10,)),
+            pltpu.SemaphoreType.DMA((10,)),
+            pltpu.SemaphoreType.DMA,
+            pltpu.SemaphoreType.DMA((2,)),
+            pltpu.SemaphoreType.DMA((2,)),
             pltpu.SemaphoreType.DMA((3,)),
             pltpu.SemaphoreType.DMA((3,)),
-            pltpu.SemaphoreType.DMA((12,)),
-            pltpu.SemaphoreType.DMA((12,)),
-            pltpu.SemaphoreType.DMA((12,)),
-            pltpu.SemaphoreType.DMA((12,)),
-            pltpu.SemaphoreType.DMA((2,)),
-            pltpu.SemaphoreType.DMA((2,)),
-            pltpu.SemaphoreType.DMA((10,)),
-            pltpu.SemaphoreType.DMA((10,)),
+            *ScatterSum.scratch(grads),
         ],
         compiler_params=pltpu.CompilerParams(
-            collective_id=16, has_side_effects=True, vmem_limit_bytes=56 << 20
+            collective_id=16, has_side_effects=True, vmem_limit_bytes=60 << 20
         ),
         cost_estimate=pl.CostEstimate(flops=0, bytes_accessed=200 << 20, transcendentals=0),
         name="finish",
-    )(parts, grads, hidden, inputs, scale, gain, gain_ffn)
+    )(parts, grads, shared_parts, router_part, stream, inputs, scale, gain, gain_ffn)
 
 
 def packed_places(shape, axis):
@@ -829,46 +1174,23 @@
     scale_one, normed_one = normalize(inputs, gain_attn)
     shards = [w_query, w_keyval, w_out, w_shared_in, w_shared_out]
     shards = [part.reshape(part.shape[0], -1) for part in shards]
-    full, group_one, group_grad = gather_start(
-        jnp.concatenate(shards, axis=1), normed_one, grad_low
-    )
-    full_parts, end = [], 0
-    for part in shards:
-        full_parts.append(full[:, end : end + part.shape[1]])
-        end += part.shape[1]
-    full_query, full_keyval, full_out, full_shared_in, full_shared_out = full_parts
+    full, group_one, group_grad = gather_start(shards, normed_one, grad_low)
+    shared_start = w_query.shape[1] + w_keyval.shape[2] + w_out.shape[1]
+    shared_width = w_shared_out.shape[1]
+    full_shared_in = full[:, shared_start : shared_start + 2 * shared_width]
+    full_shared_out = full[:, shared_start + 2 * shared_width :]
 
     segment, position = layout(doc_lengths.reshape(-1), group_tok)
     cosine, sine_table = rotary(position, head_size)
-    query_pre = matmul(group_one, full_query).reshape(group_tok, local_heads, head_size)
-    query_rot = rotate(query_pre, cosine, sine_table).astype(jnp.bfloat16)
-    keyval_pre = matmul(group_one, full_keyval).reshape(group_tok, local_kv, 2 * head_size)
-    key_rows = rotate(keyval_pre[..., :head_size], cosine, sine_table).astype(jnp.bfloat16)
-    value_rows = keyval_pre[..., head_size:].astype(jnp.bfloat16)
-    places = jnp.arange(group_tok, dtype=jnp.int32)
-    allowed = (segment[:, None] == segment[None, :]) & (places[:, None] >= places[None, :])
-    query_block = query_rot.reshape(group_tok, local_kv, group_size, head_size)
-
-    def block_scores():
-        scores = (
-            jnp.einsum("qagd,kad->agqk", query_block, key_rows, preferred_element_type=jnp.float32)
-            * inv_root
-        )
-        return jnp.where(allowed[None, None], scores, masked_score)
-
-    scores = block_scores()
-    highest = jnp.max(scores, axis=3, keepdims=True)
-    weights = jnp.exp(scores - highest)
-    totals = jnp.sum(weights, axis=3, keepdims=True)
-    weights_low = (weights / totals).astype(jnp.bfloat16)
-    attended = (
-        jnp.einsum("agqk,kad->qagd", weights_low, value_rows, preferred_element_type=jnp.float32)
-        .reshape(group_tok, local_heads * head_size)
-        .astype(jnp.bfloat16)
-    )
-    log_totals = highest + jnp.log(totals)
-    hidden_state = inputs + group_sums(matmul_t(attended, full_out), 0)
-    scale_two, normed_two = normalize(hidden_state, gain_ffn)
+    cosine = jnp.concatenate([cosine, cosine], axis=1)
+    sine_table = jnp.concatenate([-sine_table, sine_table], axis=1)
+    begin = (jnp.arange(group_tok, dtype=jnp.int32) - position)[:, None]
+    *kept, attended_parts = attention_forward(
+        group_one, full, cosine, sine_table, begin, local_heads
+    )
+    hidden_state, normed_two, scale_two = norm_rows(
+        attended_parts, block_in.reshape(rows_dev, model_width), gain_ffn[None]
+    )
 
     logits = matmul(normed_two, w_router)
     scores_sig = jnp.where(chosen, jax.nn.sigmoid(logits), 0.0)
@@ -882,30 +1204,28 @@
     received_grads = exchange(send_grads)
 
     group_two = lax.all_gather(normed_two, "row", axis=0, tiled=True)
-    shared_width = full_shared_in.shape[1] // 2
     shared_pre = matmul(group_two, full_shared_in)
     shared_gate, shared_up = shared_pre[:, :shared_width], shared_pre[:, shared_width:]
     shared_act, shared_slope = swish_parts(shared_gate)
     shared_hidden = (shared_act * shared_up).astype(jnp.bfloat16)
     shared_hidden_grad = matmul(group_grad, full_shared_out)
-    grad_shared_out = outer_sum(group_grad, shared_hidden)
     shared_pre_grad = jnp.concatenate(
         [shared_hidden_grad * shared_up * shared_slope, shared_hidden_grad * shared_act], axis=1
     ).astype(jnp.bfloat16)
-    grad_shared_in = outer_sum(group_two, shared_pre_grad)
-    shared_sums = lax.psum_scatter(
-        jnp.concatenate(
-            [
-                matmul_t(shared_hidden, full_shared_out).astype(jnp.bfloat16),
-                matmul_t(shared_pre_grad, full_shared_in).astype(jnp.bfloat16),
-            ],
-            axis=1,
-        ),
+    shared_grads = jnp.concatenate(
+        [
+            outer_sum(group_two, shared_pre_grad).astype(jnp.bfloat16),
+            outer_sum(group_grad, shared_hidden).astype(jnp.bfloat16),
+        ],
+        axis=1,
+    )
+    shared_parts = matmul_t(shared_hidden, full_shared_out).astype(jnp.bfloat16)
+    shared_input = lax.psum_scatter(
+        matmul_t(shared_pre_grad, full_shared_in).astype(jnp.bfloat16),
         "row",
         scatter_dimension=0,
         tiled=True,
     ).astype(jnp.float32)
-    shared_branch, shared_input = shared_sums[:, :model_width], shared_sums[:, model_width:]
 
     expert_in = unpack_slots(received)
     expert_pre = jnp.einsum(
@@ -938,81 +1258,53 @@
         "esd,esf->edf", expert_in, expert_pre_grad, preferred_element_type=jnp.float32
     )
     routed_branch, gate_grads = sum_gated(code, returned, send_grads, gates)
-    block_out = (hidden_state + shared_branch + routed_branch).astype(jnp.bfloat16)
+    stream = hidden_state + routed_branch
     gate_grads = gate_grads.transpose(1, 0, 2).reshape(rows_dev, expert_count)
     logit_grad = (
         (1.0 - scores_sig)
         * (gate_grads - gate_weights * jnp.sum(gate_grads, axis=1, keepdims=True))
     ).astype(jnp.bfloat16)
-    router_sum = lax.psum(outer_sum(normed_two, logit_grad), ("row", "col"))
+    router_parts = outer_sum(normed_two, logit_grad).astype(jnp.bfloat16)
+    router_parts = router_parts.reshape(row_count, -1, expert_count)
     router_input = shared_input + matmul_t(logit_grad, w_router)
-    returned_grad, router_input, block_out, grad_expert_in, grad_expert_out = (
-        lax.optimization_barrier(
-            (returned_grad, router_input, block_out, grad_expert_in, grad_expert_out)
-        )
-    )
+    shadowed = (router_input, router_parts, stream, shared_grads, group_one.T)
+    returned_grad, shadowed, grad_expert_in, grad_expert_out = lax.optimization_barrier(
+        (returned_grad, shadowed, grad_expert_in, grad_expert_out)
+    )
+    router_input, router_parts, stream, shared_grads, group_one_t = shadowed
 
     normed_two_grad = router_input + sum_tokens(code, returned_grad)
     gain_ffn_grad, hidden_back = norm_back(hidden_state, scale_two, gain_ffn, normed_two_grad)
     hidden_total = grad_rows + hidden_back
-    (group_branch,) = group_rows([hidden_total.astype(jnp.bfloat16)], 0)
-    attended_grad = matmul(group_branch, full_out).astype(jnp.bfloat16)
-    grad_out_w = outer_sum(group_branch, attended)
-
-    out_block = attended_grad.reshape(group_tok, local_kv, group_size, head_size)
-    probs_full = jnp.exp(block_scores() - log_totals)
-    prob_grad = jnp.einsum(
-        "qagd,kad->agqk", out_block, value_rows, preferred_element_type=jnp.float32
-    )
-    row_delta = jnp.sum(probs_full * prob_grad, axis=3, keepdims=True)
-    score_low = (probs_full * (prob_grad - row_delta)).astype(jnp.bfloat16)
-    query_grad = (
-        jnp.einsum("agqk,kad->qagd", score_low, key_rows, preferred_element_type=jnp.float32)
-        * inv_root
-    ).reshape(group_tok, local_heads, head_size)
-    key_grad = (
-        jnp.einsum("agqk,qagd->kad", score_low, query_block, preferred_element_type=jnp.float32)
-        * inv_root
-    )
-    value_grad = jnp.einsum(
-        "agqk,qagd->kad",
-        probs_full.astype(jnp.bfloat16),
-        out_block,
-        preferred_element_type=jnp.float32,
-    )
-    query_pre_grad = (
-        rotate(query_grad, cosine, -sine_table)
-        .astype(jnp.bfloat16)
-        .reshape(group_tok, local_heads * head_size)
-    )
-    keyval_pre_grad = (
-        jnp.concatenate([rotate(key_grad, cosine, -sine_table), value_grad], axis=2)
-        .astype(jnp.bfloat16)
-        .reshape(group_tok, local_kv * 2 * head_size)
-    )
-    grad_query_w = outer_sum(group_one, query_pre_grad)
-    grad_keyval_w = outer_sum(group_one, keyval_pre_grad)
-    normed_one_parts = matmul_t(query_pre_grad, full_query) + matmul_t(
-        keyval_pre_grad, full_keyval
-    )
-    shard_grads = [grad_query_w, grad_keyval_w, grad_out_w, grad_shared_in, grad_shared_out]
-    shard_grads = jnp.concatenate([part.astype(jnp.bfloat16) for part in shard_grads], axis=1)
-    input_total, shard_sums, gain_sums = finish(
-        normed_one_parts.astype(jnp.bfloat16).reshape(row_count, rows_dev, model_width),
+    widths = [part.shape[1] for part in shards]
+    group_branch, router_sum, shared_sums = branch_rows(
+        hidden_total.astype(jnp.bfloat16),
+        router_parts,
+        shared_grads.reshape(2, 4, 4, -1, shared_grads.shape[1]),
+        widths[3:],
+    )
+    normed_one_parts, shard_grads = attention_back(
+        group_branch, group_one_t, full, kept, cosine, sine_table, begin
+    )
+    input_back, block_out, router_sum, gain_sums, *sums = finish(
+        normed_one_parts.reshape(row_count, rows_dev, model_width),
         shard_grads.reshape(2, 4, 4, -1, shard_grads.shape[1]),
-        hidden_total,
+        shared_parts.reshape(row_count, rows_dev, model_width),
+        router_sum.reshape(32, -1, expert_count),
+        stream,
         block_in.reshape(rows_dev, model_width),
         scale_one,
         gain_attn[None],
         gain_ffn_grad[None],
-    )
-    sums, end = [], 0
-    for part, like in zip(shards, (w_query, w_keyval, w_out, w_shared_in, w_shared_out)):
-        sums.append(shard_sums[:, end : end + part.shape[1]].reshape(like.shape))
-        end += part.shape[1]
+        widths[:3],
+    )
+    sums = [
+        part.reshape(like.shape)
+        for part, like in zip(sums + shared_sums, (w_query, w_keyval, w_out, w_shared_in, w_shared_out))
+    ]
     return (
         block_out.reshape(1, rows_dev, model_width),
-        input_total.reshape(1, rows_dev, model_width),
+        (hidden_total + input_back).reshape(1, rows_dev, model_width),
         gain_sums[0],
         sums[0],
         sums[1],
@@ -1020,7 +1312,7 @@
         gain_sums[1],
         sums[3],
         sums[4],
-        router_sum,
+        router_sum.reshape(model_width, expert_count).astype(jnp.float32),
         grad_expert_in,
         grad_expert_out,
     )

time: 673 us -> 620 us (0.921)
  waiting for transfers between devices: 208 us -> 166 us
  Pallas kernels: 213 us -> 247 us
  matrix products: 103 us -> 78.6 us
  local copies, waits for them, and re-layouts: 51.9 us -> 35.6 us
    pallas_call x3 -> x5, Pallas kernels: 93.1 us -> 128 us  [the longest x1 54.9 us: gather_start(): pl.pallas_call(functools.partial(gather_kernel, count), out_shape=[jax.Sh...]
    psum x1 -> x0, waiting for transfers between devices: 25.4 us -> none  [per_device(): router_sum = lax.psum(outer_sum(normed_two, logit_grad), ('row', 'col'))]
    all_to_all x4, waiting for transfers between devices: 181 us -> 160 us  [exchange(): lax.all_to_all(pairs, ('row', 'col'), split_axis=0, concat_axis=0, tiled=...]
    concatenate x2 -> x0, local copies, waits for them, and re-layouts: 10.7 us -> none  [the longest x1 9.96 us: per_device(): jnp.concatenate([part.astype(jnp.bfloat16) for part in shard_grads], axis=1)]
    dot_general x7 -> x4, matrix products: 16.3 us -> 6.45 us  [matmul(): return jnp.dot(matrix, partner, preferred_element_type=jnp.float32)]
    dot_general x6 -> x3, matrix products: 18.9 us -> 9.07 us  [matmul_t(): lax.dot_general(matrix, partner, (((1,), (1,)), ((), ())), preferred_elem...]
    dot_general x2 -> x0, local copies, waits for them, and re-layouts: 6.96 us -> none  [matmul(): return jnp.dot(matrix, partner, preferred_element_type=jnp.float32)]
    unnamed x119 -> x78, local copies, waits for them, and re-layouts: 25.7 us -> 25 us
  transfers between devices with their start and end apart: 7 -> 6, of which waited for: 5 -> 5; matrix products, arithmetic and copies ran while one was open for 19% -> 15% of each run, Pallas kernels for 20% -> 7%
where the time goes in v4:
time: 620 us; the launch traced here: 610 us
  Pallas kernels  247 us (40%)
  waiting for transfers between devices  166 us (27%)
  matrix products  78.6 us (13%)
  starting transfers between devices  46.9 us (8%)
  local copies, waits for them, and re-layouts  35.6 us (6%)
  other arithmetic  21.4 us (3%)
  between operations  15 us (2%)
    all_to_all x4, waiting for transfers between devices, exchange(): lax.all_to_all(pairs, ('row', 'col'), split_axis=0, concat_axis=0, tiled=...  160 us
    pallas_call x1, Pallas kernels, finish(): pl.pallas_call(finish_kernel, out_shape=[jax.ShapeDtypeStruct((rows, widt...  63.7 us
    pallas_call x1, Pallas kernels, gather_start(): pl.pallas_call(functools.partial(gather_kernel, count), out_shape=[jax.Sh...  54.9 us
    all_to_all x4, starting transfers between devices, exchange(): lax.all_to_all(pairs, ('row', 'col'), split_axis=0, concat_axis=0, tiled=...  36.4 us
    unnamed x78, local copies, waits for them, and re-layouts  25 us
    pallas_call x1, Pallas kernels, branch_rows(): pl.pallas_call(branch_rows_kernel, out_shape=[jax.ShapeDtypeStruct((4, *b...  22.3 us
    pallas_call x1, Pallas kernels, norm_rows(): pl.pallas_call(norm_rows_kernel, out_shape=[jax.ShapeDtypeStruct((rows, w...  21.6 us
    pallas_call x1, Pallas kernels, attention_back(): pl.pallas_call(attention_back_kernel, out_shape=[jax.ShapeDtypeStruct((to...  17.3 us
  transfers between devices with their start and end apart: 6, of which 5 were waited for; matrix products, arithmetic and copies ran while one was open for 15% of the time, Pallas kernels for 7%

profile of v4, /device:TPU:1, one launch (start us, length us, event | category | flops | bytes accessed | tf_op | source)
XLA Modules:
  0.0 609.8 jit_solution(9899249875032287164)
XLA Ops:
  18.0 54.9 %gather_start.1 = (bf16[32,64,1664]{2,1,0:T(8,128)(2,1)}, bf16[4,128,2048]{2,1,0:T(8,128)(2,1)}, bf16[4,128,2048]{2,1,0:T(8,128)(2,1)}) custom-call(bf16[128,2048]{1,0:T(8,128)(2,1)} %fusion.8.normed, bf16[128,2048]{1,0:T(8,128)(2,1)} %bitcast.118, bf16[64,512]{1,0:T(8,128)(2,1)} %refs_0_.1, bf16[64,256]{1,0:T(8,128)(2,1)} %bitcast.153, ...), custom_call_target="tpu_custom_call" | custom-call | bytes 209715200 | tf_op jit(solution)/shard_map/gather_start/pallas_call | solution.py:219
  73.0 11.4 %attention_forward.1 = (bf16[512,512]{1,0:T(8,128)(2,1)}, bf16[512,128]{1,0:T(8,128)(2,1)}, bf16[512,128]{1,0:T(8,128)(2,1)}, bf16[512,512]{1,0:T(8,128)(2,1)}, ...) custom-call(bf16[512,2048]{1,0:T(8,128)(2,1)} %bitcast.139, bf16[2048,1664]{1,0:T(8,128)(2,1)} %bitcast.143, ...), custom_call_target="tpu_custom_call" | custom-call | flops 3758096384 | bytes 12582912 | tf_op jit(solution)/shard_map/attention_forward/pallas_call | solution.py:303
  86.0 21.6 %norm_rows.1 = (f32[128,2048]{1,0:T(8,128)S(1)}, bf16[128,2048]{1,0:T(8,128)(2,1)}, f32[128,1]{1,0:T(8,128)S(1)}) custom-call(bf16[4,128,2048]{2,1,0:T(8,128)(2,1)S(1)} %bitcast.121, bf16[128,2048]{1,0:T(8,128)(2,1)S(1)} %bitcast.114, f32[1,2048]{1,0:T(1,128)S(1)} %bitcast.132), custom_call_target="tpu_custom_call" | custom-call | bytes 67108864 | tf_op jit(solution)/shard_map/norm_rows/pallas_call | solution.py:517
  107.6 4.9 pack_tokens.3
  115.2 5.5 all-to-all-start
  122.3 6.8 %pack_tokens.2.grads = bf16[2048,1536]{1,0:T(8,128)(2,1)S(1)} custom-call(bf16[8,32,128]{2,1,0:T(8,128)(2,1)S(1)} %bitcast.124, bf16[128,2048]{1,0:T(8,128)(2,1)S(1)} %bitcast.119, bf16[8,32,128]{2,1,0:T(8,128)(2,1)S(1)} %bitcast.129, bf16[8,32,128]{2,1,0:T(8,128)(2,1)S(1)} %bitcast.127), custom_call_target="tpu_custom_call" | custom-call | flops 1610612736 | bytes 8388608 | tf_op jit(solution)/shard_map/pack_tokens/pallas_call | solution.py:948
  131.8 64.5 %all-to-all-done = bf16[128,16,1536]{2,1,0:T(8,128)(2,1)} async-done(((bf16[128,16,1536]{2,1,0:T(8,128)(2,1)}), bf16[128,16,1536]{2,1,0:T(8,128)(2,1)}, u32[]{:S(2)}, u32[]{:S(2)}) %all-to-all-start) | async-done | bytes 6291488 | tf_op jit(solution)/shard_map/all_to_all | solution.py:1128
  196.3 10.8 %all-to-all-start.1 = ((bf16[128,16,1536]{2,1,0:T(8,128)(2,1)}), bf16[128,16,1536]{2,1,0:T(8,128)(2,1)}, u32[]{:S(2)}, u32[]{:S(2)}) async-start(bf16[128,16,1536]{2,1,0:T(8,128)(2,1)} %bitcast.107), calls=%async_computation.1 | async-start | bytes 12582912 | tf_op jit(solution)/shard_map/all_to_all | solution.py:1128
  207.1 7.4 %unpack_slots.2 = bf16[2,768,2048]{2,1,0:T(8,128)(2,1)S(1)} custom-call(bf16[2048,1536]{1,0:T(8,128)(2,1)} %bitcast.19.packed), custom_call_target="tpu_custom_call" | custom-call | flops 2415919104 | bytes 14680064 | tf_op jit(solution)/shard_map/unpack_slots/pallas_call | solution.py:989
  214.5 11.3 %fusion.34 = f32[2,768,1024]{2,1,0:T(8,128)S(1)} fusion(bf16[2,768,2048]{2,1,0:T(8,128)(2,1)S(1)} %unpack_slots.2, bf16[2,2048,1024]{2,1,0:T(8,128)(2,1)} %param.23), kind=kOutput, calls=%fused_computation.85 | convolution fusion | flops 6442450944 | bytes 20971520 | tf_op jit(solution)/shard_map/esd,edf->esf/dot_general | solution.py:1231
  230.7 3.7 convolution_convert_fusion.1.values
  234.4 5.4 pack_slots.2
  242.6 40.1 %all-to-all-done.1 = bf16[128,16,1536]{2,1,0:T(8,128)(2,1)} async-done(((bf16[128,16,1536]{2,1,0:T(8,128)(2,1)}), bf16[128,16,1536]{2,1,0:T(8,128)(2,1)}, u32[]{:S(2)}, u32[]{:S(2)}) %all-to-all-start.1) | async-done | bytes 6291488 | tf_op jit(solution)/shard_map/all_to_all | solution.py:1128
  282.7 10.8 %all-to-all-start.2 = ((bf16[128,16,1536]{2,1,0:T(8,128)(2,1)}), bf16[128,16,1536]{2,1,0:T(8,128)(2,1)}, u32[]{:S(2)}, u32[]{:S(2)}) async-start(bf16[128,16,1536]{2,1,0:T(8,128)(2,1)} %bitcast.111), calls=%async_computation.2 | async-start | bytes 12582912 | tf_op jit(solution)/shard_map/all_to_all | solution.py:1128
  294.3 7.5 %unpack_slots.3 = bf16[2,768,2048]{2,1,0:T(8,128)(2,1)S(1)} custom-call(bf16[2048,1536]{1,0:T(8,128)(2,1)} %bitcast.21.packed), custom_call_target="tpu_custom_call" | custom-call | flops 2415919104 | bytes 14680064 | tf_op jit(solution)/shard_map/unpack_slots/pallas_call | solution.py:989
  301.8 8.8 %multiply_convert_fusion.1 = (bf16[2,768,512]{2,1,0:T(8,128)(2,1)S(1)}, bf16[2,768,512]{2,1,0:T(8,128)(2,1)S(1)}) fusion(f32[2,768,1024]{2,1,0:T(8,128)} %copy-done.17, bf16[2,768,2048]{2,1,0:T(8,128)(2,1)S(1)} %unpack_slots.3, bf16[2,2048,512]{2,1,0:T(8,128)(2,1)S(1)} %copy-done.27), kind=kOutput, calls=%fused_computation.4 | convolution fusion | flops 3231449088 | bytes 19922944 | tf_op jit(solution)/shard_map/esd,edf->esf/dot_general | solution.py:1243
  310.7 11.7 %convolution_convert_fusion.values = bf16[2,768,2048]{2,1,0:T(8,128)(2,1)S(1)} fusion(bf16[2,2048,1024]{2,1,0:T(8,128)(2,1)} %param.23, bf16[2,768,512]{2,1,0:T(8,128)(2,1)S(1)} %get-tuple-element.137, bf16[2,768,512]{2,1,0:T(8,128)(2,1)S(1)} %get-tuple-element.136), kind=kOutput, calls=%fused_computation | convolution fusion | flops 6451888128 | bytes 17825792 | tf_op jit(solution)/shard_map/esf,edf->esd/dot_general | solution.py:1249
  322.4 5.4 pack_slots.3
  330.5 46.2 %all-to-all-done.2 = bf16[128,16,1536]{2,1,0:T(8,128)(2,1)} async-done(((bf16[128,16,1536]{2,1,0:T(8,128)(2,1)}), bf16[128,16,1536]{2,1,0:T(8,128)(2,1)}, u32[]{:S(2)}, u32[]{:S(2)}) %all-to-all-start.2) | async-done | bytes 6291488 | tf_op jit(solution)/shard_map/all_to_all | solution.py:1128
  376.7 9.4 %all-to-all-start.3 = ((bf16[128,16,1536]{2,1,0:T(8,128)(2,1)}), bf16[128,16,1536]{2,1,0:T(8,128)(2,1)}, u32[]{:S(2)}, u32[]{:S(2)}) async-start(bf16[128,16,1536]{2,1,0:T(8,128)(2,1)} %bitcast.110), calls=%async_computation.3 | async-start | bytes 12582912 | tf_op jit(solution)/shard_map/all_to_all | solution.py:1128
  386.1 10.4 %reduce-scatter.2.cloned.1.call-start = ((), (), s32[]{:S(2)}) async-start(), calls=%async_computation.6 | async-start | bytes 2621440 | tf_op jit(solution)/shard_map/reduce_scatter | solution.py:1223
  396.5 4.0 copy.73
  406.0 3.3 convolution_convert_fusion.3
  418.9 10.3 %fusion.35 = f32[2,2048,512]{2,1,0:T(8,128)} fusion(bf16[2,768,2048]{2,1,0:T(8,128)(2,1)} %copy-done.7, bf16[2,768,512]{2,1,0:T(8,128)(2,1)S(1)} %copy-done.21), kind=kOutput, calls=%fused_computation.86 | convolution fusion | flops 3221225472 | bytes 16252928 | tf_op jit(solution)/shard_map/esd,esf->edf/dot_general | solution.py:1254
  429.3 10.4 %fusion.1 = f32[2,2048,1024]{2,1,0:T(8,128)} fusion(bf16[2,768,2048]{2,1,0:T(8,128)(2,1)S(1)} %bitcast.116, bf16[2,768,512]{2,1,0:T(8,128)(2,1)S(1)} %copy-done.31, bf16[2,768,512]{2,1,0:T(8,128)(2,1)S(1)} %copy-done.29), kind=kOutput, calls=%fused_computation.14 | convolution fusion | flops 6448742400 | bytes 26214400 | tf_op jit(solution)/shard_map/esd,esf->edf/dot_general | solution.py:1257
  439.7 10.2 %sum_gated.1 = (f32[128,2048]{1,0:T(8,128)S(1)}, f32[8,128,32]{2,1,0:T(8,128)S(1)}) custom-call(bf16[8,32,128]{2,1,0:T(8,128)(2,1)S(1)} %bitcast.125, bf16[2048,1536]{1,0:T(8,128)(2,1)} %bitcast.23.packed, bf16[2048,1536]{1,0:T(8,128)(2,1)S(1)} %bitcast.109, bf16[8,32,128]{2,1,0:T(8,128)(2,1)S(1)} %bitcast.130, bf16[8,32,128]{2,1,0:T(8,128)(2,1)S(1)} %bitcast.128), custom_call_target="tpu_custom_call" | custom-call | flops 3221225472 | bytes 14680064 | tf_op jit(solution)/shard_map/sum_gated/pallas_call | solution.py:1104
  456.1 4.8 reduce-scatter.2.cloned.1.call-done
  463.3 9.6 %all-to-all-done.3 = bf16[128,16,1536]{2,1,0:T(8,128)(2,1)} async-done(((bf16[128,16,1536]{2,1,0:T(8,128)(2,1)}), bf16[128,16,1536]{2,1,0:T(8,128)(2,1)}, u32[]{:S(2)}, u32[]{:S(2)}) %all-to-all-start.3) | async-done | bytes 6291488 | tf_op jit(solution)/shard_map/all_to_all | solution.py:1128
  472.9 7.7 %sum_tokens.1 = f32[128,2048]{1,0:T(8,128)S(1)} custom-call(bf16[8,32,128]{2,1,0:T(8,128)(2,1)S(1)} %bitcast.126, bf16[2048,1536]{1,0:T(8,128)(2,1)} %bitcast.25.packed), custom_call_target="tpu_custom_call" | custom-call | flops 1610612736 | bytes 8388608 | tf_op jit(solution)/shard_map/sum_tokens/pallas_call | solution.py:1081
  487.0 22.3 %branch_rows.1 = (bf16[4,128,2048]{2,1,0:T(8,128)(2,1)S(1)}, bf16[512,256]{1,0:T(8,128)(2,1)S(1)}, f32[64,256]{1,0:T(8,128)S(1)}, f32[64,128]{1,0:T(8,128)S(1)}) custom-call(bf16[128,2048]{1,0:T(8,128)(2,1)S(1)} %get-tuple-element.134.branch, bf16[4,512,256]{2,1,0:T(8,128)(2,1)S(1)} %bitcast.120, bf16[2,4,4,64,384]{4,3,2,1,0:T(8,128)(2,1)S(1)} %bitcast.117), custom_call_target="tpu_custom_call" | custom-call | bytes 67108864 | tf_op jit(solution)/shard_map/branch_rows/pallas_call | solution.py:686
  511.3 17.3 %attention_back.1 = (bf16[512,2048]{1,0:T(8,128)(2,1)}, bf16[2048,1280]{1,0:T(8,128)(2,1)}) custom-call(bf16[512,2048]{1,0:T(8,128)(2,1)} %bitcast.133, bf16[2048,512]{1,0:T(8,128)(2,1)} %bitcast.136, bf16[2048,1664]{1,0:T(8,128)(2,1)} %bitcast.148, bf16[512,512]{1,0:T(8,128)(2,1)} %get-tuple-element.74.query, bf16[512,128]{1,0:T(8,128)(2,1)} %get-tuple-element.75.keys, ...), custom_call_target="tpu_custom_call" | custom-call | flops 8053063680 | bytes 20971520 | tf_op jit(solution)/shard_map/attention_back/pallas_call | solution.py:428
  528.6 63.7 %finish.1 = (f32[128,2048]{1,0:T(8,128)}, bf16[128,2048]{1,0:T(8,128)(2,1)}, bf16[4,32,16,256]{3,2,1,0:T(8,128)(2,1)}, f32[2,2048]{1,0:T(2,128)}, f32[64,512]{1,...) custom-call(bf16[4,128,2048]{2,1,0:T(8,128)(2,1)} %bitcast.141, bf16[2,4,4,64,1280]{4,3,2,1,0:T(8,128)(2,1)} %bitcast.135, ...), custom_call_target="tpu_custom_call" | custom-call | bytes 209715200 | tf_op jit(solution)/shard_map/finish/pallas_call | solution.py:857
  (127 shorter events, 72.8 us)
Async XLA Ops:
  7.2 113.5 %copy-start = (bf16[2048,256]{1,0:T(8,128)(2,1)S(1)}, bf16[2048,256]{1,0:T(8,128)(2,1)}, u32[]{:S(2)}) copy-start(bf16[2048,256]{1,0:T(8,128)(2,1)} %param.22) | copy-start | bytes 3145732
  73.0 11.4 %copy-start.5 = (bf16[1,128,2048]{2,1,0:T(8,128)(2,1)S(1)}, bf16[1,128,2048]{2,1,0:T(8,128)(2,1)}, u32[]{:S(2)}) copy-start(bf16[1,128,2048]{2,1,0:T(8,128)(2,1)} %param.14) | copy-start | bytes 1572868
  73.0 11.4 %copy-start.14 = (f32[2048]{0:T(1024)S(1)}, f32[2048]{0:T(1024)}, u32[]{:S(2)}) copy-start(f32[2048]{0:T(1024)} %param.19) | copy-start | bytes 24580
  115.2 7.1 %copy-start.9 = (bf16[1,128,2048]{2,1,0:T(8,128)(2,1)S(1)}, bf16[1,128,2048]{2,1,0:T(8,128)(2,1)}, u32[]{:S(2)}) copy-start(bf16[1,128,2048]{2,1,0:T(8,128)(2,1)} %param.27) | copy-start | bytes 1572868
  115.2 81.1 %all-to-all-start = ((bf16[128,16,1536]{2,1,0:T(8,128)(2,1)}), bf16[128,16,1536]{2,1,0:T(8,128)(2,1)}, u32[]{:S(2)}, u32[]{:S(2)}) async-start(bf16[128,16,1536]{2,1,0:T(8,128)(2,1)} %bitcast.112), calls=%async_computation | async-start | bytes 12582912 | tf_op jit(solution)/shard_map/all_to_all | solution.py:1128
  196.3 86.4 %all-to-all-start.1 = ((bf16[128,16,1536]{2,1,0:T(8,128)(2,1)}), bf16[128,16,1536]{2,1,0:T(8,128)(2,1)}, u32[]{:S(2)}, u32[]{:S(2)}) async-start(bf16[128,16,1536]{2,1,0:T(8,128)(2,1)} %bitcast.107), calls=%async_computation.1 | async-start | bytes 12582912 | tf_op jit(solution)/shard_map/all_to_all | solution.py:1128
  214.5 11.3 %copy-start.6 = (bf16[2,768,2048]{2,1,0:T(8,128)(2,1)}, bf16[2,768,2048]{2,1,0:T(8,128)(2,1)S(1)}, u32[]{:S(2)}) copy-start(bf16[2,768,2048]{2,1,0:T(8,128)(2,1)S(1)} %unpack_slots.2) | copy-start | bytes 18874372
  230.7 3.7 copy-start.20
  282.7 94.0 %all-to-all-start.2 = ((bf16[128,16,1536]{2,1,0:T(8,128)(2,1)}), bf16[128,16,1536]{2,1,0:T(8,128)(2,1)}, u32[]{:S(2)}, u32[]{:S(2)}) async-start(bf16[128,16,1536]{2,1,0:T(8,128)(2,1)} %bitcast.111), calls=%async_computation.2 | async-start | bytes 12582912 | tf_op jit(solution)/shard_map/all_to_all | solution.py:1128
  293.5 107.8 %all-gather.2.cloned.1.call-start = ((), (), s32[]{:S(2)}) async-start(), calls=%async_computation.5 | async-start | bytes 2621440 | tf_op jit(solution)/shard_map/all_gather | solution.py:1206
  294.3 7.6 %copy-start.27 = (bf16[2,2048,512]{2,1,0:T(8,128)(2,1)S(1)}, bf16[2,2048,512]{2,1,0:T(8,128)(2,1)}, u32[]{:S(2)}) copy-start(bf16[2,2048,512]{2,1,0:T(8,128)(2,1)} %param.24) | copy-start | bytes 12582916
  301.8 8.8 %copy-start.7 = (bf16[2,768,2048]{2,1,0:T(8,128)(2,1)}, bf16[2,768,2048]{2,1,0:T(8,128)(2,1)S(1)}, u32[]{:S(2)}) copy-start(bf16[2,768,2048]{2,1,0:T(8,128)(2,1)S(1)} %unpack_slots.3) | copy-start | bytes 18874372
  310.7 11.7 %copy-start.28 = (bf16[2,768,512]{2,1,0:T(8,128)(2,1)}, bf16[2,768,512]{2,1,0:T(8,128)(2,1)S(1)}, u32[]{:S(2)}) copy-start(bf16[2,768,512]{2,1,0:T(8,128)(2,1)S(1)} %get-tuple-element.136) | copy-start | bytes 4718596
  310.7 11.7 %copy-start.30 = (bf16[2,768,512]{2,1,0:T(8,128)(2,1)}, bf16[2,768,512]{2,1,0:T(8,128)(2,1)S(1)}, u32[]{:S(2)}) copy-start(bf16[2,768,512]{2,1,0:T(8,128)(2,1)S(1)} %get-tuple-element.137) | copy-start | bytes 4718596
  376.7 96.2 %all-to-all-start.3 = ((bf16[128,16,1536]{2,1,0:T(8,128)(2,1)}), bf16[128,16,1536]{2,1,0:T(8,128)(2,1)}, u32[]{:S(2)}, u32[]{:S(2)}) async-start(bf16[128,16,1536]{2,1,0:T(8,128)(2,1)} %bitcast.110), calls=%async_computation.3 | async-start | bytes 12582912 | tf_op jit(solution)/shard_map/all_to_all | solution.py:1128
  386.1 74.8 %reduce-scatter.2.cloned.1.call-start = ((), (), s32[]{:S(2)}) async-start(), calls=%async_computation.6 | async-start | bytes 2621440 | tf_op jit(solution)/shard_map/reduce_scatter | solution.py:1223
  401.3 2.8 copy-start.19
  414.3 4.6 copy-start.21
  415.6 13.6 %slice-start.2 = ((s8[6291456]{0:T(1024)(128)(4,1)}), s8[4194304]{0:T(1024)(128)(4,1)S(1)}, s32[]{:S(2)}) async-start(s8[6291456]{0:T(1024)(128)(4,1)} %bitcast.115), calls=%async_computation.9 | async-start | bytes 8388608
  418.9 10.4 %slice-start.3 = ((s8[6291456]{0:T(1024)(128)(4,1)}), s8[2097152]{0:T(1024)(128)(4,1)S(1)}, s32[]{:S(2)}) async-start(s8[6291456]{0:T(1024)(128)(4,1)} %bitcast.115), calls=%async_computation.10 | async-start | bytes 4194304
  418.9 10.4 %copy-start.29 = (bf16[2,768,512]{2,1,0:T(8,128)(2,1)S(1)}, bf16[2,768,512]{2,1,0:T(8,128)(2,1)}, u32[]{:S(2)}) copy-start(bf16[2,768,512]{2,1,0:T(8,128)(2,1)} %copy-done.28) | copy-start | bytes 4718596
  418.9 10.4 %copy-start.31 = (bf16[2,768,512]{2,1,0:T(8,128)(2,1)S(1)}, bf16[2,768,512]{2,1,0:T(8,128)(2,1)}, u32[]{:S(2)}) copy-start(bf16[2,768,512]{2,1,0:T(8,128)(2,1)} %copy-done.30) | copy-start | bytes 4718596
  418.9 20.8 %slice-start = ((s8[6291456]{0:T(1024)(128)(4,1)}), s8[4194304]{0:T(1024)(128)(4,1)S(1)}, s32[]{:S(2)}) async-start(s8[6291456]{0:T(1024)(128)(4,1)} %bitcast.108), calls=%async_computation.7 | async-start | bytes 8388608
  429.3 10.5 %slice-start.1 = ((s8[6291456]{0:T(1024)(128)(4,1)}), s8[2097152]{0:T(1024)(128)(4,1)S(1)}, s32[]{:S(2)}) async-start(s8[6291456]{0:T(1024)(128)(4,1)} %bitcast.108), calls=%async_computation.8 | async-start | bytes 4194304
  472.9 7.7 %copy-start.16 = (f32[128,2048]{1,0:T(8,128)S(1)}, f32[128,2048]{1,0:T(8,128)}, u32[]{:S(2)}) copy-start(f32[128,2048]{1,0:T(8,128)} %convolution_add_fusion) | copy-start | bytes 3145732
  484.1 2.9 copy-start.8
  484.1 2.9 copy-start.10
  592.3 6.5 %copy-start.18 = (f32[128,2048]{1,0:T(8,128)S(1)}, f32[128,2048]{1,0:T(8,128)}, u32[]{:S(2)}) copy-start(f32[128,2048]{1,0:T(8,128)} %get-tuple-element.135) | copy-start | bytes 3145732
  592.3 6.5 %copy-start.22 = (f32[128,2048]{1,0:T(8,128)S(1)}, f32[128,2048]{1,0:T(8,128)}, u32[]{:S(2)}) copy-start(f32[128,2048]{1,0:T(8,128)} %get-tuple-element.84) | copy-start | bytes 3145732
  596.0 3.9 copy-start.23
  596.0 4.7 copy-start.25
  596.0 5.3 copy-start.24
  (10 other events, 20.3 us)
Sparse Core Ops, SparseCore 0:
  296.0 39.8 all-gather.1
  409.5 51.3 reduce-scatter.1

commit v5 on v4

v5 whole, which is shorter than its diff:
```python
import functools

import jax
import jax.numpy as jnp
import numpy as np
from jax import lax
from jax.experimental import pallas as pl
from jax.experimental.pallas import tpu as pltpu
from jax.sharding import PartitionSpec as P

epsilon = 1e-06
rope_base = 10000.0
masked_score = -1e30

EXPERT_ROWS = 6
PAIR_ROWS = 12
PACKED_ROWS = 16
BLOCK_PAIRS = 16
BLOCK = BLOCK_PAIRS * PACKED_ROWS
BLOCK_EXPERTS = 2 * BLOCK_PAIRS
BLOCK_SLOTS = BLOCK_PAIRS * EXPERT_ROWS
QUARTER = 512
SIDE = 128
MESH = pl.DeviceIdType.MESH
NDOC = 4


def swish_parts(pre_act):
    logistic = jax.nn.sigmoid(pre_act)
    return (pre_act * logistic, logistic * (1.0 + pre_act * (1.0 - logistic)))


def matmul(matrix, partner):
    return jnp.dot(matrix, partner, preferred_element_type=jnp.float32)


def matmul_t(matrix, partner):
    return lax.dot_general(
        matrix, partner, (((1,), (1,)), ((), ())), preferred_element_type=jnp.float32
    )


def outer_sum(matrix, partner):
    return lax.dot_general(
        matrix, partner, (((0,), (0,)), ((), ())), preferred_element_type=jnp.float32
    )


def split_low(values):
    high = values.astype(jnp.bfloat16)
    return high, (values - high.astype(jnp.float32)).astype(jnp.bfloat16)


def row_places():
    row, col = lax.axis_index("row"), lax.axis_index("col")
    chip, core = row // 2, lax.rem(row, 2)
    sibling = chip * 2 + (1 - core)
    partner = (1 - chip) * 2 + core
    across = (1 - chip) * 2 + (1 - core)
    return row, col, sibling, partner, across


def row_copies(sources, targets, send_sem, recv_sem):
    row, col, sibling, partner, _ = row_places()

    def send(origin, target, peer, i):
        return pltpu.make_async_remote_copy(
            src_ref=origin,
            dst_ref=target,
            send_sem=send_sem.at[i],
            recv_sem=recv_sem.at[i],
            device_id=(peer, col),
            device_id_type=MESH,
        )

    far, near, onward = [], [], []
    for i, (source, target) in enumerate(zip(sources, targets)):
        far.append(send(source, target.at[row], partner, 3 * i))
        near.append(send(source, target.at[row], sibling, 3 * i + 1))
        onward.append(send(target.at[partner], target.at[partner], sibling, 3 * i + 2))
    return far, near, onward


def greet(peers):
    barrier = pltpu.get_barrier_semaphore()
    for peer in peers:
        pl.semaphore_signal(barrier, inc=1, device_id=peer, device_id_type=MESH)


def await_greetings(count):
    pl.semaphore_wait(pltpu.get_barrier_semaphore(), count)


def turn(values, cosine, sine):
    return values * cosine + pltpu.roll(values, 64, 1) * sine


def score_bias(begin):
    shape = (begin.shape[0], begin.shape[0])
    keys = lax.broadcasted_iota(jnp.int32, shape, 1)
    allowed = (keys >= begin) & (keys <= lax.broadcasted_iota(jnp.int32, shape, 0))
    return jnp.where(allowed, 0.0, masked_score)


def attention_back_queries(query, keys, values, back, norms, cosine, sine, begin, refs):
    pre_grad, bias, deltas = refs
    size = keys.shape[1]
    bias[...] = score_bias(begin[...])
    scale = size ** (-0.5)
    lanes = lax.broadcasted_iota(jnp.int32, deltas.shape, 1)
    all_deltas = jnp.zeros(deltas.shape, jnp.float32)
    for head in range(query.shape[1] // size):
        columns = slice(head * size, (head + 1) * size)
        turned, outer = query[:, columns], back[:, columns]
        scores = matmul_t(turned, keys[...]) * scale + bias[...]
        probs = jnp.exp(scores - norms[:, head : head + 1])
        prob_grad = matmul_t(outer, values[...])
        delta = jnp.sum(probs * prob_grad, axis=1, keepdims=True)
        all_deltas = jnp.where(lanes == head, delta, all_deltas)
        score_grad = (probs * (prob_grad - delta)).astype(jnp.bfloat16)
        query_grad = matmul(score_grad, keys[...]) * scale
        pre_grad[:, columns] = turn(query_grad, cosine[...], -sine[...]).astype(jnp.bfloat16)
    deltas[...] = all_deltas


def attention_back_keys(query, keys, values, back, norms, cosine, sine, begin_row, refs):
    pre_grad, bias, deltas = refs
    low = jnp.bfloat16
    size = keys.shape[1]
    inner = query.shape[1]
    scale = size ** (-0.5)
    deltas_t = jnp.transpose(deltas[...])
    norms_t = jnp.transpose(norms[...])
    shape = bias.shape
    key_places = lax.broadcasted_iota(jnp.int32, shape, 0)
    allowed = (key_places >= begin_row[...]) & (
        key_places <= lax.broadcasted_iota(jnp.int32, shape, 1)
    )
    bias[...] = jnp.where(allowed, 0.0, masked_score)
    key_grad = jnp.zeros(keys.shape, jnp.float32)
    value_grad = jnp.zeros(values.shape, jnp.float32)
    for head in range(inner // size):
        columns = slice(head * size, (head + 1) * size)
        turned, outer = query[:, columns], back[:, columns]
        scores = matmul_t(keys[...], turned) * scale + bias[...]
        probs = jnp.exp(scores - norms_t[head : head + 1])
        prob_grad = matmul_t(values[...], outer)
        score_grad = (probs * (prob_grad - deltas_t[head : head + 1])).astype(low)
        key_grad = key_grad + matmul(score_grad, turned)
        value_grad = value_grad + matmul(probs.astype(low), outer)
    pre_grad[:, inner : inner + size] = turn(key_grad * scale, cosine[...], -sine[...]).astype(low)
    pre_grad[:, inner + size :] = value_grad.astype(low)


def remote(source, target, sems, at, peer):
    return pltpu.make_async_remote_copy(
        src_ref=source,
        dst_ref=target,
        send_sem=sems[0].at[at],
        recv_sem=sems[1].at[at],
        device_id=peer,
        device_id_type=MESH,
    )


def row_sum_copies(parts, near, far, outgoing, sems, at):
    _, col, sibling, partner, across = row_places()
    return [
        remote(parts.at[across], near.at[0], sems, at, (sibling, col)),
        remote(parts.at[sibling], near.at[1], sems, at + 1, (sibling, col)),
        remote(outgoing, far, sems, at + 2, (partner, col)),
    ]


def row_sum_forward(parts, near, outgoing, copies):
    _, _, _, partner, _ = row_places()
    copies[0].wait_recv()
    outgoing[...] = (parts[partner].astype(jnp.float32) + near[0].astype(jnp.float32)).astype(
        jnp.bfloat16
    )
    copies[2].start()


def row_sum_total(parts, near, far, copies):
    row = row_places()[0]
    copies[1].wait_recv()
    total = parts[row].astype(jnp.float32) + near[1].astype(jnp.float32)
    copies[2].wait_recv()
    return total + far[...].astype(jnp.float32)


class ScatterSum:
    def __init__(self, grads, scratch):
        self.grads = grads
        self.first, self.first_sum, self.second, self.second_sum, self.third = scratch[:5]
        self.one, self.two, self.three = scratch[5:7], scratch[7:9], scratch[9:11]
        row, col = lax.axis_index("row"), lax.axis_index("col")
        x, z, y = col // 16, lax.rem(col // 4, 4), lax.rem(col, 4)
        self.place = (x, z, y)
        self.half_rows = grads.shape[3] // 2
        self.y_peers = [(row, x * 16 + z * 4 + lax.rem(y + i, 4)) for i in (1, 2, 3)]
        self.z_peers = [(row, x * 16 + lax.rem(z + i, 4) * 4 + y) for i in (1, 2, 3)]
        self.x_peer = (row, (1 - x) * 16 + z * 4 + y)
        self.one_copies, self.two_copies, self.three_copies = {}, {}, []

    @staticmethod
    def scratch(grads):
        half_rows, depth = grads.shape[3] // 2, grads.shape[4]
        low = jnp.bfloat16
        return [
            pltpu.VMEM((2, 2, 3, 4, half_rows, depth), low),
            pltpu.VMEM((2, 2, 4, half_rows, depth), low),
            pltpu.VMEM((2, 2, 3, half_rows, depth), low),
            pltpu.VMEM((2, half_rows, depth), low),
            pltpu.VMEM((2, half_rows, depth), low),
        ] + [pltpu.SemaphoreType.DMA((count,)) for count in (12, 12, 12, 12, 2, 2)]

    def half(self, half):
        return pl.ds(half * self.half_rows, self.half_rows)

    def start(self):
        x, z, y = self.place
        for turn, owner_x in enumerate((1 - x, x)):
            for i in range(3):
                for half in range(2):
                    if half == 0:
                        source = self.grads.at[owner_x, :, lax.rem(y + i + 1, 4), self.half(0)]
                    else:
                        source = self.grads.at[owner_x, lax.rem(z + i + 1, 4), :, self.half(1)]
                    at = (turn * 2 + half) * 3 + i
                    peer = (self.y_peers, self.z_peers)[half][i]
                    copy = remote(source, self.first.at[turn, half, i], self.one, at, peer)
                    self.one_copies[turn, half, i] = copy
                    copy.start()

    def add_first(self, turn):
        x, z, y = self.place
        owner_x = (1 - x, x)[turn]
        for half in range(2):
            for i in range(3):
                self.one_copies[turn, half, i].wait_recv()

            def add(k, carry, half=half):
                if half == 0:
                    total = self.grads[owner_x, k, y, self.half(0)].astype(jnp.float32)
                else:
                    total = self.grads[owner_x, z, k, self.half(1)].astype(jnp.float32)
                for i in range(3):
                    total = total + self.first[turn, half, i, k].astype(jnp.float32)
                self.first_sum[turn, half, k] = total.astype(jnp.bfloat16)
                return carry

            lax.fori_loop(0, 4, add, 0)
            for i in range(3):
                away = lax.rem((z, y)[half] + i + 1, 4)
                copy = remote(
                    self.first_sum.at[turn, half, away],
                    self.second.at[turn, half, i],
                    self.two,
                    (turn * 2 + half) * 3 + i,
                    (self.z_peers, self.y_peers)[half][i],
                )
                self.two_copies[turn, half, i] = copy
                copy.start()

    def second_total(self, turn, half):
        _, z, y = self.place
        for i in range(3):
            self.two_copies[turn, half, i].wait_recv()
        total = self.first_sum[turn, half, (z, y)[half]].astype(jnp.float32)
        for i in range(3):
            total = total + self.second[turn, half, i].astype(jnp.float32)
        return total

    def add_second(self):
        for half in range(2):
            self.second_sum[half] = self.second_total(0, half).astype(jnp.bfloat16)
            copy = remote(
                self.second_sum.at[half], self.third.at[half], self.three, half, self.x_peer
            )
            self.three_copies.append(copy)
            copy.start()

    def add_third(self, pieces):
        for half in range(2):
            total = self.second_total(1, half)
            self.three_copies[half].wait_recv()
            total = total + self.third[half].astype(jnp.float32)
            start = 0
            for piece in pieces:
                piece[self.half(half)] = total[:, start : start + piece.shape[1]]
                start += piece.shape[1]

    def end(self):
        for copy in [*self.one_copies.values(), *self.two_copies.values(), *self.three_copies]:
            copy.wait_send()


def token_back_kernel(
    packed,
    marks,
    router_input,
    hidden,
    scale,
    gain,
    stream_grad,
    router,
    grads,
    group,
    hidden_total,
    gain_grad,
    router_sum,
    *refs,
):
    pieces, scratch = refs[:2], refs[2:]
    held, routed, branch, near, far, outgoing, load_sem, send, recv, own_sem = scratch[:10]
    row_send, row_recv = scratch[10:12]
    row, col, sibling, partner, _ = row_places()
    scatter = ScatterSum(grads, scratch[12:])
    greet([(sibling, col), (partner, col)])
    greet(scatter.y_peers + scatter.z_peers + [scatter.x_peer])
    steps = held.shape[0]
    depth = held.shape[1]
    loads = [
        pltpu.make_async_copy(packed.at[pl.ds(i * depth, depth)], held.at[i], load_sem.at[i])
        for i in range(steps)
    ]
    for load in loads:
        load.start()
    await_greetings(9)
    copies = row_sum_copies(router, near, far, outgoing, (row_send, row_recv), 0)
    copies[0].start()
    copies[1].start()
    scatter.start()
    row_sum_forward(router, near, outgoing, copies)

    for i in range(steps):
        loads[i].wait()
        rows = slice(i * depth, (i + 1) * depth)
        for part in range(4):
            columns = slice(part * QUARTER, (part + 1) * QUARTER)
            if part < 3:
                found = matmul(marks[0, :, rows], held[i, :, columns])
            else:
                found = matmul(marks[1, :, rows], held[i, :, :QUARTER])
                for j in (1, 2):
                    second = slice(j * QUARTER, (j + 1) * QUARTER)
                    found = found + matmul(marks[j + 1, :, rows], held[i, :, second])
            routed[:, columns] = found if i == 0 else routed[:, columns] + found

    incoming = router_input[...] + routed[...]
    values = hidden[...]
    factor = scale[...]
    weighted = gain[...] * incoming
    mean = jnp.mean(weighted * values, axis=1, keepdims=True)
    total = (
        stream_grad[...].astype(jnp.float32)
        + factor * weighted
        - values * (factor * factor * factor * mean)
    )
    hidden_total[...] = total
    branch[...] = total.astype(jnp.bfloat16)
    far_rows, near_rows, onward = row_copies([branch], [group], send, recv)
    far_rows[0].start()
    near_rows[0].start()
    own = pltpu.make_async_copy(branch, group.at[row], own_sem)
    own.start()
    gain_grad[...] = jnp.sum(incoming * values * factor, axis=0, keepdims=True)
    scatter.add_first(0)
    scatter.add_first(1)
    scatter.add_second()
    router_sum[...] = row_sum_total(router, near, far, copies).astype(jnp.bfloat16)
    far_rows[0].wait_recv()
    onward[0].start()
    scatter.add_third(pieces)
    own.wait()
    far_rows[0].wait_send()
    near_rows[0].wait()
    onward[0].wait()
    for copy in copies:
        copy.wait_send()
    scatter.end()


def token_back(packed, marks, router_input, hidden, scale, gain, stream_grad, router, grads, widths):
    away = pl.BlockSpec(memory_space=pl.ANY)
    space = pl.BlockSpec(memory_space=pltpu.VMEM)
    _, rows, width = router.shape
    tokens, model_width = hidden.shape
    low = jnp.bfloat16
    group, hidden_total, gain_grad, router_sum, *sums = pl.pallas_call(
        token_back_kernel,
        out_shape=[
            jax.ShapeDtypeStruct((4, tokens, model_width), low),
            jax.ShapeDtypeStruct((tokens, model_width), jnp.float32),
            jax.ShapeDtypeStruct((1, model_width), jnp.float32),
            jax.ShapeDtypeStruct((rows, width), low),
        ]
        + [jax.ShapeDtypeStruct((grads.shape[3], part), jnp.float32) for part in widths],
        in_specs=[away] + [space] * 8,
        out_specs=[away] + [space] * (3 + len(widths)),
        scratch_shapes=[
            pltpu.VMEM((4, packed.shape[0] // 4, packed.shape[1]), low),
            pltpu.VMEM((tokens, model_width), jnp.float32),
            pltpu.VMEM((tokens, model_width), low),
            pltpu.VMEM((2, rows, width), low),
            pltpu.VMEM((rows, width), low),
            pltpu.VMEM((rows, width), low),
            pltpu.SemaphoreType.DMA((4,)),
            pltpu.SemaphoreType.DMA((3,)),
            pltpu.SemaphoreType.DMA((3,)),
            pltpu.SemaphoreType.DMA,
            pltpu.SemaphoreType.DMA((3,)),
            pltpu.SemaphoreType.DMA((3,)),
            *ScatterSum.scratch(grads),
        ],
        compiler_params=pltpu.CompilerParams(
            collective_id=1, has_side_effects=True, vmem_limit_bytes=48 << 20
        ),
        cost_estimate=pl.CostEstimate(flops=0, bytes_accessed=100 << 20, transcendentals=0),
        name="token_back",
    )(packed, marks, router_input, hidden, scale, gain, stream_grad, router, grads)
    return group.reshape(-1, model_width), hidden_total, gain_grad, router_sum, sums


def finish_kernel(
    group_branch,
    group_one_t,
    full_pre,
    full_back,
    query,
    keys,
    values_in,
    attended,
    norms,
    cosine,
    sine,
    begin,
    begin_row,
    shared_parts,
    router_part,
    stream,
    inputs,
    scale,
    gain,
    gain_ffn,
    result,
    block_out,
    router,
    gains,
    *refs,
):
    pieces, scratch = refs[:3], refs[3:]
    near, far, outgoing, values, buffers, router_in, router_own = scratch[:7]
    row_send, row_recv, gain_send, gain_recv, own_sem = scratch[7:12]
    col_send, col_recv, pass_send, pass_recv = scratch[12:16]
    branch, rows_t, w_pre, w_back, pre_grad, back, bias, deltas, parts, load_sem = scratch[16:26]
    pre_grads, out_grads = scratch[26:28]
    pre_scatter = ScatterSum(pre_grads, scratch[28:39])
    out_scatter = ScatterSum(out_grads, scratch[39:])
    row, col, sibling, partner, across = row_places()
    row_peers = [(peer, col) for peer in (sibling, partner, across)]

    greet(row_peers)
    barrier = pltpu.get_barrier_semaphore()

    def greet_col(step, carry):
        peer = (row, lax.rem(col + step, 32))
        pl.semaphore_signal(barrier, inc=1, device_id=peer, device_id_type=MESH)
        return carry

    lax.fori_loop(1, 32, greet_col, 0)
    pre_width, inner = w_pre.shape[1], w_back.shape[1]
    loads = [
        pltpu.make_async_copy(group_branch, branch, load_sem.at[0]),
        pltpu.make_async_copy(full_back.at[:, pl.ds(0, inner)], w_back, load_sem.at[1]),
        pltpu.make_async_copy(group_one_t, rows_t, load_sem.at[2]),
        pltpu.make_async_copy(full_pre, w_pre, load_sem.at[3]),
    ]
    for load in loads:
        load.start()
    loads[0].wait()
    blocks, depth = 4, branch.shape[1] // 4

    def keep(target, block, rows):
        target[block // 2, 2 * (block % 2) : 2 * (block % 2) + 2] = rows.astype(
            jnp.bfloat16
        ).reshape(2, 4, 64, rows.shape[1])

    for block in range(blocks):
        columns = slice(block * depth, (block + 1) * depth)
        keep(out_grads, block, outer_sum(branch[:, columns], attended[...]))
    loads[1].wait()
    back[...] = matmul(branch[...], w_back[...]).astype(jnp.bfloat16)
    await_greetings(34)
    shared_copies = row_sum_copies(
        shared_parts, near.at[1], far.at[1], outgoing.at[1], (row_send, row_recv), 3
    )
    shared_copies[0].start()
    shared_copies[1].start()

    def push(source, target, at):
        def step(i, carry):
            peer = lax.rem(col + i, 32)
            pltpu.make_async_remote_copy(
                src_ref=source(peer),
                dst_ref=target,
                send_sem=col_send.at[at],
                recv_sem=col_recv.at[at],
                device_id=(row, peer),
                device_id_type=MESH,
            ).start()
            return carry

        lax.fori_loop(1, 32, step, 0)

    def await_pushes(target, sem):
        others = target.at[pl.ds(0, 31)]
        pltpu.make_async_copy(others, others, sem).wait()

    push(lambda peer: router_part.at[peer], router_in.at[col], 0)
    router_in[col] = router_part[col]
    out_scatter.start()
    row_sum_forward(shared_parts, near.at[1], outgoing.at[1], shared_copies)
    saved = (query, keys, values_in, back, norms, cosine, sine)
    attention_back_queries(*saved, begin, (pre_grad, bias, deltas))
    await_pushes(router_in, col_recv.at[0])
    router_own[...] = jnp.sum(router_in[...].astype(jnp.float32), axis=0).astype(jnp.bfloat16)
    push(lambda peer: router_own, router.at[row, col], 1)
    own = pltpu.make_async_copy(router_own, router.at[row, col], own_sem)
    own.start()
    out_scatter.add_first(0)
    attention_back_keys(*saved, begin_row, (pre_grad, bias, deltas))
    loads[3].wait()
    parts[...] = matmul_t(pre_grad[...], w_pre[...]).astype(jnp.bfloat16).reshape(parts.shape)
    attn_copies = row_sum_copies(
        parts, near.at[0], far.at[0], outgoing.at[0], (row_send, row_recv), 0
    )
    attn_copies[0].start()
    attn_copies[1].start()
    out_scatter.add_first(1)
    row_sum_forward(parts, near.at[0], outgoing.at[0], attn_copies)
    loads[2].wait()
    for block in range(blocks):
        rows = slice(block * depth, (block + 1) * depth)
        keep(pre_grads, block, matmul(rows_t[rows], pre_grad[...]))
    pre_scatter.start()
    own.wait()
    await_pushes(router.at[row], col_recv.at[1])
    far_rows, near_rows, onward = row_copies([router.at[row]], [router], pass_send, pass_recv)
    far_rows[0].start()
    near_rows[0].start()
    out_scatter.add_second()

    incoming = row_sum_total(parts, near.at[0], far.at[0], attn_copies)
    rows = inputs[...].astype(jnp.float32)
    factor = scale[...]
    weighted = gain[...] * incoming
    mean = jnp.mean(weighted * rows, axis=1, keepdims=True)
    result[...] = factor * weighted - rows * (factor * factor * factor * mean)
    values[0, 0:1] = jnp.sum(incoming * rows * factor, axis=0, keepdims=True)
    values[0, 1:2] = gain_ffn[...]

    gain_sems = (gain_send, gain_recv)
    gain_copies = []
    stages = (row_peers, pre_scatter.y_peers, pre_scatter.z_peers, [pre_scatter.x_peer])

    def start_gains(stage):
        at = 3 * stage
        for i, peer in enumerate(stages[stage]):
            gain_copies.append(
                remote(values.at[stage], buffers.at[at + i], gain_sems, at + i, peer)
            )
            gain_copies[-1].start()

    def add_gains(stage):
        at = 3 * stage
        total = values[stage]
        for i in range(len(stages[stage])):
            gain_copies[at + i].wait_recv()
            total = total + buffers[at + i]
        values[stage + 1] = total

    start_gains(0)
    shared = row_sum_total(shared_parts, near.at[1], far.at[1], shared_copies)
    block_out[...] = (stream[...] + shared).astype(jnp.bfloat16)
    out_scatter.add_third(pieces[2:])
    add_gains(0)
    start_gains(1)
    pre_scatter.add_first(0)
    add_gains(1)
    start_gains(2)
    pre_scatter.add_first(1)
    far_rows[0].wait_recv()
    onward[0].start()
    add_gains(2)
    start_gains(3)
    pre_scatter.add_second()
    add_gains(3)
    gains[...] = values[4]
    pre_scatter.add_third(pieces[:2])
    await_pushes(router_in, col_send.at[0])
    await_pushes(router.at[row], col_send.at[1])
    far_rows[0].wait_send()
    near_rows[0].wait()
    onward[0].wait()
    for done in [*attn_copies, *shared_copies, *gain_copies]:
        done.wait_send()
    pre_scatter.end()
    out_scatter.end()


def finish(group_branch, group_one_t, weights, kept, tables, rest, widths):
    space = pl.BlockSpec(memory_space=pltpu.VMEM)
    away = pl.BlockSpec(memory_space=pl.ANY)
    low = jnp.bfloat16
    shared_parts, router_part, stream, inputs = rest[:4]
    rows, width = inputs.shape
    tokens = 4 * rows
    share = router_part.shape[1:]
    inner = kept[0].shape[1]
    pre_width = widths[0] + widths[1]
    shard = width // 32
    pre_grads = jax.ShapeDtypeStruct((2, 4, 4, shard, pre_width), low)
    out_grads = jax.ShapeDtypeStruct((2, 4, 4, shard, inner), low)
    return pl.pallas_call(
        finish_kernel,
        out_shape=[
            jax.ShapeDtypeStruct((rows, width), jnp.float32),
            jax.ShapeDtypeStruct((rows, width), low),
            jax.ShapeDtypeStruct((4, 32, *share), low),
            jax.ShapeDtypeStruct((2, width), jnp.float32),
        ]
        + [jax.ShapeDtypeStruct((shard, part), jnp.float32) for part in widths],
        in_specs=[away] * 4 + [space] * 16,
        out_specs=[space, space, away, space] + [space] * len(widths),
        scratch_shapes=[
            pltpu.VMEM((2, 2, rows, width), low),
            pltpu.VMEM((2, rows, width), low),
            pltpu.VMEM((2, rows, width), low),
            pltpu.VMEM((5, 2, width), jnp.float32),
            pltpu.VMEM((10, 2, width), jnp.float32),
            pltpu.VMEM((32, *share), low),
            pltpu.VMEM(share, low),
            pltpu.SemaphoreType.DMA((6,)),
            pltpu.SemaphoreType.DMA((6,)),
            pltpu.SemaphoreType.DMA((10,)),
            pltpu.SemaphoreType.DMA((10,)),
            pltpu.SemaphoreType.DMA,
            pltpu.SemaphoreType.DMA((2,)),
            pltpu.SemaphoreType.DMA((2,)),
            pltpu.SemaphoreType.DMA((3,)),
            pltpu.SemaphoreType.DMA((3,)),
            pltpu.VMEM((tokens, width), low),
            pltpu.VMEM((width, tokens), low),
            pltpu.VMEM((width, pre_width), low),
            pltpu.VMEM((width, inner), low),
            pltpu.VMEM((tokens, pre_width), low),
            pltpu.VMEM((tokens, inner), low),
            pltpu.VMEM((tokens, tokens), jnp.float32),
            pltpu.VMEM((tokens, 128), jnp.float32),
            pltpu.VMEM((4, rows, width), low),
            pltpu.SemaphoreType.DMA((4,)),
            pltpu.VMEM(pre_grads.shape, low),
            pltpu.VMEM(out_grads.shape, low),
            *ScatterSum.scratch(pre_grads),
            *ScatterSum.scratch(out_grads),
        ],
        compiler_params=pltpu.CompilerParams(
            collective_id=16, has_side_effects=True, vmem_limit_bytes=60 << 20
        ),
        cost_estimate=pl.CostEstimate(flops=0, bytes_accessed=200 << 20, transcendentals=0),
        name="finish",
    )(group_branch, group_one_t, *weights, *kept, *tables, *rest)


def packed_places(shape, axis):
    index = lax.broadcasted_iota(jnp.int32, shape, axis)
    pair, place = index // PACKED_ROWS, lax.rem(index, PACKED_ROWS)
    found = []
    for part in range(-1, 3):
        if part < 0:
            valid, slot = place < PAIR_ROWS, place
        else:
            valid, slot = place >= PAIR_ROWS, 3 * (place - PAIR_ROWS) + part
        second = (slot >= EXPERT_ROWS).astype(jnp.int32)
        found.append((valid, pair, second, slot - EXPERT_ROWS * second))
    return found


def token_marks(code_block):
    marks = []
    wide = (BLOCK, BLOCK_EXPERTS)
    lanes = lax.broadcasted_iota(jnp.int32, wide, 1)
    for (valid, pair, second, _), (tall, _, _, order) in zip(
        packed_places(wide, 0), packed_places((BLOCK, SIDE), 0)
    ):
        owner = ((lanes == 2 * pair + second) & valid).astype(jnp.float32).astype(jnp.bfloat16)
        found = matmul(owner, code_block)
        hit = (found == order.astype(jnp.float32)) & tall
        marks.append((owner, hit.astype(jnp.float32)))
    return marks


def gate_weights_of(owner, hit, high, low):
    weights = hit * (matmul(owner, high) + matmul(owner, low))
    return split_low(weights)


def pack_tokens_kernel(code, values, high, low, packed):
    marks = token_marks(code[0])
    weights = [gate_weights_of(owner, hit, high[0], low[0]) for owner, hit in marks]
    last = values[:, 3 * QUARTER :]
    for part in range(3):
        columns = slice(part * QUARTER, (part + 1) * QUARTER)
        both = jnp.concatenate([*weights[0], *weights[part + 1]], axis=1)
        rows = jnp.concatenate([values[:, columns]] * 2 + [last] * 2, axis=0)
        packed[:, columns] = matmul(both, rows).astype(jnp.bfloat16)


def pack_tokens(code, values, gates):
    blocks = code.shape[0]
    width = 3 * QUARTER
    small = pl.BlockSpec((1, BLOCK_EXPERTS, SIDE), lambda i: (i, 0, 0))
    return pl.pallas_call(
        pack_tokens_kernel,
        grid=(blocks,),
        out_shape=jax.ShapeDtypeStruct((blocks * BLOCK, width), jnp.bfloat16),
        in_specs=[small, pl.BlockSpec(values.shape, lambda i: (0, 0)), small, small],
        out_specs=pl.BlockSpec((BLOCK, width), lambda i: (i, 0)),
        compiler_params=pltpu.CompilerParams(vmem_limit_bytes=32 << 20),
        cost_estimate=pl.CostEstimate(
            flops=blocks * BLOCK * 512 * width * 2, bytes_accessed=8 << 20, transcendentals=0
        ),
        name="pack_tokens",
    )(code, values, *gates)


def slot_marks():
    shape = (2 * BLOCK_SLOTS, BLOCK)
    rows = lax.broadcasted_iota(jnp.int32, shape, 0)
    marks = []
    for valid, pair, second, order in packed_places(shape, 1):
        hit = (rows == second * BLOCK_SLOTS + pair * EXPERT_ROWS + order) & valid
        marks.append(hit.astype(jnp.float32).astype(jnp.bfloat16))
    return marks


def unpack_slots_kernel(packed, values):
    marks = slot_marks()
    last = jnp.zeros((2 * BLOCK_SLOTS, QUARTER), jnp.float32)
    for part in range(3):
        columns = slice(part * QUARTER, (part + 1) * QUARTER)
        found = matmul(marks[0], packed[:, columns]).astype(jnp.bfloat16)
        values[0, :, columns] = found[:BLOCK_SLOTS]
        values[1, :, columns] = found[BLOCK_SLOTS:]
        last = last + matmul(marks[part + 1], packed[:, columns])
    last = last.astype(jnp.bfloat16)
    values[0, :, 3 * QUARTER :] = last[:BLOCK_SLOTS]
    values[1, :, 3 * QUARTER :] = last[BLOCK_SLOTS:]


def unpack_slots(packed):
    blocks = packed.shape[0] // BLOCK
    slots = blocks * BLOCK_SLOTS
    return pl.pallas_call(
        unpack_slots_kernel,
        grid=(blocks,),
        out_shape=jax.ShapeDtypeStruct((2, slots, 4 * QUARTER), jnp.bfloat16),
        in_specs=[pl.BlockSpec((BLOCK, 3 * QUARTER), lambda i: (i, 0))],
        out_specs=pl.BlockSpec((2, BLOCK_SLOTS, 4 * QUARTER), lambda i: (0, i, 0)),
        compiler_params=pltpu.CompilerParams(vmem_limit_bytes=32 << 20),
        cost_estimate=pl.CostEstimate(
            flops=blocks * 2 * BLOCK_SLOTS * BLOCK * 6 * QUARTER * 2,
            bytes_accessed=14 << 20,
            transcendentals=0,
        ),
        name="unpack_slots",
    )(packed)


def pack_slots_kernel(values, packed):
    marks = slot_marks()
    last = jnp.concatenate([values[0, :, 3 * QUARTER :], values[1, :, 3 * QUARTER :]], axis=0)
    for part in range(3):
        columns = slice(part * QUARTER, (part + 1) * QUARTER)
        rows = jnp.concatenate([values[0, :, columns], values[1, :, columns]], axis=0)
        found = outer_sum(marks[0], rows) + outer_sum(marks[part + 1], last)
        packed[:, columns] = found.astype(jnp.bfloat16)


def pack_slots(values):
    slots = values.shape[1]
    blocks = slots // BLOCK_SLOTS
    return pl.pallas_call(
        pack_slots_kernel,
        grid=(blocks,),
        out_shape=jax.ShapeDtypeStruct((blocks * BLOCK, 3 * QUARTER), jnp.bfloat16),
        in_specs=[pl.BlockSpec((2, BLOCK_SLOTS, 4 * QUARTER), lambda i: (0, i, 0))],
        out_specs=pl.BlockSpec((BLOCK, 3 * QUARTER), lambda i: (i, 0)),
        compiler_params=pltpu.CompilerParams(vmem_limit_bytes=32 << 20),
        cost_estimate=pl.CostEstimate(
            flops=blocks * 2 * BLOCK_SLOTS * BLOCK * 6 * QUARTER * 2,
            bytes_accessed=14 << 20,
            transcendentals=0,
        ),
        name="pack_slots",
    )(values)


def marks_kernel(code, marks):
    wide = (BLOCK_EXPERTS, BLOCK)
    owners = lax.broadcasted_iota(jnp.int32, wide, 0)
    for i, ((valid, pair, second, _), (tall, _, _, order)) in enumerate(
        zip(packed_places(wide, 1), packed_places((code.shape[1], BLOCK), 1))
    ):
        owner = ((owners == 2 * pair + second) & valid).astype(jnp.float32).astype(jnp.bfloat16)
        hit = (matmul(code[0], owner) == order.astype(jnp.float32)) & tall
        marks[i] = hit.astype(jnp.float32).astype(jnp.bfloat16)


def all_marks(code):
    blocks, experts, tokens = code.shape
    return pl.pallas_call(
        marks_kernel,
        grid=(blocks,),
        out_shape=jax.ShapeDtypeStruct((4, tokens, blocks * BLOCK), jnp.bfloat16),
        in_specs=[pl.BlockSpec((1, tokens, experts), lambda i: (i, 0, 0))],
        out_specs=pl.BlockSpec((4, tokens, BLOCK), lambda i: (0, 0, i)),
        cost_estimate=pl.CostEstimate(flops=1 << 26, bytes_accessed=4 << 20, transcendentals=0),
        name="all_marks",
    )(code.transpose(0, 2, 1))


def sum_gated_kernel(code, packed, grads, high, low, total, gate_grads):
    @pl.when(pl.program_id(0) == 0)
    def _():
        total[...] = jnp.zeros_like(total)

    marks = token_marks(code[0])
    weights = [gate_weights_of(owner, hit, high[0], low[0]) for owner, hit in marks]
    last = jnp.zeros((total.shape[0], QUARTER), jnp.float32)
    whole = jnp.zeros((BLOCK, 1), jnp.float32)
    products = []
    for part in range(3):
        columns = slice(part * QUARTER, (part + 1) * QUARTER)
        rows = packed[:, columns]
        total[:, columns] += outer_sum(weights[0][0], rows) + outer_sum(weights[0][1], rows)
        last = last + outer_sum(weights[part + 1][0], rows) + outer_sum(weights[part + 1][1], rows)
        dots = jnp.sum(
            rows.astype(jnp.float32) * grads[:, columns].astype(jnp.float32),
            axis=1,
            keepdims=True,
        )
        whole = whole + dots
        products.append(dots)
    total[:, 3 * QUARTER :] += last
    found = jnp.zeros(gate_grads.shape[1:], jnp.float32)
    for (owner, hit), dots in zip(marks, [whole, *products]):
        hit = hit.astype(jnp.bfloat16)
        for spread in split_low(dots * owner.astype(jnp.float32)):
            found = found + outer_sum(hit, spread)
    gate_grads[0] = found


def sum_gated(code, packed, grads, gates):
    blocks, _, tokens = code.shape
    small = pl.BlockSpec((1, BLOCK_EXPERTS, tokens), lambda i: (i, 0, 0))
    wide = pl.BlockSpec((BLOCK, 3 * QUARTER), lambda i: (i, 0))
    return pl.pallas_call(
        sum_gated_kernel,
        grid=(blocks,),
        out_shape=[
            jax.ShapeDtypeStruct((tokens, 4 * QUARTER), jnp.float32),
            jax.ShapeDtypeStruct((blocks, tokens, BLOCK_EXPERTS), jnp.float32),
        ],
        in_specs=[small, wide, wide, small, small],
        out_specs=[
            pl.BlockSpec((tokens, 4 * QUARTER), lambda i: (0, 0)),
            pl.BlockSpec((1, tokens, BLOCK_EXPERTS), lambda i: (i, 0, 0)),
        ],
        compiler_params=pltpu.CompilerParams(vmem_limit_bytes=32 << 20),
        cost_estimate=pl.CostEstimate(
            flops=blocks * BLOCK * 128 * 12 * QUARTER * 2,
            bytes_accessed=14 << 20,
            transcendentals=0,
        ),
        name="sum_gated",
    )(code, packed, grads, *gates)


class Gather:
    def __init__(self, mine, full, send_sem, recv_sem):
        self.mine, self.full = mine, full
        self.send_sem, self.recv_sem = send_sem, recv_sem
        self.row, self.col = lax.axis_index("row"), lax.axis_index("col")
        self.x, self.z, self.y = self.col // 16, lax.rem(self.col // 4, 4), lax.rem(self.col, 4)
        self.z_near = [lax.rem(self.z + i, 4) for i in (1, 3, 2)]
        self.y_near = [lax.rem(self.y + i, 4) for i in (1, 3, 2)]
        self.z_peers = [self.place(self.x, z, self.y) for z in self.z_near]
        self.y_peers = [self.place(self.x, self.z, y) for y in self.y_near]
        self.x_peer = self.place(1 - self.x, self.z, self.y)

    @staticmethod
    def place(x, z, y):
        return x * 16 + z * 4 + y

    def rows(self, half):
        half_rows = self.full.shape[1] // 2
        return pl.ds(half * half_rows, half_rows)

    def pass_on(self, owner, half, peers, own=False):
        target = self.full.at[owner, self.rows(half)]
        for peer in peers:
            pltpu.make_async_remote_copy(
                src_ref=self.mine.at[self.rows(half)] if own else target,
                dst_ref=target,
                send_sem=self.send_sem,
                recv_sem=self.recv_sem.at[half * 32 + owner],
                device_id=(self.row, peer),
                device_id_type=MESH,
            ).start()

    def await_half(self, owner, half):
        target = self.full.at[owner, self.rows(half)]
        pltpu.make_async_copy(target, target, self.recv_sem.at[half * 32 + owner]).wait()

    def start(self):
        for half in range(2):
            self.pass_on(self.col, half, [self.x_peer], own=True)
        self.pass_on(self.col, 0, self.z_peers, own=True)
        self.pass_on(self.col, 1, self.y_peers, own=True)

    def second(self):
        self.await_half(self.x_peer, 0)
        self.pass_on(self.x_peer, 0, self.z_peers)
        self.await_half(self.x_peer, 1)
        self.pass_on(self.x_peer, 1, self.y_peers)
        self.pass_on(self.col, 0, self.y_peers, own=True)
        self.pass_on(self.col, 1, self.z_peers, own=True)
        self.pass_on(self.x_peer, 0, self.y_peers)
        self.pass_on(self.x_peer, 1, self.z_peers)

    def third(self):
        for i in range(3):
            for x in (self.x, 1 - self.x):
                owner = self.place(x, self.z_near[i], self.y)
                self.await_half(owner, 0)
                self.pass_on(owner, 0, self.y_peers)
                owner = self.place(x, self.z, self.y_near[i])
                self.await_half(owner, 1)
                self.pass_on(owner, 1, self.z_peers)

    def await_all(self):
        for x in (self.x, 1 - self.x):
            for i in range(4):
                for j in range(3):
                    z, y = lax.rem(self.z + i, 4), lax.rem(self.y + i, 4)
                    self.await_half(self.place(x, z, self.y_near[j]), 0)
                    self.await_half(self.place(x, self.z_near[j], y), 1)

    def end(self):
        sent = self.full.at[pl.ds(0, 31)]
        pltpu.make_async_copy(sent, sent, self.send_sem).wait()


def head_kernel(
    inputs,
    gain_attn,
    gain_ffn,
    grads,
    lengths,
    routes,
    frequency,
    w_query,
    w_keyval,
    w_out,
    w_shared_in,
    w_shared_out,
    full_pre,
    full_back,
    group_one,
    group_grad,
    scale_one,
    cosine,
    sine,
    begin,
    begin_row,
    query,
    keys,
    values,
    attended,
    norms,
    hidden,
    normed_two,
    scale_two,
    packed,
    code,
    order,
    *scratch,
):
    mine_pre, mine_back, normed, rows, w_pre, w_back, pre, bias, parts = scratch[:9]
    near, far, outgoing, marks, staged = scratch[9:14]
    gather_send, recv_pre, recv_back, own_sem, row_send, row_recv = scratch[14:20]
    sum_send, sum_recv, load_sem, pack_sem = scratch[20:]
    low = jnp.bfloat16
    row, col, sibling, partner, _ = row_places()
    gathers = [
        Gather(mine_pre, full_pre, gather_send.at[0], recv_pre),
        Gather(mine_back, full_back, gather_send.at[1], recv_back),
    ]
    near_peers = gathers[0].z_peers + gathers[0].y_peers + [gathers[0].x_peer]
    greet([(row, peer) for peer in near_peers])
    greet([(sibling, col), (partner, col)])
    start = 0
    for mine, shards in ((mine_pre, (w_query, w_keyval)), (mine_back, (w_out, w_shared_in, w_shared_out))):
        start = 0
        for shard in shards:
            mine[:, start : start + shard.shape[1]] = shard[...]
            start += shard.shape[1]
    first = inputs[...].astype(jnp.float32)
    factor = lax.rsqrt(jnp.mean(first * first, axis=1, keepdims=True) + epsilon)
    scale_one[...] = factor
    normed[...] = (first * factor * gain_attn[...]).astype(low)
    own = [
        pltpu.make_async_copy(normed, group_one.at[row], own_sem.at[0]),
        pltpu.make_async_copy(grads, group_grad.at[row], own_sem.at[1]),
        pltpu.make_async_copy(mine_pre, full_pre.at[col], own_sem.at[2]),
        pltpu.make_async_copy(mine_back, full_back.at[col], own_sem.at[3]),
    ]
    for copy in own:
        copy.start()
    await_greetings(9)
    far_rows, near_rows, onward = row_copies(
        [normed, grads], [group_one, group_grad], row_send, row_recv
    )
    gathers[0].start()
    far_rows[0].start()
    near_rows[0].start()
    gathers[1].start()
    gathers[0].second()
    gathers[1].second()
    gathers[0].third()
    far_rows[1].start()
    near_rows[1].start()
    gathers[1].third()

    tokens = begin.shape[0]

    def document_starts(axis, shape):
        places = lax.broadcasted_iota(jnp.int32, shape, axis)
        found = jnp.zeros(shape, jnp.int32)
        bound = 0
        for i in range(NDOC - 1):
            bound = bound + lengths[0, i]
            found = jnp.where(places >= bound, bound, found)
        return places, found

    begin_row[...] = document_starts(1, begin_row.shape)[1]
    places, starts = document_starts(0, cosine.shape)
    begin[...] = starts[:, :1]
    angles = (places - starts).astype(jnp.float32) * frequency[...]
    lanes = lax.broadcasted_iota(jnp.int32, cosine.shape, 1)
    cosine[...] = jnp.cos(angles)
    sine[...] = jnp.where(lanes < cosine.shape[1] // 2, -1.0, 1.0) * jnp.sin(angles)
    bias[...] = score_bias(begin[...])

    experts = lax.broadcasted_iota(jnp.int32, order.shape, 1)
    chosen = jnp.zeros(order.shape, jnp.float32)
    for k in range(routes.shape[1]):
        chosen = jnp.where(routes[:, k : k + 1] == experts, 1.0, chosen)
    square = (order.shape[0], order.shape[0])
    before = lax.broadcasted_iota(jnp.int32, square, 1) < lax.broadcasted_iota(
        jnp.int32, square, 0
    )
    ahead = matmul(before.astype(jnp.float32).astype(low), chosen.astype(low))
    order[...] = jnp.where(chosen > 0.0, ahead, -1.0)
    code[...] = jnp.transpose(order[...]).astype(low).reshape(code.shape)

    def mark(block, carry):
        found = token_marks(code[block])
        for part in range(3):
            marks[block, part] = jnp.concatenate(
                [found[0][1].astype(low), found[part + 1][1].astype(low)], axis=1
            )
        return carry

    lax.fori_loop(0, code.shape[0], mark, 0)

    far_rows[0].wait_recv()
    onward[0].start()
    gathers[0].await_all()
    own[0].wait()
    own[2].wait()
    near_rows[0].wait_recv()
    onward[0].wait_recv()
    loads = [
        pltpu.make_async_copy(group_one, rows, load_sem.at[0]),
        pltpu.make_async_copy(full_pre, w_pre, load_sem.at[1]),
        pltpu.make_async_copy(
            full_back.at[:, :, pl.ds(0, w_back.shape[2])], w_back, load_sem.at[2]
        ),
    ]
    loads[0].start()
    loads[1].start()
    loads[0].wait()
    loads[1].wait()
    width = inputs.shape[1]
    pre[...] = matmul(
        rows[...].reshape(tokens, width), w_pre[...].reshape(width, w_pre.shape[2])
    )
    size = keys.shape[1]
    inner = query.shape[1]
    keys[...] = turn(pre[:, inner : inner + size], cosine[...], sine[...]).astype(low)
    values[...] = pre[:, inner + size :].astype(low)
    log_totals = jnp.zeros(norms.shape, jnp.float32)
    for head in range(inner // size):
        columns = slice(head * size, (head + 1) * size)
        turned = turn(pre[:, columns], cosine[...], sine[...]).astype(low)
        query[:, columns] = turned
        scores = matmul_t(turned, keys[...]) * (size ** (-0.5)) + bias[...]
        highest = jnp.max(scores, axis=1, keepdims=True)
        weights = jnp.exp(scores - highest)
        total = jnp.sum(weights, axis=1, keepdims=True)
        weights = (weights * (1.0 / total)).astype(low)
        attended[:, columns] = matmul(weights, values[...]).astype(low)
        log_totals = jnp.where(lanes == head, highest + jnp.log(total), log_totals)
    norms[...] = log_totals
    far_rows[1].wait_recv()
    onward[1].start()
    gathers[1].await_all()
    own[3].wait()
    loads[2].start()
    loads[2].wait()
    parts[...] = (
        matmul_t(attended[...], w_back[...].reshape(width, inner)).astype(low).reshape(parts.shape)
    )

    copies = row_sum_copies(parts, near, far, outgoing, (sum_send, sum_recv), 0)
    copies[0].start()
    copies[1].start()
    row_sum_forward(parts, near, outgoing, copies)
    total = inputs[...].astype(jnp.float32) + row_sum_total(parts, near, far, copies)
    hidden[...] = total
    factor = lax.rsqrt(jnp.mean(total * total, axis=1, keepdims=True) + epsilon)
    normed_two[...] = (total * factor * gain_ffn[...]).astype(low)
    scale_two[...] = factor

    def pack(block, carry):
        last = normed_two[:, 3 * QUARTER :]
        for part in range(3):
            columns = slice(part * QUARTER, (part + 1) * QUARTER)
            both = jnp.concatenate([normed_two[:, columns], last], axis=0)
            staged[block, :, columns] = matmul(marks[block, part], both).astype(low)
        target = packed.at[pl.ds(pl.multiple_of(block * BLOCK, BLOCK), BLOCK)]
        pltpu.make_async_copy(staged.at[block], target, pack_sem.at[block]).start()
        return carry

    lax.fori_loop(0, code.shape[0], pack, 0)

    own[1].wait()
    near_rows[0].wait_send()
    near_rows[1].wait()
    onward[0].wait_send()
    onward[1].wait()
    for copy in far_rows + copies:
        copy.wait_send()
    for gather in gathers:
        gather.end()
    for block in range(staged.shape[0]):
        target = packed.at[pl.ds(block * BLOCK, BLOCK)]
        pltpu.make_async_copy(staged.at[block], target, pack_sem.at[block]).wait()


def head(inputs, gain_attn, gain_ffn, grads, lengths, routes, shards, size, expert_count):
    space = pl.BlockSpec(memory_space=pltpu.VMEM)
    away = pl.BlockSpec(memory_space=pl.ANY)
    low = jnp.bfloat16
    rows, width = inputs.shape
    tokens = 4 * rows
    shard_rows = shards[0].shape[0]
    inner = shards[0].shape[1]
    pre_width = inner + shards[1].shape[1]
    back_width = sum(part.shape[1] for part in shards[2:])
    blocks = expert_count // BLOCK_EXPERTS
    spread = np.arange(size // 2, dtype=np.float32) * np.float32(2.0 / size)
    frequency = np.float32(rope_base) ** (-spread)
    frequency = jnp.asarray(np.concatenate([frequency, frequency])[None], jnp.float32)

    def full(shape, dtype):
        return jax.ShapeDtypeStruct(shape, dtype)

    return pl.pallas_call(
        head_kernel,
        out_shape=[
            full((32, shard_rows, pre_width), low),
            full((32, shard_rows, back_width), low),
            full((4, rows, width), low),
            full((4, rows, width), low),
            full((rows, 1), jnp.float32),
            full((tokens, size), jnp.float32),
            full((tokens, size), jnp.float32),
            full((tokens, 1), jnp.int32),
            full((1, tokens), jnp.int32),
            full((tokens, inner), low),
            full((tokens, size), low),
            full((tokens, size), low),
            full((tokens, inner), low),
            full((tokens, size), jnp.float32),
            full((rows, width), jnp.float32),
            full((rows, width), low),
            full((rows, 1), jnp.float32),
            full((blocks * BLOCK, 3 * QUARTER), low),
            full((blocks, BLOCK_EXPERTS, rows), low),
            full((rows, expert_count), jnp.float32),
        ],
        in_specs=[space] * 3
        + [away, pl.BlockSpec(memory_space=pltpu.SMEM)]
        + [space] * (2 + len(shards)),
        out_specs=[away] * 4 + [space] * 13 + [away] + [space] * 2,
        scratch_shapes=[
            pltpu.VMEM((shard_rows, pre_width), low),
            pltpu.VMEM((shard_rows, back_width), low),
            pltpu.VMEM((rows, width), low),
            pltpu.VMEM((4, rows, width), low),
            pltpu.VMEM((32, shard_rows, pre_width), low),
            pltpu.VMEM((32, shard_rows, inner), low),
            pltpu.VMEM((tokens, pre_width), jnp.float32),
            pltpu.VMEM((tokens, tokens), jnp.float32),
            pltpu.VMEM((4, rows, width), low),
            pltpu.VMEM((2, rows, width), low),
            pltpu.VMEM((rows, width), low),
            pltpu.VMEM((rows, width), low),
            pltpu.VMEM((blocks, 3, BLOCK, 2 * rows), low),
            pltpu.VMEM((blocks, BLOCK, 3 * QUARTER), low),
            pltpu.SemaphoreType.DMA((2,)),
            pltpu.SemaphoreType.DMA((64,)),
            pltpu.SemaphoreType.DMA((64,)),
            pltpu.SemaphoreType.DMA((4,)),
            pltpu.SemaphoreType.DMA((6,)),
            pltpu.SemaphoreType.DMA((6,)),
            pltpu.SemaphoreType.DMA((3,)),
            pltpu.SemaphoreType.DMA((3,)),
            pltpu.SemaphoreType.DMA((3,)),
            pltpu.SemaphoreType.DMA((blocks,)),
        ],
        compiler_params=pltpu.CompilerParams(
            collective_id=0, has_side_effects=True, vmem_limit_bytes=60 << 20
        ),
        cost_estimate=pl.CostEstimate(flops=0, bytes_accessed=300 << 20, transcendentals=0),
        name="head",
    )(inputs, gain_attn, gain_ffn, grads, lengths, routes, frequency, *shards)


def exchange(packed):
    pairs = packed.reshape(-1, PACKED_ROWS, packed.shape[1])
    swapped = lax.all_to_all(pairs, ("row", "col"), split_axis=0, concat_axis=0, tiled=True)
    return swapped.reshape(packed.shape)


def per_device(
    block_in,
    gain_attn,
    w_query,
    w_keyval,
    w_out,
    gain_ffn,
    w_shared_in,
    w_shared_out,
    w_router,
    w_expert_in,
    w_expert_out,
    doc_lengths,
    routes,
    cotangent,
):
    row_count = lax.axis_size("row")
    rows_dev = block_in.shape[1]
    model_width = block_in.shape[2]
    expert_count = w_router.shape[1]
    expert_ff = w_expert_out.shape[2]
    inputs = block_in.reshape(rows_dev, model_width)
    grad_low = cotangent.reshape(rows_dev, model_width)
    shards = [w_query, w_keyval, w_out, w_shared_in, w_shared_out]
    shards = [part.reshape(part.shape[0], -1) for part in shards]
    (
        full_pre,
        full_back,
        group_one,
        group_grad,
        scale_one,
        cosine,
        sine_table,
        begin,
        begin_row,
        *kept,
        hidden_state,
        normed_two,
        scale_two,
        send_rows,
        code,
        order,
    ) = head(
        inputs,
        gain_attn[None],
        gain_ffn[None],
        grad_low,
        doc_lengths,
        routes.reshape(rows_dev, -1),
        shards,
        w_keyval.shape[2] // 2,
        expert_count,
    )
    full_pre, full_back, group_one, group_grad = (
        part.reshape(-1, part.shape[2]) for part in (full_pre, full_back, group_one, group_grad)
    )
    received = exchange(send_rows)
    shared_start, shared_width = w_out.shape[1], w_shared_out.shape[1]
    full_shared_in = full_back[:, shared_start : shared_start + 2 * shared_width]
    full_shared_out = full_back[:, shared_start + 2 * shared_width :]

    logits = matmul(normed_two, w_router)
    scores_sig = jnp.where(order >= 0.0, jax.nn.sigmoid(logits), 0.0)
    score_sum = jnp.sum(scores_sig, axis=1, keepdims=True)
    gate_weights = scores_sig / score_sum
    gates = [
        part.T.reshape(-1, BLOCK_EXPERTS, rows_dev) for part in split_low(gate_weights)
    ]
    send_grads, received = lax.optimization_barrier((pack_tokens(code, grad_low, gates), received))
    received_grads = exchange(send_grads)

    group_two = lax.all_gather(normed_two, "row", axis=0, tiled=True)
    shared_pre = matmul(group_two, full_shared_in)
    shared_gate, shared_up = shared_pre[:, :shared_width], shared_pre[:, shared_width:]
    shared_act, shared_slope = swish_parts(shared_gate)
    shared_hidden = (shared_act * shared_up).astype(jnp.bfloat16)
    shared_hidden_grad = matmul(group_grad, full_shared_out)
    shared_pre_grad = jnp.concatenate(
        [shared_hidden_grad * shared_up * shared_slope, shared_hidden_grad * shared_act], axis=1
    ).astype(jnp.bfloat16)
    shared_grads = jnp.concatenate(
        [
            outer_sum(group_two, shared_pre_grad).astype(jnp.bfloat16),
            outer_sum(group_grad, shared_hidden).astype(jnp.bfloat16),
        ],
        axis=1,
    )
    shared_parts = matmul_t(shared_hidden, full_shared_out).astype(jnp.bfloat16)
    shared_input = lax.psum_scatter(
        matmul_t(shared_pre_grad, full_shared_in).astype(jnp.bfloat16),
        "row",
        scatter_dimension=0,
        tiled=True,
    ).astype(jnp.float32)

    expert_in = unpack_slots(received)
    expert_pre = jnp.einsum(
        "esd,edf->esf", expert_in, w_expert_in, preferred_element_type=jnp.float32
    )
    expert_act, expert_slope = swish_parts(expert_pre[..., :expert_ff])
    expert_hidden = (expert_act * expert_pre[..., expert_ff:]).astype(jnp.bfloat16)
    expert_out = jnp.einsum(
        "esf,edf->esd", expert_hidden, w_expert_out, preferred_element_type=jnp.float32
    ).astype(jnp.bfloat16)
    send_out, received_grads = lax.optimization_barrier((pack_slots(expert_out), received_grads))
    returned = exchange(send_out)

    out_grad = unpack_slots(received_grads)
    hidden_grad = jnp.einsum(
        "esd,edf->esf", out_grad, w_expert_out, preferred_element_type=jnp.float32
    )
    expert_pre_grad = jnp.concatenate(
        [hidden_grad * expert_pre[..., expert_ff:] * expert_slope, hidden_grad * expert_act], axis=2
    ).astype(jnp.bfloat16)
    slot_grad = jnp.einsum(
        "esf,edf->esd", expert_pre_grad, w_expert_in, preferred_element_type=jnp.float32
    ).astype(jnp.bfloat16)
    send_back, returned = lax.optimization_barrier((pack_slots(slot_grad), returned))
    returned_grad = exchange(send_back)
    grad_expert_out = jnp.einsum(
        "esd,esf->edf", out_grad, expert_hidden, preferred_element_type=jnp.float32
    )
    grad_expert_in = jnp.einsum(
        "esd,esf->edf", expert_in, expert_pre_grad, preferred_element_type=jnp.float32
    )
    routed_branch, gate_grads = sum_gated(code, returned, send_grads, gates)
    stream = hidden_state + routed_branch
    gate_grads = gate_grads.transpose(1, 0, 2).reshape(rows_dev, expert_count)
    logit_grad = (
        (1.0 - scores_sig)
        * (gate_grads - gate_weights * jnp.sum(gate_grads, axis=1, keepdims=True))
    ).astype(jnp.bfloat16)
    router_parts = outer_sum(normed_two, logit_grad).astype(jnp.bfloat16)
    router_parts = router_parts.reshape(row_count, -1, expert_count)
    router_input = shared_input + matmul_t(logit_grad, w_router)
    shadowed = (router_input, router_parts, stream, shared_grads, group_one.T, all_marks(code))
    returned_grad, shadowed, grad_expert_in, grad_expert_out = lax.optimization_barrier(
        (returned_grad, shadowed, grad_expert_in, grad_expert_out)
    )
    router_input, router_parts, stream, shared_grads, group_one_t, marks = shadowed

    widths = [part.shape[1] for part in shards]
    group_branch, hidden_total, gain_ffn_grad, router_sum, shared_sums = token_back(
        returned_grad,
        marks,
        router_input,
        hidden_state,
        scale_two,
        gain_ffn[None],
        grad_low,
        router_parts,
        shared_grads.reshape(2, 4, 4, -1, shared_grads.shape[1]),
        widths[3:],
    )
    input_back, block_out, router_sum, gain_sums, *sums = finish(
        group_branch,
        group_one_t,
        (full_pre, full_back),
        kept,
        (cosine, sine_table, begin, begin_row),
        (
            shared_parts.reshape(row_count, rows_dev, model_width),
            router_sum.reshape(32, -1, expert_count),
            stream,
            inputs,
            scale_one,
            gain_attn[None],
            gain_ffn_grad,
        ),
        widths[:3],
    )
    sums = [
        part.reshape(like.shape)
        for part, like in zip(sums + shared_sums, (w_query, w_keyval, w_out, w_shared_in, w_shared_out))
    ]
    return (
        block_out.reshape(1, rows_dev, model_width),
        (hidden_total + input_back).reshape(1, rows_dev, model_width),
        gain_sums[0],
        sums[0],
        sums[1],
        sums[2],
        gain_sums[1],
        sums[3],
        sums[4],
        router_sum.reshape(model_width, expert_count).astype(jnp.float32),
        grad_expert_in,
        grad_expert_out,
    )


def solution(mesh):
    in_specs = (
        P("col", "row", None),
        P(),
        P("col", "row"),
        P("col", "row", None),
        P("col", "row"),
        P(),
        P("col", None, "row"),
        P("col", "row"),
        P(),
        P(("row", "col"), None, None),
        P(("row", "col"), None, None),
        P("col", None),
        P("col", "row", None),
        P("col", "row", None),
    )
    out_specs = (
        P("col", "row", None),
        P("col", "row", None),
        P(),
        P("col", "row"),
        P("col", "row", None),
        P("col", "row"),
        P(),
        P("col", None, "row"),
        P("col", "row"),
        P(),
        P(("row", "col"), None, None),
        P(("row", "col"), None, None),
    )
    return jax.shard_map(
        per_device, mesh=mesh, in_specs=in_specs, out_specs=out_specs, check_vma=False
    )
```

time: 620 us -> 581 us (0.937)
  the two profiles are of different devices: /device:TPU:1 before, /device:TPU:4 now
where the time goes in v5:
time: 581 us; the launch traced here: 570 us
  Pallas kernels  226 us (39%)
  waiting for transfers between devices  169 us (29%)
  matrix products  76.6 us (13%)
  starting transfers between devices  40.6 us (7%)
  local copies, waits for them, and re-layouts  34.9 us (6%)
  between operations  15 us (3%)
  other arithmetic  8.77 us (2%)
    all_to_all x4, waiting for transfers between devices, exchange(): lax.all_to_all(pairs, ('row', 'col'), split_axis=0, concat_axis=0, tiled=...  168 us
    pallas_call x1, Pallas kernels, head(): pl.pallas_call(head_kernel, out_shape=[full((32, shard_rows, pre_width),...  83.9 us
    pallas_call x1, Pallas kernels, finish(): pl.pallas_call(finish_kernel, out_shape=[jax.ShapeDtypeStruct((rows, widt...  63.7 us
    all_to_all x4, starting transfers between devices, exchange(): lax.all_to_all(pairs, ('row', 'col'), split_axis=0, concat_axis=0, tiled=...  40.1 us
    pallas_call x1, Pallas kernels, token_back(): pl.pallas_call(token_back_kernel, out_shape=[jax.ShapeDtypeStruct((4, tok...  29.9 us
    unnamed x77, local copies, waits for them, and re-layouts  24.6 us
    pallas_call x2, Pallas kernels, unpack_slots(): pl.pallas_call(unpack_slots_kernel, grid=(blocks,), out_shape=jax.ShapeDt...  14.9 us
    dot_general x1, matrix products, per_device(): jnp.einsum('esf,edf->esd', expert_pre_grad, w_expert_in, preferred_elemen...  11.7 us
  transfers between devices with their start and end apart: 6, of which 4 were waited for; matrix products, arithmetic and copies ran while one was open for 15% of the time, Pallas kernels for 8%

profile of v5, /device:TPU:4, one launch (start us, length us, event | category | flops | bytes accessed | tf_op | source)
XLA Modules:
  0.0 570.4 jit_solution(12039712440065695899)
XLA Ops:
  10.1 83.9 %head.1 = (bf16[32,64,768]{2,1,0:T(8,128)(2,1)}, bf16[32,64,896]{2,1,0:T(8,128)(2,1)}, bf16[4,128,2048]{2,1,0:T(8,128)(2,1)}, bf16[4,128,2048]{2,1,0:T(8,128)(2,...) custom-call(bf16[128,2048]{1,0:T(8,128)(2,1)} %bitcast.99, ...), custom_call_target="tpu_custom_call" | custom-call | bytes 314572800 | tf_op jit(solution)/shard_map/head/pallas_call | solution.py:1193
  94.0 8.2 %all-to-all-start = ((bf16[128,16,1536]{2,1,0:T(8,128)(2,1)}), bf16[128,16,1536]{2,1,0:T(8,128)(2,1)}, u32[]{:S(2)}, u32[]{:S(2)}) async-start(bf16[128,16,1536]{2,1,0:T(8,128)(2,1)} %bitcast.92), calls=%async_computation | async-start | bytes 12582912 | tf_op jit(solution)/shard_map/all_to_all | solution.py:1257
  103.0 6.8 %pack_tokens.1.grads = bf16[2048,1536]{1,0:T(8,128)(2,1)S(1)} custom-call(bf16[8,32,128]{2,1,0:T(8,128)(2,1)S(1)} %copy-done.14, bf16[128,2048]{1,0:T(8,128)(2,1)S(1)} %bitcast.75, bf16[8,32,128]{2,1,0:T(8,128)(2,1)S(1)} %bitcast.79, bf16[8,32,128]{2,1,0:T(8,128)(2,1)S(1)} %bitcast.81), custom_call_target="tpu_custom_call" | custom-call | flops 3221225472 | bytes 8388608 | tf_op jit(solution)/shard_map/pack_tokens/pallas_call | solution.py:725
  109.8 2.7 copy-done.1
  112.5 65.0 %all-to-all-done = bf16[128,16,1536]{2,1,0:T(8,128)(2,1)} async-done(((bf16[128,16,1536]{2,1,0:T(8,128)(2,1)}), bf16[128,16,1536]{2,1,0:T(8,128)(2,1)}, u32[]{:S(2)}, u32[]{:S(2)}) %all-to-all-start) | async-done | bytes 6291488 | tf_op jit(solution)/shard_map/all_to_all | solution.py:1257
  177.5 11.2 %all-to-all-start.1 = ((bf16[128,16,1536]{2,1,0:T(8,128)(2,1)}), bf16[128,16,1536]{2,1,0:T(8,128)(2,1)}, u32[]{:S(2)}, u32[]{:S(2)}) async-start(bf16[128,16,1536]{2,1,0:T(8,128)(2,1)} %bitcast.66), calls=%async_computation.1 | async-start | bytes 12582912 | tf_op jit(solution)/shard_map/all_to_all | solution.py:1257
  188.6 7.4 %unpack_slots.2 = bf16[2,768,2048]{2,1,0:T(8,128)(2,1)S(1)} custom-call(bf16[2048,1536]{1,0:T(8,128)(2,1)} %bitcast.11.packed), custom_call_target="tpu_custom_call" | custom-call | flops 2415919104 | bytes 14680064 | tf_op jit(solution)/shard_map/unpack_slots/pallas_call | solution.py:766
  196.0 11.3 %fusion.20 = f32[2,768,1024]{2,1,0:T(8,128)S(1)} fusion(bf16[2,768,2048]{2,1,0:T(8,128)(2,1)S(1)} %unpack_slots.2, bf16[2,2048,1024]{2,1,0:T(8,128)(2,1)} %param.24), kind=kOutput, calls=%fused_computation.47 | convolution fusion | flops 6442450944 | bytes 20971520 | tf_op jit(solution)/shard_map/esd,edf->esf/dot_general | solution.py:1357
  207.4 2.7 copy-done.18
  212.3 3.7 convolution_convert_fusion.1.values
  216.0 5.4 pack_slots.2
  221.4 2.7 copy-done.3
  224.1 39.8 %all-to-all-done.1 = bf16[128,16,1536]{2,1,0:T(8,128)(2,1)} async-done(((bf16[128,16,1536]{2,1,0:T(8,128)(2,1)}), bf16[128,16,1536]{2,1,0:T(8,128)(2,1)}, u32[]{:S(2)}, u32[]{:S(2)}) %all-to-all-start.1) | async-done | bytes 6291488 | tf_op jit(solution)/shard_map/all_to_all | solution.py:1257
  263.9 11.2 %all-to-all-start.2 = ((bf16[128,16,1536]{2,1,0:T(8,128)(2,1)}), bf16[128,16,1536]{2,1,0:T(8,128)(2,1)}, u32[]{:S(2)}, u32[]{:S(2)}) async-start(bf16[128,16,1536]{2,1,0:T(8,128)(2,1)} %bitcast.70), calls=%async_computation.2 | async-start | bytes 12582912 | tf_op jit(solution)/shard_map/all_to_all | solution.py:1257
  275.8 7.5 %unpack_slots.3 = bf16[2,768,2048]{2,1,0:T(8,128)(2,1)S(1)} custom-call(bf16[2048,1536]{1,0:T(8,128)(2,1)} %bitcast.13.packed), custom_call_target="tpu_custom_call" | custom-call | flops 2415919104 | bytes 14680064 | tf_op jit(solution)/shard_map/unpack_slots/pallas_call | solution.py:766
  283.4 8.8 %multiply_convert_fusion.1 = (bf16[2,768,512]{2,1,0:T(8,128)(2,1)S(1)}, bf16[2,768,512]{2,1,0:T(8,128)(2,1)S(1)}) fusion(f32[2,768,1024]{2,1,0:T(8,128)} %copy-done.18, bf16[2,768,2048]{2,1,0:T(8,128)(2,1)S(1)} %unpack_slots.3, bf16[2,2048,512]{2,1,0:T(8,128)(2,1)S(1)} %copy-done.25), kind=kOutput, calls=%fused_computation.4 | convolution fusion | flops 3231449088 | bytes 19922944 | tf_op jit(solution)/shard_map/esd,edf->esf/dot_general | solution.py:1369
  292.2 11.7 %convolution_convert_fusion.values = bf16[2,768,2048]{2,1,0:T(8,128)(2,1)S(1)} fusion(bf16[2,2048,1024]{2,1,0:T(8,128)(2,1)} %param.24, bf16[2,768,512]{2,1,0:T(8,128)(2,1)S(1)} %get-tuple-element.137, bf16[2,768,512]{2,1,0:T(8,128)(2,1)S(1)} %get-tuple-element.136), kind=kOutput, calls=%fused_computation | convolution fusion | flops 6451888128 | bytes 17825792 | tf_op jit(solution)/shard_map/esf,edf->esd/dot_general | solution.py:1375
  303.9 5.4 pack_slots.3
  312.0 46.0 %all-to-all-done.2 = bf16[128,16,1536]{2,1,0:T(8,128)(2,1)} async-done(((bf16[128,16,1536]{2,1,0:T(8,128)(2,1)}), bf16[128,16,1536]{2,1,0:T(8,128)(2,1)}, u32[]{:S(2)}, u32[]{:S(2)}) %all-to-all-start.2) | async-done | bytes 6291488 | tf_op jit(solution)/shard_map/all_to_all | solution.py:1257
  358.0 9.6 %all-to-all-start.3 = ((bf16[128,16,1536]{2,1,0:T(8,128)(2,1)}), bf16[128,16,1536]{2,1,0:T(8,128)(2,1)}, u32[]{:S(2)}, u32[]{:S(2)}) async-start(bf16[128,16,1536]{2,1,0:T(8,128)(2,1)} %bitcast.69), calls=%async_computation.3 | async-start | bytes 12582912 | tf_op jit(solution)/shard_map/all_to_all | solution.py:1257
  372.8 3.3 convolution_convert_fusion.3
  377.0 4.1 copy.57
  381.1 5.4 all_marks.1.marks
  392.2 3.2 convolution_convert_fusion.2
  395.4 10.1 %fusion.21 = f32[2,2048,512]{2,1,0:T(8,128)} fusion(bf16[2,768,2048]{2,1,0:T(8,128)(2,1)} %copy-done.5, bf16[2,768,512]{2,1,0:T(8,128)(2,1)S(1)} %multiply_convert_fusion.2), kind=kOutput, calls=%fused_computation.48 | convolution fusion | flops 3221225472 | bytes 16252928 | tf_op jit(solution)/shard_map/esd,esf->edf/dot_general | solution.py:1380
  405.6 10.4 %fusion.1 = f32[2,2048,1024]{2,1,0:T(8,128)} fusion(bf16[2,768,2048]{2,1,0:T(8,128)(2,1)S(1)} %bitcast.72, bf16[2,768,512]{2,1,0:T(8,128)(2,1)S(1)} %copy-done.30, bf16[2,768,512]{2,1,0:T(8,128)(2,1)S(1)} %copy-done.28), kind=kOutput, calls=%fused_computation.14 | convolution fusion | flops 6448742400 | bytes 26214400 | tf_op jit(solution)/shard_map/esd,esf->edf/dot_general | solution.py:1383
  416.0 10.3 %sum_gated.1 = (f32[128,2048]{1,0:T(8,128)S(1)}, f32[8,128,32]{2,1,0:T(8,128)S(1)}) custom-call(bf16[8,32,128]{2,1,0:T(8,128)(2,1)S(1)} %copy-done.14, bf16[2048,1536]{1,0:T(8,128)(2,1)} %bitcast.15.packed, bf16[2048,1536]{1,0:T(8,128)(2,1)S(1)} %bitcast.68, bf16[8,32,128]{2,1,0:T(8,128)(2,1)S(1)} %bitcast.80, bf16[8,32,128]{2,1,0:T(8,128)(2,1)S(1)} %bitcast.82), custom_call_target="tpu_custom_call" | custom-call | flops 3221225472 | bytes 14680064 | tf_op jit(solution)/shard_map/sum_gated/pallas_call | solution.py:870
  434.2 17.6 %all-to-all-done.3 = bf16[128,16,1536]{2,1,0:T(8,128)(2,1)} async-done(((bf16[128,16,1536]{2,1,0:T(8,128)(2,1)}), bf16[128,16,1536]{2,1,0:T(8,128)(2,1)}, u32[]{:S(2)}, u32[]{:S(2)}) %all-to-all-start.3) | async-done | bytes 6291488 | tf_op jit(solution)/shard_map/all_to_all | solution.py:1257
  451.8 2.8 copy.51
  456.9 29.9 %token_back.1 = (bf16[4,128,2048]{2,1,0:T(8,128)(2,1)}, f32[128,2048]{1,0:T(8,128)S(1)}, f32[1,2048]{1,0:T(1,128)S(1)}, bf16[512,256]{1,0:T(8,128)(2,1)S(1)}, f3...) custom-call(bf16[2048,1536]{1,0:T(8,128)(2,1)} %bitcast.17.packed, bf16[4,128,2048]{2,1,0:T(8,128)(2,1)} %all_marks.1.marks, ...), custom_call_target="tpu_custom_call" | custom-call | bytes 104857600 | tf_op jit(solution)/shard_map/token_back/pallas_call | solution.py:391
  489.1 63.7 %finish.1 = (f32[128,2048]{1,0:T(8,128)}, bf16[128,2048]{1,0:T(8,128)(2,1)}, bf16[4,32,16,256]{3,2,1,0:T(8,128)(2,1)}, f32[2,2048]{1,0:T(2,128)}, f32[64,512]{1,...) custom-call(bf16[512,2048]{1,0:T(8,128)(2,1)} %bitcast.98, bf16[2048,512]{1,0:T(8,128)(2,1)} %bitcast.85, ...), custom_call_target="tpu_custom_call" | custom-call | bytes 209715200 | tf_op jit(solution)/shard_map/finish/pallas_call | solution.py:626
  556.5 2.8 bitcast_convert_fusion
  (102 shorter events, 40.9 us)
Async XLA Ops:
  7.2 95.0 %copy-start = (bf16[2048,256]{1,0:T(8,128)(2,1)S(1)}, bf16[2048,256]{1,0:T(8,128)(2,1)}, u32[]{:S(2)}) copy-start(bf16[2048,256]{1,0:T(8,128)(2,1)} %param.23) | copy-start | bytes 3145732
  93.9 8.3 %copy-start.19 = (bf16[128,2048]{1,0:T(8,128)(2,1)S(1)}, bf16[128,2048]{1,0:T(8,128)(2,1)}, u32[]{:S(2)}) copy-start(bf16[128,2048]{1,0:T(8,128)(2,1)} %get-tuple-element.64) | copy-start | bytes 1572868
  94.0 8.3 %copy-start.26 = (f32[128,256]{1,0:T(8,128)S(1)}, f32[128,256]{1,0:T(8,128)}, u32[]{:S(2)}) copy-start(f32[128,256]{1,0:T(8,128)} %get-tuple-element.63) | copy-start | bytes 393220
  94.0 9.0 %copy-start.8 = (bf16[1,128,2048]{2,1,0:T(8,128)(2,1)S(1)}, bf16[1,128,2048]{2,1,0:T(8,128)(2,1)}, u32[]{:S(2)}) copy-start(bf16[1,128,2048]{2,1,0:T(8,128)(2,1)} %param.28) | copy-start | bytes 1572868
  94.0 9.0 %copy-start.14 = (bf16[8,32,128]{2,1,0:T(8,128)(2,1)S(1)}, bf16[8,32,128]{2,1,0:T(8,128)(2,1)}, u32[]{:S(2)}) copy-start(bf16[8,32,128]{2,1,0:T(8,128)(2,1)} %get-tuple-element.62.code) | copy-start | bytes 196612
  94.0 83.5 %all-to-all-start = ((bf16[128,16,1536]{2,1,0:T(8,128)(2,1)}), bf16[128,16,1536]{2,1,0:T(8,128)(2,1)}, u32[]{:S(2)}, u32[]{:S(2)}) async-start(bf16[128,16,1536]{2,1,0:T(8,128)(2,1)} %bitcast.92), calls=%async_computation | async-start | bytes 12582912 | tf_op jit(solution)/shard_map/all_to_all | solution.py:1257
  177.5 86.4 %all-to-all-start.1 = ((bf16[128,16,1536]{2,1,0:T(8,128)(2,1)}), bf16[128,16,1536]{2,1,0:T(8,128)(2,1)}, u32[]{:S(2)}, u32[]{:S(2)}) async-start(bf16[128,16,1536]{2,1,0:T(8,128)(2,1)} %bitcast.66), calls=%async_computation.1 | async-start | bytes 12582912 | tf_op jit(solution)/shard_map/all_to_all | solution.py:1257
  196.0 11.4 %copy-start.4 = (bf16[2,768,2048]{2,1,0:T(8,128)(2,1)}, bf16[2,768,2048]{2,1,0:T(8,128)(2,1)S(1)}, u32[]{:S(2)}) copy-start(bf16[2,768,2048]{2,1,0:T(8,128)(2,1)S(1)} %unpack_slots.2) | copy-start | bytes 18874372
  207.4 2.7 copy-start.18
  221.4 2.7 copy-start.3
  263.9 94.1 %all-to-all-start.2 = ((bf16[128,16,1536]{2,1,0:T(8,128)(2,1)}), bf16[128,16,1536]{2,1,0:T(8,128)(2,1)}, u32[]{:S(2)}, u32[]{:S(2)}) async-start(bf16[128,16,1536]{2,1,0:T(8,128)(2,1)} %bitcast.70), calls=%async_computation.2 | async-start | bytes 12582912 | tf_op jit(solution)/shard_map/all_to_all | solution.py:1257
  275.1 92.6 %all-gather.2.cloned.1.call-start = ((), (), s32[]{:S(2)}) async-start(), calls=%async_computation.5 | async-start | bytes 2621440 | tf_op jit(solution)/shard_map/all_gather | solution.py:1332
  275.8 7.5 %copy-start.25 = (bf16[2,2048,512]{2,1,0:T(8,128)(2,1)S(1)}, bf16[2,2048,512]{2,1,0:T(8,128)(2,1)}, u32[]{:S(2)}) copy-start(bf16[2,2048,512]{2,1,0:T(8,128)(2,1)} %param.25) | copy-start | bytes 12582916
  283.4 8.8 %copy-start.5 = (bf16[2,768,2048]{2,1,0:T(8,128)(2,1)}, bf16[2,768,2048]{2,1,0:T(8,128)(2,1)S(1)}, u32[]{:S(2)}) copy-start(bf16[2,768,2048]{2,1,0:T(8,128)(2,1)S(1)} %unpack_slots.3) | copy-start | bytes 18874372
  292.2 11.7 %copy-start.27 = (bf16[2,768,512]{2,1,0:T(8,128)(2,1)}, bf16[2,768,512]{2,1,0:T(8,128)(2,1)S(1)}, u32[]{:S(2)}) copy-start(bf16[2,768,512]{2,1,0:T(8,128)(2,1)S(1)} %get-tuple-element.136) | copy-start | bytes 4718596
  292.2 11.7 %copy-start.29 = (bf16[2,768,512]{2,1,0:T(8,128)(2,1)}, bf16[2,768,512]{2,1,0:T(8,128)(2,1)S(1)}, u32[]{:S(2)}) copy-start(bf16[2,768,512]{2,1,0:T(8,128)(2,1)S(1)} %get-tuple-element.137) | copy-start | bytes 4718596
  358.0 93.8 %all-to-all-start.3 = ((bf16[128,16,1536]{2,1,0:T(8,128)(2,1)}), bf16[128,16,1536]{2,1,0:T(8,128)(2,1)}, u32[]{:S(2)}, u32[]{:S(2)}) async-start(bf16[128,16,1536]{2,1,0:T(8,128)(2,1)} %bitcast.69), calls=%async_computation.3 | async-start | bytes 12582912 | tf_op jit(solution)/shard_map/all_to_all | solution.py:1257
  367.6 64.1 %reduce-scatter.2.cloned.1.call-start = ((), (), s32[]{:S(2)}) async-start(), calls=%async_computation.6 | async-start | bytes 2621440 | tf_op jit(solution)/shard_map/reduce_scatter | solution.py:1349
  392.2 13.4 %slice-start.2 = ((s8[6291456]{0:T(1024)(128)(4,1)}), s8[4194304]{0:T(1024)(128)(4,1)S(1)}, s32[]{:S(2)}) async-start(s8[6291456]{0:T(1024)(128)(4,1)} %bitcast.71), calls=%async_computation.9 | async-start | bytes 8388608
  395.4 10.1 %slice-start.3 = ((s8[6291456]{0:T(1024)(128)(4,1)}), s8[2097152]{0:T(1024)(128)(4,1)S(1)}, s32[]{:S(2)}) async-start(s8[6291456]{0:T(1024)(128)(4,1)} %bitcast.71), calls=%async_computation.10 | async-start | bytes 4194304
  395.4 10.1 %copy-start.28 = (bf16[2,768,512]{2,1,0:T(8,128)(2,1)S(1)}, bf16[2,768,512]{2,1,0:T(8,128)(2,1)}, u32[]{:S(2)}) copy-start(bf16[2,768,512]{2,1,0:T(8,128)(2,1)} %copy-done.27) | copy-start | bytes 4718596
  395.4 10.1 %copy-start.30 = (bf16[2,768,512]{2,1,0:T(8,128)(2,1)S(1)}, bf16[2,768,512]{2,1,0:T(8,128)(2,1)}, u32[]{:S(2)}) copy-start(bf16[2,768,512]{2,1,0:T(8,128)(2,1)} %copy-done.29) | copy-start | bytes 4718596
  395.4 20.6 %slice-start = ((s8[6291456]{0:T(1024)(128)(4,1)}), s8[4194304]{0:T(1024)(128)(4,1)S(1)}, s32[]{:S(2)}) async-start(s8[6291456]{0:T(1024)(128)(4,1)} %bitcast.67), calls=%async_computation.7 | async-start | bytes 8388608
  405.6 10.5 %slice-start.1 = ((s8[6291456]{0:T(1024)(128)(4,1)}), s8[2097152]{0:T(1024)(128)(4,1)S(1)}, s32[]{:S(2)}) async-start(s8[6291456]{0:T(1024)(128)(4,1)} %bitcast.67), calls=%async_computation.8 | async-start | bytes 4194304
  416.0 11.7 %copy-start.6 = (f32[128,2048]{1,0:T(8,128)S(1)}, f32[128,2048]{1,0:T(8,128)}, u32[]{:S(2)}) copy-start(f32[128,2048]{1,0:T(8,128)} %get-tuple-element.75.hidden) | copy-start | bytes 3145732
  431.6 23.0 %copy-start.15 = (f32[128,1]{1,0:T(8,128)S(1)}, f32[128,1]{1,0:T(8,128)}, u32[]{:S(2)}) copy-start(f32[128,1]{1,0:T(8,128)} %get-tuple-element.81.scale) | copy-start | bytes 1540
  431.6 23.0 %copy-start.16 = (f32[2048]{0:T(1024)S(1)}, f32[2048]{0:T(1024)}, u32[]{:S(2)}) copy-start(f32[2048]{0:T(1024)} %param.20) | copy-start | bytes 24580
  552.8 6.5 %copy-start.11 = (f32[128,2048]{1,0:T(8,128)S(1)}, f32[128,2048]{1,0:T(8,128)}, u32[]{:S(2)}) copy-start(f32[128,2048]{1,0:T(8,128)} %copy-done.10) | copy-start | bytes 3145732
  552.8 6.5 %copy-start.20 = (f32[128,2048]{1,0:T(8,128)S(1)}, f32[128,2048]{1,0:T(8,128)}, u32[]{:S(2)}) copy-start(f32[128,2048]{1,0:T(8,128)} %get-tuple-element.102) | copy-start | bytes 3145732
  556.5 3.9 copy-start.21
  556.5 4.7 copy-start.23
  556.5 5.3 copy-start.22
  (9 other events, 13.1 us)
Sparse Core Ops, SparseCore 0:
  277.6 36.8 all-gather.1
  376.3 48.6 reduce-scatter.1

commit v6 on v5

--- a/solution.py
+++ b/solution.py
@@ -100,56 +100,6 @@
     keys = lax.broadcasted_iota(jnp.int32, shape, 1)
     allowed = (keys >= begin) & (keys <= lax.broadcasted_iota(jnp.int32, shape, 0))
     return jnp.where(allowed, 0.0, masked_score)
-
-
-def attention_back_queries(query, keys, values, back, norms, cosine, sine, begin, refs):
-    pre_grad, bias, deltas = refs
-    size = keys.shape[1]
-    bias[...] = score_bias(begin[...])
-    scale = size ** (-0.5)
-    lanes = lax.broadcasted_iota(jnp.int32, deltas.shape, 1)
-    all_deltas = jnp.zeros(deltas.shape, jnp.float32)
-    for head in range(query.shape[1] // size):
-        columns = slice(head * size, (head + 1) * size)
-        turned, outer = query[:, columns], back[:, columns]
-        scores = matmul_t(turned, keys[...]) * scale + bias[...]
-        probs = jnp.exp(scores - norms[:, head : head + 1])
-        prob_grad = matmul_t(outer, values[...])
-        delta = jnp.sum(probs * prob_grad, axis=1, keepdims=True)
-        all_deltas = jnp.where(lanes == head, delta, all_deltas)
-        score_grad = (probs * (prob_grad - delta)).astype(jnp.bfloat16)
-        query_grad = matmul(score_grad, keys[...]) * scale
-        pre_grad[:, columns] = turn(query_grad, cosine[...], -sine[...]).astype(jnp.bfloat16)
-    deltas[...] = all_deltas
-
-
-def attention_back_keys(query, keys, values, back, norms, cosine, sine, begin_row, refs):
-    pre_grad, bias, deltas = refs
-    low = jnp.bfloat16
-    size = keys.shape[1]
-    inner = query.shape[1]
-    scale = size ** (-0.5)
-    deltas_t = jnp.transpose(deltas[...])
-    norms_t = jnp.transpose(norms[...])
-    shape = bias.shape
-    key_places = lax.broadcasted_iota(jnp.int32, shape, 0)
-    allowed = (key_places >= begin_row[...]) & (
-        key_places <= lax.broadcasted_iota(jnp.int32, shape, 1)
-    )
-    bias[...] = jnp.where(allowed, 0.0, masked_score)
-    key_grad = jnp.zeros(keys.shape, jnp.float32)
-    value_grad = jnp.zeros(values.shape, jnp.float32)
-    for head in range(inner // size):
-        columns = slice(head * size, (head + 1) * size)
-        turned, outer = query[:, columns], back[:, columns]
-        scores = matmul_t(keys[...], turned) * scale + bias[...]
-        probs = jnp.exp(scores - norms_t[head : head + 1])
-        prob_grad = matmul_t(values[...], outer)
-        score_grad = (probs * (prob_grad - deltas_t[head : head + 1])).astype(low)
-        key_grad = key_grad + matmul(score_grad, turned)
-        value_grad = value_grad + matmul(probs.astype(low), outer)
-    pre_grad[:, inner : inner + size] = turn(key_grad * scale, cosine[...], -sine[...]).astype(low)
-    pre_grad[:, inner + size :] = value_grad.astype(low)
 
 
 def remote(source, target, sems, at, peer):
@@ -208,73 +158,71 @@
         half_rows, depth = grads.shape[3] // 2, grads.shape[4]
         low = jnp.bfloat16
         return [
-            pltpu.VMEM((2, 2, 3, 4, half_rows, depth), low),
+            pltpu.VMEM((2, 3, 2, 4, half_rows, depth), low),
             pltpu.VMEM((2, 2, 4, half_rows, depth), low),
-            pltpu.VMEM((2, 2, 3, half_rows, depth), low),
+            pltpu.VMEM((2, 3, 2, half_rows, depth), low),
             pltpu.VMEM((2, half_rows, depth), low),
             pltpu.VMEM((2, half_rows, depth), low),
-        ] + [pltpu.SemaphoreType.DMA((count,)) for count in (12, 12, 12, 12, 2, 2)]
+        ] + [pltpu.SemaphoreType.DMA((count,)) for count in (6, 6, 6, 6, 2, 2)]
 
     def half(self, half):
         return pl.ds(half * self.half_rows, self.half_rows)
 
     def start(self):
-        x, z, y = self.place
-        for turn, owner_x in enumerate((1 - x, x)):
-            for i in range(3):
-                for half in range(2):
-                    if half == 0:
-                        source = self.grads.at[owner_x, :, lax.rem(y + i + 1, 4), self.half(0)]
-                    else:
-                        source = self.grads.at[owner_x, lax.rem(z + i + 1, 4), :, self.half(1)]
-                    at = (turn * 2 + half) * 3 + i
-                    peer = (self.y_peers, self.z_peers)[half][i]
-                    copy = remote(source, self.first.at[turn, half, i], self.one, at, peer)
-                    self.one_copies[turn, half, i] = copy
-                    copy.start()
-
-    def add_first(self, turn):
-        x, z, y = self.place
-        owner_x = (1 - x, x)[turn]
+        _, z, y = self.place
+        for i in range(3):
+            for half in range(2):
+                if half == 0:
+                    source = self.grads.at[:, :, lax.rem(y + i + 1, 4), self.half(0)]
+                else:
+                    source = self.grads.at[:, lax.rem(z + i + 1, 4), :, self.half(1)]
+                peer = (self.y_peers, self.z_peers)[half][i]
+                copy = remote(source, self.first.at[half, i], self.one, half * 3 + i, peer)
+                self.one_copies[half, i] = copy
+                copy.start()
+
+    def add_first(self):
+        _, z, y = self.place
         for half in range(2):
             for i in range(3):
-                self.one_copies[turn, half, i].wait_recv()
+                self.one_copies[half, i].wait_recv()
 
             def add(k, carry, half=half):
                 if half == 0:
-                    total = self.grads[owner_x, k, y, self.half(0)].astype(jnp.float32)
+                    total = self.grads[k // 4, lax.rem(k, 4), y, self.half(0)].astype(jnp.float32)
                 else:
-                    total = self.grads[owner_x, z, k, self.half(1)].astype(jnp.float32)
+                    total = self.grads[k // 4, z, lax.rem(k, 4), self.half(1)].astype(jnp.float32)
                 for i in range(3):
-                    total = total + self.first[turn, half, i, k].astype(jnp.float32)
-                self.first_sum[turn, half, k] = total.astype(jnp.bfloat16)
+                    total = total + self.first[half, i, k // 4, lax.rem(k, 4)].astype(jnp.float32)
+                self.first_sum[half, k // 4, lax.rem(k, 4)] = total.astype(jnp.bfloat16)
                 return carry
 
-            lax.fori_loop(0, 4, add, 0)
+            lax.fori_loop(0, 8, add, 0)
             for i in range(3):
                 away = lax.rem((z, y)[half] + i + 1, 4)
                 copy = remote(
-                    self.first_sum.at[turn, half, away],
-                    self.second.at[turn, half, i],
+                    self.first_sum.at[half, :, away],
+                    self.second.at[half, i],
                     self.two,
-                    (turn * 2 + half) * 3 + i,
+                    half * 3 + i,
                     (self.z_peers, self.y_peers)[half][i],
                 )
-                self.two_copies[turn, half, i] = copy
+                self.two_copies[half, i] = copy
                 copy.start()
 
-    def second_total(self, turn, half):
+    def second_total(self, owner_x, half):
         _, z, y = self.place
+        total = self.first_sum[half, owner_x, (z, y)[half]].astype(jnp.float32)
         for i in range(3):
-            self.two_copies[turn, half, i].wait_recv()
-        total = self.first_sum[turn, half, (z, y)[half]].astype(jnp.float32)
-        for i in range(3):
-            total = total + self.second[turn, half, i].astype(jnp.float32)
+            total = total + self.second[half, i, owner_x].astype(jnp.float32)
         return total
 
     def add_second(self):
+        x = self.place[0]
         for half in range(2):
-            self.second_sum[half] = self.second_total(0, half).astype(jnp.bfloat16)
+            for i in range(3):
+                self.two_copies[half, i].wait_recv()
+            self.second_sum[half] = self.second_total(1 - x, half).astype(jnp.bfloat16)
             copy = remote(
                 self.second_sum.at[half], self.third.at[half], self.three, half, self.x_peer
             )
@@ -282,8 +230,9 @@
             copy.start()
 
     def add_third(self, pieces):
+        x = self.place[0]
         for half in range(2):
-            total = self.second_total(1, half)
+            total = self.second_total(x, half)
             self.three_copies[half].wait_recv()
             total = total + self.third[half].astype(jnp.float32)
             start = 0
@@ -296,44 +245,221 @@
             copy.wait_send()
 
 
-def token_back_kernel(
+class RouterSum:
+    def __init__(self, part, block, scratch):
+        self.part, self.block = part, block
+        self.in_y, self.sum_y, self.in_z, self.sum_z, self.in_x = scratch[:5]
+        self.sems = scratch[5:]
+        row, col = lax.axis_index("row"), lax.axis_index("col")
+        x, z, y = col // 16, lax.rem(col // 4, 4), lax.rem(col, 4)
+        self.place = (x, z, y)
+        self.y_near = [lax.rem(y + i, 4) for i in (1, 2, 3)]
+        self.z_near = [lax.rem(z + i, 4) for i in (1, 2, 3)]
+        self.y_peers = [(row, x * 16 + z * 4 + near) for near in self.y_near]
+        self.z_peers = [(row, x * 16 + near * 4 + y) for near in self.z_near]
+        self.x_peer = (row, (1 - x) * 16 + z * 4 + y)
+        self.copies = {}
+
+    @staticmethod
+    def scratch(share):
+        low = jnp.bfloat16
+        return [
+            pltpu.VMEM((3, 2, 4, *share), low),
+            pltpu.VMEM((2, 4, *share), low),
+            pltpu.VMEM((3, 2, *share), low),
+            pltpu.VMEM((2, *share), low),
+            pltpu.VMEM(share, low),
+            pltpu.SemaphoreType.DMA((14,)),
+            pltpu.SemaphoreType.DMA((14,)),
+        ]
+
+    def send(self, stage, at, sources, targets, peers):
+        copies = [
+            remote(source, target, self.sems, at + i, peer)
+            for i, (source, target, peer) in enumerate(zip(sources, targets, peers))
+        ]
+        for copy in copies:
+            copy.start()
+        self.copies[stage] = copies
+
+    def wait(self, stage):
+        for copy in self.copies[stage]:
+            copy.wait_recv()
+
+    def start(self):
+        sources = [self.part.at[:, :, near] for near in self.y_near]
+        self.send(0, 0, sources, [self.in_y.at[i] for i in range(3)], self.y_peers)
+
+    def add_y(self):
+        self.wait(0)
+        total = self.part[:, :, self.place[2]].astype(jnp.float32)
+        for i in range(3):
+            total = total + self.in_y[i].astype(jnp.float32)
+        self.sum_y[...] = total.astype(jnp.bfloat16)
+        sources = [self.sum_y.at[:, near] for near in self.z_near]
+        self.send(1, 3, sources, [self.in_z.at[i] for i in range(3)], self.z_peers)
+
+    def add_z(self):
+        self.wait(1)
+        total = self.sum_y[:, self.place[1]].astype(jnp.float32)
+        for i in range(3):
+            total = total + self.in_z[i].astype(jnp.float32)
+        self.sum_z[...] = total.astype(jnp.bfloat16)
+        self.send(2, 6, [self.sum_z.at[1 - self.place[0]]], [self.in_x], [self.x_peer])
+
+    def add_x(self):
+        self.wait(2)
+        x, z, y = self.place
+        total = self.sum_z[x].astype(jnp.float32) + self.in_x[...].astype(jnp.float32)
+        self.block[x, z, y] = total.astype(jnp.bfloat16)
+        own = self.block.at[x, z, y]
+        self.send(3, 7, [own], [own], [self.x_peer])
+
+    def spread_z(self):
+        self.wait(3)
+        own = self.block.at[:, self.place[1], self.place[2]]
+        self.send(4, 8, [own] * 3, [own] * 3, self.z_peers)
+
+    def spread_y(self):
+        self.wait(4)
+        own = self.block.at[:, :, self.place[2]]
+        self.send(5, 11, [own] * 3, [own] * 3, self.y_peers)
+
+    def end(self):
+        for copies in self.copies.values():
+            for copy in copies:
+                copy.wait_send()
+
+
+def attention_back_rows(start, refs, sums):
+    group, w_back, query, keys, values, norms, cosine, sine, begin, begin_row = refs
+    back, pre_grad, bias, bias_t, deltas, key_grad, value_grad = sums
+    low = jnp.bfloat16
+    size = keys.shape[1]
+    inner = query.shape[1]
+    count = bias.shape[0]
+    rows = pl.ds(pl.multiple_of(start, count), count)
+    scale = size ** (-0.5)
+    branch = group[pl.ds(start // 128, count // 128)].reshape(count, group.shape[2])
+    back[rows] = matmul(branch, w_back[...]).astype(low)
+    first = begin[rows]
+    key_places = lax.broadcasted_iota(jnp.int32, bias.shape, 1)
+    places = start + lax.broadcasted_iota(jnp.int32, bias.shape, 0)
+    bias[...] = jnp.where((key_places >= first) & (key_places <= places), 0.0, masked_score)
+    lanes = lax.broadcasted_iota(jnp.int32, deltas.shape, 1)
+    all_deltas = jnp.zeros(deltas.shape, jnp.float32)
+    for head in range(inner // size):
+        columns = slice(head * size, (head + 1) * size)
+        turned, outer = query[rows, columns], back[rows, columns]
+        scores = matmul_t(turned, keys[...]) * scale + bias[...]
+        probs = jnp.exp(scores - norms[rows, head : head + 1])
+        prob_grad = matmul_t(outer, values[...])
+        delta = jnp.sum(probs * prob_grad, axis=1, keepdims=True)
+        all_deltas = jnp.where(lanes == head, delta, all_deltas)
+        score_grad = (probs * (prob_grad - delta)).astype(low)
+        query_grad = matmul(score_grad, keys[...]) * scale
+        pre_grad[rows, columns] = turn(query_grad, cosine[rows], -sine[rows]).astype(low)
+    deltas[...] = all_deltas
+    deltas_t = jnp.transpose(deltas[...])
+    norms_t = jnp.transpose(norms[rows])
+    first = begin_row[:, rows]
+    key_places = lax.broadcasted_iota(jnp.int32, bias_t.shape, 0)
+    places = start + lax.broadcasted_iota(jnp.int32, bias_t.shape, 1)
+    bias_t[...] = jnp.where((key_places >= first) & (key_places <= places), 0.0, masked_score)
+    for head in range(inner // size):
+        columns = slice(head * size, (head + 1) * size)
+        turned, outer = query[rows, columns], back[rows, columns]
+        scores = matmul_t(keys[...], turned) * scale + bias_t[...]
+        probs = jnp.exp(scores - norms_t[head : head + 1])
+        prob_grad = matmul_t(values[...], outer)
+        score_grad = (probs * (prob_grad - deltas_t[head : head + 1])).astype(low)
+        key_grad[...] += matmul(score_grad, turned)
+        value_grad[...] += matmul(probs.astype(low), outer)
+
+
+def tail_kernel(
     packed,
-    marks,
-    router_input,
-    hidden,
-    scale,
-    gain,
+    marks_in,
+    router_input_in,
+    hidden_in,
+    group_one_t,
+    full_pre,
+    full_back,
+    shared_parts_in,
+    stream_in,
+    scale_two,
+    gain_ffn,
     stream_grad,
+    router_parts,
+    shared_grads,
+    query,
+    keys,
+    values_in,
+    attended,
+    norms,
+    cosine,
+    sine,
+    begin,
+    begin_row,
+    inputs,
+    scale_one,
+    gain_attn,
+    hidden_total,
+    result,
+    block_out,
     router,
-    grads,
-    group,
-    hidden_total,
-    gain_grad,
-    router_sum,
+    gain_attn_sum,
+    gain_ffn_sum,
     *refs,
 ):
-    pieces, scratch = refs[:2], refs[2:]
-    held, routed, branch, near, far, outgoing, load_sem, send, recv, own_sem = scratch[:10]
-    row_send, row_recv = scratch[10:12]
-    row, col, sibling, partner, _ = row_places()
-    scatter = ScatterSum(grads, scratch[12:])
-    greet([(sibling, col), (partner, col)])
-    greet(scatter.y_peers + scatter.z_peers + [scatter.x_peer])
-    steps = held.shape[0]
-    depth = held.shape[1]
+    pieces, scratch = refs[:5], refs[5:]
+    held, marks, router_input, hidden, rows_t, w_pre, w_back, shared_parts, stream = scratch[:9]
+    routed, group, back, pre_grad, bias, bias_t, deltas, key_grad, value_grad = scratch[9:18]
+    parts, near, far, outgoing, router_near, router_far, router_outgoing = scratch[18:25]
+    router_part, values, buffers, pre_grads, out_grads = scratch[25:30]
+    load_sem, branch_send, branch_recv, row_send, row_recv, gain_send, gain_recv = scratch[30:37]
+    pass_send, pass_recv = scratch[37:39]
+    shared_scatter = ScatterSum(shared_grads, scratch[39:50])
+    out_scatter = ScatterSum(out_grads, scratch[50:61])
+    pre_scatter = ScatterSum(pre_grads, scratch[61:72])
+    router_at = 72
+    low = jnp.bfloat16
+    row, col, sibling, partner, across = row_places()
+    row_peers = [(peer, col) for peer in (sibling, partner, across)]
+    greet(row_peers)
+    greet(pre_scatter.y_peers + pre_scatter.z_peers + [pre_scatter.x_peer])
+    steps, depth = held.shape[:2]
+    inner = query.shape[1]
+    sources = [packed.at[pl.ds(i * depth, depth)] for i in range(steps)]
+    targets = [held.at[i] for i in range(steps)]
+    sources[1:1] = [marks_in]
+    targets[1:1] = [marks]
+    sources += [router_input_in, hidden_in, full_back, shared_parts_in]
+    targets += [router_input, hidden, w_back, shared_parts]
+    sources += [full_pre, group_one_t, stream_in]
+    targets += [w_pre, rows_t, stream]
     loads = [
-        pltpu.make_async_copy(packed.at[pl.ds(i * depth, depth)], held.at[i], load_sem.at[i])
-        for i in range(steps)
+        pltpu.make_async_copy(source, target, load_sem.at[i])
+        for i, (source, target) in enumerate(zip(sources, targets))
     ]
     for load in loads:
         load.start()
-    await_greetings(9)
-    copies = row_sum_copies(router, near, far, outgoing, (row_send, row_recv), 0)
-    copies[0].start()
-    copies[1].start()
-    scatter.start()
-    row_sum_forward(router, near, outgoing, copies)
-
+    load_marks = loads.pop(1)
+    load_input, load_hidden, load_back, load_shared, load_pre, load_rows, load_stream = loads[
+        steps:
+    ]
+    await_greetings(10)
+
+    row_sems = (row_send, row_recv)
+    router_copies = row_sum_copies(
+        router_parts, router_near, router_far, router_outgoing, row_sems, 0
+    )
+    router_copies[0].start()
+    router_copies[1].start()
+    shared_scatter.start()
+    row_sum_forward(router_parts, router_near, router_outgoing, router_copies)
+
+    load_marks.wait()
     for i in range(steps):
         loads[i].wait()
         rows = slice(i * depth, (i + 1) * depth)
@@ -347,219 +473,88 @@
                     second = slice(j * QUARTER, (j + 1) * QUARTER)
                     found = found + matmul(marks[j + 1, :, rows], held[i, :, second])
             routed[:, columns] = found if i == 0 else routed[:, columns] + found
-
+    load_input.wait()
+    load_hidden.wait()
     incoming = router_input[...] + routed[...]
-    values = hidden[...]
-    factor = scale[...]
-    weighted = gain[...] * incoming
-    mean = jnp.mean(weighted * values, axis=1, keepdims=True)
+    state = hidden[...]
+    factor = scale_two[...]
+    weighted = gain_ffn[...] * incoming
+    mean = jnp.mean(weighted * state, axis=1, keepdims=True)
     total = (
         stream_grad[...].astype(jnp.float32)
         + factor * weighted
-        - values * (factor * factor * factor * mean)
+        - state * (factor * factor * factor * mean)
     )
     hidden_total[...] = total
-    branch[...] = total.astype(jnp.bfloat16)
-    far_rows, near_rows, onward = row_copies([branch], [group], send, recv)
+    group[row] = total.astype(low)
+    far_rows, near_rows, onward = row_copies([group.at[row]], [group], branch_send, branch_recv)
     far_rows[0].start()
     near_rows[0].start()
-    own = pltpu.make_async_copy(branch, group.at[row], own_sem)
-    own.start()
-    gain_grad[...] = jnp.sum(incoming * values * factor, axis=0, keepdims=True)
-    scatter.add_first(0)
-    scatter.add_first(1)
-    scatter.add_second()
-    router_sum[...] = row_sum_total(router, near, far, copies).astype(jnp.bfloat16)
+    values[0, 1:2] = jnp.sum(incoming * state * factor, axis=0, keepdims=True)
+
+    load_shared.wait()
+    shared_copies = row_sum_copies(
+        shared_parts, near.at[1], far.at[1], outgoing.at[1], row_sems, 3
+    )
+    shared_copies[0].start()
+    shared_copies[1].start()
+    router_sum = row_sum_total(router_parts, router_near, router_far, router_copies)
+    router_part[...] = router_sum.astype(low).reshape(router_part.shape)
+    router_scatter = RouterSum(router_part, router.at[row], scratch[router_at:])
+    router_scatter.start()
+    shared_scatter.add_first()
+    row_sum_forward(shared_parts, near.at[1], outgoing.at[1], shared_copies)
+    load_back.wait()
+    near_rows[0].wait_recv()
+    key_grad[...] = jnp.zeros_like(key_grad)
+    value_grad[...] = jnp.zeros_like(value_grad)
+    refs = (group, w_back, query, keys, values_in, norms, cosine, sine, begin, begin_row)
+    sums = (back, pre_grad, bias, bias_t, deltas, key_grad, value_grad)
+    chip = row // 2
+    chip_rows = bias.shape[0]
+    attention_back_rows(chip * chip_rows, refs, sums)
+    shared_scatter.add_second()
+    router_scatter.add_y()
     far_rows[0].wait_recv()
     onward[0].start()
-    scatter.add_third(pieces)
-    own.wait()
-    far_rows[0].wait_send()
-    near_rows[0].wait()
-    onward[0].wait()
-    for copy in copies:
-        copy.wait_send()
-    scatter.end()
-
-
-def token_back(packed, marks, router_input, hidden, scale, gain, stream_grad, router, grads, widths):
-    away = pl.BlockSpec(memory_space=pl.ANY)
-    space = pl.BlockSpec(memory_space=pltpu.VMEM)
-    _, rows, width = router.shape
-    tokens, model_width = hidden.shape
-    low = jnp.bfloat16
-    group, hidden_total, gain_grad, router_sum, *sums = pl.pallas_call(
-        token_back_kernel,
-        out_shape=[
-            jax.ShapeDtypeStruct((4, tokens, model_width), low),
-            jax.ShapeDtypeStruct((tokens, model_width), jnp.float32),
-            jax.ShapeDtypeStruct((1, model_width), jnp.float32),
-            jax.ShapeDtypeStruct((rows, width), low),
-        ]
-        + [jax.ShapeDtypeStruct((grads.shape[3], part), jnp.float32) for part in widths],
-        in_specs=[away] + [space] * 8,
-        out_specs=[away] + [space] * (3 + len(widths)),
-        scratch_shapes=[
-            pltpu.VMEM((4, packed.shape[0] // 4, packed.shape[1]), low),
-            pltpu.VMEM((tokens, model_width), jnp.float32),
-            pltpu.VMEM((tokens, model_width), low),
-            pltpu.VMEM((2, rows, width), low),
-            pltpu.VMEM((rows, width), low),
-            pltpu.VMEM((rows, width), low),
-            pltpu.SemaphoreType.DMA((4,)),
-            pltpu.SemaphoreType.DMA((3,)),
-            pltpu.SemaphoreType.DMA((3,)),
-            pltpu.SemaphoreType.DMA,
-            pltpu.SemaphoreType.DMA((3,)),
-            pltpu.SemaphoreType.DMA((3,)),
-            *ScatterSum.scratch(grads),
-        ],
-        compiler_params=pltpu.CompilerParams(
-            collective_id=1, has_side_effects=True, vmem_limit_bytes=48 << 20
-        ),
-        cost_estimate=pl.CostEstimate(flops=0, bytes_accessed=100 << 20, transcendentals=0),
-        name="token_back",
-    )(packed, marks, router_input, hidden, scale, gain, stream_grad, router, grads)
-    return group.reshape(-1, model_width), hidden_total, gain_grad, router_sum, sums
-
-
-def finish_kernel(
-    group_branch,
-    group_one_t,
-    full_pre,
-    full_back,
-    query,
-    keys,
-    values_in,
-    attended,
-    norms,
-    cosine,
-    sine,
-    begin,
-    begin_row,
-    shared_parts,
-    router_part,
-    stream,
-    inputs,
-    scale,
-    gain,
-    gain_ffn,
-    result,
-    block_out,
-    router,
-    gains,
-    *refs,
-):
-    pieces, scratch = refs[:3], refs[3:]
-    near, far, outgoing, values, buffers, router_in, router_own = scratch[:7]
-    row_send, row_recv, gain_send, gain_recv, own_sem = scratch[7:12]
-    col_send, col_recv, pass_send, pass_recv = scratch[12:16]
-    branch, rows_t, w_pre, w_back, pre_grad, back, bias, deltas, parts, load_sem = scratch[16:26]
-    pre_grads, out_grads = scratch[26:28]
-    pre_scatter = ScatterSum(pre_grads, scratch[28:39])
-    out_scatter = ScatterSum(out_grads, scratch[39:])
-    row, col, sibling, partner, across = row_places()
-    row_peers = [(peer, col) for peer in (sibling, partner, across)]
-
-    greet(row_peers)
-    barrier = pltpu.get_barrier_semaphore()
-
-    def greet_col(step, carry):
-        peer = (row, lax.rem(col + step, 32))
-        pl.semaphore_signal(barrier, inc=1, device_id=peer, device_id_type=MESH)
-        return carry
-
-    lax.fori_loop(1, 32, greet_col, 0)
-    pre_width, inner = w_pre.shape[1], w_back.shape[1]
-    loads = [
-        pltpu.make_async_copy(group_branch, branch, load_sem.at[0]),
-        pltpu.make_async_copy(full_back.at[:, pl.ds(0, inner)], w_back, load_sem.at[1]),
-        pltpu.make_async_copy(group_one_t, rows_t, load_sem.at[2]),
-        pltpu.make_async_copy(full_pre, w_pre, load_sem.at[3]),
-    ]
-    for load in loads:
-        load.start()
-    loads[0].wait()
-    blocks, depth = 4, branch.shape[1] // 4
+    onward[0].wait_recv()
 
     def keep(target, block, rows):
-        target[block // 2, 2 * (block % 2) : 2 * (block % 2) + 2] = rows.astype(
-            jnp.bfloat16
-        ).reshape(2, 4, 64, rows.shape[1])
-
+        shaped = rows.astype(low).reshape(2, 4, 64, rows.shape[1])
+        target[block // 2, 2 * (block % 2) : 2 * (block % 2) + 2] = shaped
+
+    blocks, width = 4, group.shape[2] // 4
     for block in range(blocks):
-        columns = slice(block * depth, (block + 1) * depth)
-        keep(out_grads, block, outer_sum(branch[:, columns], attended[...]))
-    loads[1].wait()
-    back[...] = matmul(branch[...], w_back[...]).astype(jnp.bfloat16)
-    await_greetings(34)
-    shared_copies = row_sum_copies(
-        shared_parts, near.at[1], far.at[1], outgoing.at[1], (row_send, row_recv), 3
-    )
-    shared_copies[0].start()
-    shared_copies[1].start()
-
-    def push(source, target, at):
-        def step(i, carry):
-            peer = lax.rem(col + i, 32)
-            pltpu.make_async_remote_copy(
-                src_ref=source(peer),
-                dst_ref=target,
-                send_sem=col_send.at[at],
-                recv_sem=col_recv.at[at],
-                device_id=(row, peer),
-                device_id_type=MESH,
-            ).start()
-            return carry
-
-        lax.fori_loop(1, 32, step, 0)
-
-    def await_pushes(target, sem):
-        others = target.at[pl.ds(0, 31)]
-        pltpu.make_async_copy(others, others, sem).wait()
-
-    push(lambda peer: router_part.at[peer], router_in.at[col], 0)
-    router_in[col] = router_part[col]
+        columns = slice(block * width, (block + 1) * width)
+        rows = group[:, :, columns].reshape(4 * group.shape[1], width)
+        keep(out_grads, block, outer_sum(rows, attended[...]))
     out_scatter.start()
-    row_sum_forward(shared_parts, near.at[1], outgoing.at[1], shared_copies)
-    saved = (query, keys, values_in, back, norms, cosine, sine)
-    attention_back_queries(*saved, begin, (pre_grad, bias, deltas))
-    await_pushes(router_in, col_recv.at[0])
-    router_own[...] = jnp.sum(router_in[...].astype(jnp.float32), axis=0).astype(jnp.bfloat16)
-    push(lambda peer: router_own, router.at[row, col], 1)
-    own = pltpu.make_async_copy(router_own, router.at[row, col], own_sem)
-    own.start()
-    out_scatter.add_first(0)
-    attention_back_keys(*saved, begin_row, (pre_grad, bias, deltas))
-    loads[3].wait()
-    parts[...] = matmul_t(pre_grad[...], w_pre[...]).astype(jnp.bfloat16).reshape(parts.shape)
-    attn_copies = row_sum_copies(
-        parts, near.at[0], far.at[0], outgoing.at[0], (row_send, row_recv), 0
-    )
+    router_scatter.add_z()
+    attention_back_rows((1 - chip) * chip_rows, refs, sums)
+    size = keys.shape[1]
+    scale = size ** (-0.5)
+    pre_grad[:, inner : inner + size] = turn(key_grad[...] * scale, cosine[...], -sine[...]).astype(
+        low
+    )
+    pre_grad[:, inner + size :] = value_grad[...].astype(low)
+    load_pre.wait()
+    load_rows.wait()
+    block_rows = parts.shape[1]
+    for block in range(4):
+        rows = slice(block * block_rows, (block + 1) * block_rows)
+        parts[block] = matmul_t(pre_grad[rows], w_pre[...]).astype(low)
+    attn_copies = row_sum_copies(parts, near.at[0], far.at[0], outgoing.at[0], row_sems, 6)
     attn_copies[0].start()
     attn_copies[1].start()
-    out_scatter.add_first(1)
     row_sum_forward(parts, near.at[0], outgoing.at[0], attn_copies)
-    loads[2].wait()
     for block in range(blocks):
-        rows = slice(block * depth, (block + 1) * depth)
+        rows = slice(block * width, (block + 1) * width)
         keep(pre_grads, block, matmul(rows_t[rows], pre_grad[...]))
     pre_scatter.start()
-    own.wait()
-    await_pushes(router.at[row], col_recv.at[1])
-    far_rows, near_rows, onward = row_copies([router.at[row]], [router], pass_send, pass_recv)
-    far_rows[0].start()
-    near_rows[0].start()
-    out_scatter.add_second()
-
-    incoming = row_sum_total(parts, near.at[0], far.at[0], attn_copies)
-    rows = inputs[...].astype(jnp.float32)
-    factor = scale[...]
-    weighted = gain[...] * incoming
-    mean = jnp.mean(weighted * rows, axis=1, keepdims=True)
-    result[...] = factor * weighted - rows * (factor * factor * factor * mean)
-    values[0, 0:1] = jnp.sum(incoming * rows * factor, axis=0, keepdims=True)
-    values[0, 1:2] = gain_ffn[...]
+    router_scatter.add_x()
+    out_scatter.add_first()
+    shared_scatter.add_third(pieces[3:])
+    router_scatter.spread_z()
 
     gain_sems = (gain_send, gain_recv)
     gain_copies = []
@@ -581,97 +576,133 @@
             total = total + buffers[at + i]
         values[stage + 1] = total
 
+    incoming = row_sum_total(parts, near.at[0], far.at[0], attn_copies)
+    first = inputs[...].astype(jnp.float32)
+    factor = scale_one[...]
+    weighted = gain_attn[...] * incoming
+    mean = jnp.mean(weighted * first, axis=1, keepdims=True)
+    result[...] = factor * weighted - first * (factor * factor * factor * mean)
+    values[0, 0:1] = jnp.sum(incoming * first * factor, axis=0, keepdims=True)
     start_gains(0)
+    router_scatter.spread_y()
+    out_scatter.add_second()
+    load_stream.wait()
     shared = row_sum_total(shared_parts, near.at[1], far.at[1], shared_copies)
-    block_out[...] = (stream[...] + shared).astype(jnp.bfloat16)
-    out_scatter.add_third(pieces[2:])
+    block_out[...] = (stream[...] + shared).astype(low)
     add_gains(0)
     start_gains(1)
-    pre_scatter.add_first(0)
+    pre_scatter.add_first()
+    router_scatter.wait(5)
+    router_rows = row_copies([router.at[row]], [router], pass_send, pass_recv)
+    router_rows[0][0].start()
+    router_rows[1][0].start()
+    out_scatter.add_third(pieces[2:3])
     add_gains(1)
     start_gains(2)
-    pre_scatter.add_first(1)
-    far_rows[0].wait_recv()
-    onward[0].start()
+    pre_scatter.add_second()
     add_gains(2)
     start_gains(3)
-    pre_scatter.add_second()
+    router_rows[0][0].wait_recv()
+    router_rows[2][0].start()
+    pre_scatter.add_third(pieces[:2])
     add_gains(3)
-    gains[...] = values[4]
-    pre_scatter.add_third(pieces[:2])
-    await_pushes(router_in, col_send.at[0])
-    await_pushes(router.at[row], col_send.at[1])
+    gain_attn_sum[...] = values[4, 0:1]
+    gain_ffn_sum[...] = values[4, 1:2]
+
+    router_scatter.end()
     far_rows[0].wait_send()
-    near_rows[0].wait()
-    onward[0].wait()
-    for done in [*attn_copies, *shared_copies, *gain_copies]:
+    near_rows[0].wait_send()
+    onward[0].wait_send()
+    router_rows[0][0].wait_send()
+    router_rows[1][0].wait()
+    router_rows[2][0].wait()
+    for done in [*router_copies, *attn_copies, *shared_copies, *gain_copies]:
         done.wait_send()
-    pre_scatter.end()
-    out_scatter.end()
-
-
-def finish(group_branch, group_one_t, weights, kept, tables, rest, widths):
+    for scatter in (shared_scatter, out_scatter, pre_scatter):
+        scatter.end()
+
+
+def tail(streamed, local, kept, tables, last, widths):
     space = pl.BlockSpec(memory_space=pltpu.VMEM)
     away = pl.BlockSpec(memory_space=pl.ANY)
     low = jnp.bfloat16
-    shared_parts, router_part, stream, inputs = rest[:4]
-    rows, width = inputs.shape
+    packed, marks = streamed[:2]
+    router_parts, shared_grads = local[3:]
+    rows, width = last[0].shape
     tokens = 4 * rows
-    share = router_part.shape[1:]
+    _, router_rows, experts = router_parts.shape
+    share = (router_rows // 32, experts)
+    size = kept[1].shape[1]
     inner = kept[0].shape[1]
     pre_width = widths[0] + widths[1]
     shard = width // 32
     pre_grads = jax.ShapeDtypeStruct((2, 4, 4, shard, pre_width), low)
     out_grads = jax.ShapeDtypeStruct((2, 4, 4, shard, inner), low)
+    dma = pltpu.SemaphoreType.DMA
     return pl.pallas_call(
-        finish_kernel,
+        tail_kernel,
         out_shape=[
             jax.ShapeDtypeStruct((rows, width), jnp.float32),
+            jax.ShapeDtypeStruct((rows, width), jnp.float32),
             jax.ShapeDtypeStruct((rows, width), low),
-            jax.ShapeDtypeStruct((4, 32, *share), low),
-            jax.ShapeDtypeStruct((2, width), jnp.float32),
+            jax.ShapeDtypeStruct((4, 2, 4, 4, *share), low),
+            jax.ShapeDtypeStruct((1, width), jnp.float32),
+            jax.ShapeDtypeStruct((1, width), jnp.float32),
         ]
         + [jax.ShapeDtypeStruct((shard, part), jnp.float32) for part in widths],
-        in_specs=[away] * 4 + [space] * 16,
-        out_specs=[space, space, away, space] + [space] * len(widths),
+        in_specs=[away] * 9 + [space] * 17,
+        out_specs=[space] * (6 + len(widths)),
         scratch_shapes=[
+            pltpu.VMEM((4, packed.shape[0] // 4, packed.shape[1]), low),
+            pltpu.VMEM(marks.shape, low),
+            pltpu.VMEM((rows, width), jnp.float32),
+            pltpu.VMEM((rows, width), jnp.float32),
+            pltpu.VMEM((width, tokens), low),
+            pltpu.VMEM((width, pre_width), low),
+            pltpu.VMEM((width, inner), low),
+            pltpu.VMEM((4, rows, width), low),
+            pltpu.VMEM((rows, width), jnp.float32),
+            pltpu.VMEM((rows, width), jnp.float32),
+            pltpu.VMEM((4, rows, width), low),
+            pltpu.VMEM((tokens, inner), low),
+            pltpu.VMEM((tokens, pre_width), low),
+            pltpu.VMEM((tokens // 2, tokens), jnp.float32),
+            pltpu.VMEM((tokens, tokens // 2), jnp.float32),
+            pltpu.VMEM((tokens // 2, 128), jnp.float32),
+            pltpu.VMEM((tokens, size), jnp.float32),
+            pltpu.VMEM((tokens, size), jnp.float32),
+            pltpu.VMEM((4, rows, width), low),
             pltpu.VMEM((2, 2, rows, width), low),
             pltpu.VMEM((2, rows, width), low),
             pltpu.VMEM((2, rows, width), low),
+            pltpu.VMEM((2, router_rows, experts), low),
+            pltpu.VMEM((router_rows, experts), low),
+            pltpu.VMEM((router_rows, experts), low),
+            pltpu.VMEM((2, 4, 4, *share), low),
             pltpu.VMEM((5, 2, width), jnp.float32),
             pltpu.VMEM((10, 2, width), jnp.float32),
-            pltpu.VMEM((32, *share), low),
-            pltpu.VMEM(share, low),
-            pltpu.SemaphoreType.DMA((6,)),
-            pltpu.SemaphoreType.DMA((6,)),
-            pltpu.SemaphoreType.DMA((10,)),
-            pltpu.SemaphoreType.DMA((10,)),
-            pltpu.SemaphoreType.DMA,
-            pltpu.SemaphoreType.DMA((2,)),
-            pltpu.SemaphoreType.DMA((2,)),
-            pltpu.SemaphoreType.DMA((3,)),
-            pltpu.SemaphoreType.DMA((3,)),
-            pltpu.VMEM((tokens, width), low),
-            pltpu.VMEM((width, tokens), low),
-            pltpu.VMEM((width, pre_width), low),
-            pltpu.VMEM((width, inner), low),
-            pltpu.VMEM((tokens, pre_width), low),
-            pltpu.VMEM((tokens, inner), low),
-            pltpu.VMEM((tokens, tokens), jnp.float32),
-            pltpu.VMEM((tokens, 128), jnp.float32),
-            pltpu.VMEM((4, rows, width), low),
-            pltpu.SemaphoreType.DMA((4,)),
             pltpu.VMEM(pre_grads.shape, low),
             pltpu.VMEM(out_grads.shape, low),
+            dma((12,)),
+            dma((3,)),
+            dma((3,)),
+            dma((9,)),
+            dma((9,)),
+            dma((10,)),
+            dma((10,)),
+            dma((3,)),
+            dma((3,)),
+            *ScatterSum.scratch(shared_grads),
+            *ScatterSum.scratch(out_grads),
             *ScatterSum.scratch(pre_grads),
-            *ScatterSum.scratch(out_grads),
+            *RouterSum.scratch(share),
         ],
         compiler_params=pltpu.CompilerParams(
             collective_id=16, has_side_effects=True, vmem_limit_bytes=60 << 20
         ),
-        cost_estimate=pl.CostEstimate(flops=0, bytes_accessed=200 << 20, transcendentals=0),
-        name="finish",
-    )(group_branch, group_one_t, *weights, *kept, *tables, *rest)
+        cost_estimate=pl.CostEstimate(flops=0, bytes_accessed=300 << 20, transcendentals=0),
+        name="tail",
+    )(*streamed, *local, *kept, *tables, *last)
 
 
 def packed_places(shape, axis):
@@ -892,76 +923,65 @@
 class Gather:
     def __init__(self, mine, full, send_sem, recv_sem):
         self.mine, self.full = mine, full
-        self.send_sem, self.recv_sem = send_sem, recv_sem
-        self.row, self.col = lax.axis_index("row"), lax.axis_index("col")
-        self.x, self.z, self.y = self.col // 16, lax.rem(self.col // 4, 4), lax.rem(self.col, 4)
-        self.z_near = [lax.rem(self.z + i, 4) for i in (1, 3, 2)]
-        self.y_near = [lax.rem(self.y + i, 4) for i in (1, 3, 2)]
-        self.z_peers = [self.place(self.x, z, self.y) for z in self.z_near]
-        self.y_peers = [self.place(self.x, self.z, y) for y in self.y_near]
-        self.x_peer = self.place(1 - self.x, self.z, self.y)
-
-    @staticmethod
-    def place(x, z, y):
-        return x * 16 + z * 4 + y
+        self.sems = (send_sem, recv_sem)
+        row, col = lax.axis_index("row"), lax.axis_index("col")
+        x, z, y = col // 16, lax.rem(col // 4, 4), lax.rem(col, 4)
+        self.place = (x, z, y)
+        self.z_peers = [(row, x * 16 + lax.rem(z + i, 4) * 4 + y) for i in (1, 3, 2)]
+        self.y_peers = [(row, x * 16 + z * 4 + lax.rem(y + i, 4)) for i in (1, 3, 2)]
+        self.x_peer = (row, (1 - x) * 16 + z * 4 + y)
+        self.copies = {}
 
     def rows(self, half):
-        half_rows = self.full.shape[1] // 2
+        half_rows = self.full.shape[3] // 2
         return pl.ds(half * half_rows, half_rows)
 
-    def pass_on(self, owner, half, peers, own=False):
-        target = self.full.at[owner, self.rows(half)]
-        for peer in peers:
-            pltpu.make_async_remote_copy(
-                src_ref=self.mine.at[self.rows(half)] if own else target,
-                dst_ref=target,
-                send_sem=self.send_sem,
-                recv_sem=self.recv_sem.at[half * 32 + owner],
-                device_id=(self.row, peer),
-                device_id_type=MESH,
-            ).start()
-
-    def await_half(self, owner, half):
-        target = self.full.at[owner, self.rows(half)]
-        pltpu.make_async_copy(target, target, self.recv_sem.at[half * 32 + owner]).wait()
+    def send(self, key, source, target, peers):
+        at = 1 + 3 * len(self.copies) - 3 if self.copies else 0
+        copies = [
+            remote(source, target, self.sems, at + i, peer) for i, peer in enumerate(peers)
+        ]
+        for copy in copies:
+            copy.start()
+        self.copies[key] = copies
+
+    def wait(self, *keys):
+        for key in keys:
+            for copy in self.copies[key]:
+                copy.wait_recv()
 
     def start(self):
-        for half in range(2):
-            self.pass_on(self.col, half, [self.x_peer], own=True)
-        self.pass_on(self.col, 0, self.z_peers, own=True)
-        self.pass_on(self.col, 1, self.y_peers, own=True)
+        x, z, y = self.place
+        self.send("x", self.mine, self.full.at[x, z, y], [self.x_peer])
+        for half, peers in enumerate((self.z_peers, self.y_peers)):
+            rows = self.rows(half)
+            target = self.full.at[x, z, y, rows]
+            self.send((0, half), self.mine.at[rows], target, peers)
 
     def second(self):
-        self.await_half(self.x_peer, 0)
-        self.pass_on(self.x_peer, 0, self.z_peers)
-        self.await_half(self.x_peer, 1)
-        self.pass_on(self.x_peer, 1, self.y_peers)
-        self.pass_on(self.col, 0, self.y_peers, own=True)
-        self.pass_on(self.col, 1, self.z_peers, own=True)
-        self.pass_on(self.x_peer, 0, self.y_peers)
-        self.pass_on(self.x_peer, 1, self.z_peers)
+        x, z, y = self.place
+        self.wait("x")
+        for half, peers in enumerate((self.z_peers, self.y_peers)):
+            target = self.full.at[1 - x, z, y, self.rows(half)]
+            self.send((1, half), target, target, peers)
 
     def third(self):
-        for i in range(3):
-            for x in (self.x, 1 - self.x):
-                owner = self.place(x, self.z_near[i], self.y)
-                self.await_half(owner, 0)
-                self.pass_on(owner, 0, self.y_peers)
-                owner = self.place(x, self.z, self.y_near[i])
-                self.await_half(owner, 1)
-                self.pass_on(owner, 1, self.z_peers)
+        x, z, y = self.place
+        for turn, owner_x in enumerate((x, 1 - x)):
+            self.wait((turn, 0))
+            target = self.full.at[owner_x, :, y, self.rows(0)]
+            self.send((2 + turn, 0), target, target, self.y_peers)
+            self.wait((turn, 1))
+            target = self.full.at[owner_x, z, :, self.rows(1)]
+            self.send((2 + turn, 1), target, target, self.z_peers)
 
     def await_all(self):
-        for x in (self.x, 1 - self.x):
-            for i in range(4):
-                for j in range(3):
-                    z, y = lax.rem(self.z + i, 4), lax.rem(self.y + i, 4)
-                    self.await_half(self.place(x, z, self.y_near[j]), 0)
-                    self.await_half(self.place(x, self.z_near[j], y), 1)
+        self.wait((2, 0), (2, 1), (3, 0), (3, 1))
 
     def end(self):
-        sent = self.full.at[pl.ds(0, 31)]
-        pltpu.make_async_copy(sent, sent, self.send_sem).wait()
+        for copies in self.copies.values():
+            for copy in copies:
+                copy.wait_send()
 
 
 def head_kernel(
@@ -979,6 +999,7 @@
     w_shared_out,
     full_pre,
     full_back,
+    full_shared,
     group_one,
     group_grad,
     scale_one,
@@ -999,25 +1020,27 @@
     order,
     *scratch,
 ):
-    mine_pre, mine_back, normed, rows, w_pre, w_back, pre, bias, parts = scratch[:9]
-    near, far, outgoing, marks, staged = scratch[9:14]
-    gather_send, recv_pre, recv_back, own_sem, row_send, row_recv = scratch[14:20]
+    mine_pre, mine_back, mine_shared, normed, rows, w_pre, w_back, pre, bias, parts = scratch[:10]
+    near, far, outgoing, marks, staged = scratch[10:15]
+    gather_send, gather_recv, own_sem, row_send, row_recv = scratch[15:20]
     sum_send, sum_recv, load_sem, pack_sem = scratch[20:]
     low = jnp.bfloat16
     row, col, sibling, partner, _ = row_places()
     gathers = [
-        Gather(mine_pre, full_pre, gather_send.at[0], recv_pre),
-        Gather(mine_back, full_back, gather_send.at[1], recv_back),
+        Gather(mine_pre, full_pre, gather_send.at[0], gather_recv.at[0]),
+        Gather(mine_back, full_back, gather_send.at[1], gather_recv.at[1]),
+        Gather(mine_shared, full_shared, gather_send.at[2], gather_recv.at[2]),
     ]
-    near_peers = gathers[0].z_peers + gathers[0].y_peers + [gathers[0].x_peer]
-    greet([(row, peer) for peer in near_peers])
+    place = gathers[0].place
+    greet(gathers[0].z_peers + gathers[0].y_peers + [gathers[0].x_peer])
     greet([(sibling, col), (partner, col)])
-    start = 0
-    for mine, shards in ((mine_pre, (w_query, w_keyval)), (mine_back, (w_out, w_shared_in, w_shared_out))):
+    pairs = ((mine_pre, (w_query, w_keyval)), (mine_shared, (w_shared_in, w_shared_out)))
+    for mine, shards in pairs:
         start = 0
         for shard in shards:
             mine[:, start : start + shard.shape[1]] = shard[...]
             start += shard.shape[1]
+    mine_back[...] = w_out[...]
     first = inputs[...].astype(jnp.float32)
     factor = lax.rsqrt(jnp.mean(first * first, axis=1, keepdims=True) + epsilon)
     scale_one[...] = factor
@@ -1025,8 +1048,9 @@
     own = [
         pltpu.make_async_copy(normed, group_one.at[row], own_sem.at[0]),
         pltpu.make_async_copy(grads, group_grad.at[row], own_sem.at[1]),
-        pltpu.make_async_copy(mine_pre, full_pre.at[col], own_sem.at[2]),
-        pltpu.make_async_copy(mine_back, full_back.at[col], own_sem.at[3]),
+        pltpu.make_async_copy(mine_pre, full_pre.at[place], own_sem.at[2]),
+        pltpu.make_async_copy(mine_back, full_back.at[place], own_sem.at[3]),
+        pltpu.make_async_copy(mine_shared, full_shared.at[place], own_sem.at[4]),
     ]
     for copy in own:
         copy.start()
@@ -1038,8 +1062,11 @@
     far_rows[0].start()
     near_rows[0].start()
     gathers[1].start()
+    gathers[2].start()
     gathers[0].second()
     gathers[1].second()
+    for copy in own[2:]:
+        copy.wait()
     gathers[0].third()
     far_rows[1].start()
     near_rows[1].start()
@@ -1091,15 +1118,12 @@
     onward[0].start()
     gathers[0].await_all()
     own[0].wait()
-    own[2].wait()
     near_rows[0].wait_recv()
     onward[0].wait_recv()
     loads = [
         pltpu.make_async_copy(group_one, rows, load_sem.at[0]),
         pltpu.make_async_copy(full_pre, w_pre, load_sem.at[1]),
-        pltpu.make_async_copy(
-            full_back.at[:, :, pl.ds(0, w_back.shape[2])], w_back, load_sem.at[2]
-        ),
+        pltpu.make_async_copy(full_back, w_back, load_sem.at[2]),
     ]
     loads[0].start()
     loads[1].start()
@@ -1107,7 +1131,7 @@
     loads[1].wait()
     width = inputs.shape[1]
     pre[...] = matmul(
-        rows[...].reshape(tokens, width), w_pre[...].reshape(width, w_pre.shape[2])
+        rows[...].reshape(tokens, width), w_pre[...].reshape(width, w_pre.shape[4])
     )
     size = keys.shape[1]
     inner = query.shape[1]
@@ -1126,10 +1150,7 @@
         attended[:, columns] = matmul(weights, values[...]).astype(low)
         log_totals = jnp.where(lanes == head, highest + jnp.log(total), log_totals)
     norms[...] = log_totals
-    far_rows[1].wait_recv()
-    onward[1].start()
     gathers[1].await_all()
-    own[3].wait()
     loads[2].start()
     loads[2].wait()
     parts[...] = (
@@ -1139,7 +1160,11 @@
     copies = row_sum_copies(parts, near, far, outgoing, (sum_send, sum_recv), 0)
     copies[0].start()
     copies[1].start()
+    gathers[2].second()
     row_sum_forward(parts, near, outgoing, copies)
+    far_rows[1].wait_recv()
+    onward[1].start()
+    gathers[2].third()
     total = inputs[...].astype(jnp.float32) + row_sum_total(parts, near, far, copies)
     hidden[...] = total
     factor = lax.rsqrt(jnp.mean(total * total, axis=1, keepdims=True) + epsilon)
@@ -1158,6 +1183,7 @@
 
     lax.fori_loop(0, code.shape[0], pack, 0)
 
+    gathers[2].await_all()
     own[1].wait()
     near_rows[0].wait_send()
     near_rows[1].wait()
@@ -1181,7 +1207,7 @@
     shard_rows = shards[0].shape[0]
     inner = shards[0].shape[1]
     pre_width = inner + shards[1].shape[1]
-    back_width = sum(part.shape[1] for part in shards[2:])
+    shared_width = shards[3].shape[1] + shards[4].shape[1]
     blocks = expert_count // BLOCK_EXPERTS
     spread = np.arange(size // 2, dtype=np.float32) * np.float32(2.0 / size)
     frequency = np.float32(rope_base) ** (-spread)
@@ -1193,8 +1219,9 @@
     return pl.pallas_call(
         head_kernel,
         out_shape=[
-            full((32, shard_rows, pre_width), low),
-            full((32, shard_rows, back_width), low),
+            full((2, 4, 4, shard_rows, pre_width), low),
+            full((2, 4, 4, shard_rows, inner), low),
+            full((2, 4, 4, shard_rows, shared_width), low),
             full((4, rows, width), low),
             full((4, rows, width), low),
             full((rows, 1), jnp.float32),
@@ -1217,14 +1244,15 @@
         in_specs=[space] * 3
         + [away, pl.BlockSpec(memory_space=pltpu.SMEM)]
         + [space] * (2 + len(shards)),
-        out_specs=[away] * 4 + [space] * 13 + [away] + [space] * 2,
+        out_specs=[away] * 5 + [space] * 13 + [away] + [space] * 2,
         scratch_shapes=[
             pltpu.VMEM((shard_rows, pre_width), low),
-            pltpu.VMEM((shard_rows, back_width), low),
+            pltpu.VMEM((shard_rows, inner), low),
+            pltpu.VMEM((shard_rows, shared_width), low),
             pltpu.VMEM((rows, width), low),
             pltpu.VMEM((4, rows, width), low),
-            pltpu.VMEM((32, shard_rows, pre_width), low),
-            pltpu.VMEM((32, shard_rows, inner), low),
+            pltpu.VMEM((2, 4, 4, shard_rows, pre_width), low),
+            pltpu.VMEM((2, 4, 4, shard_rows, inner), low),
             pltpu.VMEM((tokens, pre_width), jnp.float32),
             pltpu.VMEM((tokens, tokens), jnp.float32),
             pltpu.VMEM((4, rows, width), low),
@@ -1233,10 +1261,9 @@
             pltpu.VMEM((rows, width), low),
             pltpu.VMEM((blocks, 3, BLOCK, 2 * rows), low),
             pltpu.VMEM((blocks, BLOCK, 3 * QUARTER), low),
-            pltpu.SemaphoreType.DMA((2,)),
-            pltpu.SemaphoreType.DMA((64,)),
-            pltpu.SemaphoreType.DMA((64,)),
-            pltpu.SemaphoreType.DMA((4,)),
+            pltpu.SemaphoreType.DMA((3, 25)),
+            pltpu.SemaphoreType.DMA((3, 25)),
+            pltpu.SemaphoreType.DMA((5,)),
             pltpu.SemaphoreType.DMA((6,)),
             pltpu.SemaphoreType.DMA((6,)),
             pltpu.SemaphoreType.DMA((3,)),
@@ -1250,6 +1277,21 @@
         cost_estimate=pl.CostEstimate(flops=0, bytes_accessed=300 << 20, transcendentals=0),
         name="head",
     )(inputs, gain_attn, gain_ffn, grads, lengths, routes, frequency, *shards)
+
+
+def side_by_side_kernel(first, second, both):
+    both[:, : first.shape[1]] = first[...]
+    both[:, first.shape[1] :] = second[...]
+
+
+def side_by_side(first, second):
+    shape = (first.shape[0], first.shape[1] + second.shape[1])
+    return pl.pallas_call(
+        side_by_side_kernel,
+        out_shape=jax.ShapeDtypeStruct(shape, first.dtype),
+        cost_estimate=pl.CostEstimate(flops=0, bytes_accessed=3 << 20, transcendentals=0),
+        name="side_by_side",
+    )(first, second)
 
 
 def exchange(packed):
@@ -1286,6 +1328,7 @@
     (
         full_pre,
         full_back,
+        full_shared,
         group_one,
         group_grad,
         scale_one,
@@ -1311,13 +1354,14 @@
         w_keyval.shape[2] // 2,
         expert_count,
     )
-    full_pre, full_back, group_one, group_grad = (
-        part.reshape(-1, part.shape[2]) for part in (full_pre, full_back, group_one, group_grad)
+    full_pre, full_back, full_shared, group_one, group_grad = (
+        part.reshape(-1, part.shape[-1])
+        for part in (full_pre, full_back, full_shared, group_one, group_grad)
     )
     received = exchange(send_rows)
-    shared_start, shared_width = w_out.shape[1], w_shared_out.shape[1]
-    full_shared_in = full_back[:, shared_start : shared_start + 2 * shared_width]
-    full_shared_out = full_back[:, shared_start + 2 * shared_width :]
+    shared_width = w_shared_out.shape[1]
+    full_shared_in = full_shared[:, : 2 * shared_width]
+    full_shared_out = full_shared[:, 2 * shared_width :]
 
     logits = matmul(normed_two, w_router)
     scores_sig = jnp.where(order >= 0.0, jax.nn.sigmoid(logits), 0.0)
@@ -1338,12 +1382,9 @@
     shared_pre_grad = jnp.concatenate(
         [shared_hidden_grad * shared_up * shared_slope, shared_hidden_grad * shared_act], axis=1
     ).astype(jnp.bfloat16)
-    shared_grads = jnp.concatenate(
-        [
-            outer_sum(group_two, shared_pre_grad).astype(jnp.bfloat16),
-            outer_sum(group_grad, shared_hidden).astype(jnp.bfloat16),
-        ],
-        axis=1,
+    shared_grads = side_by_side(
+        outer_sum(group_two, shared_pre_grad).astype(jnp.bfloat16),
+        outer_sum(group_grad, shared_hidden).astype(jnp.bfloat16),
     )
     shared_parts = matmul_t(shared_hidden, full_shared_out).astype(jnp.bfloat16)
     shared_input = lax.psum_scatter(
@@ -1400,47 +1441,42 @@
     router_input, router_parts, stream, shared_grads, group_one_t, marks = shadowed
 
     widths = [part.shape[1] for part in shards]
-    group_branch, hidden_total, gain_ffn_grad, router_sum, shared_sums = token_back(
-        returned_grad,
-        marks,
-        router_input,
-        hidden_state,
-        scale_two,
-        gain_ffn[None],
-        grad_low,
-        router_parts,
-        shared_grads.reshape(2, 4, 4, -1, shared_grads.shape[1]),
-        widths[3:],
-    )
-    input_back, block_out, router_sum, gain_sums, *sums = finish(
-        group_branch,
-        group_one_t,
-        (full_pre, full_back),
+    hidden_total, input_back, block_out, router_sum, gain_attn_sum, gain_ffn_sum, *sums = tail(
+        (
+            returned_grad,
+            marks,
+            router_input,
+            hidden_state,
+            group_one_t,
+            full_pre,
+            full_back,
+            shared_parts.reshape(row_count, rows_dev, model_width),
+            stream,
+        ),
+        (
+            scale_two,
+            gain_ffn[None],
+            grad_low,
+            router_parts,
+            shared_grads.reshape(2, 4, 4, -1, shared_grads.shape[1]),
+        ),
         kept,
         (cosine, sine_table, begin, begin_row),
-        (
-            shared_parts.reshape(row_count, rows_dev, model_width),
-            router_sum.reshape(32, -1, expert_count),
-            stream,
-            inputs,
-            scale_one,
-            gain_attn[None],
-            gain_ffn_grad,
-        ),
-        widths[:3],
+        (inputs, scale_one, gain_attn[None]),
+        widths,
     )
     sums = [
         part.reshape(like.shape)
-        for part, like in zip(sums + shared_sums, (w_query, w_keyval, w_out, w_shared_in, w_shared_out))
+        for part, like in zip(sums, (w_query, w_keyval, w_out, w_shared_in, w_shared_out))
     ]
     return (
         block_out.reshape(1, rows_dev, model_width),
         (hidden_total + input_back).reshape(1, rows_dev, model_width),
-        gain_sums[0],
+        gain_attn_sum[0],
         sums[0],
         sums[1],
         sums[2],
-        gain_sums[1],
+        gain_ffn_sum[0],
         sums[3],
         sums[4],
         router_sum.reshape(model_width, expert_count).astype(jnp.float32),

time: 581 us -> 561 us (0.966)
  the two profiles are of different devices: /device:TPU:4 before, /device:TPU:1 now
where the time goes in v6:
time: 561 us; the launch traced here: 551 us
  Pallas kernels  217 us (39%)
  waiting for transfers between devices  172 us (31%)
  matrix products  74.6 us (13%)
  starting transfers between devices  36.4 us (6%)
  local copies, waits for them, and re-layouts  28.9 us (5%)
  between operations  15 us (3%)
  other arithmetic  7.48 us (1%)
    all_to_all x4, waiting for transfers between devices, exchange(): lax.all_to_all(pairs, ('row', 'col'), split_axis=0, concat_axis=0, tiled=...  172 us
    pallas_call x1, Pallas kernels, tail(): pl.pallas_call(tail_kernel, out_shape=[jax.ShapeDtypeStruct((rows, width)...  83.9 us
    pallas_call x1, Pallas kernels, head(): pl.pallas_call(head_kernel, out_shape=[full((2, 4, 4, shard_rows, pre_wid...  82.1 us
    all_to_all x4, starting transfers between devices, exchange(): lax.all_to_all(pairs, ('row', 'col'), split_axis=0, concat_axis=0, tiled=...  35.9 us
    unnamed x75, local copies, waits for them, and re-layouts  20.4 us
    pallas_call x2, Pallas kernels, unpack_slots(): pl.pallas_call(unpack_slots_kernel, grid=(blocks,), out_shape=jax.ShapeDt...  14.9 us
    dot_general x1, matrix products, per_device(): jnp.einsum('esf,edf->esd', expert_pre_grad, w_expert_in, preferred_elemen...  11.7 us
    dot_general x1, matrix products, per_device(): jnp.einsum('esd,edf->esf', expert_in, w_expert_in, preferred_element_type...  11.3 us
  transfers between devices with their start and end apart: 6, of which 4 were waited for; matrix products, arithmetic and copies ran while one was open for 15% of the time, Pallas kernels for 9%

profile of v6, /device:TPU:1, one launch (start us, length us, event | category | flops | bytes accessed | tf_op | source)
XLA Modules:
  0.0 551.4 jit_solution(15106213265635314749)
XLA Ops:
  10.1 82.1 %head.1 = (bf16[2,4,4,64,768]{4,3,2,1,0:T(8,128)(2,1)}, bf16[2,4,4,64,512]{4,3,2,1,0:T(8,128)(2,1)}, bf16[2,4,4,64,384]{4,3,2,1,0:T(8,128)(2,1)}, bf16[4,128,204...) custom-call(bf16[128,2048]{1,0:T(8,128)(2,1)} %bitcast.89, ...), custom_call_target="tpu_custom_call" | custom-call | bytes 314572800 | tf_op jit(solution)/shard_map/head/pallas_call | solution.py:1219
  92.3 4.9 all-to-all-start
  98.0 6.8 %pack_tokens.1.grads = bf16[2048,1536]{1,0:T(8,128)(2,1)S(1)} custom-call(bf16[8,32,128]{2,1,0:T(8,128)(2,1)S(1)} %copy-done.7, bf16[128,2048]{1,0:T(8,128)(2,1)S(1)} %bitcast.74, bf16[8,32,128]{2,1,0:T(8,128)(2,1)S(1)} %bitcast.76, bf16[8,32,128]{2,1,0:T(8,128)(2,1)S(1)} %bitcast.78), custom_call_target="tpu_custom_call" | custom-call | flops 3221225472 | bytes 8388608 | tf_op jit(solution)/shard_map/pack_tokens/pallas_call | solution.py:756
  104.8 2.7 copy-done.1
  107.4 65.4 %all-to-all-done = bf16[128,16,1536]{2,1,0:T(8,128)(2,1)} async-done(((bf16[128,16,1536]{2,1,0:T(8,128)(2,1)}), bf16[128,16,1536]{2,1,0:T(8,128)(2,1)}, u32[]{:S(2)}, u32[]{:S(2)}) %all-to-all-start) | async-done | bytes 6291488 | tf_op jit(solution)/shard_map/all_to_all | solution.py:1299
  172.8 10.8 %all-to-all-start.1 = ((bf16[128,16,1536]{2,1,0:T(8,128)(2,1)}), bf16[128,16,1536]{2,1,0:T(8,128)(2,1)}, u32[]{:S(2)}, u32[]{:S(2)}) async-start(bf16[128,16,1536]{2,1,0:T(8,128)(2,1)} %bitcast.65), calls=%async_computation.1 | async-start | bytes 12582912 | tf_op jit(solution)/shard_map/all_to_all | solution.py:1299
  183.6 7.4 %unpack_slots.2 = bf16[2,768,2048]{2,1,0:T(8,128)(2,1)S(1)} custom-call(bf16[2048,1536]{1,0:T(8,128)(2,1)} %bitcast.11.packed), custom_call_target="tpu_custom_call" | custom-call | flops 2415919104 | bytes 14680064 | tf_op jit(solution)/shard_map/unpack_slots/pallas_call | solution.py:797
  191.0 11.3 %fusion.19 = f32[2,768,1024]{2,1,0:T(8,128)S(1)} fusion(bf16[2,768,2048]{2,1,0:T(8,128)(2,1)S(1)} %unpack_slots.2, bf16[2,2048,1024]{2,1,0:T(8,128)(2,1)} %param.24), kind=kOutput, calls=%fused_computation.45 | convolution fusion | flops 6442450944 | bytes 20971520 | tf_op jit(solution)/shard_map/esd,edf->esf/dot_general | solution.py:1398
  202.4 2.7 copy-done.8
  207.3 3.7 convolution_convert_fusion.1.values
  211.0 5.4 pack_slots.2
  216.4 2.7 copy-done.3
  219.1 40.1 %all-to-all-done.1 = bf16[128,16,1536]{2,1,0:T(8,128)(2,1)} async-done(((bf16[128,16,1536]{2,1,0:T(8,128)(2,1)}), bf16[128,16,1536]{2,1,0:T(8,128)(2,1)}, u32[]{:S(2)}, u32[]{:S(2)}) %all-to-all-start.1) | async-done | bytes 6291488 | tf_op jit(solution)/shard_map/all_to_all | solution.py:1299
  259.2 10.8 %all-to-all-start.2 = ((bf16[128,16,1536]{2,1,0:T(8,128)(2,1)}), bf16[128,16,1536]{2,1,0:T(8,128)(2,1)}, u32[]{:S(2)}, u32[]{:S(2)}) async-start(bf16[128,16,1536]{2,1,0:T(8,128)(2,1)} %bitcast.69), calls=%async_computation.2 | async-start | bytes 12582912 | tf_op jit(solution)/shard_map/all_to_all | solution.py:1299
  270.8 7.5 %unpack_slots.3 = bf16[2,768,2048]{2,1,0:T(8,128)(2,1)S(1)} custom-call(bf16[2048,1536]{1,0:T(8,128)(2,1)} %bitcast.13.packed), custom_call_target="tpu_custom_call" | custom-call | flops 2415919104 | bytes 14680064 | tf_op jit(solution)/shard_map/unpack_slots/pallas_call | solution.py:797
  278.4 8.8 %multiply_convert_fusion.1 = (bf16[2,768,512]{2,1,0:T(8,128)(2,1)S(1)}, bf16[2,768,512]{2,1,0:T(8,128)(2,1)S(1)}) fusion(f32[2,768,1024]{2,1,0:T(8,128)} %copy-done.8, bf16[2,768,2048]{2,1,0:T(8,128)(2,1)S(1)} %unpack_slots.3, bf16[2,2048,512]{2,1,0:T(8,128)(2,1)S(1)} %copy-done.22), kind=kOutput, calls=%fused_computation.4 | convolution fusion | flops 3231449088 | bytes 19922944 | tf_op jit(solution)/shard_map/esd,edf->esf/dot_general | solution.py:1410
  287.2 11.7 %convolution_convert_fusion.values = bf16[2,768,2048]{2,1,0:T(8,128)(2,1)S(1)} fusion(bf16[2,2048,1024]{2,1,0:T(8,128)(2,1)} %param.24, bf16[2,768,512]{2,1,0:T(8,128)(2,1)S(1)} %get-tuple-element.135, bf16[2,768,512]{2,1,0:T(8,128)(2,1)S(1)} %get-tuple-element.134), kind=kOutput, calls=%fused_computation | convolution fusion | flops 6451888128 | bytes 17825792 | tf_op jit(solution)/shard_map/esf,edf->esd/dot_general | solution.py:1416
  298.9 5.4 pack_slots.3
  304.3 2.6 copy-done.2
  307.0 46.2 %all-to-all-done.2 = bf16[128,16,1536]{2,1,0:T(8,128)(2,1)} async-done(((bf16[128,16,1536]{2,1,0:T(8,128)(2,1)}), bf16[128,16,1536]{2,1,0:T(8,128)(2,1)}, u32[]{:S(2)}, u32[]{:S(2)}) %all-to-all-start.2) | async-done | bytes 6291488 | tf_op jit(solution)/shard_map/all_to_all | solution.py:1299
  353.2 9.4 %all-to-all-start.3 = ((bf16[128,16,1536]{2,1,0:T(8,128)(2,1)}), bf16[128,16,1536]{2,1,0:T(8,128)(2,1)}, u32[]{:S(2)}, u32[]{:S(2)}) async-start(bf16[128,16,1536]{2,1,0:T(8,128)(2,1)} %bitcast.68), calls=%async_computation.3 | async-start | bytes 12582912 | tf_op jit(solution)/shard_map/all_to_all | solution.py:1299
  370.4 4.1 copy.55
  374.5 5.4 all_marks.1.marks_in
  379.9 3.3 convolution_convert_fusion.6.second
  385.0 2.7 side_by_side.1
  389.7 10.2 %fusion.20 = f32[2,2048,512]{2,1,0:T(8,128)} fusion(bf16[2,768,2048]{2,1,0:T(8,128)(2,1)} %copy-done.5, bf16[2,768,512]{2,1,0:T(8,128)(2,1)} %copy-done.12), kind=kOutput, calls=%fused_computation.46 | convolution fusion | flops 3221225472 | bytes 16252928 | tf_op jit(solution)/shard_map/esd,esf->edf/dot_general | solution.py:1421
  400.0 10.4 %fusion.1 = f32[2,2048,1024]{2,1,0:T(8,128)} fusion(bf16[2,768,2048]{2,1,0:T(8,128)(2,1)S(1)} %bitcast.71, bf16[2,768,512]{2,1,0:T(8,128)(2,1)S(1)} %copy-done.28, bf16[2,768,512]{2,1,0:T(8,128)(2,1)S(1)} %copy-done.26), kind=kOutput, calls=%fused_computation.14 | convolution fusion | flops 6448742400 | bytes 26214400 | tf_op jit(solution)/shard_map/esd,esf->edf/dot_general | solution.py:1424
  410.4 10.2 %sum_gated.1 = (f32[128,2048]{1,0:T(8,128)S(1)}, f32[8,128,32]{2,1,0:T(8,128)S(1)}) custom-call(bf16[8,32,128]{2,1,0:T(8,128)(2,1)S(1)} %copy-done.7, bf16[2048,1536]{1,0:T(8,128)(2,1)} %bitcast.15.packed, bf16[2048,1536]{1,0:T(8,128)(2,1)S(1)} %bitcast.67, bf16[8,32,128]{2,1,0:T(8,128)(2,1)S(1)} %bitcast.77, bf16[8,32,128]{2,1,0:T(8,128)(2,1)S(1)} %bitcast.79), custom_call_target="tpu_custom_call" | custom-call | flops 3221225472 | bytes 14680064 | tf_op jit(solution)/shard_map/sum_gated/pallas_call | solution.py:901
  426.5 2.5 convolution_add_fusion.router_input_in
  429.0 20.3 %all-to-all-done.3 = bf16[128,16,1536]{2,1,0:T(8,128)(2,1)} async-done(((bf16[128,16,1536]{2,1,0:T(8,128)(2,1)}), bf16[128,16,1536]{2,1,0:T(8,128)(2,1)}, u32[]{:S(2)}, u32[]{:S(2)}) %all-to-all-start.3) | async-done | bytes 6291488 | tf_op jit(solution)/shard_map/all_to_all | solution.py:1299
  449.3 83.9 %tail.1 = (f32[128,2048]{1,0:T(8,128)}, f32[128,2048]{1,0:T(8,128)}, bf16[128,2048]{1,0:T(8,128)(2,1)}, bf16[4,2,4,4,16,256]{5,4,3,2,1,0:T(8,128)(2,1)}, f32[1,2...) custom-call(bf16[2048,1536]{1,0:T(8,128)(2,1)} %bitcast.17.packed, ...), custom_call_target="tpu_custom_call" | custom-call | bytes 314572800 | tf_op jit(solution)/shard_map/tail/pallas_call | solution.py:642
  536.3 2.8 bitcast_convert_fusion
  (97 shorter events, 32.2 us)
Async XLA Ops:
  7.2 90.0 %copy-start = (bf16[2048,256]{1,0:T(8,128)(2,1)S(1)}, bf16[2048,256]{1,0:T(8,128)(2,1)}, u32[]{:S(2)}) copy-start(bf16[2048,256]{1,0:T(8,128)(2,1)} %param.23) | copy-start | bytes 3145732
  92.2 5.0 copy-start.9
  92.2 5.0 copy-start.24
  92.2 5.7 %copy-start.6 = (bf16[1,128,2048]{2,1,0:T(8,128)(2,1)S(1)}, bf16[1,128,2048]{2,1,0:T(8,128)(2,1)}, u32[]{:S(2)}) copy-start(bf16[1,128,2048]{2,1,0:T(8,128)(2,1)} %param.28) | copy-start | bytes 1572868
  92.3 5.7 %copy-start.7 = (bf16[8,32,128]{2,1,0:T(8,128)(2,1)S(1)}, bf16[8,32,128]{2,1,0:T(8,128)(2,1)}, u32[]{:S(2)}) copy-start(bf16[8,32,128]{2,1,0:T(8,128)(2,1)} %get-tuple-element.61.code) | copy-start | bytes 196612
  92.3 80.5 %all-to-all-start = ((bf16[128,16,1536]{2,1,0:T(8,128)(2,1)}), bf16[128,16,1536]{2,1,0:T(8,128)(2,1)}, u32[]{:S(2)}, u32[]{:S(2)}) async-start(bf16[128,16,1536]{2,1,0:T(8,128)(2,1)} %bitcast.84), calls=%async_computation | async-start | bytes 12582912 | tf_op jit(solution)/shard_map/all_to_all | solution.py:1299
  172.8 86.4 %all-to-all-start.1 = ((bf16[128,16,1536]{2,1,0:T(8,128)(2,1)}), bf16[128,16,1536]{2,1,0:T(8,128)(2,1)}, u32[]{:S(2)}, u32[]{:S(2)}) async-start(bf16[128,16,1536]{2,1,0:T(8,128)(2,1)} %bitcast.65), calls=%async_computation.1 | async-start | bytes 12582912 | tf_op jit(solution)/shard_map/all_to_all | solution.py:1299
  191.0 11.4 %copy-start.4 = (bf16[2,768,2048]{2,1,0:T(8,128)(2,1)}, bf16[2,768,2048]{2,1,0:T(8,128)(2,1)S(1)}, u32[]{:S(2)}) copy-start(bf16[2,768,2048]{2,1,0:T(8,128)(2,1)S(1)} %unpack_slots.2) | copy-start | bytes 18874372
  259.2 94.0 %all-to-all-start.2 = ((bf16[128,16,1536]{2,1,0:T(8,128)(2,1)}), bf16[128,16,1536]{2,1,0:T(8,128)(2,1)}, u32[]{:S(2)}, u32[]{:S(2)}) async-start(bf16[128,16,1536]{2,1,0:T(8,128)(2,1)} %bitcast.69), calls=%async_computation.2 | async-start | bytes 12582912 | tf_op jit(solution)/shard_map/all_to_all | solution.py:1299
  270.1 92.6 %all-gather.2.cloned.1.call-start = ((), (), s32[]{:S(2)}) async-start(), calls=%async_computation.5 | async-start | bytes 2621440 | tf_op jit(solution)/shard_map/all_gather | solution.py:1376
  270.8 7.5 %copy-start.22 = (bf16[2,2048,512]{2,1,0:T(8,128)(2,1)S(1)}, bf16[2,2048,512]{2,1,0:T(8,128)(2,1)}, u32[]{:S(2)}) copy-start(bf16[2,2048,512]{2,1,0:T(8,128)(2,1)} %param.25) | copy-start | bytes 12582916
  278.3 8.8 %copy-start.5 = (bf16[2,768,2048]{2,1,0:T(8,128)(2,1)}, bf16[2,768,2048]{2,1,0:T(8,128)(2,1)S(1)}, u32[]{:S(2)}) copy-start(bf16[2,768,2048]{2,1,0:T(8,128)(2,1)S(1)} %unpack_slots.3) | copy-start | bytes 18874372
  287.2 11.7 %copy-start.25 = (bf16[2,768,512]{2,1,0:T(8,128)(2,1)}, bf16[2,768,512]{2,1,0:T(8,128)(2,1)S(1)}, u32[]{:S(2)}) copy-start(bf16[2,768,512]{2,1,0:T(8,128)(2,1)S(1)} %get-tuple-element.134) | copy-start | bytes 4718596
  287.2 11.7 %copy-start.27 = (bf16[2,768,512]{2,1,0:T(8,128)(2,1)}, bf16[2,768,512]{2,1,0:T(8,128)(2,1)S(1)}, u32[]{:S(2)}) copy-start(bf16[2,768,512]{2,1,0:T(8,128)(2,1)S(1)} %get-tuple-element.135) | copy-start | bytes 4718596
  353.2 9.4 %copy-start.11 = (bf16[2,4,4,64,384]{4,3,2,1,0:T(8,128)(2,1)S(1)}, bf16[2,4,4,64,384]{4,3,2,1,0:T(8,128)(2,1)}, u32[]{:S(2)}) copy-start(bf16[2,4,4,64,384]{4,3,2,1,0:T(8,128)(2,1)} %get-tuple-element.71) | copy-start | bytes 4718596
  353.2 96.0 %all-to-all-start.3 = ((bf16[128,16,1536]{2,1,0:T(8,128)(2,1)}), bf16[128,16,1536]{2,1,0:T(8,128)(2,1)}, u32[]{:S(2)}, u32[]{:S(2)}) async-start(bf16[128,16,1536]{2,1,0:T(8,128)(2,1)} %bitcast.68), calls=%async_computation.3 | async-start | bytes 12582912 | tf_op jit(solution)/shard_map/all_to_all | solution.py:1299
  362.6 63.9 %reduce-scatter.2.cloned.1.call-start = ((), (), s32[]{:S(2)}) async-start(), calls=%async_computation.6 | async-start | bytes 2621440 | tf_op jit(solution)/shard_map/reduce_scatter | solution.py:1390
  387.6 12.4 %slice-start.2 = ((s8[6291456]{0:T(1024)(128)(4,1)}), s8[4194304]{0:T(1024)(128)(4,1)S(1)}, s32[]{:S(2)}) async-start(s8[6291456]{0:T(1024)(128)(4,1)} %bitcast.70), calls=%async_computation.9 | async-start | bytes 8388608
  389.7 10.3 %slice-start.3 = ((s8[6291456]{0:T(1024)(128)(4,1)}), s8[2097152]{0:T(1024)(128)(4,1)S(1)}, s32[]{:S(2)}) async-start(s8[6291456]{0:T(1024)(128)(4,1)} %bitcast.70), calls=%async_computation.10 | async-start | bytes 4194304
  389.7 10.3 %copy-start.26 = (bf16[2,768,512]{2,1,0:T(8,128)(2,1)S(1)}, bf16[2,768,512]{2,1,0:T(8,128)(2,1)}, u32[]{:S(2)}) copy-start(bf16[2,768,512]{2,1,0:T(8,128)(2,1)} %copy-done.25) | copy-start | bytes 4718596
  389.7 10.3 %copy-start.28 = (bf16[2,768,512]{2,1,0:T(8,128)(2,1)S(1)}, bf16[2,768,512]{2,1,0:T(8,128)(2,1)}, u32[]{:S(2)}) copy-start(bf16[2,768,512]{2,1,0:T(8,128)(2,1)} %copy-done.27) | copy-start | bytes 4718596
  389.7 20.7 %slice-start = ((s8[6291456]{0:T(1024)(128)(4,1)}), s8[4194304]{0:T(1024)(128)(4,1)S(1)}, s32[]{:S(2)}) async-start(s8[6291456]{0:T(1024)(128)(4,1)} %bitcast.66), calls=%async_computation.7 | async-start | bytes 8388608
  400.0 10.4 %slice-start.1 = ((s8[6291456]{0:T(1024)(128)(4,1)}), s8[2097152]{0:T(1024)(128)(4,1)S(1)}, s32[]{:S(2)}) async-start(s8[6291456]{0:T(1024)(128)(4,1)} %bitcast.66), calls=%async_computation.8 | async-start | bytes 4194304
  420.7 4.3 copy-start.10
  533.1 6.0 %copy-start.13 = (f32[128,2048]{1,0:T(8,128)S(1)}, f32[128,2048]{1,0:T(8,128)}, u32[]{:S(2)}) copy-start(f32[128,2048]{1,0:T(8,128)} %get-tuple-element.98) | copy-start | bytes 3145732
  533.1 6.0 %copy-start.14 = (f32[128,2048]{1,0:T(8,128)S(1)}, f32[128,2048]{1,0:T(8,128)}, u32[]{:S(2)}) copy-start(f32[128,2048]{1,0:T(8,128)} %get-tuple-element.99) | copy-start | bytes 3145732
  536.3 3.9 copy-start.15
  536.3 4.7 copy-start.20
  536.3 5.3 copy-start.17
  536.3 5.9 %copy-start.16 = (f32[64,512]{1,0:T(8,128)S(1)}, f32[64,512]{1,0:T(8,128)}, u32[]{:S(2)}) copy-start(f32[64,512]{1,0:T(8,128)} %get-tuple-element.160) | copy-start | bytes 393220
  539.1 3.8 copy-start.19
  539.1 4.4 copy-start.18
  (7 other events, 19.9 us)
Sparse Core Ops, SparseCore 0:
  272.6 39.8 all-gather.1
  369.7 51.3 reduce-scatter.1

commit v7 on v6

--- a/solution.py
+++ b/solution.py
@@ -387,6 +387,7 @@
     full_back,
     shared_parts_in,
     stream_in,
+    shared_input_in,
     scale_two,
     gain_ffn,
     stream_grad,
@@ -418,11 +419,11 @@
     parts, near, far, outgoing, router_near, router_far, router_outgoing = scratch[18:25]
     router_part, values, buffers, pre_grads, out_grads = scratch[25:30]
     load_sem, branch_send, branch_recv, row_send, row_recv, gain_send, gain_recv = scratch[30:37]
-    pass_send, pass_recv = scratch[37:39]
-    shared_scatter = ScatterSum(shared_grads, scratch[39:50])
-    out_scatter = ScatterSum(out_grads, scratch[50:61])
-    pre_scatter = ScatterSum(pre_grads, scratch[61:72])
-    router_at = 72
+    pass_send, pass_recv, input_parts, core_near, share_sums, share_low = scratch[37:43]
+    shared_scatter = ScatterSum(shared_grads, scratch[43:54])
+    out_scatter = ScatterSum(out_grads, scratch[54:65])
+    pre_scatter = ScatterSum(pre_grads, scratch[65:76])
+    router_at = 76
     low = jnp.bfloat16
     row, col, sibling, partner, across = row_places()
     row_peers = [(peer, col) for peer in (sibling, partner, across)]
@@ -442,6 +443,8 @@
         pltpu.make_async_copy(source, target, load_sem.at[i])
         for i, (source, target) in enumerate(zip(sources, targets))
     ]
+    load_parts = pltpu.make_async_copy(shared_input_in, input_parts, load_sem.at[len(loads)])
+    load_parts.start()
     for load in loads:
         load.start()
     load_marks = loads.pop(1)
@@ -456,6 +459,10 @@
     )
     router_copies[0].start()
     router_copies[1].start()
+    core = lax.rem(row, 2)
+    load_parts.wait()
+    input_copy = remote(input_parts.at[1 - core], core_near.at[0], row_sems, 3, (sibling, col))
+    input_copy.start()
     shared_scatter.start()
     row_sum_forward(router_parts, router_near, router_outgoing, router_copies)
 
@@ -475,7 +482,9 @@
             routed[:, columns] = found if i == 0 else routed[:, columns] + found
     load_input.wait()
     load_hidden.wait()
-    incoming = router_input[...] + routed[...]
+    input_copy.wait_recv()
+    shared_input = input_parts[core].astype(jnp.float32) + core_near[0].astype(jnp.float32)
+    incoming = router_input[...] + routed[...] + shared_input
     state = hidden[...]
     factor = scale_two[...]
     weighted = gain_ffn[...] * incoming
@@ -493,17 +502,13 @@
     values[0, 1:2] = jnp.sum(incoming * state * factor, axis=0, keepdims=True)
 
     load_shared.wait()
-    shared_copies = row_sum_copies(
-        shared_parts, near.at[1], far.at[1], outgoing.at[1], row_sems, 3
-    )
-    shared_copies[0].start()
-    shared_copies[1].start()
+    shared_copy = remote(shared_parts.at[1 - core], core_near.at[1], row_sems, 4, (sibling, col))
+    shared_copy.start()
     router_sum = row_sum_total(router_parts, router_near, router_far, router_copies)
     router_part[...] = router_sum.astype(low).reshape(router_part.shape)
     router_scatter = RouterSum(router_part, router.at[row], scratch[router_at:])
     router_scatter.start()
     shared_scatter.add_first()
-    row_sum_forward(shared_parts, near.at[1], outgoing.at[1], shared_copies)
     load_back.wait()
     near_rows[0].wait_recv()
     key_grad[...] = jnp.zeros_like(key_grad)
@@ -553,7 +558,10 @@
     pre_scatter.start()
     router_scatter.add_x()
     out_scatter.add_first()
-    shared_scatter.add_third(pieces[3:])
+    shared_scatter.add_third([share_sums.at[0], share_sums.at[1]])
+    share_low[0] = share_sums[1].astype(low)
+    share_copy = remote(share_low.at[0], share_low.at[1], row_sems, 5, (partner, col))
+    share_copy.start()
     router_scatter.spread_z()
 
     gain_sems = (gain_send, gain_recv)
@@ -587,7 +595,8 @@
     router_scatter.spread_y()
     out_scatter.add_second()
     load_stream.wait()
-    shared = row_sum_total(shared_parts, near.at[1], far.at[1], shared_copies)
+    shared_copy.wait_recv()
+    shared = shared_parts[core].astype(jnp.float32) + core_near[1].astype(jnp.float32)
     block_out[...] = (stream[...] + shared).astype(low)
     add_gains(0)
     start_gains(1)
@@ -604,6 +613,10 @@
     start_gains(3)
     router_rows[0][0].wait_recv()
     router_rows[2][0].start()
+    share_copy.wait_recv()
+    share = share_sums[0] + share_low[1].astype(jnp.float32)
+    pieces[3][...] = share[:, : pieces[3].shape[1]]
+    pieces[4][...] = share[:, pieces[3].shape[1] :]
     pre_scatter.add_third(pieces[:2])
     add_gains(3)
     gain_attn_sum[...] = values[4, 0:1]
@@ -616,7 +629,7 @@
     router_rows[0][0].wait_send()
     router_rows[1][0].wait()
     router_rows[2][0].wait()
-    for done in [*router_copies, *attn_copies, *shared_copies, *gain_copies]:
+    for done in [*router_copies, *attn_copies, *gain_copies, input_copy, shared_copy, share_copy]:
         done.wait_send()
     for scatter in (shared_scatter, out_scatter, pre_scatter):
         scatter.end()
@@ -650,7 +663,7 @@
             jax.ShapeDtypeStruct((1, width), jnp.float32),
         ]
         + [jax.ShapeDtypeStruct((shard, part), jnp.float32) for part in widths],
-        in_specs=[away] * 9 + [space] * 17,
+        in_specs=[away] * 10 + [space] * 17,
         out_specs=[space] * (6 + len(widths)),
         scratch_shapes=[
             pltpu.VMEM((4, packed.shape[0] // 4, packed.shape[1]), low),
@@ -660,7 +673,7 @@
             pltpu.VMEM((width, tokens), low),
             pltpu.VMEM((width, pre_width), low),
             pltpu.VMEM((width, inner), low),
-            pltpu.VMEM((4, rows, width), low),
+            pltpu.VMEM((2, rows, width), low),
             pltpu.VMEM((rows, width), jnp.float32),
             pltpu.VMEM((rows, width), jnp.float32),
             pltpu.VMEM((4, rows, width), low),
@@ -672,9 +685,9 @@
             pltpu.VMEM((tokens, size), jnp.float32),
             pltpu.VMEM((tokens, size), jnp.float32),
             pltpu.VMEM((4, rows, width), low),
-            pltpu.VMEM((2, 2, rows, width), low),
-            pltpu.VMEM((2, rows, width), low),
-            pltpu.VMEM((2, rows, width), low),
+            pltpu.VMEM((1, 2, rows, width), low),
+            pltpu.VMEM((1, rows, width), low),
+            pltpu.VMEM((1, rows, width), low),
             pltpu.VMEM((2, router_rows, experts), low),
             pltpu.VMEM((router_rows, experts), low),
             pltpu.VMEM((router_rows, experts), low),
@@ -683,7 +696,7 @@
             pltpu.VMEM((10, 2, width), jnp.float32),
             pltpu.VMEM(pre_grads.shape, low),
             pltpu.VMEM(out_grads.shape, low),
-            dma((12,)),
+            dma((13,)),
             dma((3,)),
             dma((3,)),
             dma((9,)),
@@ -692,6 +705,10 @@
             dma((10,)),
             dma((3,)),
             dma((3,)),
+            pltpu.VMEM((2, rows, width), low),
+            pltpu.VMEM((2, rows, width), low),
+            pltpu.VMEM((2, shard, widths[3] + widths[4]), jnp.float32),
+            pltpu.VMEM((2, shard, widths[3] + widths[4]), low),
             *ScatterSum.scratch(shared_grads),
             *ScatterSum.scratch(out_grads),
             *ScatterSum.scratch(pre_grads),
@@ -1001,7 +1018,8 @@
     full_back,
     full_shared,
     group_one,
-    group_grad,
+    chip_grad,
+    chip_two,
     scale_one,
     cosine,
     sine,
@@ -1023,7 +1041,7 @@
     mine_pre, mine_back, mine_shared, normed, rows, w_pre, w_back, pre, bias, parts = scratch[:10]
     near, far, outgoing, marks, staged = scratch[10:15]
     gather_send, gather_recv, own_sem, row_send, row_recv = scratch[15:20]
-    sum_send, sum_recv, load_sem, pack_sem = scratch[20:]
+    sum_send, sum_recv, chip_send, chip_recv, load_sem, pack_sem = scratch[20:]
     low = jnp.bfloat16
     row, col, sibling, partner, _ = row_places()
     gathers = [
@@ -1045,32 +1063,45 @@
     factor = lax.rsqrt(jnp.mean(first * first, axis=1, keepdims=True) + epsilon)
     scale_one[...] = factor
     normed[...] = (first * factor * gain_attn[...]).astype(low)
+    core = lax.rem(row, 2)
     own = [
         pltpu.make_async_copy(normed, group_one.at[row], own_sem.at[0]),
-        pltpu.make_async_copy(grads, group_grad.at[row], own_sem.at[1]),
+        pltpu.make_async_copy(grads, chip_grad.at[core], own_sem.at[1]),
         pltpu.make_async_copy(mine_pre, full_pre.at[place], own_sem.at[2]),
         pltpu.make_async_copy(mine_back, full_back.at[place], own_sem.at[3]),
         pltpu.make_async_copy(mine_shared, full_shared.at[place], own_sem.at[4]),
+        pltpu.make_async_copy(normed_two, chip_two.at[core], own_sem.at[5]),
     ]
-    for copy in own:
+    for copy in own[:4]:
         copy.start()
     await_greetings(9)
-    far_rows, near_rows, onward = row_copies(
-        [normed, grads], [group_one, group_grad], row_send, row_recv
-    )
+    far_rows, near_rows, onward = row_copies([normed], [group_one], row_send, row_recv)
+    chip_sems = (chip_send, chip_recv)
+    share = mine_shared.shape[1] // 2
+    other_shard = remote(
+        mine_shared.at[:, pl.ds(0, share)],
+        mine_shared.at[:, pl.ds(share, share)],
+        chip_sems,
+        0,
+        (partner, col),
+    )
+    near_grads = remote(grads, chip_grad.at[core], chip_sems, 1, (sibling, col))
+    near_two = remote(normed_two, chip_two.at[core], chip_sems, 2, (sibling, col))
+    other_shard.start()
     gathers[0].start()
     far_rows[0].start()
     near_rows[0].start()
     gathers[1].start()
-    gathers[2].start()
     gathers[0].second()
     gathers[1].second()
-    for copy in own[2:]:
+    for copy in own[2:4]:
         copy.wait()
     gathers[0].third()
-    far_rows[1].start()
-    near_rows[1].start()
+    near_grads.start()
     gathers[1].third()
+    other_shard.wait_recv()
+    own[4].start()
+    gathers[2].start()
 
     tokens = begin.shape[0]
 
@@ -1162,14 +1193,15 @@
     copies[1].start()
     gathers[2].second()
     row_sum_forward(parts, near, outgoing, copies)
-    far_rows[1].wait_recv()
-    onward[1].start()
+    own[4].wait()
     gathers[2].third()
     total = inputs[...].astype(jnp.float32) + row_sum_total(parts, near, far, copies)
     hidden[...] = total
     factor = lax.rsqrt(jnp.mean(total * total, axis=1, keepdims=True) + epsilon)
     normed_two[...] = (total * factor * gain_ffn[...]).astype(low)
     scale_two[...] = factor
+    near_two.start()
+    own[5].start()
 
     def pack(block, carry):
         last = normed_two[:, 3 * QUARTER :]
@@ -1185,10 +1217,12 @@
 
     gathers[2].await_all()
     own[1].wait()
+    own[5].wait()
+    near_grads.wait()
+    near_two.wait()
+    other_shard.wait_send()
     near_rows[0].wait_send()
-    near_rows[1].wait()
     onward[0].wait_send()
-    onward[1].wait()
     for copy in far_rows + copies:
         copy.wait_send()
     for gather in gathers:
@@ -1221,9 +1255,10 @@
         out_shape=[
             full((2, 4, 4, shard_rows, pre_width), low),
             full((2, 4, 4, shard_rows, inner), low),
-            full((2, 4, 4, shard_rows, shared_width), low),
+            full((2, 4, 4, shard_rows, 2 * shared_width), low),
             full((4, rows, width), low),
-            full((4, rows, width), low),
+            full((2, rows, width), low),
+            full((2, rows, width), low),
             full((rows, 1), jnp.float32),
             full((tokens, size), jnp.float32),
             full((tokens, size), jnp.float32),
@@ -1244,11 +1279,11 @@
         in_specs=[space] * 3
         + [away, pl.BlockSpec(memory_space=pltpu.SMEM)]
         + [space] * (2 + len(shards)),
-        out_specs=[away] * 5 + [space] * 13 + [away] + [space] * 2,
+        out_specs=[away] * 6 + [space] * 13 + [away] + [space] * 2,
         scratch_shapes=[
             pltpu.VMEM((shard_rows, pre_width), low),
             pltpu.VMEM((shard_rows, inner), low),
-            pltpu.VMEM((shard_rows, shared_width), low),
+            pltpu.VMEM((shard_rows, 2 * shared_width), low),
             pltpu.VMEM((rows, width), low),
             pltpu.VMEM((4, rows, width), low),
             pltpu.VMEM((2, 4, 4, shard_rows, pre_width), low),
@@ -1263,9 +1298,11 @@
             pltpu.VMEM((blocks, BLOCK, 3 * QUARTER), low),
             pltpu.SemaphoreType.DMA((3, 25)),
             pltpu.SemaphoreType.DMA((3, 25)),
-            pltpu.SemaphoreType.DMA((5,)),
             pltpu.SemaphoreType.DMA((6,)),
-            pltpu.SemaphoreType.DMA((6,)),
+            pltpu.SemaphoreType.DMA((3,)),
+            pltpu.SemaphoreType.DMA((3,)),
+            pltpu.SemaphoreType.DMA((3,)),
+            pltpu.SemaphoreType.DMA((3,)),
             pltpu.SemaphoreType.DMA((3,)),
             pltpu.SemaphoreType.DMA((3,)),
             pltpu.SemaphoreType.DMA((3,)),
@@ -1279,19 +1316,21 @@
     )(inputs, gain_attn, gain_ffn, grads, lengths, routes, frequency, *shards)
 
 
-def side_by_side_kernel(first, second, both):
-    both[:, : first.shape[1]] = first[...]
-    both[:, first.shape[1] :] = second[...]
-
-
-def side_by_side(first, second):
-    shape = (first.shape[0], first.shape[1] + second.shape[1])
+def side_by_side_kernel(*refs):
+    both, start = refs[-1], 0
+    for part in refs[:-1]:
+        both[:, start : start + part.shape[1]] = part[...]
+        start += part.shape[1]
+
+
+def side_by_side(*parts):
+    shape = (parts[0].shape[0], sum(part.shape[1] for part in parts))
     return pl.pallas_call(
         side_by_side_kernel,
-        out_shape=jax.ShapeDtypeStruct(shape, first.dtype),
-        cost_estimate=pl.CostEstimate(flops=0, bytes_accessed=3 << 20, transcendentals=0),
+        out_shape=jax.ShapeDtypeStruct(shape, parts[0].dtype),
+        cost_estimate=pl.CostEstimate(flops=0, bytes_accessed=6 << 20, transcendentals=0),
         name="side_by_side",
-    )(first, second)
+    )(*parts)
 
 
 def exchange(packed):
@@ -1330,7 +1369,8 @@
         full_back,
         full_shared,
         group_one,
-        group_grad,
+        chip_grad,
+        chip_two,
         scale_one,
         cosine,
         sine_table,
@@ -1354,15 +1394,11 @@
         w_keyval.shape[2] // 2,
         expert_count,
     )
-    full_pre, full_back, full_shared, group_one, group_grad = (
+    full_pre, full_back, full_shared, group_one, chip_grad, chip_two = (
         part.reshape(-1, part.shape[-1])
-        for part in (full_pre, full_back, full_shared, group_one, group_grad)
+        for part in (full_pre, full_back, full_shared, group_one, chip_grad, chip_two)
     )
     received = exchange(send_rows)
-    shared_width = w_shared_out.shape[1]
-    full_shared_in = full_shared[:, : 2 * shared_width]
-    full_shared_out = full_shared[:, 2 * shared_width :]
-
     logits = matmul(normed_two, w_router)
     scores_sig = jnp.where(order >= 0.0, jax.nn.sigmoid(logits), 0.0)
     score_sum = jnp.sum(scores_sig, axis=1, keepdims=True)
@@ -1373,26 +1409,29 @@
     send_grads, received = lax.optimization_barrier((pack_tokens(code, grad_low, gates), received))
     received_grads = exchange(send_grads)
 
-    group_two = lax.all_gather(normed_two, "row", axis=0, tiled=True)
-    shared_pre = matmul(group_two, full_shared_in)
-    shared_gate, shared_up = shared_pre[:, :shared_width], shared_pre[:, shared_width:]
-    shared_act, shared_slope = swish_parts(shared_gate)
-    shared_hidden = (shared_act * shared_up).astype(jnp.bfloat16)
-    shared_hidden_grad = matmul(group_grad, full_shared_out)
-    shared_pre_grad = jnp.concatenate(
-        [shared_hidden_grad * shared_up * shared_slope, shared_hidden_grad * shared_act], axis=1
-    ).astype(jnp.bfloat16)
-    shared_grads = side_by_side(
-        outer_sum(group_two, shared_pre_grad).astype(jnp.bfloat16),
-        outer_sum(group_grad, shared_hidden).astype(jnp.bfloat16),
-    )
-    shared_parts = matmul_t(shared_hidden, full_shared_out).astype(jnp.bfloat16)
-    shared_input = lax.psum_scatter(
-        matmul_t(shared_pre_grad, full_shared_in).astype(jnp.bfloat16),
-        "row",
-        scatter_dimension=0,
-        tiled=True,
-    ).astype(jnp.float32)
+    shared_width = w_shared_out.shape[1]
+    shared_grads, shared_parts, shared_input = [], 0.0, 0.0
+    for start in (0, 3 * shared_width):
+        in_weights = full_shared[:, start : start + 2 * shared_width]
+        out_weights = full_shared[:, start + 2 * shared_width : start + 3 * shared_width]
+        shared_pre = matmul(chip_two, in_weights)
+        shared_gate, shared_up = shared_pre[:, :shared_width], shared_pre[:, shared_width:]
+        shared_act, shared_slope = swish_parts(shared_gate)
+        shared_hidden = (shared_act * shared_up).astype(jnp.bfloat16)
+        shared_hidden_grad = matmul(chip_grad, out_weights)
+        shared_pre_grad = jnp.concatenate(
+            [shared_hidden_grad * shared_up * shared_slope, shared_hidden_grad * shared_act],
+            axis=1,
+        ).astype(jnp.bfloat16)
+        shared_grads.append(outer_sum(chip_two, shared_pre_grad).astype(jnp.bfloat16))
+        shared_grads.append(outer_sum(chip_grad, shared_hidden).astype(jnp.bfloat16))
+        shared_parts = shared_parts + matmul_t(shared_hidden, out_weights)
+        shared_input = shared_input + matmul_t(shared_pre_grad, in_weights)
+    shared_grads = side_by_side(*shared_grads)
+    shared_parts, shared_input = (
+        part.astype(jnp.bfloat16).reshape(2, rows_dev, model_width)
+        for part in (shared_parts, shared_input)
+    )
 
     expert_in = unpack_slots(received)
     expert_pre = jnp.einsum(
@@ -1433,7 +1472,7 @@
     ).astype(jnp.bfloat16)
     router_parts = outer_sum(normed_two, logit_grad).astype(jnp.bfloat16)
     router_parts = router_parts.reshape(row_count, -1, expert_count)
-    router_input = shared_input + matmul_t(logit_grad, w_router)
+    router_input = matmul_t(logit_grad, w_router)
     shadowed = (router_input, router_parts, stream, shared_grads, group_one.T, all_marks(code))
     returned_grad, shadowed, grad_expert_in, grad_expert_out = lax.optimization_barrier(
         (returned_grad, shadowed, grad_expert_in, grad_expert_out)
@@ -1450,8 +1489,9 @@
             group_one_t,
             full_pre,
             full_back,
-            shared_parts.reshape(row_count, rows_dev, model_width),
+            shared_parts,
             stream,
+            shared_input,
         ),
         (
             scale_two,

time: 561 us -> 553 us (0.986)
  waiting for transfers between devices: 172 us -> 152 us
  Pallas kernels: 217 us -> 231 us
  between operations: 15 us -> 1.61 us
  starting transfers between devices: 36.4 us -> 47.2 us
    all_to_all x4, waiting for transfers between devices: 172 us -> 152 us  [exchange(): lax.all_to_all(pairs, ('row', 'col'), split_axis=0, concat_axis=0, tiled=...]
    all_to_all x4, starting transfers between devices: 35.9 us -> 47.2 us  [exchange(): lax.all_to_all(pairs, ('row', 'col'), split_axis=0, concat_axis=0, tiled=...]
    pallas_call x1, Pallas kernels: 83.9 us -> 92.3 us  [tail(): pl.pallas_call(tail_kernel, out_shape=[jax.ShapeDtypeStruct((rows, width)...]
    unnamed x75 -> x79, local copies, waits for them, and re-layouts: 20.4 us -> 20.4 us
  transfers between devices with their start and end apart: 6 -> 4, of which waited for: 4 -> 4; matrix products, arithmetic and copies ran while one was open for 15% -> 16% of each run, Pallas kernels for 9% -> 10%
where the time goes in v7:
time: 553 us; the launch traced here: 544 us
  Pallas kernels  231 us (42%)
  waiting for transfers between devices  152 us (27%)
  matrix products  76 us (14%)
  starting transfers between devices  47.2 us (9%)
  local copies, waits for them, and re-layouts  28.8 us (5%)
  other arithmetic  7.51 us (1%)
    all_to_all x4, waiting for transfers between devices, exchange(): lax.all_to_all(pairs, ('row', 'col'), split_axis=0, concat_axis=0, tiled=...  152 us
    pallas_call x1, Pallas kernels, tail(): pl.pallas_call(tail_kernel, out_shape=[jax.ShapeDtypeStruct((rows, width)...  92.3 us
    pallas_call x1, Pallas kernels, head(): pl.pallas_call(head_kernel, out_shape=[full((2, 4, 4, shard_rows, pre_wid...  86.5 us
    all_to_all x4, starting transfers between devices, exchange(): lax.all_to_all(pairs, ('row', 'col'), split_axis=0, concat_axis=0, tiled=...  47.2 us
    unnamed x79, local copies, waits for them, and re-layouts  20.4 us
    pallas_call x2, Pallas kernels, unpack_slots(): pl.pallas_call(unpack_slots_kernel, grid=(blocks,), out_shape=jax.ShapeDt...  14.9 us
    dot_general x1, matrix products, per_device(): jnp.einsum('esf,edf->esd', expert_pre_grad, w_expert_in, preferred_elemen...  11.7 us
    dot_general x1, matrix products, per_device(): jnp.einsum('esd,edf->esf', expert_in, w_expert_in, preferred_element_type...  11.3 us
  transfers between devices with their start and end apart: 4, of which 4 were waited for; matrix products, arithmetic and copies ran while one was open for 16% of the time, Pallas kernels for 10%

profile of v7, /device:TPU:1, one launch (start us, length us, event | category | flops | bytes accessed | tf_op | source)
XLA Modules:
  0.0 543.6 jit_solution(13641570469107665220)
XLA Ops:
  3.5 86.5 %head.1 = (bf16[2,4,4,64,768]{4,3,2,1,0:T(8,128)(2,1)}, bf16[2,4,4,64,512]{4,3,2,1,0:T(8,128)(2,1)}, bf16[2,4,4,64,768]{4,3,2,1,0:T(8,128)(2,1)}, bf16[4,128,204...) custom-call(bf16[128,2048]{1,0:T(8,128)(2,1)} %bitcast.111, ...), custom_call_target="tpu_custom_call" | custom-call | bytes 314572800 | tf_op jit(solution)/shard_map/head/pallas_call | solution.py:1253
  90.1 6.1 %all-to-all-start = ((bf16[128,16,1536]{2,1,0:T(8,128)(2,1)}), bf16[128,16,1536]{2,1,0:T(8,128)(2,1)}, u32[]{:S(2)}, u32[]{:S(2)}) async-start(bf16[128,16,1536]{2,1,0:T(8,128)(2,1)} %bitcast.90), calls=%async_computation | async-start | bytes 12582912 | tf_op jit(solution)/shard_map/all_to_all | solution.py:1338
  97.1 6.8 %pack_tokens.1.grads = bf16[2048,1536]{1,0:T(8,128)(2,1)S(1)} custom-call(bf16[8,32,128]{2,1,0:T(8,128)(2,1)S(1)} %copy-done.7, bf16[128,2048]{1,0:T(8,128)(2,1)S(1)} %bitcast.82, bf16[8,32,128]{2,1,0:T(8,128)(2,1)S(1)} %bitcast.86, bf16[8,32,128]{2,1,0:T(8,128)(2,1)S(1)} %bitcast.84), custom_call_target="tpu_custom_call" | custom-call | flops 3221225472 | bytes 8388608 | tf_op jit(solution)/shard_map/pack_tokens/pallas_call | solution.py:773
  103.8 2.7 copy-done.1
  106.5 65.3 %all-to-all-done = bf16[128,16,1536]{2,1,0:T(8,128)(2,1)} async-done(((bf16[128,16,1536]{2,1,0:T(8,128)(2,1)}), bf16[128,16,1536]{2,1,0:T(8,128)(2,1)}, u32[]{:S(2)}, u32[]{:S(2)}) %all-to-all-start) | async-done | bytes 6291488 | tf_op jit(solution)/shard_map/all_to_all | solution.py:1338
  171.9 10.8 %all-to-all-start.1 = ((bf16[128,16,1536]{2,1,0:T(8,128)(2,1)}), bf16[128,16,1536]{2,1,0:T(8,128)(2,1)}, u32[]{:S(2)}, u32[]{:S(2)}) async-start(bf16[128,16,1536]{2,1,0:T(8,128)(2,1)} %bitcast.73), calls=%async_computation.1 | async-start | bytes 12582912 | tf_op jit(solution)/shard_map/all_to_all | solution.py:1338
  182.7 7.4 %unpack_slots.2 = bf16[2,768,2048]{2,1,0:T(8,128)(2,1)S(1)} custom-call(bf16[2048,1536]{1,0:T(8,128)(2,1)} %bitcast.11.packed), custom_call_target="tpu_custom_call" | custom-call | flops 2415919104 | bytes 14680064 | tf_op jit(solution)/shard_map/unpack_slots/pallas_call | solution.py:814
  190.1 11.3 %fusion.33 = f32[2,768,1024]{2,1,0:T(8,128)S(1)} fusion(bf16[2,768,2048]{2,1,0:T(8,128)(2,1)S(1)} %unpack_slots.2, bf16[2,2048,1024]{2,1,0:T(8,128)(2,1)} %param.24), kind=kOutput, calls=%fused_computation.65 | convolution fusion | flops 6442450944 | bytes 20971520 | tf_op jit(solution)/shard_map/esd,edf->esf/dot_general | solution.py:1437
  201.5 2.7 copy-done.8
  206.3 3.7 convolution_convert_fusion.1.values
  210.0 5.4 pack_slots.2
  215.5 2.7 copy-done.3
  218.2 40.1 %all-to-all-done.1 = bf16[128,16,1536]{2,1,0:T(8,128)(2,1)} async-done(((bf16[128,16,1536]{2,1,0:T(8,128)(2,1)}), bf16[128,16,1536]{2,1,0:T(8,128)(2,1)}, u32[]{:S(2)}, u32[]{:S(2)}) %all-to-all-start.1) | async-done | bytes 6291488 | tf_op jit(solution)/shard_map/all_to_all | solution.py:1338
  258.3 10.8 %all-to-all-start.2 = ((bf16[128,16,1536]{2,1,0:T(8,128)(2,1)}), bf16[128,16,1536]{2,1,0:T(8,128)(2,1)}, u32[]{:S(2)}, u32[]{:S(2)}) async-start(bf16[128,16,1536]{2,1,0:T(8,128)(2,1)} %bitcast.77), calls=%async_computation.2 | async-start | bytes 12582912 | tf_op jit(solution)/shard_map/all_to_all | solution.py:1338
  270.0 3.9 copy.55
  273.9 7.5 %unpack_slots.3 = bf16[2,768,2048]{2,1,0:T(8,128)(2,1)S(1)} custom-call(bf16[2048,1536]{1,0:T(8,128)(2,1)} %bitcast.13.packed), custom_call_target="tpu_custom_call" | custom-call | flops 2415919104 | bytes 14680064 | tf_op jit(solution)/shard_map/unpack_slots/pallas_call | solution.py:814
  281.5 8.8 %multiply_convert_fusion.1 = (bf16[2,768,512]{2,1,0:T(8,128)(2,1)S(1)}, bf16[2,768,512]{2,1,0:T(8,128)(2,1)S(1)}) fusion(f32[2,768,1024]{2,1,0:T(8,128)} %copy-done.8, bf16[2,768,2048]{2,1,0:T(8,128)(2,1)S(1)} %unpack_slots.3, bf16[2,2048,512]{2,1,0:T(8,128)(2,1)S(1)} %copy-done.25), kind=kOutput, calls=%fused_computation.4 | convolution fusion | flops 3231449088 | bytes 19922944 | tf_op jit(solution)/shard_map/esd,edf->esf/dot_general | solution.py:1449
  290.3 11.7 %convolution_convert_fusion.values = bf16[2,768,2048]{2,1,0:T(8,128)(2,1)S(1)} fusion(bf16[2,2048,1024]{2,1,0:T(8,128)(2,1)} %param.24, bf16[2,768,512]{2,1,0:T(8,128)(2,1)S(1)} %get-tuple-element.137, bf16[2,768,512]{2,1,0:T(8,128)(2,1)S(1)} %get-tuple-element.136), kind=kOutput, calls=%fused_computation | convolution fusion | flops 6451888128 | bytes 17825792 | tf_op jit(solution)/shard_map/esf,edf->esd/dot_general | solution.py:1455
  302.0 5.4 pack_slots.3
  307.5 2.6 copy-done.2
  310.1 34.6 %all-to-all-done.2 = bf16[128,16,1536]{2,1,0:T(8,128)(2,1)} async-done(((bf16[128,16,1536]{2,1,0:T(8,128)(2,1)}), bf16[128,16,1536]{2,1,0:T(8,128)(2,1)}, u32[]{:S(2)}, u32[]{:S(2)}) %all-to-all-start.2) | async-done | bytes 6291488 | tf_op jit(solution)/shard_map/all_to_all | solution.py:1338
  344.7 19.4 %all-to-all-start.3 = ((bf16[128,16,1536]{2,1,0:T(8,128)(2,1)}), bf16[128,16,1536]{2,1,0:T(8,128)(2,1)}, u32[]{:S(2)}, u32[]{:S(2)}) async-start(bf16[128,16,1536]{2,1,0:T(8,128)(2,1)} %bitcast.76), calls=%async_computation.3 | async-start | bytes 12582912 | tf_op jit(solution)/shard_map/all_to_all | solution.py:1338
  364.2 1.9 fusion.13
  374.5 3.8 side_by_side.1
  378.3 5.4 all_marks.1.marks_in
  390.0 10.1 %fusion.34 = f32[2,2048,512]{2,1,0:T(8,128)} fusion(bf16[2,768,2048]{2,1,0:T(8,128)(2,1)} %copy-done.5, bf16[2,768,512]{2,1,0:T(8,128)(2,1)S(1)} %copy-done.14), kind=kOutput, calls=%fused_computation.66 | convolution fusion | flops 3221225472 | bytes 16252928 | tf_op jit(solution)/shard_map/esd,esf->edf/dot_general | solution.py:1460
  400.1 10.4 %fusion.3 = f32[2,2048,1024]{2,1,0:T(8,128)} fusion(bf16[2,768,2048]{2,1,0:T(8,128)(2,1)S(1)} %bitcast.79, bf16[2,768,512]{2,1,0:T(8,128)(2,1)S(1)} %copy-done.30, bf16[2,768,512]{2,1,0:T(8,128)(2,1)S(1)} %copy-done.28), kind=kOutput, calls=%fused_computation.17 | convolution fusion | flops 6448742400 | bytes 26214400 | tf_op jit(solution)/shard_map/esd,esf->edf/dot_general | solution.py:1463
  410.6 10.4 %sum_gated.1 = (f32[128,2048]{1,0:T(8,128)S(1)}, f32[8,128,32]{2,1,0:T(8,128)S(1)}) custom-call(bf16[8,32,128]{2,1,0:T(8,128)(2,1)S(1)} %copy-done.7, bf16[2048,1536]{1,0:T(8,128)(2,1)} %bitcast.15.packed, bf16[2048,1536]{1,0:T(8,128)(2,1)S(1)} %bitcast.75, bf16[8,32,128]{2,1,0:T(8,128)(2,1)S(1)} %bitcast.87, bf16[8,32,128]{2,1,0:T(8,128)(2,1)S(1)} %bitcast.85), custom_call_target="tpu_custom_call" | custom-call | flops 3221225472 | bytes 14680064 | tf_op jit(solution)/shard_map/sum_gated/pallas_call | solution.py:918
  423.0 2.3 add.36.stream_in
  428.3 11.5 %all-to-all-done.3 = bf16[128,16,1536]{2,1,0:T(8,128)(2,1)} async-done(((bf16[128,16,1536]{2,1,0:T(8,128)(2,1)}), bf16[128,16,1536]{2,1,0:T(8,128)(2,1)}, u32[]{:S(2)}, u32[]{:S(2)}) %all-to-all-start.3) | async-done | bytes 6291488 | tf_op jit(solution)/shard_map/all_to_all | solution.py:1338
  439.8 92.3 %tail.1 = (f32[128,2048]{1,0:T(8,128)}, f32[128,2048]{1,0:T(8,128)}, bf16[128,2048]{1,0:T(8,128)(2,1)}, bf16[4,2,4,4,16,256]{5,4,3,2,1,0:T(8,128)(2,1)}, f32[1,2...) custom-call(bf16[2048,1536]{1,0:T(8,128)(2,1)} %bitcast.17.packed, ...), custom_call_target="tpu_custom_call" | custom-call | bytes 314572800 | tf_op jit(solution)/shard_map/tail/pallas_call | solution.py:655
  535.3 2.8 bitcast_convert_fusion
  (101 shorter events, 34.6 us)
Async XLA Ops:
  0.6 95.6 %copy-start = (bf16[2048,256]{1,0:T(8,128)(2,1)S(1)}, bf16[2048,256]{1,0:T(8,128)(2,1)}, u32[]{:S(2)}) copy-start(bf16[2048,256]{1,0:T(8,128)(2,1)} %param.23) | copy-start | bytes 3145732
  90.1 6.2 %copy-start.17 = (bf16[128,2048]{1,0:T(8,128)(2,1)S(1)}, bf16[128,2048]{1,0:T(8,128)(2,1)}, u32[]{:S(2)}) copy-start(bf16[128,2048]{1,0:T(8,128)(2,1)} %get-tuple-element.64) | copy-start | bytes 1572868
  90.1 6.2 %copy-start.26 = (f32[128,256]{1,0:T(8,128)S(1)}, f32[128,256]{1,0:T(8,128)}, u32[]{:S(2)}) copy-start(f32[128,256]{1,0:T(8,128)} %get-tuple-element.63) | copy-start | bytes 393220
  90.1 7.0 %copy-start.6 = (bf16[1,128,2048]{2,1,0:T(8,128)(2,1)S(1)}, bf16[1,128,2048]{2,1,0:T(8,128)(2,1)}, u32[]{:S(2)}) copy-start(bf16[1,128,2048]{2,1,0:T(8,128)(2,1)} %param.28) | copy-start | bytes 1572868
  90.1 7.0 %copy-start.7 = (bf16[8,32,128]{2,1,0:T(8,128)(2,1)S(1)}, bf16[8,32,128]{2,1,0:T(8,128)(2,1)}, u32[]{:S(2)}) copy-start(bf16[8,32,128]{2,1,0:T(8,128)(2,1)} %get-tuple-element.62.code) | copy-start | bytes 196612
  90.1 81.8 %all-to-all-start = ((bf16[128,16,1536]{2,1,0:T(8,128)(2,1)}), bf16[128,16,1536]{2,1,0:T(8,128)(2,1)}, u32[]{:S(2)}, u32[]{:S(2)}) async-start(bf16[128,16,1536]{2,1,0:T(8,128)(2,1)} %bitcast.90), calls=%async_computation | async-start | bytes 12582912 | tf_op jit(solution)/shard_map/all_to_all | solution.py:1338
  171.9 86.4 %all-to-all-start.1 = ((bf16[128,16,1536]{2,1,0:T(8,128)(2,1)}), bf16[128,16,1536]{2,1,0:T(8,128)(2,1)}, u32[]{:S(2)}, u32[]{:S(2)}) async-start(bf16[128,16,1536]{2,1,0:T(8,128)(2,1)} %bitcast.73), calls=%async_computation.1 | async-start | bytes 12582912 | tf_op jit(solution)/shard_map/all_to_all | solution.py:1338
  190.1 11.4 %copy-start.4 = (bf16[2,768,2048]{2,1,0:T(8,128)(2,1)}, bf16[2,768,2048]{2,1,0:T(8,128)(2,1)S(1)}, u32[]{:S(2)}) copy-start(bf16[2,768,2048]{2,1,0:T(8,128)(2,1)S(1)} %unpack_slots.2) | copy-start | bytes 18874372
  206.3 3.7 copy-start.13
  258.3 86.4 %all-to-all-start.2 = ((bf16[128,16,1536]{2,1,0:T(8,128)(2,1)}), bf16[128,16,1536]{2,1,0:T(8,128)(2,1)}, u32[]{:S(2)}, u32[]{:S(2)}) async-start(bf16[128,16,1536]{2,1,0:T(8,128)(2,1)} %bitcast.77), calls=%async_computation.2 | async-start | bytes 12582912 | tf_op jit(solution)/shard_map/all_to_all | solution.py:1338
  273.9 7.6 %copy-start.25 = (bf16[2,2048,512]{2,1,0:T(8,128)(2,1)S(1)}, bf16[2,2048,512]{2,1,0:T(8,128)(2,1)}, u32[]{:S(2)}) copy-start(bf16[2,2048,512]{2,1,0:T(8,128)(2,1)} %param.25) | copy-start | bytes 12582916
  281.5 8.8 %copy-start.5 = (bf16[2,768,2048]{2,1,0:T(8,128)(2,1)}, bf16[2,768,2048]{2,1,0:T(8,128)(2,1)S(1)}, u32[]{:S(2)}) copy-start(bf16[2,768,2048]{2,1,0:T(8,128)(2,1)S(1)} %unpack_slots.3) | copy-start | bytes 18874372
  290.3 11.7 %copy-start.27 = (bf16[2,768,512]{2,1,0:T(8,128)(2,1)}, bf16[2,768,512]{2,1,0:T(8,128)(2,1)S(1)}, u32[]{:S(2)}) copy-start(bf16[2,768,512]{2,1,0:T(8,128)(2,1)S(1)} %get-tuple-element.136) | copy-start | bytes 4718596
  290.3 11.7 %copy-start.29 = (bf16[2,768,512]{2,1,0:T(8,128)(2,1)}, bf16[2,768,512]{2,1,0:T(8,128)(2,1)S(1)}, u32[]{:S(2)}) copy-start(bf16[2,768,512]{2,1,0:T(8,128)(2,1)S(1)} %get-tuple-element.137) | copy-start | bytes 4718596
  344.7 19.4 %copy-start.9 = (bf16[2,128,2048]{2,1,0:T(8,128)(2,1)S(1)}, bf16[2,128,2048]{2,1,0:T(8,128)(2,1)}, u32[]{:S(2)}) copy-start(bf16[2,128,2048]{2,1,0:T(8,128)(2,1)} %get-tuple-element.75) | copy-start | bytes 3145732
  344.7 95.1 %all-to-all-start.3 = ((bf16[128,16,1536]{2,1,0:T(8,128)(2,1)}), bf16[128,16,1536]{2,1,0:T(8,128)(2,1)}, u32[]{:S(2)}, u32[]{:S(2)}) async-start(bf16[128,16,1536]{2,1,0:T(8,128)(2,1)} %bitcast.76), calls=%async_computation.3 | async-start | bytes 12582912 | tf_op jit(solution)/shard_map/all_to_all | solution.py:1338
  364.2 3.8 copy-start.10
  364.2 5.1 copy-start.11
  388.5 11.6 %slice-start.2 = ((s8[6291456]{0:T(1024)(128)(4,1)}), s8[4194304]{0:T(1024)(128)(4,1)S(1)}, s32[]{:S(2)}) async-start(s8[6291456]{0:T(1024)(128)(4,1)} %bitcast.78), calls=%async_computation.6 | async-start | bytes 8388608
  390.0 10.1 %slice-start.3 = ((s8[6291456]{0:T(1024)(128)(4,1)}), s8[2097152]{0:T(1024)(128)(4,1)S(1)}, s32[]{:S(2)}) async-start(s8[6291456]{0:T(1024)(128)(4,1)} %bitcast.78), calls=%async_computation.7 | async-start | bytes 4194304
  390.0 10.1 %copy-start.28 = (bf16[2,768,512]{2,1,0:T(8,128)(2,1)S(1)}, bf16[2,768,512]{2,1,0:T(8,128)(2,1)}, u32[]{:S(2)}) copy-start(bf16[2,768,512]{2,1,0:T(8,128)(2,1)} %copy-done.27) | copy-start | bytes 4718596
  390.0 10.1 %copy-start.30 = (bf16[2,768,512]{2,1,0:T(8,128)(2,1)S(1)}, bf16[2,768,512]{2,1,0:T(8,128)(2,1)}, u32[]{:S(2)}) copy-start(bf16[2,768,512]{2,1,0:T(8,128)(2,1)} %copy-done.29) | copy-start | bytes 4718596
  390.0 20.6 %slice-start = ((s8[6291456]{0:T(1024)(128)(4,1)}), s8[4194304]{0:T(1024)(128)(4,1)S(1)}, s32[]{:S(2)}) async-start(s8[6291456]{0:T(1024)(128)(4,1)} %bitcast.74), calls=%async_computation.4 | async-start | bytes 8388608
  400.1 10.5 %slice-start.1 = ((s8[6291456]{0:T(1024)(128)(4,1)}), s8[2097152]{0:T(1024)(128)(4,1)S(1)}, s32[]{:S(2)}) async-start(s8[6291456]{0:T(1024)(128)(4,1)} %bitcast.74), calls=%async_computation.5 | async-start | bytes 4194304
  532.1 6.0 %copy-start.15 = (f32[128,2048]{1,0:T(8,128)S(1)}, f32[128,2048]{1,0:T(8,128)}, u32[]{:S(2)}) copy-start(f32[128,2048]{1,0:T(8,128)} %get-tuple-element.100) | copy-start | bytes 3145732
  532.1 6.0 %copy-start.16 = (f32[128,2048]{1,0:T(8,128)S(1)}, f32[128,2048]{1,0:T(8,128)}, u32[]{:S(2)}) copy-start(f32[128,2048]{1,0:T(8,128)} %get-tuple-element.101) | copy-start | bytes 3145732
  535.3 3.9 copy-start.18
  535.3 4.7 copy-start.23
  535.3 5.3 copy-start.20
  535.3 5.9 %copy-start.19 = (f32[64,512]{1,0:T(8,128)S(1)}, f32[64,512]{1,0:T(8,128)}, u32[]{:S(2)}) copy-start(f32[64,512]{1,0:T(8,128)} %get-tuple-element.165) | copy-start | bytes 393220
  538.1 3.8 copy-start.22
  538.1 4.4 copy-start.21
  (7 other events, 19.3 us)

commit v8 on v7

--- a/solution.py
+++ b/solution.py
@@ -237,8 +237,12 @@
             total = total + self.third[half].astype(jnp.float32)
             start = 0
             for piece in pieces:
-                piece[self.half(half)] = total[:, start : start + piece.shape[1]]
-                start += piece.shape[1]
+                width = piece.shape[-1]
+                if len(piece.shape) == 3:
+                    piece[self.half(half), 0] = total[:, start : start + width]
+                else:
+                    piece[self.half(half)] = total[:, start : start + width]
+                start += width
 
     def end(self):
         for copy in [*self.one_copies.values(), *self.two_copies.values(), *self.three_copies]:
@@ -429,10 +433,10 @@
     row_peers = [(peer, col) for peer in (sibling, partner, across)]
     greet(row_peers)
     greet(pre_scatter.y_peers + pre_scatter.z_peers + [pre_scatter.x_peer])
-    steps, depth = held.shape[:2]
+    steps, depth = 4, held.shape[1]
     inner = query.shape[1]
     sources = [packed.at[pl.ds(i * depth, depth)] for i in range(steps)]
-    targets = [held.at[i] for i in range(steps)]
+    targets = [held.at[i % 2] for i in range(steps)]
     sources[1:1] = [marks_in]
     targets[1:1] = [marks]
     sources += [router_input_in, hidden_in, full_back, shared_parts_in]
@@ -445,9 +449,10 @@
     ]
     load_parts = pltpu.make_async_copy(shared_input_in, input_parts, load_sem.at[len(loads)])
     load_parts.start()
-    for load in loads:
+    load_marks = loads.pop(1)
+    load_marks.start()
+    for load in loads[:2] + loads[steps:]:
         load.start()
-    load_marks = loads.pop(1)
     load_input, load_hidden, load_back, load_shared, load_pre, load_rows, load_stream = loads[
         steps:
     ]
@@ -473,13 +478,15 @@
         for part in range(4):
             columns = slice(part * QUARTER, (part + 1) * QUARTER)
             if part < 3:
-                found = matmul(marks[0, :, rows], held[i, :, columns])
+                found = matmul(marks[0, :, rows], held[i % 2, :, columns])
             else:
-                found = matmul(marks[1, :, rows], held[i, :, :QUARTER])
+                found = matmul(marks[1, :, rows], held[i % 2, :, :QUARTER])
                 for j in (1, 2):
                     second = slice(j * QUARTER, (j + 1) * QUARTER)
-                    found = found + matmul(marks[j + 1, :, rows], held[i, :, second])
+                    found = found + matmul(marks[j + 1, :, rows], held[i % 2, :, second])
             routed[:, columns] = found if i == 0 else routed[:, columns] + found
+        if i + 2 < steps:
+            loads[i + 2].start()
     load_input.wait()
     load_hidden.wait()
     input_copy.wait_recv()
@@ -615,8 +622,10 @@
     router_rows[2][0].start()
     share_copy.wait_recv()
     share = share_sums[0] + share_low[1].astype(jnp.float32)
-    pieces[3][...] = share[:, : pieces[3].shape[1]]
-    pieces[4][...] = share[:, pieces[3].shape[1] :]
+    part = pieces[3].shape[2]
+    for i in range(2):
+        pieces[3][:, i] = share[:, i * part : (i + 1) * part]
+    pieces[4][...] = share[:, 2 * part :]
     pre_scatter.add_third(pieces[:2])
     add_gains(3)
     gain_attn_sum[...] = values[4, 0:1]
@@ -662,11 +671,20 @@
             jax.ShapeDtypeStruct((1, width), jnp.float32),
             jax.ShapeDtypeStruct((1, width), jnp.float32),
         ]
-        + [jax.ShapeDtypeStruct((shard, part), jnp.float32) for part in widths],
+        + [
+            jax.ShapeDtypeStruct(shape, jnp.float32)
+            for shape in (
+                (shard, widths[0]),
+                (shard, 1, widths[1]),
+                (shard, widths[2]),
+                (shard, 2, widths[3] // 2),
+                (shard, widths[4]),
+            )
+        ],
         in_specs=[away] * 10 + [space] * 17,
         out_specs=[space] * (6 + len(widths)),
         scratch_shapes=[
-            pltpu.VMEM((4, packed.shape[0] // 4, packed.shape[1]), low),
+            pltpu.VMEM((2, packed.shape[0] // 4, packed.shape[1]), low),
             pltpu.VMEM(marks.shape, low),
             pltpu.VMEM((rows, width), jnp.float32),
             pltpu.VMEM((rows, width), jnp.float32),
@@ -1052,13 +1070,13 @@
     place = gathers[0].place
     greet(gathers[0].z_peers + gathers[0].y_peers + [gathers[0].x_peer])
     greet([(sibling, col), (partner, col)])
-    pairs = ((mine_pre, (w_query, w_keyval)), (mine_shared, (w_shared_in, w_shared_out)))
-    for mine, shards in pairs:
-        start = 0
-        for shard in shards:
-            mine[:, start : start + shard.shape[1]] = shard[...]
-            start += shard.shape[1]
+    pre_start, shared_start = w_query.shape[1], w_shared_in.shape[2]
+    mine_pre[:, :pre_start] = w_query[...]
+    mine_pre[:, pre_start:] = w_keyval[:, 0]
     mine_back[...] = w_out[...]
+    for i in range(2):
+        mine_shared[:, i * shared_start : (i + 1) * shared_start] = w_shared_in[:, i]
+    mine_shared[:, 2 * shared_start : 3 * shared_start] = w_shared_out[...]
     first = inputs[...].astype(jnp.float32)
     factor = lax.rsqrt(jnp.mean(first * first, axis=1, keepdims=True) + epsilon)
     scale_one[...] = factor
@@ -1092,16 +1110,17 @@
     far_rows[0].start()
     near_rows[0].start()
     gathers[1].start()
+    other_shard.wait_recv()
+    own[4].start()
+    gathers[2].start()
     gathers[0].second()
     gathers[1].second()
-    for copy in own[2:4]:
+    for copy in own[2:5]:
         copy.wait()
     gathers[0].third()
     near_grads.start()
     gathers[1].third()
-    other_shard.wait_recv()
-    own[4].start()
-    gathers[2].start()
+    gathers[2].second()
 
     tokens = begin.shape[0]
 
@@ -1181,6 +1200,7 @@
         attended[:, columns] = matmul(weights, values[...]).astype(low)
         log_totals = jnp.where(lanes == head, highest + jnp.log(total), log_totals)
     norms[...] = log_totals
+    gathers[2].third()
     gathers[1].await_all()
     loads[2].start()
     loads[2].wait()
@@ -1191,10 +1211,7 @@
     copies = row_sum_copies(parts, near, far, outgoing, (sum_send, sum_recv), 0)
     copies[0].start()
     copies[1].start()
-    gathers[2].second()
     row_sum_forward(parts, near, outgoing, copies)
-    own[4].wait()
-    gathers[2].third()
     total = inputs[...].astype(jnp.float32) + row_sum_total(parts, near, far, copies)
     hidden[...] = total
     factor = lax.rsqrt(jnp.mean(total * total, axis=1, keepdims=True) + epsilon)
@@ -1240,8 +1257,8 @@
     tokens = 4 * rows
     shard_rows = shards[0].shape[0]
     inner = shards[0].shape[1]
-    pre_width = inner + shards[1].shape[1]
-    shared_width = shards[3].shape[1] + shards[4].shape[1]
+    pre_width = inner + shards[1].shape[2]
+    shared_width = 2 * shards[3].shape[2] + shards[4].shape[1]
     blocks = expert_count // BLOCK_EXPERTS
     spread = np.arange(size // 2, dtype=np.float32) * np.float32(2.0 / size)
     frequency = np.float32(rope_base) ** (-spread)
@@ -1363,7 +1380,6 @@
     inputs = block_in.reshape(rows_dev, model_width)
     grad_low = cotangent.reshape(rows_dev, model_width)
     shards = [w_query, w_keyval, w_out, w_shared_in, w_shared_out]
-    shards = [part.reshape(part.shape[0], -1) for part in shards]
     (
         full_pre,
         full_back,
@@ -1479,7 +1495,7 @@
     )
     router_input, router_parts, stream, shared_grads, group_one_t, marks = shadowed
 
-    widths = [part.shape[1] for part in shards]
+    widths = [part.size // part.shape[0] for part in shards]
     hidden_total, input_back, block_out, router_sum, gain_attn_sum, gain_ffn_sum, *sums = tail(
         (
             returned_grad,
@@ -1505,10 +1521,6 @@
         (inputs, scale_one, gain_attn[None]),
         widths,
     )
-    sums = [
-        part.reshape(like.shape)
-        for part, like in zip(sums, (w_query, w_keyval, w_out, w_shared_in, w_shared_out))
-    ]
     return (
         block_out.reshape(1, rows_dev, model_width),
         (hidden_total + input_back).reshape(1, rows_dev, model_width),

time: 553 us -> 545 us (0.986)
  starting transfers between devices: 47.2 us -> 37.6 us
    all_to_all x4, starting transfers between devices: 47.2 us -> 37.6 us  [exchange(): lax.all_to_all(pairs, ('row', 'col'), split_axis=0, concat_axis=0, tiled=...]
    unnamed x79 -> x84, local copies, waits for them, and re-layouts: 20.4 us -> 20.1 us
where the time goes in v8:
time: 545 us; the launch traced here: 535 us
  Pallas kernels  234 us (43%)
  waiting for transfers between devices  151 us (28%)
  matrix products  76 us (14%)
  starting transfers between devices  37.6 us (7%)
  local copies, waits for them, and re-layouts  26.9 us (5%)
  other arithmetic  7.58 us (1%)
    all_to_all x4, waiting for transfers between devices, exchange(): lax.all_to_all(pairs, ('row', 'col'), split_axis=0, concat_axis=0, tiled=...  151 us
    pallas_call x1, Pallas kernels, tail(): pl.pallas_call(tail_kernel, out_shape=[jax.ShapeDtypeStruct((rows, width)...  93.5 us
    pallas_call x1, Pallas kernels, head(): pl.pallas_call(head_kernel, out_shape=[full((2, 4, 4, shard_rows, pre_wid...  88.7 us
    all_to_all x4, starting transfers between devices, exchange(): lax.all_to_all(pairs, ('row', 'col'), split_axis=0, concat_axis=0, tiled=...  37.6 us
    unnamed x84, local copies, waits for them, and re-layouts  20.1 us
    pallas_call x2, Pallas kernels, unpack_slots(): pl.pallas_call(unpack_slots_kernel, grid=(blocks,), out_shape=jax.ShapeDt...  14.9 us
    dot_general x1, matrix products, per_device(): jnp.einsum('esf,edf->esd', expert_pre_grad, w_expert_in, preferred_elemen...  11.7 us
    dot_general x1, matrix products, per_device(): jnp.einsum('esd,edf->esf', expert_in, w_expert_in, preferred_element_type...  11.3 us
  transfers between devices with their start and end apart: 4, of which 4 were waited for; matrix products, arithmetic and copies ran while one was open for 16% of the time, Pallas kernels for 10%

profile of v8, /device:TPU:1, one launch (start us, length us, event | category | flops | bytes accessed | tf_op | source)
XLA Modules:
  0.0 535.4 jit_solution(5828629160956572159)
XLA Ops:
  3.6 88.7 %head.1 = (bf16[2,4,4,64,768]{4,3,2,1,0:T(8,128)(2,1)}, bf16[2,4,4,64,512]{4,3,2,1,0:T(8,128)(2,1)}, bf16[2,4,4,64,768]{4,3,2,1,0:T(8,128)(2,1)}, bf16[4,128,204...) custom-call(bf16[128,2048]{1,0:T(8,128)(2,1)} %bitcast.105, ...), custom_call_target="tpu_custom_call" | custom-call | bytes 314572800 | tf_op jit(solution)/shard_map/head/pallas_call | solution.py:1270
  92.3 4.9 all-to-all-start
  98.0 6.8 %pack_tokens.1.grads = bf16[2048,1536]{1,0:T(8,128)(2,1)S(1)} custom-call(bf16[8,32,128]{2,1,0:T(8,128)(2,1)S(1)} %copy-done.7, bf16[128,2048]{1,0:T(8,128)(2,1)S(1)} %bitcast.76, bf16[8,32,128]{2,1,0:T(8,128)(2,1)S(1)} %bitcast.80, bf16[8,32,128]{2,1,0:T(8,128)(2,1)S(1)} %bitcast.78), custom_call_target="tpu_custom_call" | custom-call | flops 3221225472 | bytes 8388608 | tf_op jit(solution)/shard_map/pack_tokens/pallas_call | solution.py:791
  104.8 2.7 copy-done.1
  107.5 64.9 %all-to-all-done = bf16[128,16,1536]{2,1,0:T(8,128)(2,1)} async-done(((bf16[128,16,1536]{2,1,0:T(8,128)(2,1)}), bf16[128,16,1536]{2,1,0:T(8,128)(2,1)}, u32[]{:S(2)}, u32[]{:S(2)}) %all-to-all-start) | async-done | bytes 6291488 | tf_op jit(solution)/shard_map/all_to_all | solution.py:1355
  172.5 10.8 %all-to-all-start.1 = ((bf16[128,16,1536]{2,1,0:T(8,128)(2,1)}), bf16[128,16,1536]{2,1,0:T(8,128)(2,1)}, u32[]{:S(2)}, u32[]{:S(2)}) async-start(bf16[128,16,1536]{2,1,0:T(8,128)(2,1)} %bitcast.67), calls=%async_computation.1 | async-start | bytes 12582912 | tf_op jit(solution)/shard_map/all_to_all | solution.py:1355
  183.3 7.4 %unpack_slots.2 = bf16[2,768,2048]{2,1,0:T(8,128)(2,1)S(1)} custom-call(bf16[2048,1536]{1,0:T(8,128)(2,1)} %bitcast.10.packed), custom_call_target="tpu_custom_call" | custom-call | flops 2415919104 | bytes 14680064 | tf_op jit(solution)/shard_map/unpack_slots/pallas_call | solution.py:832
  190.7 11.3 %fusion.33 = f32[2,768,1024]{2,1,0:T(8,128)S(1)} fusion(bf16[2,768,2048]{2,1,0:T(8,128)(2,1)S(1)} %unpack_slots.2, bf16[2,2048,1024]{2,1,0:T(8,128)(2,1)} %param.24), kind=kOutput, calls=%fused_computation.64 | convolution fusion | flops 6442450944 | bytes 20971520 | tf_op jit(solution)/shard_map/esd,edf->esf/dot_general | solution.py:1453
  202.0 2.7 copy-done.8
  206.9 3.7 convolution_convert_fusion.1.values
  210.6 5.4 %pack_slots.2 = bf16[2048,1536]{1,0:T(8,128)(2,1)S(1)} custom-call(bf16[2,768,2048]{2,1,0:T(8,128)(2,1)S(1)} %convolution_convert_fusion.1.values), custom_call_target="tpu_custom_call" | custom-call | flops 2415919104 | bytes 14680064 | tf_op jit(solution)/shard_map/pack_slots/pallas_call | solution.py:861
  216.1 2.7 copy-done.3
  218.8 40.1 %all-to-all-done.1 = bf16[128,16,1536]{2,1,0:T(8,128)(2,1)} async-done(((bf16[128,16,1536]{2,1,0:T(8,128)(2,1)}), bf16[128,16,1536]{2,1,0:T(8,128)(2,1)}, u32[]{:S(2)}, u32[]{:S(2)}) %all-to-all-start.1) | async-done | bytes 6291488 | tf_op jit(solution)/shard_map/all_to_all | solution.py:1355
  258.9 10.8 %all-to-all-start.2 = ((bf16[128,16,1536]{2,1,0:T(8,128)(2,1)}), bf16[128,16,1536]{2,1,0:T(8,128)(2,1)}, u32[]{:S(2)}, u32[]{:S(2)}) async-start(bf16[128,16,1536]{2,1,0:T(8,128)(2,1)} %bitcast.71), calls=%async_computation.2 | async-start | bytes 12582912 | tf_op jit(solution)/shard_map/all_to_all | solution.py:1355
  270.6 3.9 copy.55
  274.5 7.6 %unpack_slots.3 = bf16[2,768,2048]{2,1,0:T(8,128)(2,1)S(1)} custom-call(bf16[2048,1536]{1,0:T(8,128)(2,1)} %bitcast.12.packed), custom_call_target="tpu_custom_call" | custom-call | flops 2415919104 | bytes 14680064 | tf_op jit(solution)/shard_map/unpack_slots/pallas_call | solution.py:832
  282.1 8.8 %multiply_convert_fusion.1 = (bf16[2,768,512]{2,1,0:T(8,128)(2,1)S(1)}, bf16[2,768,512]{2,1,0:T(8,128)(2,1)S(1)}) fusion(f32[2,768,1024]{2,1,0:T(8,128)} %copy-done.8, bf16[2,768,2048]{2,1,0:T(8,128)(2,1)S(1)} %unpack_slots.3, bf16[2,2048,512]{2,1,0:T(8,128)(2,1)S(1)} %copy-done.27), kind=kOutput, calls=%fused_computation.4 | convolution fusion | flops 3231449088 | bytes 19922944 | tf_op jit(solution)/shard_map/esd,edf->esf/dot_general | solution.py:1465
  290.9 11.7 %convolution_convert_fusion.values = bf16[2,768,2048]{2,1,0:T(8,128)(2,1)S(1)} fusion(bf16[2,2048,1024]{2,1,0:T(8,128)(2,1)} %param.24, bf16[2,768,512]{2,1,0:T(8,128)(2,1)S(1)} %get-tuple-element.113, bf16[2,768,512]{2,1,0:T(8,128)(2,1)S(1)} %get-tuple-element.112), kind=kOutput, calls=%fused_computation | convolution fusion | flops 6451888128 | bytes 17825792 | tf_op jit(solution)/shard_map/esf,edf->esd/dot_general | solution.py:1471
  302.6 5.4 %pack_slots.3 = bf16[2048,1536]{1,0:T(8,128)(2,1)S(1)} custom-call(bf16[2,768,2048]{2,1,0:T(8,128)(2,1)S(1)} %convolution_convert_fusion.values), custom_call_target="tpu_custom_call" | custom-call | flops 2415919104 | bytes 14680064 | tf_op jit(solution)/shard_map/pack_slots/pallas_call | solution.py:861
  308.0 2.6 copy-done.2
  310.7 34.7 %all-to-all-done.2 = bf16[128,16,1536]{2,1,0:T(8,128)(2,1)} async-done(((bf16[128,16,1536]{2,1,0:T(8,128)(2,1)}), bf16[128,16,1536]{2,1,0:T(8,128)(2,1)}, u32[]{:S(2)}, u32[]{:S(2)}) %all-to-all-start.2) | async-done | bytes 6291488 | tf_op jit(solution)/shard_map/all_to_all | solution.py:1355
  345.3 11.2 %all-to-all-start.3 = ((bf16[128,16,1536]{2,1,0:T(8,128)(2,1)}), bf16[128,16,1536]{2,1,0:T(8,128)(2,1)}, u32[]{:S(2)}, u32[]{:S(2)}) async-start(bf16[128,16,1536]{2,1,0:T(8,128)(2,1)} %bitcast.70), calls=%async_computation.3 | async-start | bytes 12582912 | tf_op jit(solution)/shard_map/all_to_all | solution.py:1355
  356.5 1.9 fusion.13
  366.8 3.8 side_by_side.1
  370.6 5.4 %all_marks.1.marks_in = bf16[4,128,2048]{2,1,0:T(8,128)(2,1)} custom-call(bf16[8,128,32]{2,1,0:T(8,128)(2,1)} %bitcast.109), custom_call_target="tpu_custom_call" | custom-call | flops 67108864 | bytes 4194304 | tf_op jit(solution)/shard_map/all_marks/pallas_call | solution.py:890
  382.3 10.1 %fusion.34 = f32[2,2048,512]{2,1,0:T(8,128)} fusion(bf16[2,768,2048]{2,1,0:T(8,128)(2,1)} %copy-done.5, bf16[2,768,512]{2,1,0:T(8,128)(2,1)S(1)} %copy-done.14), kind=kOutput, calls=%fused_computation.65 | convolution fusion | flops 3221225472 | bytes 16252928 | tf_op jit(solution)/shard_map/esd,esf->edf/dot_general | solution.py:1476
  392.5 10.4 %fusion.3 = f32[2,2048,1024]{2,1,0:T(8,128)} fusion(bf16[2,768,2048]{2,1,0:T(8,128)(2,1)S(1)} %bitcast.73, bf16[2,768,512]{2,1,0:T(8,128)(2,1)S(1)} %copy-done.32, bf16[2,768,512]{2,1,0:T(8,128)(2,1)S(1)} %copy-done.30), kind=kOutput, calls=%fused_computation.17 | convolution fusion | flops 6448742400 | bytes 26214400 | tf_op jit(solution)/shard_map/esd,esf->edf/dot_general | solution.py:1479
  402.9 10.4 %sum_gated.1 = (f32[128,2048]{1,0:T(8,128)S(1)}, f32[8,128,32]{2,1,0:T(8,128)S(1)}) custom-call(bf16[8,32,128]{2,1,0:T(8,128)(2,1)S(1)} %copy-done.7, bf16[2048,1536]{1,0:T(8,128)(2,1)} %bitcast.14.packed, bf16[2048,1536]{1,0:T(8,128)(2,1)S(1)} %bitcast.69, bf16[8,32,128]{2,1,0:T(8,128)(2,1)S(1)} %bitcast.81, bf16[8,32,128]{2,1,0:T(8,128)(2,1)S(1)} %bitcast.79), custom_call_target="tpu_custom_call" | custom-call | flops 3221225472 | bytes 14680064 | tf_op jit(solution)/shard_map/sum_gated/pallas_call | solution.py:936
  415.3 2.3 add.36.stream_in
  420.6 11.5 %all-to-all-done.3 = bf16[128,16,1536]{2,1,0:T(8,128)(2,1)} async-done(((bf16[128,16,1536]{2,1,0:T(8,128)(2,1)}), bf16[128,16,1536]{2,1,0:T(8,128)(2,1)}, u32[]{:S(2)}, u32[]{:S(2)}) %all-to-all-start.3) | async-done | bytes 6291488 | tf_op jit(solution)/shard_map/all_to_all | solution.py:1355
  432.2 93.5 %tail.1 = (f32[128,2048]{1,0:T(8,128)}, f32[128,2048]{1,0:T(8,128)}, bf16[128,2048]{1,0:T(8,128)(2,1)}, bf16[4,2,4,4,16,256]{5,4,3,2,1,0:T(8,128)(2,1)}, f32[1,2...) custom-call(bf16[2048,1536]{1,0:T(8,128)(2,1)} %bitcast.16.packed, ...), custom_call_target="tpu_custom_call" | custom-call | bytes 314572800 | tf_op jit(solution)/shard_map/tail/pallas_call | solution.py:664
  525.8 2.9 bitcast_convert_fusion
  (105 shorter events, 32.7 us)
Async XLA Ops:
  0.6 96.6 %copy-start = (bf16[2048,256]{1,0:T(8,128)(2,1)S(1)}, bf16[2048,256]{1,0:T(8,128)(2,1)}, u32[]{:S(2)}) copy-start(bf16[2048,256]{1,0:T(8,128)(2,1)} %param.23) | copy-start | bytes 3145732
  92.3 4.9 copy-start.17
  92.3 4.9 copy-start.28
  92.3 5.7 %copy-start.6 = (bf16[1,128,2048]{2,1,0:T(8,128)(2,1)S(1)}, bf16[1,128,2048]{2,1,0:T(8,128)(2,1)}, u32[]{:S(2)}) copy-start(bf16[1,128,2048]{2,1,0:T(8,128)(2,1)} %param.28) | copy-start | bytes 1572868
  92.3 5.7 %copy-start.7 = (bf16[8,32,128]{2,1,0:T(8,128)(2,1)S(1)}, bf16[8,32,128]{2,1,0:T(8,128)(2,1)}, u32[]{:S(2)}) copy-start(bf16[8,32,128]{2,1,0:T(8,128)(2,1)} %get-tuple-element.62.code) | copy-start | bytes 196612
  92.3 80.1 %all-to-all-start = ((bf16[128,16,1536]{2,1,0:T(8,128)(2,1)}), bf16[128,16,1536]{2,1,0:T(8,128)(2,1)}, u32[]{:S(2)}, u32[]{:S(2)}) async-start(bf16[128,16,1536]{2,1,0:T(8,128)(2,1)} %bitcast.84), calls=%async_computation | async-start | bytes 12582912 | tf_op jit(solution)/shard_map/all_to_all | solution.py:1355
  172.5 86.4 %all-to-all-start.1 = ((bf16[128,16,1536]{2,1,0:T(8,128)(2,1)}), bf16[128,16,1536]{2,1,0:T(8,128)(2,1)}, u32[]{:S(2)}, u32[]{:S(2)}) async-start(bf16[128,16,1536]{2,1,0:T(8,128)(2,1)} %bitcast.67), calls=%async_computation.1 | async-start | bytes 12582912 | tf_op jit(solution)/shard_map/all_to_all | solution.py:1355
  190.7 11.4 %copy-start.4 = (bf16[2,768,2048]{2,1,0:T(8,128)(2,1)}, bf16[2,768,2048]{2,1,0:T(8,128)(2,1)S(1)}, u32[]{:S(2)}) copy-start(bf16[2,768,2048]{2,1,0:T(8,128)(2,1)S(1)} %unpack_slots.2) | copy-start | bytes 18874372
  206.9 3.7 copy-start.13
  258.9 86.4 %all-to-all-start.2 = ((bf16[128,16,1536]{2,1,0:T(8,128)(2,1)}), bf16[128,16,1536]{2,1,0:T(8,128)(2,1)}, u32[]{:S(2)}, u32[]{:S(2)}) async-start(bf16[128,16,1536]{2,1,0:T(8,128)(2,1)} %bitcast.71), calls=%async_computation.2 | async-start | bytes 12582912 | tf_op jit(solution)/shard_map/all_to_all | solution.py:1355
  274.5 7.6 %copy-start.27 = (bf16[2,2048,512]{2,1,0:T(8,128)(2,1)S(1)}, bf16[2,2048,512]{2,1,0:T(8,128)(2,1)}, u32[]{:S(2)}) copy-start(bf16[2,2048,512]{2,1,0:T(8,128)(2,1)} %param.25) | copy-start | bytes 12582916
  282.0 8.8 %copy-start.5 = (bf16[2,768,2048]{2,1,0:T(8,128)(2,1)}, bf16[2,768,2048]{2,1,0:T(8,128)(2,1)S(1)}, u32[]{:S(2)}) copy-start(bf16[2,768,2048]{2,1,0:T(8,128)(2,1)S(1)} %unpack_slots.3) | copy-start | bytes 18874372
  290.9 11.7 %copy-start.29 = (bf16[2,768,512]{2,1,0:T(8,128)(2,1)}, bf16[2,768,512]{2,1,0:T(8,128)(2,1)S(1)}, u32[]{:S(2)}) copy-start(bf16[2,768,512]{2,1,0:T(8,128)(2,1)S(1)} %get-tuple-element.112) | copy-start | bytes 4718596
  290.9 11.7 %copy-start.31 = (bf16[2,768,512]{2,1,0:T(8,128)(2,1)}, bf16[2,768,512]{2,1,0:T(8,128)(2,1)S(1)}, u32[]{:S(2)}) copy-start(bf16[2,768,512]{2,1,0:T(8,128)(2,1)S(1)} %get-tuple-element.113) | copy-start | bytes 4718596
  345.3 11.2 %copy-start.9 = (bf16[2,128,2048]{2,1,0:T(8,128)(2,1)S(1)}, bf16[2,128,2048]{2,1,0:T(8,128)(2,1)}, u32[]{:S(2)}) copy-start(bf16[2,128,2048]{2,1,0:T(8,128)(2,1)} %get-tuple-element.75) | copy-start | bytes 3145732
  345.3 86.8 %all-to-all-start.3 = ((bf16[128,16,1536]{2,1,0:T(8,128)(2,1)}), bf16[128,16,1536]{2,1,0:T(8,128)(2,1)}, u32[]{:S(2)}, u32[]{:S(2)}) async-start(bf16[128,16,1536]{2,1,0:T(8,128)(2,1)} %bitcast.70), calls=%async_computation.3 | async-start | bytes 12582912 | tf_op jit(solution)/shard_map/all_to_all | solution.py:1355
  356.5 3.8 copy-start.10
  356.5 5.1 copy-start.11
  380.8 11.6 %slice-start.2 = ((s8[6291456]{0:T(1024)(128)(4,1)}), s8[4194304]{0:T(1024)(128)(4,1)S(1)}, s32[]{:S(2)}) async-start(s8[6291456]{0:T(1024)(128)(4,1)} %bitcast.72), calls=%async_computation.6 | async-start | bytes 8388608
  382.3 10.1 %slice-start.3 = ((s8[6291456]{0:T(1024)(128)(4,1)}), s8[2097152]{0:T(1024)(128)(4,1)S(1)}, s32[]{:S(2)}) async-start(s8[6291456]{0:T(1024)(128)(4,1)} %bitcast.72), calls=%async_computation.7 | async-start | bytes 4194304
  382.3 10.1 %copy-start.30 = (bf16[2,768,512]{2,1,0:T(8,128)(2,1)S(1)}, bf16[2,768,512]{2,1,0:T(8,128)(2,1)}, u32[]{:S(2)}) copy-start(bf16[2,768,512]{2,1,0:T(8,128)(2,1)} %copy-done.29) | copy-start | bytes 4718596
  382.3 10.1 %copy-start.32 = (bf16[2,768,512]{2,1,0:T(8,128)(2,1)S(1)}, bf16[2,768,512]{2,1,0:T(8,128)(2,1)}, u32[]{:S(2)}) copy-start(bf16[2,768,512]{2,1,0:T(8,128)(2,1)} %copy-done.31) | copy-start | bytes 4718596
  382.3 20.6 %slice-start = ((s8[6291456]{0:T(1024)(128)(4,1)}), s8[4194304]{0:T(1024)(128)(4,1)S(1)}, s32[]{:S(2)}) async-start(s8[6291456]{0:T(1024)(128)(4,1)} %bitcast.68), calls=%async_computation.4 | async-start | bytes 8388608
  392.5 10.5 %slice-start.1 = ((s8[6291456]{0:T(1024)(128)(4,1)}), s8[2097152]{0:T(1024)(128)(4,1)S(1)}, s32[]{:S(2)}) async-start(s8[6291456]{0:T(1024)(128)(4,1)} %bitcast.68), calls=%async_computation.5 | async-start | bytes 4194304
  525.7 4.0 copy-start.18
  525.7 4.8 copy-start.25
  525.7 5.4 %copy-start.20 = (f32[64,512]{1,0:T(8,128)S(1)}, f32[64,512]{1,0:T(8,128)}, u32[]{:S(2)}) copy-start(f32[64,512]{1,0:T(8,128)} %get-tuple-element.139) | copy-start | bytes 393220
  525.8 6.0 %copy-start.22 = (f32[64,1,256]{2,1,0:T(1,128)S(1)}, f32[64,1,256]{2,1,0:T(1,128)}, u32[]{:S(2)}) copy-start(f32[64,1,256]{2,1,0:T(1,128)} %get-tuple-element.140) | copy-start | bytes 196612
  525.8 6.7 %copy-start.19 = (f32[64,512]{1,0:T(8,128)S(1)}, f32[64,512]{1,0:T(8,128)}, u32[]{:S(2)}) copy-start(f32[64,512]{1,0:T(8,128)} %get-tuple-element.141) | copy-start | bytes 393220
  528.6 4.5 copy-start.24
  528.6 5.1 copy-start.21
  528.6 5.7 %copy-start.23 = (f32[64,128]{1,0:T(8,128)S(1)}, f32[64,128]{1,0:T(8,128)}, u32[]{:S(2)}) copy-start(f32[64,128]{1,0:T(8,128)} %get-tuple-element.144) | copy-start | bytes 98308
  (9 other events, 25.1 us)

commit v9 on v8

--- a/solution.py
+++ b/solution.py
@@ -515,7 +515,6 @@
     router_part[...] = router_sum.astype(low).reshape(router_part.shape)
     router_scatter = RouterSum(router_part, router.at[row], scratch[router_at:])
     router_scatter.start()
-    shared_scatter.add_first()
     load_back.wait()
     near_rows[0].wait_recv()
     key_grad[...] = jnp.zeros_like(key_grad)
@@ -525,7 +524,7 @@
     chip = row // 2
     chip_rows = bias.shape[0]
     attention_back_rows(chip * chip_rows, refs, sums)
-    shared_scatter.add_second()
+    shared_scatter.add_first()
     router_scatter.add_y()
     far_rows[0].wait_recv()
     onward[0].start()
@@ -541,8 +540,9 @@
         rows = group[:, :, columns].reshape(4 * group.shape[1], width)
         keep(out_grads, block, outer_sum(rows, attended[...]))
     out_scatter.start()
+    attention_back_rows((1 - chip) * chip_rows, refs, sums)
     router_scatter.add_z()
-    attention_back_rows((1 - chip) * chip_rows, refs, sums)
+    shared_scatter.add_second()
     size = keys.shape[1]
     scale = size ** (-0.5)
     pre_grad[:, inner : inner + size] = turn(key_grad[...] * scale, cosine[...], -sine[...]).astype(
@@ -564,11 +564,6 @@
         keep(pre_grads, block, matmul(rows_t[rows], pre_grad[...]))
     pre_scatter.start()
     router_scatter.add_x()
-    out_scatter.add_first()
-    shared_scatter.add_third([share_sums.at[0], share_sums.at[1]])
-    share_low[0] = share_sums[1].astype(low)
-    share_copy = remote(share_low.at[0], share_low.at[1], row_sems, 5, (partner, col))
-    share_copy.start()
     router_scatter.spread_z()
 
     gain_sems = (gain_send, gain_recv)
@@ -599,6 +594,11 @@
     result[...] = factor * weighted - first * (factor * factor * factor * mean)
     values[0, 0:1] = jnp.sum(incoming * first * factor, axis=0, keepdims=True)
     start_gains(0)
+    out_scatter.add_first()
+    shared_scatter.add_third([share_sums.at[0], share_sums.at[1]])
+    share_low[0] = share_sums[1].astype(low)
+    share_copy = remote(share_low.at[0], share_low.at[1], row_sems, 5, (partner, col))
+    share_copy.start()
     router_scatter.spread_y()
     out_scatter.add_second()
     load_stream.wait()

time: 545 us -> 537 us (0.985)
  Pallas kernels: 234 us -> 226 us
    pallas_call x1, Pallas kernels: 93.5 us -> 85.5 us  [tail(): pl.pallas_call(tail_kernel, out_shape=[jax.ShapeDtypeStruct((rows, width)...]
where the time goes in v9:
time: 537 us; the launch traced here: 527 us
  Pallas kernels  226 us (42%)
  waiting for transfers between devices  151 us (28%)
  matrix products  76 us (14%)
  starting transfers between devices  37.6 us (7%)
  local copies, waits for them, and re-layouts  26.9 us (5%)
  other arithmetic  7.58 us (1%)
    all_to_all x4, waiting for transfers between devices, exchange(): lax.all_to_all(pairs, ('row', 'col'), split_axis=0, concat_axis=0, tiled=...  151 us
    pallas_call x1, Pallas kernels, head(): pl.pallas_call(head_kernel, out_shape=[full((2, 4, 4, shard_rows, pre_wid...  88.7 us
    pallas_call x1, Pallas kernels, tail(): pl.pallas_call(tail_kernel, out_shape=[jax.ShapeDtypeStruct((rows, width)...  85.5 us
    all_to_all x4, starting transfers between devices, exchange(): lax.all_to_all(pairs, ('row', 'col'), split_axis=0, concat_axis=0, tiled=...  37.6 us
    unnamed x84, local copies, waits for them, and re-layouts  20.1 us
    pallas_call x2, Pallas kernels, unpack_slots(): pl.pallas_call(unpack_slots_kernel, grid=(blocks,), out_shape=jax.ShapeDt...  14.9 us
    dot_general x1, matrix products, per_device(): jnp.einsum('esf,edf->esd', expert_pre_grad, w_expert_in, preferred_elemen...  11.7 us
    dot_general x1, matrix products, per_device(): jnp.einsum('esd,edf->esf', expert_in, w_expert_in, preferred_element_type...  11.3 us
  transfers between devices with their start and end apart: 4, of which 4 were waited for; matrix products, arithmetic and copies ran while one was open for 16% of the time, Pallas kernels for 10%

profile of v9, /device:TPU:1, one launch (start us, length us, event | category | flops | bytes accessed | tf_op | source)
XLA Modules:
  0.0 527.4 jit_solution(15567069155246976606)
XLA Ops:
  3.6 88.7 %head.1 = (bf16[2,4,4,64,768]{4,3,2,1,0:T(8,128)(2,1)}, bf16[2,4,4,64,512]{4,3,2,1,0:T(8,128)(2,1)}, bf16[2,4,4,64,768]{4,3,2,1,0:T(8,128)(2,1)}, bf16[4,128,204...) custom-call(bf16[128,2048]{1,0:T(8,128)(2,1)} %bitcast.105, ...), custom_call_target="tpu_custom_call" | custom-call | bytes 314572800 | tf_op jit(solution)/shard_map/head/pallas_call | solution.py:1270
  92.3 4.9 all-to-all-start
  98.0 6.8 %pack_tokens.1.grads = bf16[2048,1536]{1,0:T(8,128)(2,1)S(1)} custom-call(bf16[8,32,128]{2,1,0:T(8,128)(2,1)S(1)} %copy-done.7, bf16[128,2048]{1,0:T(8,128)(2,1)S(1)} %bitcast.76, bf16[8,32,128]{2,1,0:T(8,128)(2,1)S(1)} %bitcast.80, bf16[8,32,128]{2,1,0:T(8,128)(2,1)S(1)} %bitcast.78), custom_call_target="tpu_custom_call" | custom-call | flops 3221225472 | bytes 8388608 | tf_op jit(solution)/shard_map/pack_tokens/pallas_call | solution.py:791
  104.8 2.7 copy-done.1
  107.5 64.9 %all-to-all-done = bf16[128,16,1536]{2,1,0:T(8,128)(2,1)} async-done(((bf16[128,16,1536]{2,1,0:T(8,128)(2,1)}), bf16[128,16,1536]{2,1,0:T(8,128)(2,1)}, u32[]{:S(2)}, u32[]{:S(2)}) %all-to-all-start) | async-done | bytes 6291488 | tf_op jit(solution)/shard_map/all_to_all | solution.py:1355
  172.5 10.8 %all-to-all-start.1 = ((bf16[128,16,1536]{2,1,0:T(8,128)(2,1)}), bf16[128,16,1536]{2,1,0:T(8,128)(2,1)}, u32[]{:S(2)}, u32[]{:S(2)}) async-start(bf16[128,16,1536]{2,1,0:T(8,128)(2,1)} %bitcast.67), calls=%async_computation.1 | async-start | bytes 12582912 | tf_op jit(solution)/shard_map/all_to_all | solution.py:1355
  183.3 7.4 %unpack_slots.2 = bf16[2,768,2048]{2,1,0:T(8,128)(2,1)S(1)} custom-call(bf16[2048,1536]{1,0:T(8,128)(2,1)} %bitcast.10.packed), custom_call_target="tpu_custom_call" | custom-call | flops 2415919104 | bytes 14680064 | tf_op jit(solution)/shard_map/unpack_slots/pallas_call | solution.py:832
  190.7 11.3 %fusion.33 = f32[2,768,1024]{2,1,0:T(8,128)S(1)} fusion(bf16[2,768,2048]{2,1,0:T(8,128)(2,1)S(1)} %unpack_slots.2, bf16[2,2048,1024]{2,1,0:T(8,128)(2,1)} %param.24), kind=kOutput, calls=%fused_computation.64 | convolution fusion | flops 6442450944 | bytes 20971520 | tf_op jit(solution)/shard_map/esd,edf->esf/dot_general | solution.py:1453
  202.0 2.7 copy-done.8
  206.9 3.7 convolution_convert_fusion.1.values
  210.6 5.4 %pack_slots.2 = bf16[2048,1536]{1,0:T(8,128)(2,1)S(1)} custom-call(bf16[2,768,2048]{2,1,0:T(8,128)(2,1)S(1)} %convolution_convert_fusion.1.values), custom_call_target="tpu_custom_call" | custom-call | flops 2415919104 | bytes 14680064 | tf_op jit(solution)/shard_map/pack_slots/pallas_call | solution.py:861
  216.1 2.7 copy-done.3
  218.8 40.1 %all-to-all-done.1 = bf16[128,16,1536]{2,1,0:T(8,128)(2,1)} async-done(((bf16[128,16,1536]{2,1,0:T(8,128)(2,1)}), bf16[128,16,1536]{2,1,0:T(8,128)(2,1)}, u32[]{:S(2)}, u32[]{:S(2)}) %all-to-all-start.1) | async-done | bytes 6291488 | tf_op jit(solution)/shard_map/all_to_all | solution.py:1355
  258.9 10.8 %all-to-all-start.2 = ((bf16[128,16,1536]{2,1,0:T(8,128)(2,1)}), bf16[128,16,1536]{2,1,0:T(8,128)(2,1)}, u32[]{:S(2)}, u32[]{:S(2)}) async-start(bf16[128,16,1536]{2,1,0:T(8,128)(2,1)} %bitcast.71), calls=%async_computation.2 | async-start | bytes 12582912 | tf_op jit(solution)/shard_map/all_to_all | solution.py:1355
  270.6 3.9 copy.55
  274.5 7.6 %unpack_slots.3 = bf16[2,768,2048]{2,1,0:T(8,128)(2,1)S(1)} custom-call(bf16[2048,1536]{1,0:T(8,128)(2,1)} %bitcast.12.packed), custom_call_target="tpu_custom_call" | custom-call | flops 2415919104 | bytes 14680064 | tf_op jit(solution)/shard_map/unpack_slots/pallas_call | solution.py:832
  282.1 8.8 %multiply_convert_fusion.1 = (bf16[2,768,512]{2,1,0:T(8,128)(2,1)S(1)}, bf16[2,768,512]{2,1,0:T(8,128)(2,1)S(1)}) fusion(f32[2,768,1024]{2,1,0:T(8,128)} %copy-done.8, bf16[2,768,2048]{2,1,0:T(8,128)(2,1)S(1)} %unpack_slots.3, bf16[2,2048,512]{2,1,0:T(8,128)(2,1)S(1)} %copy-done.27), kind=kOutput, calls=%fused_computation.4 | convolution fusion | flops 3231449088 | bytes 19922944 | tf_op jit(solution)/shard_map/esd,edf->esf/dot_general | solution.py:1465
  290.9 11.7 %convolution_convert_fusion.values = bf16[2,768,2048]{2,1,0:T(8,128)(2,1)S(1)} fusion(bf16[2,2048,1024]{2,1,0:T(8,128)(2,1)} %param.24, bf16[2,768,512]{2,1,0:T(8,128)(2,1)S(1)} %get-tuple-element.113, bf16[2,768,512]{2,1,0:T(8,128)(2,1)S(1)} %get-tuple-element.112), kind=kOutput, calls=%fused_computation | convolution fusion | flops 6451888128 | bytes 17825792 | tf_op jit(solution)/shard_map/esf,edf->esd/dot_general | solution.py:1471
  302.6 5.4 %pack_slots.3 = bf16[2048,1536]{1,0:T(8,128)(2,1)S(1)} custom-call(bf16[2,768,2048]{2,1,0:T(8,128)(2,1)S(1)} %convolution_convert_fusion.values), custom_call_target="tpu_custom_call" | custom-call | flops 2415919104 | bytes 14680064 | tf_op jit(solution)/shard_map/pack_slots/pallas_call | solution.py:861
  308.0 2.6 copy-done.2
  310.7 34.7 %all-to-all-done.2 = bf16[128,16,1536]{2,1,0:T(8,128)(2,1)} async-done(((bf16[128,16,1536]{2,1,0:T(8,128)(2,1)}), bf16[128,16,1536]{2,1,0:T(8,128)(2,1)}, u32[]{:S(2)}, u32[]{:S(2)}) %all-to-all-start.2) | async-done | bytes 6291488 | tf_op jit(solution)/shard_map/all_to_all | solution.py:1355
  345.3 11.2 %all-to-all-start.3 = ((bf16[128,16,1536]{2,1,0:T(8,128)(2,1)}), bf16[128,16,1536]{2,1,0:T(8,128)(2,1)}, u32[]{:S(2)}, u32[]{:S(2)}) async-start(bf16[128,16,1536]{2,1,0:T(8,128)(2,1)} %bitcast.70), calls=%async_computation.3 | async-start | bytes 12582912 | tf_op jit(solution)/shard_map/all_to_all | solution.py:1355
  356.5 1.9 fusion.13
  366.8 3.8 side_by_side.1
  370.6 5.4 %all_marks.1.marks_in = bf16[4,128,2048]{2,1,0:T(8,128)(2,1)} custom-call(bf16[8,128,32]{2,1,0:T(8,128)(2,1)} %bitcast.109), custom_call_target="tpu_custom_call" | custom-call | flops 67108864 | bytes 4194304 | tf_op jit(solution)/shard_map/all_marks/pallas_call | solution.py:890
  382.3 10.1 %fusion.34 = f32[2,2048,512]{2,1,0:T(8,128)} fusion(bf16[2,768,2048]{2,1,0:T(8,128)(2,1)} %copy-done.5, bf16[2,768,512]{2,1,0:T(8,128)(2,1)S(1)} %copy-done.14), kind=kOutput, calls=%fused_computation.65 | convolution fusion | flops 3221225472 | bytes 16252928 | tf_op jit(solution)/shard_map/esd,esf->edf/dot_general | solution.py:1476
  392.5 10.4 %fusion.3 = f32[2,2048,1024]{2,1,0:T(8,128)} fusion(bf16[2,768,2048]{2,1,0:T(8,128)(2,1)S(1)} %bitcast.73, bf16[2,768,512]{2,1,0:T(8,128)(2,1)S(1)} %copy-done.32, bf16[2,768,512]{2,1,0:T(8,128)(2,1)S(1)} %copy-done.30), kind=kOutput, calls=%fused_computation.17 | convolution fusion | flops 6448742400 | bytes 26214400 | tf_op jit(solution)/shard_map/esd,esf->edf/dot_general | solution.py:1479
  402.9 10.4 %sum_gated.1 = (f32[128,2048]{1,0:T(8,128)S(1)}, f32[8,128,32]{2,1,0:T(8,128)S(1)}) custom-call(bf16[8,32,128]{2,1,0:T(8,128)(2,1)S(1)} %copy-done.7, bf16[2048,1536]{1,0:T(8,128)(2,1)} %bitcast.14.packed, bf16[2048,1536]{1,0:T(8,128)(2,1)S(1)} %bitcast.69, bf16[8,32,128]{2,1,0:T(8,128)(2,1)S(1)} %bitcast.81, bf16[8,32,128]{2,1,0:T(8,128)(2,1)S(1)} %bitcast.79), custom_call_target="tpu_custom_call" | custom-call | flops 3221225472 | bytes 14680064 | tf_op jit(solution)/shard_map/sum_gated/pallas_call | solution.py:936
  415.3 2.3 add.36.stream_in
  420.6 11.5 %all-to-all-done.3 = bf16[128,16,1536]{2,1,0:T(8,128)(2,1)} async-done(((bf16[128,16,1536]{2,1,0:T(8,128)(2,1)}), bf16[128,16,1536]{2,1,0:T(8,128)(2,1)}, u32[]{:S(2)}, u32[]{:S(2)}) %all-to-all-start.3) | async-done | bytes 6291488 | tf_op jit(solution)/shard_map/all_to_all | solution.py:1355
  432.2 85.5 %tail.1 = (f32[128,2048]{1,0:T(8,128)}, f32[128,2048]{1,0:T(8,128)}, bf16[128,2048]{1,0:T(8,128)(2,1)}, bf16[4,2,4,4,16,256]{5,4,3,2,1,0:T(8,128)(2,1)}, f32[1,2...) custom-call(bf16[2048,1536]{1,0:T(8,128)(2,1)} %bitcast.16.packed, ...), custom_call_target="tpu_custom_call" | custom-call | bytes 314572800 | tf_op jit(solution)/shard_map/tail/pallas_call | solution.py:664
  517.8 2.9 bitcast_convert_fusion
  (105 shorter events, 32.7 us)
Async XLA Ops:
  0.6 96.6 %copy-start = (bf16[2048,256]{1,0:T(8,128)(2,1)S(1)}, bf16[2048,256]{1,0:T(8,128)(2,1)}, u32[]{:S(2)}) copy-start(bf16[2048,256]{1,0:T(8,128)(2,1)} %param.23) | copy-start | bytes 3145732
  92.3 4.9 copy-start.17
  92.3 4.9 copy-start.28
  92.3 5.7 %copy-start.6 = (bf16[1,128,2048]{2,1,0:T(8,128)(2,1)S(1)}, bf16[1,128,2048]{2,1,0:T(8,128)(2,1)}, u32[]{:S(2)}) copy-start(bf16[1,128,2048]{2,1,0:T(8,128)(2,1)} %param.28) | copy-start | bytes 1572868
  92.3 5.7 %copy-start.7 = (bf16[8,32,128]{2,1,0:T(8,128)(2,1)S(1)}, bf16[8,32,128]{2,1,0:T(8,128)(2,1)}, u32[]{:S(2)}) copy-start(bf16[8,32,128]{2,1,0:T(8,128)(2,1)} %get-tuple-element.62.code) | copy-start | bytes 196612
  92.3 80.1 %all-to-all-start = ((bf16[128,16,1536]{2,1,0:T(8,128)(2,1)}), bf16[128,16,1536]{2,1,0:T(8,128)(2,1)}, u32[]{:S(2)}, u32[]{:S(2)}) async-start(bf16[128,16,1536]{2,1,0:T(8,128)(2,1)} %bitcast.84), calls=%async_computation | async-start | bytes 12582912 | tf_op jit(solution)/shard_map/all_to_all | solution.py:1355
  172.5 86.4 %all-to-all-start.1 = ((bf16[128,16,1536]{2,1,0:T(8,128)(2,1)}), bf16[128,16,1536]{2,1,0:T(8,128)(2,1)}, u32[]{:S(2)}, u32[]{:S(2)}) async-start(bf16[128,16,1536]{2,1,0:T(8,128)(2,1)} %bitcast.67), calls=%async_computation.1 | async-start | bytes 12582912 | tf_op jit(solution)/shard_map/all_to_all | solution.py:1355
  190.7 11.4 %copy-start.4 = (bf16[2,768,2048]{2,1,0:T(8,128)(2,1)}, bf16[2,768,2048]{2,1,0:T(8,128)(2,1)S(1)}, u32[]{:S(2)}) copy-start(bf16[2,768,2048]{2,1,0:T(8,128)(2,1)S(1)} %unpack_slots.2) | copy-start | bytes 18874372
  206.9 3.7 copy-start.13
  258.9 86.4 %all-to-all-start.2 = ((bf16[128,16,1536]{2,1,0:T(8,128)(2,1)}), bf16[128,16,1536]{2,1,0:T(8,128)(2,1)}, u32[]{:S(2)}, u32[]{:S(2)}) async-start(bf16[128,16,1536]{2,1,0:T(8,128)(2,1)} %bitcast.71), calls=%async_computation.2 | async-start | bytes 12582912 | tf_op jit(solution)/shard_map/all_to_all | solution.py:1355
  274.5 7.6 %copy-start.27 = (bf16[2,2048,512]{2,1,0:T(8,128)(2,1)S(1)}, bf16[2,2048,512]{2,1,0:T(8,128)(2,1)}, u32[]{:S(2)}) copy-start(bf16[2,2048,512]{2,1,0:T(8,128)(2,1)} %param.25) | copy-start | bytes 12582916
  282.0 8.8 %copy-start.5 = (bf16[2,768,2048]{2,1,0:T(8,128)(2,1)}, bf16[2,768,2048]{2,1,0:T(8,128)(2,1)S(1)}, u32[]{:S(2)}) copy-start(bf16[2,768,2048]{2,1,0:T(8,128)(2,1)S(1)} %unpack_slots.3) | copy-start | bytes 18874372
  290.9 11.7 %copy-start.29 = (bf16[2,768,512]{2,1,0:T(8,128)(2,1)}, bf16[2,768,512]{2,1,0:T(8,128)(2,1)S(1)}, u32[]{:S(2)}) copy-start(bf16[2,768,512]{2,1,0:T(8,128)(2,1)S(1)} %get-tuple-element.112) | copy-start | bytes 4718596
  290.9 11.7 %copy-start.31 = (bf16[2,768,512]{2,1,0:T(8,128)(2,1)}, bf16[2,768,512]{2,1,0:T(8,128)(2,1)S(1)}, u32[]{:S(2)}) copy-start(bf16[2,768,512]{2,1,0:T(8,128)(2,1)S(1)} %get-tuple-element.113) | copy-start | bytes 4718596
  345.3 11.2 %copy-start.9 = (bf16[2,128,2048]{2,1,0:T(8,128)(2,1)S(1)}, bf16[2,128,2048]{2,1,0:T(8,128)(2,1)}, u32[]{:S(2)}) copy-start(bf16[2,128,2048]{2,1,0:T(8,128)(2,1)} %get-tuple-element.75) | copy-start | bytes 3145732
  345.3 86.8 %all-to-all-start.3 = ((bf16[128,16,1536]{2,1,0:T(8,128)(2,1)}), bf16[128,16,1536]{2,1,0:T(8,128)(2,1)}, u32[]{:S(2)}, u32[]{:S(2)}) async-start(bf16[128,16,1536]{2,1,0:T(8,128)(2,1)} %bitcast.70), calls=%async_computation.3 | async-start | bytes 12582912 | tf_op jit(solution)/shard_map/all_to_all | solution.py:1355
  356.5 3.8 copy-start.10
  356.5 5.1 copy-start.11
  380.8 11.6 %slice-start.2 = ((s8[6291456]{0:T(1024)(128)(4,1)}), s8[4194304]{0:T(1024)(128)(4,1)S(1)}, s32[]{:S(2)}) async-start(s8[6291456]{0:T(1024)(128)(4,1)} %bitcast.72), calls=%async_computation.6 | async-start | bytes 8388608
  382.3 10.1 %slice-start.3 = ((s8[6291456]{0:T(1024)(128)(4,1)}), s8[2097152]{0:T(1024)(128)(4,1)S(1)}, s32[]{:S(2)}) async-start(s8[6291456]{0:T(1024)(128)(4,1)} %bitcast.72), calls=%async_computation.7 | async-start | bytes 4194304
  382.3 10.1 %copy-start.30 = (bf16[2,768,512]{2,1,0:T(8,128)(2,1)S(1)}, bf16[2,768,512]{2,1,0:T(8,128)(2,1)}, u32[]{:S(2)}) copy-start(bf16[2,768,512]{2,1,0:T(8,128)(2,1)} %copy-done.29) | copy-start | bytes 4718596
  382.3 10.1 %copy-start.32 = (bf16[2,768,512]{2,1,0:T(8,128)(2,1)S(1)}, bf16[2,768,512]{2,1,0:T(8,128)(2,1)}, u32[]{:S(2)}) copy-start(bf16[2,768,512]{2,1,0:T(8,128)(2,1)} %copy-done.31) | copy-start | bytes 4718596
  382.3 20.6 %slice-start = ((s8[6291456]{0:T(1024)(128)(4,1)}), s8[4194304]{0:T(1024)(128)(4,1)S(1)}, s32[]{:S(2)}) async-start(s8[6291456]{0:T(1024)(128)(4,1)} %bitcast.68), calls=%async_computation.4 | async-start | bytes 8388608
  392.5 10.5 %slice-start.1 = ((s8[6291456]{0:T(1024)(128)(4,1)}), s8[2097152]{0:T(1024)(128)(4,1)S(1)}, s32[]{:S(2)}) async-start(s8[6291456]{0:T(1024)(128)(4,1)} %bitcast.68), calls=%async_computation.5 | async-start | bytes 4194304
  517.7 4.0 copy-start.18
  517.7 4.8 copy-start.25
  517.7 5.4 %copy-start.20 = (f32[64,512]{1,0:T(8,128)S(1)}, f32[64,512]{1,0:T(8,128)}, u32[]{:S(2)}) copy-start(f32[64,512]{1,0:T(8,128)} %get-tuple-element.139) | copy-start | bytes 393220
  517.8 6.0 %copy-start.22 = (f32[64,1,256]{2,1,0:T(1,128)S(1)}, f32[64,1,256]{2,1,0:T(1,128)}, u32[]{:S(2)}) copy-start(f32[64,1,256]{2,1,0:T(1,128)} %get-tuple-element.140) | copy-start | bytes 196612
  517.8 6.7 %copy-start.19 = (f32[64,512]{1,0:T(8,128)S(1)}, f32[64,512]{1,0:T(8,128)}, u32[]{:S(2)}) copy-start(f32[64,512]{1,0:T(8,128)} %get-tuple-element.141) | copy-start | bytes 393220
  520.6 4.5 copy-start.24
  520.6 5.1 copy-start.21
  520.6 5.7 %copy-start.23 = (f32[64,128]{1,0:T(8,128)S(1)}, f32[64,128]{1,0:T(8,128)}, u32[]{:S(2)}) copy-start(f32[64,128]{1,0:T(8,128)} %get-tuple-element.144) | copy-start | bytes 98308
  (9 other events, 25.1 us)
